TPU v7x, 32 devices: a whole 2x2x4 slice. The times are simulated.
32 devices in a mesh: groups: 2 (over y), tensor: 4 (over z), batch: 4 (over x, core).
Axes of the slice: x: 2, y: 2, z: 4, core: 2. Of those that a mesh axis runs over, the one named last changes fastest.
Arguments:
- queries: bfloat16 [256, 32, 128], P(('groups', 'batch'), 'tensor'), parts along dimension 0
- key_cache: bfloat16 [256, 4, 96, 128], P(('groups', 'batch')), parts along dimension 0
- value_cache: bfloat16 [256, 4, 96, 128], P(('groups', 'batch')), parts along dimension 0, may hold values from -6 to 6
- new_key: bfloat16 [256, 4, 128], P(('groups', 'batch')), parts along dimension 0, may hold values from -6 to 6
- new_value: bfloat16 [256, 4, 128], P(('groups', 'batch')), parts along dimension 0, may hold values from -6 to 6
- lengths: int32 [256], P(('groups', 'batch')), parts along dimension 0, may hold values from 1 to 96
- out_weight: bfloat16 [4096, 8192], P('tensor'), may hold values from -0.09375 to 0.09375
- shrink_weight: bfloat16 [16, 4096, 64], P('batch', 'tensor'), may hold values from -0.09375 to 0.09375
- expand_weight: bfloat16 [16, 64, 8192], P('batch', None, 'tensor'), may hold values from -0.75 to 0.75
- adapter_rank: int32 [16], P('batch'), may hold values from 8 to 64
- adapter_list: int32 [64], P(('groups', 'batch')), parts along dimension 0, may hold values from 0 to 15, as said below
- row_adapter: int32 [256], P(('groups', 'batch')), parts along dimension 0, may hold values from 0 to 7
Outputs:
- mixed: bfloat16 [256, 8192], P(('groups', 'batch'), 'tensor'), parts along dimension 0
There are 2 independent parts, one for each index of `groups`. A program takes and returns all parts, laid end to end along the dimension named above; an argument that names none is the same for every part. Nothing has to cross between parts.
Inputs may be any that keep to these rules, and one draw needn't show every extreme that they name: `adapter_list`: the 8 ids of one batch group are distinct; at most 2 of them lie among the ids b * 4 to (b + 1) * 4 - 1 of any one batch index b, and in every group exactly 2 lie on some index.
All inputs are finite; a program needn't handle non-finite values.
Results may differ from a plain program's by a relative error of at most 0.0075.
Values may be sent and summed in bfloat16 or wider, within the bound.
No kernel may reach another device: no remote copies, remote signals or barrier semaphores. Data moves between devices by JAX's collectives and lax.ppermute only.
A program may use at most 128 MiB of HBM per device.

v0:
```python
import jax
import jax.numpy as jnp
from jax import lax
from jax.sharding import PartitionSpec as P

HQ = 32
KVH = 4


def attend(queries, key_cache, value_cache, new_key, new_value, lengths):
    row_count, head_count, head_width = queries.shape
    per_group = HQ // KVH
    kv_local = max(1, head_count // per_group)
    first_group = lax.axis_index("tensor") * head_count // per_group
    key_local = lax.dynamic_slice_in_dim(key_cache, first_group, kv_local, 1)
    value_local = lax.dynamic_slice_in_dim(value_cache, first_group, kv_local, 1)
    newkey_local = lax.dynamic_slice_in_dim(new_key, first_group, kv_local, 1)
    newvalue_local = lax.dynamic_slice_in_dim(new_value, first_group, kv_local, 1)
    positions = key_cache.shape[2]
    score_scale = head_width ** (-0.5)
    grouped = queries.reshape(row_count, kv_local, head_count // kv_local, head_width)
    scores = (
        jnp.einsum("rgqd,rgpd->rgqp", grouped, key_local, preferred_element_type=jnp.float32)
        * score_scale
    )
    fresh = (
        jnp.einsum("rgqd,rgd->rgq", grouped, newkey_local, preferred_element_type=jnp.float32)
        * score_scale
    )
    valid = jnp.arange(positions)[None, :] < lengths[:, None]
    masked = jnp.where(valid[:, None, None, :], scores, jnp.float32(-1e30))
    highest = jnp.maximum(jnp.max(masked, axis=-1), fresh)
    cached_exp = jnp.where(
        valid[:, None, None, :], jnp.exp(masked - highest[..., None]), jnp.float32(0.0)
    )
    fresh_exp = jnp.exp(fresh - highest)
    totals = jnp.sum(cached_exp, axis=-1) + fresh_exp
    cached_w = (cached_exp / totals[..., None]).astype(jnp.bfloat16)
    fresh_w = (fresh_exp / totals).astype(jnp.bfloat16)
    attended = jnp.einsum(
        "rgqp,rgpd->rgqd", cached_w, value_local, preferred_element_type=jnp.float32
    )
    attended = (
        attended
        + fresh_w.astype(jnp.float32)[..., None] * newvalue_local.astype(jnp.float32)[:, :, None, :]
    )
    return attended.astype(jnp.bfloat16).reshape(row_count, head_count * head_width)


def local(
    queries,
    key_cache,
    value_cache,
    new_key,
    new_value,
    lengths,
    out_weight,
    shrink_weight,
    expand_weight,
    adapter_rank,
    adapter_list,
    row_adapter,
):
    attended = attend(queries, key_cache, value_cache, new_key, new_value, lengths)
    row_count = attended.shape[0]
    rank_width = shrink_weight.shape[2]
    needed = adapter_list.shape[0]
    keep_cols = (jnp.arange(rank_width)[None, :] < adapter_rank[:, None]).astype(jnp.bfloat16)
    masked_shrink = shrink_weight * keep_cols[:, None, :]
    every_shrink, every_expand = (
        lax.all_gather(masked_shrink, "batch", axis=0, tiled=True),
        lax.all_gather(expand_weight, "batch", axis=0, tiled=True),
    )
    page_shrink = jnp.take(every_shrink, adapter_list, axis=0)
    page_expand = jnp.take(every_expand, adapter_list, axis=0)
    slot_hot = row_adapter[:, None] == jnp.arange(needed)[None, :]
    shrink_terms = jnp.einsum(
        "rq,nqk->rnk", attended, page_shrink, preferred_element_type=jnp.float32
    )
    shrink_part = jnp.sum(jnp.where(slot_hot[:, :, None], shrink_terms, jnp.float32(0.0)), axis=1)
    shrink_total = lax.psum(shrink_part, "tensor")
    base = lax.psum_scatter(
        lax.dot_general(
            out_weight, attended, (((0,), (1,)), ((), ())), preferred_element_type=jnp.float32
        ),
        "tensor",
        scatter_dimension=0,
        tiled=True,
    ).T
    shrink = shrink_total.astype(jnp.bfloat16)
    spread = (slot_hot.astype(jnp.bfloat16)[:, :, None] * shrink[:, None, :]).reshape(
        row_count, needed * rank_width
    )
    delta = jnp.dot(
        spread,
        page_expand.reshape(needed * rank_width, page_expand.shape[2]),
        preferred_element_type=jnp.float32,
    )
    return (base + delta).astype(jnp.bfloat16)


def solution(mesh):
    placed = (
        P(("groups", "batch"), "tensor", None),
        P(("groups", "batch"), None, None, None),
        P(("groups", "batch"), None, None, None),
        P(("groups", "batch"), None, None),
        P(("groups", "batch"), None, None),
        P(("groups", "batch")),
        P("tensor", None),
        P("batch", "tensor", None),
        P("batch", None, "tensor"),
        P("batch"),
        P(("groups", "batch")),
        P(("groups", "batch")),
    )
    return jax.shard_map(
        local,
        mesh=mesh,
        in_specs=placed,
        out_specs=P(("groups", "batch"), "tensor"),
        check_vma=False,
    )
```

profile of v0, /device:TPU:0, one launch (start us, length us, event | category | flops | bytes accessed | tf_op | source)
XLA Modules:
  0.0 86.4 jit_solution(596378808429750091)
XLA Ops:
  7.4 0.0 copy-start
  7.4 0.0 copy-start.2
  7.4 0.0 copy-start.3
  7.4 0.0 copy-start.4
  7.4 0.0 copy-start.1
  7.4 0.0 all-gather.3.cloned.1.call-start
  7.4 0.9 %fusion.30 = bf16[4,64]{1,0:T(4,128)(2,1)S(1)} fusion(s32[4]{0:T(128)} %param.21), kind=kLoop, calls=%fused_computation.50 | loop fusion | flops 512 | bytes 528 | tf_op jit(solution)/shard_map/convert_element_type | solution.py:68
  8.3 2.0 %broadcast_multiply_fusion = bf16[4,1024,64]{1,2,0:T(8,128)(2,1)} fusion(bf16[4,1024,64]{1,2,0:T(8,128)(2,1)} %param.19, bf16[4,64]{1,0:T(4,128)(2,1)S(1)} %fusion.30), kind=kLoop, calls=%fused_computation.23 | loop fusion | flops 262144 | bytes 1049088 | tf_op jit(solution)/shard_map/mul | solution.py:69
  10.3 0.0 all-gather.3.cloned.1.call-update
  10.3 0.0 all-gather.5.cloned.1.call-start
  10.4 0.7 all-gather.5.cloned.1.call-update
  11.1 0.0 reduce-scatter.2.cloned.1.call-start
  11.2 0.0 copy-done.2
  11.2 0.0 copy-done.3
  11.2 0.0 copy-done.4
  11.3 0.1 iota_compare_fusion
  11.3 0.0 copy-done.1
  11.3 0.1 fusion.26
  11.5 1.7 %fusion.37 = (f32[32,8]{1,0:T(8,128)S(1)}, f32[32,8,96]{2,1,0:T(8,128)S(1)}) fusion(bf16[32,8,128]{2,1,0:T(8,128)(2,1)S(1)} %copy-done.1, bf16[32,4,96,128]{3,2,1,0:T(8,128)(2,1)} %param.13, s32[]{:T(128)S(6)} %select_n.43, pred[32,96]{1,0:T(8,128)(4,1)S(1)} %iota_compare_fusion), kind=kOutput, calls=%fused_computation.59 | convolution fusion | flops 6364928 | bytes 954372 | tf_op jit(solution)/shard_map/rgqd,rgpd->rgqp/dot_general | solution.py:23
  13.2 0.2 fusion.16
  13.5 0.0 copy-done
  13.5 0.4 fusion.6
  13.9 0.0 copy-start.6
  13.9 0.0 copy-start.5
  13.9 9.9 %convolution_bitcast_fusion = f32[8192,32]{0,1:T(8,128)} fusion(bf16[1024,8192]{1,0:T(8,128)(2,1)} %param.18, bf16[4,8,8,128]{3,2,1,0:T(8,128)(2,1)S(1)} %bitcast.35), kind=kOutput, calls=%fused_computation.2 | convolution fusion | flops 536870912 | bytes 17891328 | tf_op jit(solution)/shard_map/dot_general | solution.py:83
  23.8 0.0 reduce-scatter.2.cloned.1.call-update
  23.8 0.0 copy-done.6
  23.9 0.0 copy-done.5
  23.9 11.9 %all-gather.3.cloned.1.call-done = bf16[16,1024,64]{1,2,0:T(8,128)(2,1)} async-done(((bf16[4,1024,64]{1,2,0:T(8,128)(2,1)}), bf16[16,1024,64]{1,2,0:T(8,128)(2,1)}) %all-gather.3.cloned.1.call-update) | async-done | bytes 2097168 | tf_op jit(solution)/shard_map/all_gather | solution.py:71
  35.8 3.2 %gather_fusion = bf16[8,1024,64]{1,2,0:T(8,128)(2,1)} fusion(bf16[16,1024,64]{1,2,0:T(8,128)(2,1)} %all-gather.3.cloned.1.call-done, s32[1024]{0:T(1024)S(1)} %pad_clamp_fusion), kind=kCustom, calls=%fused_computation | custom fusion | bytes 2097184 | tf_op jit(solution)/shard_map/jit(_take)/gather | solution.py:74
  39.0 1.9 %fusion.7 = f32[32,64]{1,0:T(8,128)S(1)} fusion(bf16[32,1024,1]{1,0,2:T(8,128)(2,1)S(1)} %reshape.172, bf16[8,1024,64]{1,2,0:T(8,128)(2,1)} %gather_fusion, pred[8]{0:T(512)(128)(4,1)S(1)} %compare_and_fusion, pred[32,8]{0,1:T(8,128)(4,1)S(1)} %get-tuple-element.8), kind=kOutput, calls=%fused_computation.14 | convolution fusion | flops 34109440 | bytes 1122568 | tf_op jit(solution)/shard_map/rq,nqk->rnk/dot_general | solution.py:77
  40.9 19.1 %psum.7 = bf16[32,64]{1,0:T(8,128)(2,1)S(1)} all-reduce(f32[32,64]{1,0:T(8,128)S(1)} %fusion.7), channel_id=1, replica_groups=mesh['groups'=2,'tensor'=4,'batch'=4] {'tensor'}, use_global_device_ids=true, to_apply=%region_4.5 | all-reduce | flops 2048 | bytes 12288 | tf_op jit(solution)/shard_map/psum | solution.py:81
  60.0 11.9 %all-gather.5.cloned.1.call-done = bf16[16,64,2048]{2,1,0:T(8,128)(2,1)} async-done(((bf16[4,64,2048]{2,1,0:T(8,128)(2,1)}), bf16[16,64,2048]{2,1,0:T(8,128)(2,1)}) %all-gather.5.cloned.1.call-update) | async-done | bytes 4194320 | tf_op jit(solution)/shard_map/all_gather | solution.py:72
  71.9 4.2 %gather_fusion.1 = bf16[8,64,2048]{2,1,0:T(8,128)(2,1)} fusion(bf16[16,64,2048]{2,1,0:T(8,128)(2,1)} %all-gather.5.cloned.1.call-done, s32[1024]{0:T(1024)S(1)} %pad_clamp_fusion), kind=kCustom, calls=%fused_computation.1 | custom fusion | bytes 4194336 | tf_op jit(solution)/shard_map/jit(_take)/gather | solution.py:75
  76.1 0.0 reduce-scatter.2.cloned.1.call-done
  76.1 2.8 %fusion.1 = bf16[32,2048]{1,0:T(8,128)(2,1)} fusion(bf16[8,64,2048]{2,1,0:T(8,128)(2,1)} %gather_fusion.1, pred[8]{0:T(512)(128)(4,1)S(1)} %compare_and_fusion, f32[2048,32]{0,1:T(8,128)} %reduce-scatter.2.cloned.1.call-done, bf16[32,64]{1,0:T(8,128)(2,1)S(1)} %psum.7, bf16[32,8]{0,1:T(8,128)(2,1)S(1)} %get-tuple-element.7), kind=kOutput, calls=%fused_computation.5 | convolution fusion | flops 68304896 | bytes 2494984 | tf_op jit(solution)/shard_map/dot_general | solution.py:94
  (9 shorter events, 0.1 us)
Async XLA Ops:
  7.4 6.1 %copy-start = (bf16[32,4,96,128]{3,2,1,0:T(8,128)(2,1)S(1)}, bf16[32,4,96,128]{3,2,1,0:T(8,128)(2,1)}, u32[]{:S(2)}) copy-start(bf16[32,4,96,128]{3,2,1,0:T(8,128)(2,1)} %param.14) | copy-start | bytes 9437188
  7.4 3.8 %copy-start.2 = (bf16[32,4,128]{2,1,0:T(4,128)(2,1)S(1)}, bf16[32,4,128]{2,1,0:T(4,128)(2,1)}, u32[]{:S(2)}) copy-start(bf16[32,4,128]{2,1,0:T(4,128)(2,1)} %param.16) | copy-start | bytes 98308
  7.4 3.8 %copy-start.3 = (bf16[32,4,128]{2,1,0:T(4,128)(2,1)S(1)}, bf16[32,4,128]{2,1,0:T(4,128)(2,1)}, u32[]{:S(2)}) copy-start(bf16[32,4,128]{2,1,0:T(4,128)(2,1)} %param.15) | copy-start | bytes 98308
  7.4 3.9 %copy-start.4 = (s32[32]{0:T(128)S(1)}, s32[32]{0:T(128)}, u32[]{:S(2)}) copy-start(s32[32]{0:T(128)} %param.17) | copy-start | bytes 388
  7.4 4.0 %copy-start.1 = (bf16[32,8,128]{2,1,0:T(8,128)(2,1)S(1)}, bf16[32,8,128]{2,1,0:T(8,128)(2,1)}, u32[]{:S(2)}) copy-start(bf16[32,8,128]{2,1,0:T(8,128)(2,1)} %param.12) | copy-start | bytes 196612
  7.4 28.4 %all-gather.3.cloned.1.call-start = ((), (), s32[]{:S(2)}) async-start(), calls=%async_computation.2 | async-start | bytes 2621440 | tf_op jit(solution)/shard_map/all_gather | solution.py:71
  10.3 61.6 %all-gather.5.cloned.1.call-start = ((), (), s32[]{:S(2)}) async-start(), calls=%async_computation.3 | async-start | bytes 5242880 | tf_op jit(solution)/shard_map/all_gather | solution.py:72
  11.1 65.0 %reduce-scatter.2.cloned.1.call-start = ((), (), s32[]{:S(2)}) async-start(), calls=%async_computation.1 | async-start | bytes 1310720 | tf_op jit(solution)/shard_map/reduce_scatter | solution.py:82
  13.9 10.0 %copy-start.6 = (s32[8]{0:T(128)S(1)}, s32[8]{0:T(128)}, u32[]{:S(2)}) copy-start(s32[8]{0:T(128)} %param.22) | copy-start | bytes 100
  13.9 10.0 %copy-start.5 = (s32[32]{0:T(128)S(1)}, s32[32]{0:T(128)}, u32[]{:S(2)}) copy-start(s32[32]{0:T(128)} %param.23) | copy-start | bytes 388
Sparse Core Ops, SparseCore 0:
  10.5 25.2 all-gather.2
  37.3 34.5 all-gather.4
Sparse Core Ops, SparseCore 1:
  23.9 30.4 reduce-scatter.1
where the time goes:
time: 86.7 us; the launch traced here: 86.4 us
  waiting for transfers between devices  24.5 us (28%)
  blocking collectives  19.1 us (22%)
  matrix products  16.9 us (19%)
  between operations  15 us (17%)
  local copies, waits for them, and re-layouts  7.46 us (9%)
  other arithmetic  3.26 us (4%)
    psum x1, blocking collectives, local(): shrink_total = lax.psum(shrink_part, 'tensor')  19.1 us
    all_gather x1, waiting for transfers between devices, local(): lax.all_gather(masked_shrink, 'batch', axis=0, tiled=True)  11.9 us
    all_gather x1, waiting for transfers between devices, local(): lax.all_gather(expand_weight, 'batch', axis=0, tiled=True)  11.9 us
    dot_general x1, matrix products, local(): lax.dot_general(out_weight, attended, (((0,), (1,)), ((), ())), preferred...  9.89 us
    gather x1, local copies, waits for them, and re-layouts, local(): page_expand = jnp.take(every_expand, adapter_list, axis=0)  4.18 us
    gather x1, local copies, waits for them, and re-layouts, local(): page_shrink = jnp.take(every_shrink, adapter_list, axis=0)  3.21 us
    dot_general x1, matrix products, local(): jnp.dot(spread, page_expand.reshape(needed * rank_width, page_expand.shap...  2.83 us
    mul x1, other arithmetic, local(): masked_shrink = shrink_weight * keep_cols[:, None, :]  2.02 us
  transfers between devices with their start and end apart: 3, of which 2 were waited for; matrix products, arithmetic and copies ran while one was open for 25% of the time, Pallas kernels for 0%

commit v1 on v0

--- a/solution.py
+++ b/solution.py
@@ -47,7 +47,13 @@
     return attended.astype(jnp.bfloat16).reshape(row_count, head_count * head_width)
 
 
+def shifted(array, axis, size, shift):
+    return lax.ppermute(array, axis, [(i, (i + shift) % size) for i in range(size)])
+
+
 def local(
+    tensor_size,
+    batch_size,
     queries,
     key_cache,
     value_cache,
@@ -61,42 +67,59 @@
     adapter_list,
     row_adapter,
 ):
+    f32, bf16 = jnp.float32, jnp.bfloat16
+    tensor_at = lax.axis_index("tensor")
+    batch_at = lax.axis_index("batch")
+    pool, _, rank_width = shrink_weight.shape
+    block = expand_weight.shape[2]
+    adapter = jnp.take(adapter_list, row_adapter)
     attended = attend(queries, key_cache, value_cache, new_key, new_value, lengths)
-    row_count = attended.shape[0]
-    rank_width = shrink_weight.shape[2]
-    needed = adapter_list.shape[0]
-    keep_cols = (jnp.arange(rank_width)[None, :] < adapter_rank[:, None]).astype(jnp.bfloat16)
-    masked_shrink = shrink_weight * keep_cols[:, None, :]
-    every_shrink, every_expand = (
-        lax.all_gather(masked_shrink, "batch", axis=0, tiled=True),
-        lax.all_gather(expand_weight, "batch", axis=0, tiled=True),
+    rows, width = attended.shape
+
+    tagged = jnp.concatenate(
+        [attended, jnp.broadcast_to(adapter.astype(bf16)[:, None], (rows, 128))], axis=1
     )
-    page_shrink = jnp.take(every_shrink, adapter_list, axis=0)
-    page_expand = jnp.take(every_expand, adapter_list, axis=0)
-    slot_hot = row_adapter[:, None] == jnp.arange(needed)[None, :]
-    shrink_terms = jnp.einsum(
-        "rq,nqk->rnk", attended, page_shrink, preferred_element_type=jnp.float32
+    visitors = [tagged] + [
+        shifted(tagged, "batch", batch_size, shift) for shift in range(1, batch_size)
+    ]
+    everyone = jnp.concatenate(visitors, axis=0)
+
+    def base_block(shift):
+        start = ((tensor_at + shift) % tensor_size) * block
+        weight = lax.dynamic_slice_in_dim(out_weight, start, block, 1)
+        return jnp.dot(attended, weight, preferred_element_type=f32)
+
+    base_in = [
+        shifted(base_block(shift).astype(bf16), "tensor", tensor_size, shift)
+        for shift in range(1, tensor_size)
+    ]
+    base = base_block(0)
+
+    all_rows = rows * batch_size
+    slot = everyone[:, width].astype(jnp.int32) - batch_at * pool
+    terms = jnp.einsum(
+        "rq,nqk->rnk", everyone[:, :width], shrink_weight, preferred_element_type=f32
     )
-    shrink_part = jnp.sum(jnp.where(slot_hot[:, :, None], shrink_terms, jnp.float32(0.0)), axis=1)
-    shrink_total = lax.psum(shrink_part, "tensor")
-    base = lax.psum_scatter(
-        lax.dot_general(
-            out_weight, attended, (((0,), (1,)), ((), ())), preferred_element_type=jnp.float32
-        ),
-        "tensor",
-        scatter_dimension=0,
-        tiled=True,
-    ).T
-    shrink = shrink_total.astype(jnp.bfloat16)
-    spread = (slot_hot.astype(jnp.bfloat16)[:, :, None] * shrink[:, None, :]).reshape(
-        row_count, needed * rank_width
+    hot = slot[:, None] == jnp.arange(pool)[None, :]
+    keep = jnp.arange(rank_width)[None, :] < adapter_rank[:, None]
+    part = jnp.sum(jnp.where(hot[:, :, None] & keep[None], terms, f32(0.0)), axis=1)
+    total = part
+    for shift in range(1, tensor_size):
+        total = total + shifted(part, "tensor", tensor_size, shift)
+    shrink = total.astype(bf16)
+    spread = (hot.astype(bf16)[:, :, None] * shrink[:, None, :]).reshape(
+        all_rows, pool * rank_width
     )
     delta = jnp.dot(
-        spread,
-        page_expand.reshape(needed * rank_width, page_expand.shape[2]),
-        preferred_element_type=jnp.float32,
+        spread, expand_weight.reshape(pool * rank_width, block), preferred_element_type=f32
     )
-    return (base + delta).astype(jnp.bfloat16)
+    result = base + delta[:rows]
+    for shift in range(1, batch_size):
+        home = delta[shift * rows : (shift + 1) * rows].astype(bf16)
+        result = result + shifted(home, "batch", batch_size, -shift).astype(f32)
+    for arrived in base_in:
+        result = result + arrived.astype(f32)
+    return result.astype(bf16)
 
 
 def solution(mesh):
@@ -114,8 +137,12 @@
         P(("groups", "batch")),
         P(("groups", "batch")),
     )
+
+    def placed_local(*arrays):
+        return local(mesh.shape["tensor"], mesh.shape["batch"], *arrays)
+
     return jax.shard_map(
-        local,
+        placed_local,
         mesh=mesh,
         in_specs=placed,
         out_specs=P(("groups", "batch"), "tensor"),

time: 86.7 us -> 49.7 us (0.57)
  blocking collectives: 19.1 us -> 0 us
  waiting for transfers between devices: 24.5 us -> 7.25 us
  between operations: 15 us -> 0.12 us
  starting transfers between devices: 0.12 us -> 13.9 us
  local copies, waits for them, and re-layouts: 7.46 us -> 2.2 us
  matrix products: 16.9 us -> 20.9 us
  other arithmetic: 3.26 us -> 5.08 us
    all_gather x2 -> x0, waiting for transfers between devices: 23.8 us -> none  [the longest x1 11.9 us: local(): lax.all_gather(masked_shrink, 'batch', axis=0, tiled=True)]
    psum x1 -> x0, blocking collectives: 19.1 us -> none  [local(): shrink_total = lax.psum(shrink_part, 'tensor')]
    ppermute x0 -> x12, starting transfers between devices: none -> 13.9 us  [shifted(): lax.ppermute(array, axis, [(i, (i + shift) % size) for i in range(size)])]
    ppermute x0 -> x12, waiting for transfers between devices: none -> 7.25 us  [shifted(): lax.ppermute(array, axis, [(i, (i + shift) % size) for i in range(size)])]
    gather x2 -> x1, local copies, waits for them, and re-layouts: 7.39 us -> 1.35 us  [local(): adapter = jnp.take(adapter_list, row_adapter)]
    mul x1 -> x0, other arithmetic: 2.02 us -> none  [local(): masked_shrink = shrink_weight * keep_cols[:, None, :]]
    dot_general x3 -> x5, matrix products: 14.6 us -> 16.3 us  [the longest x4 15 us: base_block(): return jnp.dot(attended, weight, preferred_element_type=f32)]
    unnamed x0 -> x1, matrix products: none -> 1.46 us
  transfers between devices with their start and end apart: 3 -> 12, of which waited for: 2 -> 4; matrix products, arithmetic and copies ran while one was open for 25% -> 32% of each run, Pallas kernels for 0% -> 0%
where the time goes in v1:
time: 49.7 us; the launch traced here: 49.4 us
  matrix products  20.9 us (42%)
  starting transfers between devices  13.9 us (28%)
  waiting for transfers between devices  7.25 us (15%)
  other arithmetic  5.08 us (10%)
  local copies, waits for them, and re-layouts  2.2 us (4%)
    dot_general x4, matrix products, base_block(): return jnp.dot(attended, weight, preferred_element_type=f32)  15 us
    ppermute x12, starting transfers between devices, shifted(): lax.ppermute(array, axis, [(i, (i + shift) % size) for i in range(size)])  13.9 us
    ppermute x12, waiting for transfers between devices, shifted(): lax.ppermute(array, axis, [(i, (i + shift) % size) for i in range(size)])  7.25 us
    dot_general x1, matrix products, attend(): jnp.einsum('rgqd,rgpd->rgqp', grouped, key_local, preferred_element_type=...  1.73 us
    unnamed x1, matrix products  1.46 us
    gather x1, local copies, waits for them, and re-layouts, local(): adapter = jnp.take(adapter_list, row_adapter)  1.35 us
    dot_general x1, matrix products, local(): jnp.dot(spread, expand_weight.reshape(pool * rank_width, block), preferre...  1.31 us
  transfers between devices with their start and end apart: 12, of which 4 were waited for; matrix products, arithmetic and copies ran while one was open for 32% of the time, Pallas kernels for 0%

profile of v1, /device:TPU:0, one launch (start us, length us, event | category | flops | bytes accessed | tf_op | source)
XLA Modules:
  0.0 49.4 jit_solution(11393827247150258004)
XLA Ops:
  0.0 0.0 copy-start
  0.0 0.9 %iota_compare_fusion = pred[32,96]{1,0:T(8,128)(4,1)S(1)} fusion(s32[32]{0:T(128)} %param.17), kind=kLoop, calls=%fused_computation.48 | loop fusion | flops 3072 | bytes 3200 | tf_op jit(solution)/shard_map/lt | solution.py:30
  0.9 0.9 %dynamic-slice_convert_fusion = (f32[32,1,128]{2,1,0:T(1,128)S(1)}, bf16[32,1,128]{2,1,0:T(2,128)(2,1)S(1)}) fusion(bf16[32,4,128]{2,1,0:T(4,128)(2,1)} %param.16, s32[]{:T(128)S(6)} %select_n.69, bf16[32,4,128]{2,1,0:T(4,128)(2,1)} %param.15), kind=kLoop, calls=%fused_computation.45 | loop fusion | flops 4096 | bytes 40964 | tf_op jit(solution)/shard_map/mul | solution.py:45
  1.8 1.0 %fusion.37 = f32[32,1,8]{2,1,0:T(1,128)S(1)} fusion(bf16[32,8,128]{2,1,0:T(8,128)(2,1)} %param.12, bf16[32,128,1]{1,0,2:T(8,128)(2,1)S(1)} %bitcast.49), kind=kOutput, calls=%fused_computation.49 | convolution fusion | flops 65536 | bytes 74752 | tf_op jit(solution)/shard_map/rgqd,rgd->rgq/dot_general | solution.py:27
  2.8 1.7 %fusion.52 = (f32[32,8]{1,0:T(8,128)S(1)}, f32[32,8,96]{2,1,0:T(8,128)S(1)}) fusion(bf16[32,8,128]{2,1,0:T(8,128)(2,1)} %param.12, bf16[32,4,96,128]{3,2,1,0:T(8,128)(2,1)} %param.13, s32[]{:T(128)S(6)} %select_n.69, pred[32,96]{1,0:T(8,128)(4,1)S(1)} %iota_compare_fusion), kind=kOutput, calls=%fused_computation.72 | convolution fusion | flops 6364928 | bytes 954372 | tf_op jit(solution)/shard_map/rgqd,rgpd->rgqp/dot_general | solution.py:23
  4.5 0.2 fusion.29
  4.8 0.0 copy-done
  4.8 0.4 fusion.22
  5.2 0.7 %compare_select_fusion = s32[32]{0:T(128)S(1)} fusion(s32[32]{0:T(128)} %param.23), kind=kLoop, calls=%fused_computation.56 | loop fusion | flops 96 | bytes 256 | tf_op jit(solution)/shard_map/jit(_take)/jit(_where)/select_n | solution.py:75
  5.8 1.4 %gather_fusion = s32[32]{0:T(128)S(1)} fusion(s32[8]{0:T(128)} %param.22, s32[1024]{0:T(1024)S(1)} %pad_clamp_fusion), kind=kCustom, calls=%fused_computation | custom fusion | bytes 384 | tf_op jit(solution)/shard_map/jit(_take)/gather | solution.py:75
  7.2 0.7 %fusion.47 = bf16[32]{0:T(256)(128)(2,1)S(1)} fusion(s32[32]{0:T(128)S(1)} %gather_fusion, s32[32]{0:T(128)} %param.23), kind=kLoop, calls=%fused_computation.67 | loop fusion | flops 256 | bytes 320 | tf_op jit(solution)/shard_map/convert_element_type | solution.py:80
  7.9 0.1 broadcast_in_dim.60
  7.9 0.6 %pad_maximum_fusion.8 = bf16[32,1152]{1,0:T(8,128)(2,1)} fusion(bf16[32,128]{1,0:T(8,128)(2,1)S(1)} %broadcast_in_dim.60, bf16[32,1024]{1,0:T(8,128)(2,1)S(1)} %bitcast.42), kind=kLoop, calls=%fused_computation.34 | loop fusion | flops 147456 | bytes 147456 | tf_op jit(solution)/shard_map/concatenate | solution.py:79
  8.6 0.5 collective-permute-start
  9.0 2.5 %collective-permute-start.1 = (bf16[32,1152]{1,0:T(8,128)(2,1)}, bf16[32,1152]{1,0:T(8,128)(2,1)}, u32[]{:S(2)}, u32[]{:S(2)}) collective-permute-start(bf16[32,1152]{1,0:T(8,128)(2,1)} %pad_maximum_fusion.8), channel_id=1, source_target_pairs={{0,2},{1,3},{2,0},{3,1},{4,6},{5,7},{6,4},{7,5},{8,10},{9,11},{10,... | collective-permute-start | bytes 221192 | tf_op jit(solution)/shard_map/ppermute | solution.py:51
  11.6 1.4 %collective-permute-start.2 = (bf16[32,1152]{1,0:T(8,128)(2,1)}, bf16[32,1152]{1,0:T(8,128)(2,1)}, u32[]{:S(2)}, u32[]{:S(2)}) collective-permute-start(bf16[32,1152]{1,0:T(8,128)(2,1)} %pad_maximum_fusion.8), channel_id=1, source_target_pairs={{0,3},{1,0},{2,1},{3,2},{4,7},{5,4},{6,5},{7,6},{8,11},{9,8},{10,9... | collective-permute-start | bytes 221192 | tf_op jit(solution)/shard_map/ppermute | solution.py:51
  13.0 0.0 copy-start.2
  13.0 3.7 %fusion.11 = bf16[32,2048]{1,0:T(8,128)(2,1)} fusion(bf16[1024,8192]{1,0:T(8,128)(2,1)} %param.18, s32[]{:T(128)S(6)} %select_n.79, bf16[4,8,8,128]{3,2,1,0:T(8,128)(2,1)S(1)} %bitcast.38), kind=kOutput, calls=%fused_computation.11 | convolution fusion | flops 134283264 | bytes 4390916 | tf_op jit(solution)/shard_map/dot_general | solution.py:90
  16.7 1.6 %collective-permute-start.9 = (bf16[32,2048]{1,0:T(8,128)(2,1)}, bf16[32,2048]{1,0:T(8,128)(2,1)S(1)}, u32[]{:S(2)}, u32[]{:S(2)}) collective-permute-start(bf16[32,2048]{1,0:T(8,128)(2,1)} %fusion.11), channel_id=1, source_target_pairs={{0,4},{4,8},{8,12},{12,0},{1,5},{5,9},{9,13},{13,1},{2,6},{6,10},{... | collective-permute-start | bytes 393224 | tf_op jit(solution)/shard_map/ppermute | solution.py:51
  18.2 3.7 %fusion.14 = bf16[32,2048]{1,0:T(8,128)(2,1)} fusion(bf16[1024,8192]{1,0:T(8,128)(2,1)} %param.18, s32[]{:T(128)S(6)} %select_n.81, bf16[4,8,8,128]{3,2,1,0:T(8,128)(2,1)S(1)} %bitcast.39), kind=kOutput, calls=%fused_computation.12 | convolution fusion | flops 134283264 | bytes 4390916 | tf_op jit(solution)/shard_map/dot_general | solution.py:90
  21.9 2.6 %collective-permute-start.10 = (bf16[32,2048]{1,0:T(8,128)(2,1)}, bf16[32,2048]{1,0:T(8,128)(2,1)S(1)}, u32[]{:S(2)}, u32[]{:S(2)}) collective-permute-start(bf16[32,2048]{1,0:T(8,128)(2,1)} %fusion.14), channel_id=1, source_target_pairs={{0,8},{4,12},{8,0},{12,4},{1,9},{5,13},{9,1},{13,5},{2,10},{6,14},... | collective-permute-start | bytes 393224 | tf_op jit(solution)/shard_map/ppermute | solution.py:51
  24.5 0.0 copy-done.2
  24.5 0.1 iota_compare_fusion.1
  24.6 0.0 copy-start.1
  24.6 0.0 collective-permute-done
  24.6 0.0 collective-permute-done.1
  24.6 0.0 collective-permute-done.2
  24.6 0.9 %subtract_reduce_fusion = s32[128]{0:T(128)S(1)} fusion(bf16[32,1152]{1,0:T(8,128)(2,1)} %collective-permute-done.2, bf16[32,1152]{1,0:T(8,128)(2,1)} %collective-permute-done.1, bf16[32,1152]{1,0:T(8,128)(2,1)} %collective-permute-done, bf16[32,128]{1,0:T(8,128)(2,1)S(1)} %broadcast_in_dim.60, bf16[32,1024]{1,0:T(8,128)(2,1)S(1)} %bitcast.43, s32[]{:T(128)S(6)} %mul.75), kind=kLoop, calls=%fused_computation.37 | loop fusion | flops 1408 | bytes 295428 | tf_op jit(solution)/shard_map/sub | solution.py:99
  25.5 1.5 %fusion.27 = f32[128,256]{0,1:S(1)} fusion(bf16[1024,256]{0,1:T(8,128)(2,1)} %bitcast.50, bf16[32,1152]{1,0:T(8,128)(2,1)} %collective-permute-done.2, bf16[32,1152]{1,0:T(8,128)(2,1)} %collective-permute-done.1, bf16[32,1152]{1,0:T(8,128)(2,1)} %collective-permute-done, bf16[32,128]{1,0:T(8,128)(2,1)S(1)} %broadcast_in_dim.60, ...), kind=kOutput, calls=%fused_computation.24 | convolution fusion | flops 68419584 | bytes 950272
  27.0 0.1 select_reduce_fusion
  27.1 0.3 collective-permute-start.3
  27.4 1.7 %collective-permute-start.4 = (f32[128,64]{0,1:T(8,128)S(1)}, f32[128,64]{0,1:T(8,128)S(1)}, u32[]{:S(2)}, u32[]{:S(2)}) collective-permute-start(f32[128,64]{0,1:T(8,128)S(1)} %select_reduce_fusion), channel_id=1, source_target_pairs={{0,8},{4,12},{8,0},{12,4},{1,9},{5,13},{9,1},{13,5},{2,10},{6,14},... | collective-permute-start | bytes 98312 | tf_op jit(solution)/shard_map/ppermute | solution.py:51
  29.1 1.9 %collective-permute-start.5 = (f32[128,64]{0,1:T(8,128)S(1)}, f32[128,64]{0,1:T(8,128)S(1)}, u32[]{:S(2)}, u32[]{:S(2)}) collective-permute-start(f32[128,64]{0,1:T(8,128)S(1)} %select_reduce_fusion), channel_id=1, source_target_pairs={{0,12},{4,0},{8,4},{12,8},{1,13},{5,1},{9,5},{13,9},{2,14},{6,2},{... | collective-permute-start | bytes 98312 | tf_op jit(solution)/shard_map/ppermute | solution.py:51
  31.0 3.7 %fusion.17 = bf16[32,2048]{1,0:T(8,128)(2,1)} fusion(bf16[1024,8192]{1,0:T(8,128)(2,1)} %param.18, s32[]{:T(128)S(6)} %select_n.83, bf16[4,8,8,128]{3,2,1,0:T(8,128)(2,1)S(1)} %bitcast.40), kind=kOutput, calls=%fused_computation.13 | convolution fusion | flops 134283264 | bytes 4390916 | tf_op jit(solution)/shard_map/dot_general | solution.py:90
  34.7 0.0 collective-permute-done.3
  34.7 0.8 %collective-permute-start.11 = (bf16[32,2048]{1,0:T(8,128)(2,1)}, bf16[32,2048]{1,0:T(8,128)(2,1)}, u32[]{:S(2)}, u32[]{:S(2)}) collective-permute-start(bf16[32,2048]{1,0:T(8,128)(2,1)} %fusion.17), channel_id=1, source_target_pairs={{0,12},{4,0},{8,4},{12,8},{1,13},{5,1},{9,5},{13,9},{2,14},{6,2},{... | collective-permute-start | bytes 393224 | tf_op jit(solution)/shard_map/ppermute | solution.py:51
  35.5 0.0 collective-permute-done.4
  35.5 0.0 collective-permute-done.5
  35.5 0.0 copy-done.1
  35.5 1.3 %fusion.53 = (bf16[128,2048]{1,0:T(8,128)(2,1)S(1)}, f32[128,2048]{1,0:T(8,128)}) fusion(bf16[4,64,2048]{2,1,0:T(8,128)(2,1)S(1)} %copy-done.1, bf16[128,64]{0,1:T(8,128)(2,1)S(1)} %add_convert_fusion.1, bf16[128,4]{0,1:T(4,128)(2,1)S(1)} %get-tuple-element.10), kind=kOutput, calls=%fused_computation.73 | convolution fusion | flops 134512640 | bytes 2638848 | tf_op jit(solution)/shard_map/dot_general | solution.py:113
  36.8 0.7 %fusion.51 = (bf16[32,2048]{1,0:T(8,128)(2,1)}, bf16[32,2048]{1,0:T(8,128)(2,1)}, bf16[32,2048]{1,0:T(8,128)(2,1)}) fusion(bf16[128,2048]{1,0:T(8,128)(2,1)S(1)} %get-tuple-element.14), kind=kLoop, calls=%fused_computation.71 | loop fusion | bytes 786432 | tf_op jit(solution)/shard_map/slice | solution.py:118
  37.5 0.0 collective-permute-start.6
  37.5 0.4 collective-permute-start.7
  37.9 0.0 collective-permute-done.9
  37.9 0.2 collective-permute-start.8
  38.2 0.0 collective-permute-done.10
  38.2 1.8 %collective-permute-done.11 = bf16[32,2048]{1,0:T(8,128)(2,1)} collective-permute-done((bf16[32,2048]{1,0:T(8,128)(2,1)}, bf16[32,2048]{1,0:T(8,128)(2,1)}, u32[]{:S(2)}, u32[]{:S(2)}) %collective-permute-start.11) | collective-permute-done | bytes 131104 | tf_op jit(solution)/shard_map/ppermute | solution.py:51
  40.0 1.8 %collective-permute-done.6 = bf16[32,2048]{1,0:T(8,128)(2,1)} collective-permute-done((bf16[32,2048]{1,0:T(8,128)(2,1)}, bf16[32,2048]{1,0:T(8,128)(2,1)}, u32[]{:S(2)}, u32[]{:S(2)}) %collective-permute-start.6) | collective-permute-done | bytes 131104 | tf_op jit(solution)/shard_map/ppermute | solution.py:51
  41.8 2.7 %collective-permute-done.7 = bf16[32,2048]{1,0:T(8,128)(2,1)} collective-permute-done((bf16[32,2048]{1,0:T(8,128)(2,1)}, bf16[32,2048]{1,0:T(8,128)(2,1)}, u32[]{:S(2)}, u32[]{:S(2)}) %collective-permute-start.7) | collective-permute-done | bytes 131104 | tf_op jit(solution)/shard_map/ppermute | solution.py:51
  44.5 0.9 %collective-permute-done.8 = bf16[32,2048]{1,0:T(8,128)(2,1)} collective-permute-done((bf16[32,2048]{1,0:T(8,128)(2,1)}, bf16[32,2048]{1,0:T(8,128)(2,1)}, u32[]{:S(2)}, u32[]{:S(2)}) %collective-permute-start.8) | collective-permute-done | bytes 131104 | tf_op jit(solution)/shard_map/ppermute | solution.py:51
  45.4 4.0 %add_convert_fusion = bf16[32,2048]{1,0:T(8,128)(2,1)} fusion(bf16[32,2048]{1,0:T(8,128)(2,1)} %collective-permute-done.11, bf16[32,2048]{1,0:T(8,128)(2,1)S(1)} %collective-permute-done.10, bf16[32,2048]{1,0:T(8,128)(2,1)S(1)} %collective-permute-done.9, bf16[32,2048]{1,0:T(8,128)(2,1)} %collective-permute-done.8, ...), kind=kOutput, calls=%fused_computation.29 | convolution fusion | flops 135135232 | bytes 5439492 | tf_op jit(solution)/shard_map/dot_general | solution.py:90
  (7 shorter events, 0.1 us)
Async XLA Ops:
  0.0 4.8 %copy-start = (bf16[32,4,96,128]{3,2,1,0:T(8,128)(2,1)S(1)}, bf16[32,4,96,128]{3,2,1,0:T(8,128)(2,1)}, u32[]{:S(2)}) copy-start(bf16[32,4,96,128]{3,2,1,0:T(8,128)(2,1)} %param.14) | copy-start | bytes 9437188
  8.6 16.0 %collective-permute-start = (bf16[32,1152]{1,0:T(8,128)(2,1)}, bf16[32,1152]{1,0:T(8,128)(2,1)}, u32[]{:S(2)}, u32[]{:S(2)}) collective-permute-start(bf16[32,1152]{1,0:T(8,128)(2,1)} %pad_maximum_fusion.8), channel_id=1, source_target_pairs={{0,1},{1,2},{2,3},{3,0},{4,5},{5,6},{6,7},{7,4},{8,9},{9,10},{10,1... | collective-permute-start | bytes 221192 | tf_op jit(solution)/shard_map/ppermute | solution.py:51
  9.0 15.6 %collective-permute-start.1 = (bf16[32,1152]{1,0:T(8,128)(2,1)}, bf16[32,1152]{1,0:T(8,128)(2,1)}, u32[]{:S(2)}, u32[]{:S(2)}) collective-permute-start(bf16[32,1152]{1,0:T(8,128)(2,1)} %pad_maximum_fusion.8), channel_id=1, source_target_pairs={{0,2},{1,3},{2,0},{3,1},{4,6},{5,7},{6,4},{7,5},{8,10},{9,11},{10,... | collective-permute-start | bytes 221192 | tf_op jit(solution)/shard_map/ppermute | solution.py:51
  11.6 13.0 %collective-permute-start.2 = (bf16[32,1152]{1,0:T(8,128)(2,1)}, bf16[32,1152]{1,0:T(8,128)(2,1)}, u32[]{:S(2)}, u32[]{:S(2)}) collective-permute-start(bf16[32,1152]{1,0:T(8,128)(2,1)} %pad_maximum_fusion.8), channel_id=1, source_target_pairs={{0,3},{1,0},{2,1},{3,2},{4,7},{5,4},{6,5},{7,6},{8,11},{9,8},{10,9... | collective-permute-start | bytes 221192 | tf_op jit(solution)/shard_map/ppermute | solution.py:51
  13.0 11.5 %copy-start.2 = (s32[4]{0:T(128)S(1)}, s32[4]{0:T(128)}, u32[]{:S(2)}) copy-start(s32[4]{0:T(128)} %param.21) | copy-start | bytes 52
  16.7 21.3 %collective-permute-start.9 = (bf16[32,2048]{1,0:T(8,128)(2,1)}, bf16[32,2048]{1,0:T(8,128)(2,1)S(1)}, u32[]{:S(2)}, u32[]{:S(2)}) collective-permute-start(bf16[32,2048]{1,0:T(8,128)(2,1)} %fusion.11), channel_id=1, source_target_pairs={{0,4},{4,8},{8,12},{12,0},{1,5},{5,9},{9,13},{13,1},{2,6},{6,10},{... | collective-permute-start | bytes 393224 | tf_op jit(solution)/shard_map/ppermute | solution.py:51
  21.9 16.3 %collective-permute-start.10 = (bf16[32,2048]{1,0:T(8,128)(2,1)}, bf16[32,2048]{1,0:T(8,128)(2,1)S(1)}, u32[]{:S(2)}, u32[]{:S(2)}) collective-permute-start(bf16[32,2048]{1,0:T(8,128)(2,1)} %fusion.14), channel_id=1, source_target_pairs={{0,8},{4,12},{8,0},{12,4},{1,9},{5,13},{9,1},{13,5},{2,10},{6,14},... | collective-permute-start | bytes 393224 | tf_op jit(solution)/shard_map/ppermute | solution.py:51
  24.6 10.9 %copy-start.1 = (bf16[4,64,2048]{2,1,0:T(8,128)(2,1)S(1)}, bf16[4,64,2048]{2,1,0:T(8,128)(2,1)}, u32[]{:S(2)}) copy-start(bf16[4,64,2048]{2,1,0:T(8,128)(2,1)} %param.20) | copy-start | bytes 3145732
  27.1 7.6 %collective-permute-start.3 = (f32[128,64]{0,1:T(8,128)S(1)}, f32[128,64]{0,1:T(8,128)S(1)}, u32[]{:S(2)}, u32[]{:S(2)}) collective-permute-start(f32[128,64]{0,1:T(8,128)S(1)} %select_reduce_fusion), channel_id=1, source_target_pairs={{0,4},{4,8},{8,12},{12,0},{1,5},{5,9},{9,13},{13,1},{2,6},{6,10},{... | collective-permute-start | bytes 98312 | tf_op jit(solution)/shard_map/ppermute | solution.py:51
  27.4 8.1 %collective-permute-start.4 = (f32[128,64]{0,1:T(8,128)S(1)}, f32[128,64]{0,1:T(8,128)S(1)}, u32[]{:S(2)}, u32[]{:S(2)}) collective-permute-start(f32[128,64]{0,1:T(8,128)S(1)} %select_reduce_fusion), channel_id=1, source_target_pairs={{0,8},{4,12},{8,0},{12,4},{1,9},{5,13},{9,1},{13,5},{2,10},{6,14},... | collective-permute-start | bytes 98312 | tf_op jit(solution)/shard_map/ppermute | solution.py:51
  29.1 6.4 %collective-permute-start.5 = (f32[128,64]{0,1:T(8,128)S(1)}, f32[128,64]{0,1:T(8,128)S(1)}, u32[]{:S(2)}, u32[]{:S(2)}) collective-permute-start(f32[128,64]{0,1:T(8,128)S(1)} %select_reduce_fusion), channel_id=1, source_target_pairs={{0,12},{4,0},{8,4},{12,8},{1,13},{5,1},{9,5},{13,9},{2,14},{6,2},{... | collective-permute-start | bytes 98312 | tf_op jit(solution)/shard_map/ppermute | solution.py:51
  34.7 5.3 %collective-permute-start.11 = (bf16[32,2048]{1,0:T(8,128)(2,1)}, bf16[32,2048]{1,0:T(8,128)(2,1)}, u32[]{:S(2)}, u32[]{:S(2)}) collective-permute-start(bf16[32,2048]{1,0:T(8,128)(2,1)} %fusion.17), channel_id=1, source_target_pairs={{0,12},{4,0},{8,4},{12,8},{1,13},{5,1},{9,5},{13,9},{2,14},{6,2},{... | collective-permute-start | bytes 393224 | tf_op jit(solution)/shard_map/ppermute | solution.py:51
  37.5 4.2 %collective-permute-start.6 = (bf16[32,2048]{1,0:T(8,128)(2,1)}, bf16[32,2048]{1,0:T(8,128)(2,1)}, u32[]{:S(2)}, u32[]{:S(2)}) collective-permute-start(bf16[32,2048]{1,0:T(8,128)(2,1)} %get-tuple-element.5), channel_id=1, source_target_pairs={{0,3},{1,0},{2,1},{3,2},{4,7},{5,4},{6,5},{7,6},{8,11},{9,8},{10,9... | collective-permute-start | bytes 393224 | tf_op jit(solution)/shard_map/ppermute | solution.py:51
  37.5 6.9 %collective-permute-start.7 = (bf16[32,2048]{1,0:T(8,128)(2,1)}, bf16[32,2048]{1,0:T(8,128)(2,1)}, u32[]{:S(2)}, u32[]{:S(2)}) collective-permute-start(bf16[32,2048]{1,0:T(8,128)(2,1)} %get-tuple-element.7), channel_id=1, source_target_pairs={{0,2},{1,3},{2,0},{3,1},{4,6},{5,7},{6,4},{7,5},{8,10},{9,11},{10,... | collective-permute-start | bytes 393224 | tf_op jit(solution)/shard_map/ppermute | solution.py:51
  37.9 7.5 %collective-permute-start.8 = (bf16[32,2048]{1,0:T(8,128)(2,1)}, bf16[32,2048]{1,0:T(8,128)(2,1)}, u32[]{:S(2)}, u32[]{:S(2)}) collective-permute-start(bf16[32,2048]{1,0:T(8,128)(2,1)} %get-tuple-element.6), channel_id=1, source_target_pairs={{0,1},{1,2},{2,3},{3,0},{4,5},{5,6},{6,7},{7,4},{8,9},{9,10},{10,1... | collective-permute-start | bytes 393224 | tf_op jit(solution)/shard_map/ppermute | solution.py:51

commit v2 on v0

v2 whole, which is shorter than its diff:
```python
import functools

import jax
import jax.numpy as jnp
from jax import lax
from jax.experimental import pallas as pl
from jax.experimental.pallas import tpu as pltpu
from jax.sharding import PartitionSpec as P

HQ = 32
KVH = 4
LANES = 128
VMEM = pltpu.VMEM
F32, BF16 = jnp.float32, jnp.bfloat16


def shifted(array, axis, size, shift):
    return lax.ppermute(array, axis, [(i, (i + shift) % size) for i in range(size)])


def lane_of(shape):
    return lax.broadcasted_iota(jnp.int32, shape, len(shape) - 1)


def attend_kernel(
    parts,
    lengths,
    row_adapter,
    adapter_list,
    group_at,
    queries,
    key_cache,
    value_cache,
    new_key,
    new_value,
    tagged,
    keys,
    values,
    spread_out,
    key_sems,
    value_sems,
):
    rows, heads, width = queries.shape
    positions = key_cache.shape[2]
    group = group_at[0]
    some = rows // parts

    def copies(part):
        at = pl.ds(part * some, some)
        return (
            pltpu.make_async_copy(key_cache.at[at, group], keys.at[at], key_sems.at[part]),
            pltpu.make_async_copy(value_cache.at[at, group], values.at[at], value_sems.at[part]),
        )

    for part in range(parts):
        for copy in copies(part):
            copy.start()
    at_row = lax.broadcasted_iota(jnp.int32, (rows, LANES), 0)
    tag = jnp.zeros((rows, LANES), jnp.int32)
    for row in range(rows):
        tag = jnp.where(at_row == row, adapter_list[row_adapter[row]], tag)
    tagged[:, heads * width :] = tag.astype(F32).astype(BF16)

    group_row = lax.broadcasted_iota(jnp.int32, new_key.shape, 1) == group
    fresh_key = jnp.sum(
        jnp.where(group_row, new_key[...].astype(F32), F32(0.0)), axis=1, keepdims=True
    )
    fresh_value = jnp.sum(
        jnp.where(group_row, new_value[...].astype(F32), F32(0.0)), axis=1, keepdims=True
    )
    score_scale = width ** (-0.5)
    fresh = jnp.sum(queries[...].astype(F32) * fresh_key, axis=-1, keepdims=True) * score_scale
    for part in range(parts):
        at = slice(part * some, (part + 1) * some)
        key_copy, value_copy = copies(part)
        key_copy.wait()
        scores = (
            lax.dot_general(
                queries[at], keys[at], (((2,), (2,)), ((0,), (0,))), preferred_element_type=F32
            )
            * score_scale
        )
        length = jnp.stack(
            [
                jnp.full((heads, positions), lengths[row], jnp.int32)
                for row in range(part * some, (part + 1) * some)
            ]
        )
        valid = lane_of(scores.shape) < length
        masked = jnp.where(valid, scores, F32(-1e30))
        highest = jnp.maximum(jnp.max(masked, axis=-1, keepdims=True), fresh[at])
        cached_exp = jnp.where(valid, jnp.exp(masked - highest), F32(0.0))
        fresh_exp = jnp.exp(fresh[at] - highest)
        totals = jnp.sum(cached_exp, axis=-1, keepdims=True) + fresh_exp
        cached_w = (cached_exp / totals).astype(BF16)
        fresh_w = (fresh_exp / totals).astype(BF16).astype(F32)
        value_copy.wait()
        attended = lax.dot_general(
            cached_w, values[at], (((2,), (1,)), ((0,), (0,))), preferred_element_type=F32
        )
        attended = attended + fresh_w * fresh_value[at]
        spread_out[pl.ds(part * some * heads, some * heads)] = attended.reshape(
            some * heads, width
        )
    for head in range(heads):
        tagged[:, head * width : (head + 1) * width] = spread_out[
            pl.ds(head, rows, stride=heads)
        ].astype(BF16)


def attend(queries, key_cache, value_cache, new_key, new_value, lengths, adapter_list, row_adapter):
    rows, heads, width = queries.shape
    positions = key_cache.shape[2]
    per_group = HQ // KVH
    group_at = (lax.axis_index("tensor") * heads // per_group).reshape(1).astype(jnp.int32)
    full = -(-heads // 8) * 8
    if full != heads:
        queries = jnp.pad(queries, ((0, 0), (0, full - heads), (0, 0)))
    parts = 2
    smem = pl.BlockSpec(memory_space=pltpu.SMEM)
    whole = pl.BlockSpec(memory_space=VMEM)
    away = pl.BlockSpec(memory_space=pl.ANY)
    tagged = pl.pallas_call(
        functools.partial(attend_kernel, parts),
        out_shape=jax.ShapeDtypeStruct((rows, full * width + LANES), BF16),
        in_specs=[smem] * 4 + [whole, away, away, whole, whole],
        out_specs=whole,
        scratch_shapes=[
            VMEM((rows, positions, width), BF16),
            VMEM((rows, positions, width), BF16),
            VMEM((rows * full, width), F32),
            pltpu.SemaphoreType.DMA((parts,)),
            pltpu.SemaphoreType.DMA((parts,)),
        ],
        compiler_params=pltpu.CompilerParams(vmem_limit_bytes=8 << 20),
        cost_estimate=pl.CostEstimate(
            flops=4 * rows * heads * positions * width,
            bytes_accessed=4 * rows * positions * width,
            transcendentals=rows * heads * positions,
        ),
        name="attention",
    )(lengths, row_adapter, adapter_list, group_at, queries, key_cache, value_cache, new_key, new_value)
    if full != heads:
        tagged = jnp.concatenate([tagged[:, : heads * width], tagged[:, full * width :]], axis=1)
    return tagged


def base_kernel(shifts, tensor_size, block, piece, column_at, tagged, out_weight, *rest):
    outs, (held, sems) = rest[: len(shifts)], rest[len(shifts) :]
    width = out_weight.shape[0]
    pieces = block // piece

    def copy(which, part):
        start = column_at[which] * block + part * piece
        at = which * pieces + part
        return pltpu.make_async_copy(
            out_weight.at[:, pl.ds(pl.multiple_of(start, piece), piece)],
            held.at[at],
            sems.at[at],
        )

    for which in range(len(shifts)):
        for part in range(pieces):
            copy(which, part).start()
    for which, out in enumerate(outs):
        for part in range(pieces):
            copy(which, part).wait()
            out[:, part * piece : (part + 1) * piece] = jnp.dot(
                tagged[:, :width], held[which * pieces + part], preferred_element_type=F32
            ).astype(out.dtype)


def base_blocks(tagged, out_weight, tensor_size, block, shifts):
    rows = tagged.shape[0]
    width = out_weight.shape[0]
    piece = min(block, 512)
    here = lax.axis_index("tensor")
    column_at = jnp.stack([(here + shift) % tensor_size for shift in shifts]).astype(jnp.int32)
    whole = pl.BlockSpec(memory_space=VMEM)
    held = len(shifts) * block // piece
    return pl.pallas_call(
        functools.partial(base_kernel, shifts, tensor_size, block, piece),
        out_shape=[
            jax.ShapeDtypeStruct((rows, block), BF16 if shift else F32) for shift in shifts
        ],
        in_specs=[pl.BlockSpec(memory_space=pltpu.SMEM), whole, pl.BlockSpec(memory_space=pl.ANY)],
        out_specs=[whole] * len(shifts),
        scratch_shapes=[VMEM((held, width, piece), BF16), pltpu.SemaphoreType.DMA((held,))],
        compiler_params=pltpu.CompilerParams(
            vmem_limit_bytes=(2 * held * width * piece) + (8 << 20)
        ),
        cost_estimate=pl.CostEstimate(
            flops=2 * rows * width * block * len(shifts),
            bytes_accessed=2 * width * block * len(shifts),
            transcendentals=0,
        ),
        name="base_" + "_".join(str(shift) for shift in shifts),
    )(column_at, tagged, out_weight)


def slots_of(tags, first):
    return tags.astype(F32).astype(jnp.int32) - first


def shrink_kernel(count, first_at, rank, *refs):
    blocks, (factors, out) = refs[:count], refs[count:]
    pool, rank_width, width = factors.shape
    rows = jnp.concatenate([block[:, :width] for block in blocks], axis=0)
    slot = slots_of(jnp.concatenate([block[:, width:] for block in blocks], axis=0), first_at[0])
    terms = lax.dot_general(
        rows,
        factors[...].reshape(pool * rank_width, width),
        (((1,), (1,)), ((), ())),
        preferred_element_type=F32,
    )
    lane = lane_of(slot.shape)
    per = LANES // rank_width
    kept = jnp.zeros(slot.shape, F32)
    for tile in range(pool // per):
        mine, limit = tile * per + lane // rank_width, jnp.zeros_like(lane)
        for n in range(tile * per, (tile + 1) * per):
            limit = jnp.where(mine == n, rank[n], limit)
        keep = (slot == mine) & (lane % rank_width < limit)
        kept = kept + jnp.where(keep, terms[:, tile * LANES : (tile + 1) * LANES], F32(0.0))
    both = kept + pltpu.roll(kept, rank_width, 1)
    half = both.shape[0] // 2
    out[...] = jnp.where(lane[:half] < rank_width, both[:half], both[half:]).astype(out.dtype)


def shrink_part(blocks, shrink_weight, adapter_rank, first_at):
    pool, width, rank_width = shrink_weight.shape
    rows = blocks[0].shape[0] * len(blocks)
    smem = pl.BlockSpec(memory_space=pltpu.SMEM)
    whole = pl.BlockSpec(memory_space=VMEM)
    return pl.pallas_call(
        functools.partial(shrink_kernel, len(blocks)),
        out_shape=jax.ShapeDtypeStruct((rows // 2, LANES), BF16),
        in_specs=[smem, smem] + [whole] * (len(blocks) + 1),
        out_specs=whole,
        compiler_params=pltpu.CompilerParams(vmem_limit_bytes=8 << 20),
        cost_estimate=pl.CostEstimate(
            flops=2 * rows * width * pool * rank_width,
            bytes_accessed=2 * width * (rows + pool * rank_width),
            transcendentals=0,
        ),
        name="shrink",
    )(first_at, adapter_rank, *blocks, jnp.swapaxes(shrink_weight, 1, 2))


def expand_kernel(count, sums, rank_width, first_at, *refs):
    tags, refs = refs[:count], refs[count:]
    parts, (factors, base), outs = refs[:sums], refs[sums : sums + 2], refs[sums + 2 :]
    slot = slots_of(jnp.concatenate([tag[...] for tag in tags], axis=0), first_at[0])
    total = parts[0][...].astype(F32)
    for part in parts[1:]:
        total = total + part[...].astype(F32)
    total = total.astype(BF16).astype(F32)
    other = pltpu.roll(total, rank_width, 1)
    low = lane_of(total.shape) < rank_width
    shrink = jnp.concatenate(
        [jnp.where(low, total, other), jnp.where(low, other, total)], axis=0
    )
    lane = lane_of(slot.shape)
    per = LANES // rank_width
    spread = jnp.concatenate(
        [
            jnp.where(slot == tile * per + lane // rank_width, shrink, F32(0.0)).astype(BF16)
            for tile in range(factors.shape[0] // LANES)
        ],
        axis=1,
    )
    rows, block = base.shape
    piece = min(block, 512)
    for at in range(0, block, piece):
        delta = jnp.dot(spread, factors[:, at : at + piece], preferred_element_type=F32)
        outs[0][:, at : at + piece] = base[:, at : at + piece] + delta[:rows]
        for which in range(1, count):
            outs[which][:, at : at + piece] = delta[which * rows : (which + 1) * rows].astype(BF16)


def expand(blocks, parts, expand_weight, base, first_at):
    pool, rank_width, block = expand_weight.shape
    rows, tagged_width = blocks[0].shape
    count = len(blocks)
    whole = pl.BlockSpec(memory_space=VMEM)
    tag = pl.BlockSpec((rows, LANES), lambda i: (0, tagged_width // LANES - 1))
    full = pl.BlockSpec((pool * rank_width, block), lambda i: (0, 0))
    part = pl.BlockSpec(parts[0].shape, lambda i: (0, 0))
    one = pl.BlockSpec((rows, block), lambda i: (0, 0))
    return pl.pallas_call(
        functools.partial(expand_kernel, count, len(parts), rank_width),
        grid=(1,),
        out_shape=[
            jax.ShapeDtypeStruct((rows, block), BF16 if which else F32) for which in range(count)
        ],
        in_specs=[pl.BlockSpec(memory_space=pltpu.SMEM)]
        + [tag] * count
        + [part] * len(parts)
        + [full, one],
        out_specs=[one] * count,
        compiler_params=pltpu.CompilerParams(vmem_limit_bytes=16 << 20),
        cost_estimate=pl.CostEstimate(
            flops=2 * rows * count * pool * rank_width * block,
            bytes_accessed=2 * pool * rank_width * block,
            transcendentals=0,
        ),
        name="expand",
    )(first_at, *blocks, *parts, expand_weight.reshape(pool * rank_width, block), base)


def local(
    tensor_size,
    batch_size,
    queries,
    key_cache,
    value_cache,
    new_key,
    new_value,
    lengths,
    out_weight,
    shrink_weight,
    expand_weight,
    adapter_rank,
    adapter_list,
    row_adapter,
):
    pool = shrink_weight.shape[0]
    block = expand_weight.shape[2]
    first_at = (lax.axis_index("batch") * pool).reshape(1).astype(jnp.int32)
    tagged = attend(
        queries, key_cache, value_cache, new_key, new_value, lengths, adapter_list, row_adapter
    )
    visitors = [tagged] + [
        shifted(tagged, "batch", batch_size, shift) for shift in range(1, batch_size)
    ]
    order = sorted(range(1, tensor_size), key=lambda s: -min(s, tensor_size - s)) + [0]
    half = tensor_size // 2
    terms = dict(zip(order[:half], base_blocks(tagged, out_weight, tensor_size, block, order[:half])))
    terms.update(
        zip(order[half:], base_blocks(tagged, out_weight, tensor_size, block, order[half:]))
    )
    base_in = [shifted(terms[shift], "tensor", tensor_size, shift) for shift in order[:-1]]

    part = shrink_part(visitors, shrink_weight, adapter_rank, first_at)
    parts = [part] + [
        shifted(part, "tensor", tensor_size, shift) for shift in range(1, tensor_size)
    ]
    homes = expand(visitors, parts, expand_weight, terms[0], first_at)
    result = homes[0]
    for arrived in base_in:
        result = result + arrived.astype(F32)
    for shift in range(1, batch_size):
        result = result + shifted(homes[shift], "batch", batch_size, -shift).astype(F32)
    return result.astype(BF16)


def solution(mesh):
    placed = (
        P(("groups", "batch"), "tensor", None),
        P(("groups", "batch"), None, None, None),
        P(("groups", "batch"), None, None, None),
        P(("groups", "batch"), None, None),
        P(("groups", "batch"), None, None),
        P(("groups", "batch")),
        P("tensor", None),
        P("batch", "tensor", None),
        P("batch", None, "tensor"),
        P("batch"),
        P(("groups", "batch")),
        P(("groups", "batch")),
    )

    def placed_local(*arrays):
        return local(mesh.shape["tensor"], mesh.shape["batch"], *arrays)

    return jax.shard_map(
        placed_local,
        mesh=mesh,
        in_specs=placed,
        out_specs=P(("groups", "batch"), "tensor"),
        check_vma=False,
    )
```

time: 86.7 us -> 54.9 us (0.63)
  blocking collectives: 19.1 us -> 0 us
  waiting for transfers between devices: 24.5 us -> 5.46 us
  matrix products: 16.9 us -> 0 us
  starting transfers between devices: 0.12 us -> 16.4 us
  between operations: 15 us -> 0.12 us
  local copies, waits for them, and re-layouts: 7.46 us -> 19.6 us
  Pallas kernels: 0 us -> 11.9 us
  other arithmetic: 3.26 us -> 0.93 us
    all_gather x2 -> x0, waiting for transfers between devices: 23.8 us -> none  [the longest x1 11.9 us: local(): lax.all_gather(masked_shrink, 'batch', axis=0, tiled=True)]
    unnamed x15 -> x26, local copies, waits for them, and re-layouts: 0.03 us -> 19.6 us
    psum x1 -> x0, blocking collectives: 19.1 us -> none  [local(): shrink_total = lax.psum(shrink_part, 'tensor')]
    dot_general x6 -> x0, matrix products: 16.9 us -> none  [the longest x1 9.89 us: local(): lax.dot_general(out_weight, attended, (((0,), (1,)), ((), ())), preferred...]
    ppermute x0 -> x12, starting transfers between devices: none -> 16.4 us  [shifted(): lax.ppermute(array, axis, [(i, (i + shift) % size) for i in range(size)])]
    pallas_call x0 -> x5, Pallas kernels: none -> 11.9 us  [the longest x2 8.3 us: base_blocks(): pl.pallas_call(functools.partial(base_kernel, shifts, tensor_size, block,...]
    gather x2 -> x0, local copies, waits for them, and re-layouts: 7.39 us -> none  [the longest x1 4.18 us: local(): page_expand = jnp.take(every_expand, adapter_list, axis=0)]
    ppermute x0 -> x12, waiting for transfers between devices: none -> 5.46 us  [shifted(): lax.ppermute(array, axis, [(i, (i + shift) % size) for i in range(size)])]
  transfers between devices with their start and end apart: 3 -> 12, of which waited for: 2 -> 1; matrix products, arithmetic and copies ran while one was open for 25% -> 0% of each run, Pallas kernels for 0% -> 18%
where the time goes in v2:
time: 54.9 us; the launch traced here: 54.5 us
  local copies, waits for them, and re-layouts  19.6 us (36%)
  starting transfers between devices  16.4 us (30%)
  Pallas kernels  11.9 us (22%)
  waiting for transfers between devices  5.46 us (10%)
  other arithmetic  0.93 us (2%)
    unnamed x26, local copies, waits for them, and re-layouts  19.6 us
    ppermute x12, starting transfers between devices, shifted(): lax.ppermute(array, axis, [(i, (i + shift) % size) for i in range(size)])  16.4 us
    pallas_call x2, Pallas kernels, base_blocks(): pl.pallas_call(functools.partial(base_kernel, shifts, tensor_size, block,...  8.3 us
    ppermute x12, waiting for transfers between devices, shifted(): lax.ppermute(array, axis, [(i, (i + shift) % size) for i in range(size)])  5.46 us
    pallas_call x1, Pallas kernels, attend(): pl.pallas_call(functools.partial(attend_kernel, parts), out_shape=jax.Sha...  2.32 us
  transfers between devices with their start and end apart: 12, of which 1 were waited for; matrix products, arithmetic and copies ran while one was open for 0% of the time, Pallas kernels for 18%

profile of v2, /device:TPU:0, one launch (start us, length us, event | category | flops | bytes accessed | tf_op | source)
XLA Modules:
  0.0 54.5 jit_solution(882017863044072141)
XLA Ops:
  0.0 0.0 copy-start.2
  0.0 1.9 %copy-done.2 = bf16[32,4,96,128]{3,2,1,0:T(8,128)(2,1)S(1)} copy-done((bf16[32,4,96,128]{3,2,1,0:T(8,128)(2,1)S(1)}, bf16[32,4,96,128]{3,2,1,0:T(8,128)(2,1)}, u32[]{:S(2)}) %copy-start.2) | copy-done | bytes 3145752
  1.9 0.0 copy-start.3
  1.9 1.9 %copy-done.3 = bf16[32,4,96,128]{3,2,1,0:T(8,128)(2,1)S(1)} copy-done((bf16[32,4,96,128]{3,2,1,0:T(8,128)(2,1)S(1)}, bf16[32,4,96,128]{3,2,1,0:T(8,128)(2,1)}, u32[]{:S(2)}) %copy-start.3) | copy-done | bytes 3145752
  3.8 0.0 copy-start.6
  3.8 0.8 %copy-done.6 = bf16[32,8,128]{2,1,0:T(8,128)(2,1)S(1)} copy-done((bf16[32,8,128]{2,1,0:T(8,128)(2,1)S(1)}, bf16[32,8,128]{2,1,0:T(8,128)(2,1)}, u32[]{:S(2)}) %copy-start.6) | copy-done | bytes 65560
  4.6 0.0 copy-start.7
  4.6 0.8 %copy-done.7 = bf16[32,4,128]{2,1,0:T(4,128)(2,1)S(1)} copy-done((bf16[32,4,128]{2,1,0:T(4,128)(2,1)S(1)}, bf16[32,4,128]{2,1,0:T(4,128)(2,1)}, u32[]{:S(2)}) %copy-start.7) | copy-done | bytes 32792
  5.4 0.0 copy-start.8
  5.4 0.8 %copy-done.8 = bf16[32,4,128]{2,1,0:T(4,128)(2,1)S(1)} copy-done((bf16[32,4,128]{2,1,0:T(4,128)(2,1)S(1)}, bf16[32,4,128]{2,1,0:T(4,128)(2,1)}, u32[]{:S(2)}) %copy-start.8) | copy-done | bytes 32792
  6.1 0.0 copy-start.9
  6.1 0.7 %copy-done.9 = s32[32]{0:T(128)S(1)} copy-done((s32[32]{0:T(128)S(1)}, s32[32]{0:T(128)}, u32[]{:S(2)}) %copy-start.9) | copy-done | bytes 152
  6.8 0.0 copy-start.10
  6.8 0.7 %copy-done.10 = s32[32]{0:T(128)S(1)} copy-done((s32[32]{0:T(128)S(1)}, s32[32]{0:T(128)}, u32[]{:S(2)}) %copy-start.10) | copy-done | bytes 152
  7.4 0.0 copy-start.11
  7.5 0.7 %copy-done.11 = s32[8]{0:T(128)S(1)} copy-done((s32[8]{0:T(128)S(1)}, s32[8]{0:T(128)}, u32[]{:S(2)}) %copy-start.11) | copy-done | bytes 56
  8.1 2.3 %attention.1.refs_0_.tagged = bf16[32,1152]{1,0:T(8,128)(2,1)S(1)} custom-call(s32[32]{0:T(128)S(1)} %copy-done.9, s32[32]{0:T(128)S(1)} %copy-done.10, s32[8]{0:T(128)S(1)} %copy-done.11, s32[1]{0:T(128)} %bitcast.1.group_at, bf16[32,8,128]{2,1,0:T(8,128)(2,1)S(1)} %copy-done.6, bf16[32,4,96,128]{3,2,1,0:T(8,128)(2,1)S(1)} %copy-done.2, ...), custom_call_target="tpu_custom_call" | custom-call | flops 12582912 | bytes 1572864 | tf_op jit(solution)/shard_map/attention/pallas_call | solution.py:123
  10.4 0.5 collective-permute-start
  10.9 2.6 %collective-permute-start.1 = (bf16[32,1152]{1,0:T(8,128)(2,1)S(1)}, bf16[32,1152]{1,0:T(8,128)(2,1)S(1)}, u32[]{:S(2)}, u32[]{:S(2)}) collective-permute-start(bf16[32,1152]{1,0:T(8,128)(2,1)S(1)} %attention.1.refs_0_.tagged), channel_id=1, source_target_pairs={{0,2},{1,3},{2,0},{3,1},{4,6},{5,7},{6,4},{7,5},{8,10},{9,11},{10,... | collective-permute-start | bytes 221192 | tf_op jit(solution)/shard_map/ppermute | solution.py:18
  13.5 1.4 %collective-permute-start.2 = (bf16[32,1152]{1,0:T(8,128)(2,1)S(1)}, bf16[32,1152]{1,0:T(8,128)(2,1)S(1)}, u32[]{:S(2)}, u32[]{:S(2)}) collective-permute-start(bf16[32,1152]{1,0:T(8,128)(2,1)S(1)} %attention.1.refs_0_.tagged), channel_id=1, source_target_pairs={{0,3},{1,0},{2,1},{3,2},{4,7},{5,4},{6,5},{7,6},{8,11},{9,8},{10,9... | collective-permute-start | bytes 221192 | tf_op jit(solution)/shard_map/ppermute | solution.py:18
  14.9 0.1 pad_add_fusion.column_at
  15.0 0.0 copy-start
  15.0 5.8 %copy-done = bf16[1024,8192]{1,0:T(8,128)(2,1)S(1)} copy-done((bf16[1024,8192]{1,0:T(8,128)(2,1)S(1)}, bf16[1024,8192]{1,0:T(8,128)(2,1)}, u32[]{:S(2)}) %copy-start) | copy-done | bytes 16777240
  20.7 0.0 copy-start.5
  20.7 0.0 copy-start.12
  20.7 4.1 %base_3_0.1 = (bf16[32,2048]{1,0:T(8,128)(2,1)S(1)}, f32[32,2048]{1,0:T(8,128)S(1)}) custom-call(s32[2]{0:T(128)S(1)} %pad_add_fusion.column_at, bf16[32,1152]{1,0:T(8,128)(2,1)S(1)} %attention.1.refs_0_.tagged, bf16[1024,8192]{1,0:T(8,128)(2,1)S(1)} %copy-done), custom_call_target="tpu_custom_call" | custom-call | flops 268435456 | bytes 8388608 | tf_op jit(solution)/shard_map/base_3_0/pallas_call | solution.py:181
  24.8 3.7 %collective-permute-start.8 = (bf16[32,2048]{1,0:T(8,128)(2,1)S(1)}, bf16[32,2048]{1,0:T(8,128)(2,1)S(1)}, u32[]{:S(2)}, u32[]{:S(2)}) collective-permute-start(bf16[32,2048]{1,0:T(8,128)(2,1)S(1)} %get-tuple-element.17), channel_id=1, source_target_pairs={{0,12},{4,0},{8,4},{12,8},{1,13},{5,1},{9,5},{13,9},{2,14},{6,2},{... | collective-permute-start | bytes 393224 | tf_op jit(solution)/shard_map/ppermute | solution.py:18
  28.5 0.1 pad_add_fusion.1.column_at
  28.5 0.0 collective-permute-done.refs_1_
  28.5 0.0 collective-permute-done.1.refs_2_
  28.5 0.0 collective-permute-done.2.refs_3_
  28.6 0.0 copy-done.5
  28.6 0.0 copy-done.12
  28.6 0.9 %shrink.1.refs_4_ = bf16[64,128]{1,0:T(8,128)(2,1)S(1)} custom-call(s32[1]{0:T(128)} %bitcast.first_at, s32[4]{0:T(128)S(1)} %copy-done.12, bf16[32,1152]{1,0:T(8,128)(2,1)S(1)} %attention.1.refs_0_.tagged, bf16[32,1152]{1,0:T(8,128)(2,1)S(1)} %collective-permute-done.refs_1_, bf16[32,1152]{1,0:T(8,128)(2,1)S(1)} %collective-permute-done.1.refs_2_, ...), custom_call_target="tpu_custom_call" | custom-call | flops 67108864 | bytes 786432 | tf_op jit(solution)/shard_map/shrink/pallas_call | solution.py:235
  29.5 0.1 collective-permute-start.3
  29.6 1.0 %collective-permute-start.4 = (bf16[64,128]{1,0:T(8,128)(2,1)S(1)}, bf16[64,128]{1,0:T(8,128)(2,1)S(1)}, u32[]{:S(2)}, u32[]{:S(2)}) collective-permute-start(bf16[64,128]{1,0:T(8,128)(2,1)S(1)} %shrink.1.refs_4_), channel_id=1, source_target_pairs={{0,8},{4,12},{8,0},{12,4},{1,9},{5,13},{9,1},{13,5},{2,10},{6,14},... | collective-permute-start | bytes 49160 | tf_op jit(solution)/shard_map/ppermute | solution.py:18
  30.6 2.8 %collective-permute-start.5 = (bf16[64,128]{1,0:T(8,128)(2,1)S(1)}, bf16[64,128]{1,0:T(8,128)(2,1)S(1)}, u32[]{:S(2)}, u32[]{:S(2)}) collective-permute-start(bf16[64,128]{1,0:T(8,128)(2,1)S(1)} %shrink.1.refs_4_), channel_id=1, source_target_pairs={{0,12},{4,0},{8,4},{12,8},{1,13},{5,1},{9,5},{13,9},{2,14},{6,2},{... | collective-permute-start | bytes 49160 | tf_op jit(solution)/shard_map/ppermute | solution.py:18
  33.4 0.0 copy-start.1
  33.4 5.8 %copy-done.1 = bf16[1024,8192]{1,0:T(8,128)(2,1)S(1)} copy-done((bf16[1024,8192]{1,0:T(8,128)(2,1)S(1)}, bf16[1024,8192]{1,0:T(8,128)(2,1)}, u32[]{:S(2)}) %copy-start.1) | copy-done | bytes 16777240
  39.1 0.0 copy-start.4
  39.1 4.2 %base_2_1.1 = (bf16[32,2048]{1,0:T(8,128)(2,1)S(1)}, bf16[32,2048]{1,0:T(8,128)(2,1)S(1)}) custom-call(s32[2]{0:T(128)S(1)} %pad_add_fusion.1.column_at, bf16[32,1152]{1,0:T(8,128)(2,1)S(1)} %attention.1.refs_0_.tagged, bf16[1024,8192]{1,0:T(8,128)(2,1)S(1)} %copy-done.1), custom_call_target="tpu_custom_call" | custom-call | flops 268435456 | bytes 8388608 | tf_op jit(solution)/shard_map/base_2_1/pallas_call | solution.py:181
  43.4 2.1 %collective-permute-start.6 = (bf16[32,2048]{1,0:T(8,128)(2,1)S(1)}, bf16[32,2048]{1,0:T(8,128)(2,1)S(1)}, u32[]{:S(2)}, u32[]{:S(2)}) collective-permute-start(bf16[32,2048]{1,0:T(8,128)(2,1)S(1)} %get-tuple-element.15), channel_id=1, source_target_pairs={{0,8},{4,12},{8,0},{12,4},{1,9},{5,13},{9,1},{13,5},{2,10},{6,14},... | collective-permute-start | bytes 393224 | tf_op jit(solution)/shard_map/ppermute | solution.py:18
  45.5 0.0 collective-permute-done.3.refs_5_
  45.5 0.0 collective-permute-start.7
  45.5 0.0 collective-permute-done.4.refs_6_
  45.5 0.0 collective-permute-done.5.refs_7_
  45.5 0.0 copy-done.4
  45.5 0.4 expand.1
  45.9 0.6 %collective-permute-start.10 = (bf16[32,2048]{1,0:T(8,128)(2,1)S(1)}, bf16[32,2048]{1,0:T(8,128)(2,1)S(1)}, u32[]{:S(2)}, u32[]{:S(2)}) collective-permute-start(bf16[32,2048]{1,0:T(8,128)(2,1)S(1)} %get-tuple-element.19), channel_id=1, source_target_pairs={{0,2},{1,3},{2,0},{3,1},{4,6},{5,7},{6,4},{7,5},{8,10},{9,11},{10,... | collective-permute-start | bytes 393224 | tf_op jit(solution)/shard_map/ppermute | solution.py:18
  46.5 0.0 collective-permute-start.11
  46.5 0.0 collective-permute-done.8
  46.5 1.7 %collective-permute-start.9 = (bf16[32,2048]{1,0:T(8,128)(2,1)S(1)}, bf16[32,2048]{1,0:T(8,128)(2,1)S(1)}, u32[]{:S(2)}, u32[]{:S(2)}) collective-permute-start(bf16[32,2048]{1,0:T(8,128)(2,1)S(1)} %get-tuple-element.18), channel_id=1, source_target_pairs={{0,3},{1,0},{2,1},{3,2},{4,7},{5,4},{6,5},{7,6},{8,11},{9,8},{10,9... | collective-permute-start | bytes 393224 | tf_op jit(solution)/shard_map/ppermute | solution.py:18
  48.2 5.4 %collective-permute-done.6 = bf16[32,2048]{1,0:T(8,128)(2,1)S(1)} collective-permute-done((bf16[32,2048]{1,0:T(8,128)(2,1)S(1)}, bf16[32,2048]{1,0:T(8,128)(2,1)S(1)}, u32[]{:S(2)}, u32[]{:S(2)}) %collective-permute-start.6) | collective-permute-done | bytes 131104 | tf_op jit(solution)/shard_map/ppermute | solution.py:18
  53.7 0.0 collective-permute-done.7
  53.7 0.0 collective-permute-done.10
  53.7 0.0 collective-permute-done.11
  53.7 0.0 collective-permute-done.9
  53.7 0.8 %add_convert_fusion = bf16[32,2048]{1,0:T(8,128)(2,1)} fusion(bf16[32,2048]{1,0:T(8,128)(2,1)S(1)} %collective-permute-done.11, bf16[32,2048]{1,0:T(8,128)(2,1)S(1)} %collective-permute-done.10, bf16[32,2048]{1,0:T(8,128)(2,1)S(1)} %collective-permute-done.9, bf16[32,2048]{1,0:T(8,128)(2,1)S(1)} %collective-permute-done.8, ...), kind=kLoop, calls=%fused_computation | loop fusion | flops 851968 | bytes 1179648 | tf_op jit(solution)/shard_map/convert_element_type | solution.py:354
Async XLA Ops:
  0.0 1.9 %copy-start.2 = (bf16[32,4,96,128]{3,2,1,0:T(8,128)(2,1)S(1)}, bf16[32,4,96,128]{3,2,1,0:T(8,128)(2,1)}, u32[]{:S(2)}) copy-start(bf16[32,4,96,128]{3,2,1,0:T(8,128)(2,1)} %key_cache.1) | copy-start | bytes 9437188
  1.9 1.9 %copy-start.3 = (bf16[32,4,96,128]{3,2,1,0:T(8,128)(2,1)S(1)}, bf16[32,4,96,128]{3,2,1,0:T(8,128)(2,1)}, u32[]{:S(2)}) copy-start(bf16[32,4,96,128]{3,2,1,0:T(8,128)(2,1)} %value_cache.1) | copy-start | bytes 9437188
  3.8 0.8 %copy-start.6 = (bf16[32,8,128]{2,1,0:T(8,128)(2,1)S(1)}, bf16[32,8,128]{2,1,0:T(8,128)(2,1)}, u32[]{:S(2)}) copy-start(bf16[32,8,128]{2,1,0:T(8,128)(2,1)} %queries.1) | copy-start | bytes 196612
  4.6 0.8 %copy-start.7 = (bf16[32,4,128]{2,1,0:T(4,128)(2,1)S(1)}, bf16[32,4,128]{2,1,0:T(4,128)(2,1)}, u32[]{:S(2)}) copy-start(bf16[32,4,128]{2,1,0:T(4,128)(2,1)} %new_key.1) | copy-start | bytes 98308
  5.4 0.8 %copy-start.8 = (bf16[32,4,128]{2,1,0:T(4,128)(2,1)S(1)}, bf16[32,4,128]{2,1,0:T(4,128)(2,1)}, u32[]{:S(2)}) copy-start(bf16[32,4,128]{2,1,0:T(4,128)(2,1)} %new_value.1) | copy-start | bytes 98308
  6.1 0.7 %copy-start.9 = (s32[32]{0:T(128)S(1)}, s32[32]{0:T(128)}, u32[]{:S(2)}) copy-start(s32[32]{0:T(128)} %lengths.1) | copy-start | bytes 388
  6.8 0.7 %copy-start.10 = (s32[32]{0:T(128)S(1)}, s32[32]{0:T(128)}, u32[]{:S(2)}) copy-start(s32[32]{0:T(128)} %row_adapter.1) | copy-start | bytes 388
  7.4 0.7 %copy-start.11 = (s32[8]{0:T(128)S(1)}, s32[8]{0:T(128)}, u32[]{:S(2)}) copy-start(s32[8]{0:T(128)} %adapter_list.1) | copy-start | bytes 100
  10.4 18.1 %collective-permute-start = (bf16[32,1152]{1,0:T(8,128)(2,1)S(1)}, bf16[32,1152]{1,0:T(8,128)(2,1)S(1)}, u32[]{:S(2)}, u32[]{:S(2)}) collective-permute-start(bf16[32,1152]{1,0:T(8,128)(2,1)S(1)} %attention.1.refs_0_.tagged), channel_id=1, source_target_pairs={{0,1},{1,2},{2,3},{3,0},{4,5},{5,6},{6,7},{7,4},{8,9},{9,10},{10,1... | collective-permute-start | bytes 221192 | tf_op jit(solution)/shard_map/ppermute | solution.py:18
  10.9 17.6 %collective-permute-start.1 = (bf16[32,1152]{1,0:T(8,128)(2,1)S(1)}, bf16[32,1152]{1,0:T(8,128)(2,1)S(1)}, u32[]{:S(2)}, u32[]{:S(2)}) collective-permute-start(bf16[32,1152]{1,0:T(8,128)(2,1)S(1)} %attention.1.refs_0_.tagged), channel_id=1, source_target_pairs={{0,2},{1,3},{2,0},{3,1},{4,6},{5,7},{6,4},{7,5},{8,10},{9,11},{10,... | collective-permute-start | bytes 221192 | tf_op jit(solution)/shard_map/ppermute | solution.py:18
  13.5 15.0 %collective-permute-start.2 = (bf16[32,1152]{1,0:T(8,128)(2,1)S(1)}, bf16[32,1152]{1,0:T(8,128)(2,1)S(1)}, u32[]{:S(2)}, u32[]{:S(2)}) collective-permute-start(bf16[32,1152]{1,0:T(8,128)(2,1)S(1)} %attention.1.refs_0_.tagged), channel_id=1, source_target_pairs={{0,3},{1,0},{2,1},{3,2},{4,7},{5,4},{6,5},{7,6},{8,11},{9,8},{10,9... | collective-permute-start | bytes 221192 | tf_op jit(solution)/shard_map/ppermute | solution.py:18
  15.0 5.8 %copy-start = (bf16[1024,8192]{1,0:T(8,128)(2,1)S(1)}, bf16[1024,8192]{1,0:T(8,128)(2,1)}, u32[]{:S(2)}) copy-start(bf16[1024,8192]{1,0:T(8,128)(2,1)} %out_weight.3) | copy-start | bytes 50331652
  20.7 7.8 %copy-start.5 = (bf16[4,1024,64]{1,2,0:T(8,128)(2,1)S(1)}, bf16[4,1024,64]{1,2,0:T(8,128)(2,1)}, u32[]{:S(2)}) copy-start(bf16[4,1024,64]{1,2,0:T(8,128)(2,1)} %param.19) | copy-start | bytes 1572868
  20.7 7.8 %copy-start.12 = (s32[4]{0:T(128)S(1)}, s32[4]{0:T(128)}, u32[]{:S(2)}) copy-start(s32[4]{0:T(128)} %rank.1) | copy-start | bytes 52
  24.8 21.7 %collective-permute-start.8 = (bf16[32,2048]{1,0:T(8,128)(2,1)S(1)}, bf16[32,2048]{1,0:T(8,128)(2,1)S(1)}, u32[]{:S(2)}, u32[]{:S(2)}) collective-permute-start(bf16[32,2048]{1,0:T(8,128)(2,1)S(1)} %get-tuple-element.17), channel_id=1, source_target_pairs={{0,12},{4,0},{8,4},{12,8},{1,13},{5,1},{9,5},{13,9},{2,14},{6,2},{... | collective-permute-start | bytes 393224 | tf_op jit(solution)/shard_map/ppermute | solution.py:18
  29.5 16.0 %collective-permute-start.3 = (bf16[64,128]{1,0:T(8,128)(2,1)S(1)}, bf16[64,128]{1,0:T(8,128)(2,1)S(1)}, u32[]{:S(2)}, u32[]{:S(2)}) collective-permute-start(bf16[64,128]{1,0:T(8,128)(2,1)S(1)} %shrink.1.refs_4_), channel_id=1, source_target_pairs={{0,4},{4,8},{8,12},{12,0},{1,5},{5,9},{9,13},{13,1},{2,6},{6,10},{... | collective-permute-start | bytes 49160 | tf_op jit(solution)/shard_map/ppermute | solution.py:18
  29.6 15.9 %collective-permute-start.4 = (bf16[64,128]{1,0:T(8,128)(2,1)S(1)}, bf16[64,128]{1,0:T(8,128)(2,1)S(1)}, u32[]{:S(2)}, u32[]{:S(2)}) collective-permute-start(bf16[64,128]{1,0:T(8,128)(2,1)S(1)} %shrink.1.refs_4_), channel_id=1, source_target_pairs={{0,8},{4,12},{8,0},{12,4},{1,9},{5,13},{9,1},{13,5},{2,10},{6,14},... | collective-permute-start | bytes 49160 | tf_op jit(solution)/shard_map/ppermute | solution.py:18
  30.6 14.9 %collective-permute-start.5 = (bf16[64,128]{1,0:T(8,128)(2,1)S(1)}, bf16[64,128]{1,0:T(8,128)(2,1)S(1)}, u32[]{:S(2)}, u32[]{:S(2)}) collective-permute-start(bf16[64,128]{1,0:T(8,128)(2,1)S(1)} %shrink.1.refs_4_), channel_id=1, source_target_pairs={{0,12},{4,0},{8,4},{12,8},{1,13},{5,1},{9,5},{13,9},{2,14},{6,2},{... | collective-permute-start | bytes 49160 | tf_op jit(solution)/shard_map/ppermute | solution.py:18
  33.4 5.8 %copy-start.1 = (bf16[1024,8192]{1,0:T(8,128)(2,1)S(1)}, bf16[1024,8192]{1,0:T(8,128)(2,1)}, u32[]{:S(2)}) copy-start(bf16[1024,8192]{1,0:T(8,128)(2,1)} %out_weight.3) | copy-start | bytes 50331652
  39.1 6.4 %copy-start.4 = (bf16[4,64,2048]{2,1,0:T(8,128)(2,1)S(1)}, bf16[4,64,2048]{2,1,0:T(8,128)(2,1)}, u32[]{:S(2)}) copy-start(bf16[4,64,2048]{2,1,0:T(8,128)(2,1)} %param.20) | copy-start | bytes 3145732
  43.4 10.3 %collective-permute-start.6 = (bf16[32,2048]{1,0:T(8,128)(2,1)S(1)}, bf16[32,2048]{1,0:T(8,128)(2,1)S(1)}, u32[]{:S(2)}, u32[]{:S(2)}) collective-permute-start(bf16[32,2048]{1,0:T(8,128)(2,1)S(1)} %get-tuple-element.15), channel_id=1, source_target_pairs={{0,8},{4,12},{8,0},{12,4},{1,9},{5,13},{9,1},{13,5},{2,10},{6,14},... | collective-permute-start | bytes 393224 | tf_op jit(solution)/shard_map/ppermute | solution.py:18
  45.5 8.2 %collective-permute-start.7 = (bf16[32,2048]{1,0:T(8,128)(2,1)S(1)}, bf16[32,2048]{1,0:T(8,128)(2,1)S(1)}, u32[]{:S(2)}, u32[]{:S(2)}) collective-permute-start(bf16[32,2048]{1,0:T(8,128)(2,1)S(1)} %get-tuple-element.16), channel_id=1, source_target_pairs={{0,4},{4,8},{8,12},{12,0},{1,5},{5,9},{9,13},{13,1},{2,6},{6,10},{... | collective-permute-start | bytes 393224 | tf_op jit(solution)/shard_map/ppermute | solution.py:18
  45.9 7.8 %collective-permute-start.10 = (bf16[32,2048]{1,0:T(8,128)(2,1)S(1)}, bf16[32,2048]{1,0:T(8,128)(2,1)S(1)}, u32[]{:S(2)}, u32[]{:S(2)}) collective-permute-start(bf16[32,2048]{1,0:T(8,128)(2,1)S(1)} %get-tuple-element.19), channel_id=1, source_target_pairs={{0,2},{1,3},{2,0},{3,1},{4,6},{5,7},{6,4},{7,5},{8,10},{9,11},{10,... | collective-permute-start | bytes 393224 | tf_op jit(solution)/shard_map/ppermute | solution.py:18
  46.5 7.2 %collective-permute-start.11 = (bf16[32,2048]{1,0:T(8,128)(2,1)S(1)}, bf16[32,2048]{1,0:T(8,128)(2,1)S(1)}, u32[]{:S(2)}, u32[]{:S(2)}) collective-permute-start(bf16[32,2048]{1,0:T(8,128)(2,1)S(1)} %get-tuple-element.20), channel_id=1, source_target_pairs={{0,1},{1,2},{2,3},{3,0},{4,5},{5,6},{6,7},{7,4},{8,9},{9,10},{10,1... | collective-permute-start | bytes 393224 | tf_op jit(solution)/shard_map/ppermute | solution.py:18
  46.5 7.2 %collective-permute-start.9 = (bf16[32,2048]{1,0:T(8,128)(2,1)S(1)}, bf16[32,2048]{1,0:T(8,128)(2,1)S(1)}, u32[]{:S(2)}, u32[]{:S(2)}) collective-permute-start(bf16[32,2048]{1,0:T(8,128)(2,1)S(1)} %get-tuple-element.18), channel_id=1, source_target_pairs={{0,3},{1,0},{2,1},{3,2},{4,7},{5,4},{6,5},{7,6},{8,11},{9,8},{10,9... | collective-permute-start | bytes 393224 | tf_op jit(solution)/shard_map/ppermute | solution.py:18

commit v3 on v2

--- a/solution.py
+++ b/solution.py
@@ -11,6 +11,7 @@
 KVH = 4
 LANES = 128
 VMEM = pltpu.VMEM
+GRANT = 56 << 20
 F32, BF16 = jnp.float32, jnp.bfloat16
 
 
@@ -132,7 +133,7 @@
             pltpu.SemaphoreType.DMA((parts,)),
             pltpu.SemaphoreType.DMA((parts,)),
         ],
-        compiler_params=pltpu.CompilerParams(vmem_limit_bytes=8 << 20),
+        compiler_params=pltpu.CompilerParams(vmem_limit_bytes=GRANT),
         cost_estimate=pl.CostEstimate(
             flops=4 * rows * heads * positions * width,
             bytes_accessed=4 * rows * positions * width,
@@ -186,9 +187,7 @@
         in_specs=[pl.BlockSpec(memory_space=pltpu.SMEM), whole, pl.BlockSpec(memory_space=pl.ANY)],
         out_specs=[whole] * len(shifts),
         scratch_shapes=[VMEM((held, width, piece), BF16), pltpu.SemaphoreType.DMA((held,))],
-        compiler_params=pltpu.CompilerParams(
-            vmem_limit_bytes=(2 * held * width * piece) + (8 << 20)
-        ),
+        compiler_params=pltpu.CompilerParams(vmem_limit_bytes=GRANT),
         cost_estimate=pl.CostEstimate(
             flops=2 * rows * width * block * len(shifts),
             bytes_accessed=2 * width * block * len(shifts),

time: 54.9 us -> 40.6 us (0.74)
  local copies, waits for them, and re-layouts: 19.6 us -> 0.03 us
  Pallas kernels: 11.9 us -> 16.1 us
  other arithmetic: 0.93 us -> 2.03 us
    unnamed x26 -> x12, local copies, waits for them, and re-layouts: 19.6 us -> 0.03 us
    pallas_call x2, Pallas kernels: 8.3 us -> 10.8 us  [base_blocks(): pl.pallas_call(functools.partial(base_kernel, shifts, tensor_size, block,...]
    pallas_call x1, Pallas kernels: 2.32 us -> 3.98 us  [attend(): pl.pallas_call(functools.partial(attend_kernel, parts), out_shape=jax.Sha...]
    another operation x2, other arithmetic: 0.15 us -> 1.26 us  [base_blocks(): jnp.stack([(here + shift) % tensor_size for shift in shifts])]
  transfers between devices with their start and end apart: 12 -> 12, of which waited for: 1 -> 1; matrix products, arithmetic and copies ran while one was open for 0% -> 3% of each run, Pallas kernels for 18% -> 30%
where the time goes in v3:
time: 40.6 us; the launch traced here: 40.4 us
  starting transfers between devices  16.4 us (40%)
  Pallas kernels  16.1 us (40%)
  waiting for transfers between devices  5.65 us (14%)
  other arithmetic  2.03 us (5%)
    ppermute x12, starting transfers between devices, shifted(): lax.ppermute(array, axis, [(i, (i + shift) % size) for i in range(size)])  16.4 us
    pallas_call x2, Pallas kernels, base_blocks(): pl.pallas_call(functools.partial(base_kernel, shifts, tensor_size, block,...  10.8 us
    ppermute x12, waiting for transfers between devices, shifted(): lax.ppermute(array, axis, [(i, (i + shift) % size) for i in range(size)])  5.65 us
    pallas_call x1, Pallas kernels, attend(): pl.pallas_call(functools.partial(attend_kernel, parts), out_shape=jax.Sha...  3.98 us
    another operation x2, other arithmetic, base_blocks(): jnp.stack([(here + shift) % tensor_size for shift in shifts])  1.26 us
    pallas_call x1, Pallas kernels, shrink_part(): pl.pallas_call(functools.partial(shrink_kernel, len(blocks)), out_shape=j...  0.92 us
  transfers between devices with their start and end apart: 12, of which 1 were waited for; matrix products, arithmetic and copies ran while one was open for 3% of the time, Pallas kernels for 30%

profile of v3, /device:TPU:0, one launch (start us, length us, event | category | flops | bytes accessed | tf_op | source)
XLA Modules:
  0.0 40.4 jit_solution(11557098887429710765)
XLA Ops:
  0.0 4.0 %attention.1.refs_0_.tagged = bf16[32,1152]{1,0:T(8,128)(2,1)} custom-call(s32[32]{0:T(128)} %lengths.1, s32[32]{0:T(128)} %row_adapter.1, s32[8]{0:T(128)} %adapter_list.1, s32[1]{0:T(128)} %bitcast.1.group_at, bf16[32,8,128]{2,1,0:T(8,128)(2,1)} %queries.1, bf16[32,4,96,128]{3,2,1,0:T(8,128)(2,1)} %key_cache.1, bf16[32,4,96,128]{3,2,1,0:T(8,128)(2,1)} %value_cache.1, ...), custom_call_target="tpu_custom_call" | custom-call | flops 12582912 | bytes 1572864 | tf_op jit(solution)/shard_map/attention/pallas_call | solution.py:124
  4.0 0.5 %collective-permute-start = (bf16[32,1152]{1,0:T(8,128)(2,1)}, bf16[32,1152]{1,0:T(8,128)(2,1)S(1)}, u32[]{:S(2)}, u32[]{:S(2)}) collective-permute-start(bf16[32,1152]{1,0:T(8,128)(2,1)} %attention.1.refs_0_.tagged), channel_id=1, source_target_pairs={{0,1},{1,2},{2,3},{3,0},{4,5},{5,6},{6,7},{7,4},{8,9},{9,10},{10,1... | collective-permute-start | bytes 221192 | tf_op jit(solution)/shard_map/ppermute | solution.py:19
  4.5 2.6 %collective-permute-start.1 = (bf16[32,1152]{1,0:T(8,128)(2,1)}, bf16[32,1152]{1,0:T(8,128)(2,1)S(1)}, u32[]{:S(2)}, u32[]{:S(2)}) collective-permute-start(bf16[32,1152]{1,0:T(8,128)(2,1)} %attention.1.refs_0_.tagged), channel_id=1, source_target_pairs={{0,2},{1,3},{2,0},{3,1},{4,6},{5,7},{6,4},{7,5},{8,10},{9,11},{10,... | collective-permute-start | bytes 221192 | tf_op jit(solution)/shard_map/ppermute | solution.py:19
  7.1 1.4 %collective-permute-start.2 = (bf16[32,1152]{1,0:T(8,128)(2,1)}, bf16[32,1152]{1,0:T(8,128)(2,1)S(1)}, u32[]{:S(2)}, u32[]{:S(2)}) collective-permute-start(bf16[32,1152]{1,0:T(8,128)(2,1)} %attention.1.refs_0_.tagged), channel_id=1, source_target_pairs={{0,3},{1,0},{2,1},{3,2},{4,7},{5,4},{6,5},{7,6},{8,11},{9,8},{10,9... | collective-permute-start | bytes 221192 | tf_op jit(solution)/shard_map/ppermute | solution.py:19
  8.4 0.6 %pad_add_fusion.column_at = s32[2]{0:T(128)} fusion(s32[1]{0:T(128)} %bitcast.5, s32[1]{0:T(128)} %bitcast.4), kind=kLoop, calls=%fused_computation.1 | loop fusion | flops 2 | bytes 16 | tf_op jit(solution)/shard_map/stack | solution.py:179
  9.1 0.0 copy-start
  9.1 0.0 copy-start.3
  9.1 0.0 copy-start.5
  9.1 5.5 %base_3_0.1 = (bf16[32,2048]{1,0:T(8,128)(2,1)}, f32[32,2048]{1,0:T(8,128)}) custom-call(s32[2]{0:T(128)} %pad_add_fusion.column_at, bf16[32,1152]{1,0:T(8,128)(2,1)} %attention.1.refs_0_.tagged, bf16[1024,8192]{1,0:T(8,128)(2,1)} %out_weight.3), custom_call_target="tpu_custom_call" | custom-call | flops 268435456 | bytes 8388608 | tf_op jit(solution)/shard_map/base_3_0/pallas_call | solution.py:182
  14.6 3.7 %collective-permute-start.8 = (bf16[32,2048]{1,0:T(8,128)(2,1)}, bf16[32,2048]{1,0:T(8,128)(2,1)S(1)}, u32[]{:S(2)}, u32[]{:S(2)}) collective-permute-start(bf16[32,2048]{1,0:T(8,128)(2,1)} %get-tuple-element.17), channel_id=1, source_target_pairs={{0,12},{4,0},{8,4},{12,8},{1,13},{5,1},{9,5},{13,9},{2,14},{6,2},{... | collective-permute-start | bytes 393224 | tf_op jit(solution)/shard_map/ppermute | solution.py:19
  18.3 0.6 %pad_add_fusion.1.column_at = s32[2]{0:T(128)} fusion(s32[1]{0:T(128)} %bitcast.7, s32[1]{0:T(128)} %bitcast.6), kind=kLoop, calls=%fused_computation.2 | loop fusion | flops 2 | bytes 16 | tf_op jit(solution)/shard_map/stack | solution.py:179
  18.9 0.0 collective-permute-done.refs_1_
  18.9 0.0 collective-permute-done.1.refs_2_
  18.9 0.0 collective-permute-done.2.refs_3_
  18.9 0.0 copy-done
  18.9 0.0 copy-done.3
  18.9 0.0 copy-done.5
  18.9 0.9 %shrink.1.refs_4_ = bf16[64,128]{1,0:T(8,128)(2,1)S(1)} custom-call(s32[1]{0:T(128)} %bitcast.first_at, s32[4]{0:T(128)S(1)} %copy-done.5, bf16[32,1152]{1,0:T(8,128)(2,1)S(1)} %copy-done, bf16[32,1152]{1,0:T(8,128)(2,1)S(1)} %collective-permute-done.refs_1_, bf16[32,1152]{1,0:T(8,128)(2,1)S(1)} %collective-permute-done.1.refs_2_, ...), custom_call_target="tpu_custom_call" | custom-call | flops 67108864 | bytes 786432 | tf_op jit(solution)/shard_map/shrink/pallas_call | solution.py:234
  19.8 0.0 copy-start.1
  19.8 0.0 copy-start.2
  19.9 0.0 copy-start.4
  19.9 0.1 collective-permute-start.3
  19.9 1.0 %collective-permute-start.4 = (bf16[64,128]{1,0:T(8,128)(2,1)S(1)}, bf16[64,128]{1,0:T(8,128)(2,1)S(1)}, u32[]{:S(2)}, u32[]{:S(2)}) collective-permute-start(bf16[64,128]{1,0:T(8,128)(2,1)S(1)} %shrink.1.refs_4_), channel_id=1, source_target_pairs={{0,8},{4,12},{8,0},{12,4},{1,9},{5,13},{9,1},{13,5},{2,10},{6,14},... | collective-permute-start | bytes 49160 | tf_op jit(solution)/shard_map/ppermute | solution.py:19
  20.9 2.8 %collective-permute-start.5 = (bf16[64,128]{1,0:T(8,128)(2,1)S(1)}, bf16[64,128]{1,0:T(8,128)(2,1)S(1)}, u32[]{:S(2)}, u32[]{:S(2)}) collective-permute-start(bf16[64,128]{1,0:T(8,128)(2,1)S(1)} %shrink.1.refs_4_), channel_id=1, source_target_pairs={{0,12},{4,0},{8,4},{12,8},{1,13},{5,1},{9,5},{13,9},{2,14},{6,2},{... | collective-permute-start | bytes 49160 | tf_op jit(solution)/shard_map/ppermute | solution.py:19
  23.7 5.4 %base_2_1.1 = (bf16[32,2048]{1,0:T(8,128)(2,1)}, bf16[32,2048]{1,0:T(8,128)(2,1)}) custom-call(s32[2]{0:T(128)} %pad_add_fusion.1.column_at, bf16[32,1152]{1,0:T(8,128)(2,1)} %attention.1.refs_0_.tagged, bf16[1024,8192]{1,0:T(8,128)(2,1)} %out_weight.3), custom_call_target="tpu_custom_call" | custom-call | flops 268435456 | bytes 8388608 | tf_op jit(solution)/shard_map/base_2_1/pallas_call | solution.py:182
  29.1 2.1 %collective-permute-start.6 = (bf16[32,2048]{1,0:T(8,128)(2,1)}, bf16[32,2048]{1,0:T(8,128)(2,1)S(1)}, u32[]{:S(2)}, u32[]{:S(2)}) collective-permute-start(bf16[32,2048]{1,0:T(8,128)(2,1)} %get-tuple-element.15), channel_id=1, source_target_pairs={{0,8},{4,12},{8,0},{12,4},{1,9},{5,13},{9,1},{13,5},{2,10},{6,14},... | collective-permute-start | bytes 393224 | tf_op jit(solution)/shard_map/ppermute | solution.py:19
  31.2 0.0 collective-permute-done.3.refs_5_
  31.2 0.0 collective-permute-start.7
  31.2 0.0 collective-permute-done.4.refs_6_
  31.2 0.0 collective-permute-done.5.refs_7_
  31.2 0.0 copy-done.1
  31.2 0.0 copy-done.2
  31.3 0.0 copy-done.4
  31.3 0.4 expand.1
  31.6 0.6 %collective-permute-start.10 = (bf16[32,2048]{1,0:T(8,128)(2,1)S(1)}, bf16[32,2048]{1,0:T(8,128)(2,1)S(1)}, u32[]{:S(2)}, u32[]{:S(2)}) collective-permute-start(bf16[32,2048]{1,0:T(8,128)(2,1)S(1)} %get-tuple-element.19), channel_id=1, source_target_pairs={{0,2},{1,3},{2,0},{3,1},{4,6},{5,7},{6,4},{7,5},{8,10},{9,11},{10,... | collective-permute-start | bytes 393224 | tf_op jit(solution)/shard_map/ppermute | solution.py:19
  32.2 0.0 collective-permute-start.11
  32.2 0.0 collective-permute-done.8
  32.2 1.7 %collective-permute-start.9 = (bf16[32,2048]{1,0:T(8,128)(2,1)S(1)}, bf16[32,2048]{1,0:T(8,128)(2,1)S(1)}, u32[]{:S(2)}, u32[]{:S(2)}) collective-permute-start(bf16[32,2048]{1,0:T(8,128)(2,1)S(1)} %get-tuple-element.18), channel_id=1, source_target_pairs={{0,3},{1,0},{2,1},{3,2},{4,7},{5,4},{6,5},{7,6},{8,11},{9,8},{10,9... | collective-permute-start | bytes 393224 | tf_op jit(solution)/shard_map/ppermute | solution.py:19
  34.0 5.6 %collective-permute-done.6 = bf16[32,2048]{1,0:T(8,128)(2,1)S(1)} collective-permute-done((bf16[32,2048]{1,0:T(8,128)(2,1)}, bf16[32,2048]{1,0:T(8,128)(2,1)S(1)}, u32[]{:S(2)}, u32[]{:S(2)}) %collective-permute-start.6) | collective-permute-done | bytes 131104 | tf_op jit(solution)/shard_map/ppermute | solution.py:19
  39.6 0.0 collective-permute-done.7
  39.6 0.0 collective-permute-done.10
  39.6 0.0 collective-permute-done.11
  39.6 0.0 collective-permute-done.9
  39.6 0.8 %add_convert_fusion = bf16[32,2048]{1,0:T(8,128)(2,1)} fusion(bf16[32,2048]{1,0:T(8,128)(2,1)S(1)} %collective-permute-done.11, bf16[32,2048]{1,0:T(8,128)(2,1)S(1)} %collective-permute-done.10, bf16[32,2048]{1,0:T(8,128)(2,1)S(1)} %collective-permute-done.9, bf16[32,2048]{1,0:T(8,128)(2,1)S(1)} %collective-permute-done.8, ...), kind=kLoop, calls=%fused_computation | loop fusion | flops 851968 | bytes 1179648 | tf_op jit(solution)/shard_map/convert_element_type | solution.py:353
Async XLA Ops:
  4.0 14.9 %collective-permute-start = (bf16[32,1152]{1,0:T(8,128)(2,1)}, bf16[32,1152]{1,0:T(8,128)(2,1)S(1)}, u32[]{:S(2)}, u32[]{:S(2)}) collective-permute-start(bf16[32,1152]{1,0:T(8,128)(2,1)} %attention.1.refs_0_.tagged), channel_id=1, source_target_pairs={{0,1},{1,2},{2,3},{3,0},{4,5},{5,6},{6,7},{7,4},{8,9},{9,10},{10,1... | collective-permute-start | bytes 221192 | tf_op jit(solution)/shard_map/ppermute | solution.py:19
  4.5 14.4 %collective-permute-start.1 = (bf16[32,1152]{1,0:T(8,128)(2,1)}, bf16[32,1152]{1,0:T(8,128)(2,1)S(1)}, u32[]{:S(2)}, u32[]{:S(2)}) collective-permute-start(bf16[32,1152]{1,0:T(8,128)(2,1)} %attention.1.refs_0_.tagged), channel_id=1, source_target_pairs={{0,2},{1,3},{2,0},{3,1},{4,6},{5,7},{6,4},{7,5},{8,10},{9,11},{10,... | collective-permute-start | bytes 221192 | tf_op jit(solution)/shard_map/ppermute | solution.py:19
  7.1 11.8 %collective-permute-start.2 = (bf16[32,1152]{1,0:T(8,128)(2,1)}, bf16[32,1152]{1,0:T(8,128)(2,1)S(1)}, u32[]{:S(2)}, u32[]{:S(2)}) collective-permute-start(bf16[32,1152]{1,0:T(8,128)(2,1)} %attention.1.refs_0_.tagged), channel_id=1, source_target_pairs={{0,3},{1,0},{2,1},{3,2},{4,7},{5,4},{6,5},{7,6},{8,11},{9,8},{10,9... | collective-permute-start | bytes 221192 | tf_op jit(solution)/shard_map/ppermute | solution.py:19
  9.1 9.8 %copy-start = (bf16[32,1152]{1,0:T(8,128)(2,1)S(1)}, bf16[32,1152]{1,0:T(8,128)(2,1)}, u32[]{:S(2)}) copy-start(bf16[32,1152]{1,0:T(8,128)(2,1)} %attention.1.refs_0_.tagged) | copy-start | bytes 221188
  9.1 9.8 %copy-start.3 = (bf16[4,1024,64]{1,2,0:T(8,128)(2,1)S(1)}, bf16[4,1024,64]{1,2,0:T(8,128)(2,1)}, u32[]{:S(2)}) copy-start(bf16[4,1024,64]{1,2,0:T(8,128)(2,1)} %param.19) | copy-start | bytes 1572868
  9.1 9.8 %copy-start.5 = (s32[4]{0:T(128)S(1)}, s32[4]{0:T(128)}, u32[]{:S(2)}) copy-start(s32[4]{0:T(128)} %rank.1) | copy-start | bytes 52
  14.6 17.6 %collective-permute-start.8 = (bf16[32,2048]{1,0:T(8,128)(2,1)}, bf16[32,2048]{1,0:T(8,128)(2,1)S(1)}, u32[]{:S(2)}, u32[]{:S(2)}) collective-permute-start(bf16[32,2048]{1,0:T(8,128)(2,1)} %get-tuple-element.17), channel_id=1, source_target_pairs={{0,12},{4,0},{8,4},{12,8},{1,13},{5,1},{9,5},{13,9},{2,14},{6,2},{... | collective-permute-start | bytes 393224 | tf_op jit(solution)/shard_map/ppermute | solution.py:19
  19.8 11.4 %copy-start.1 = (bf16[32,1152]{1,0:T(8,128)(2,1)S(1)}, bf16[32,1152]{1,0:T(8,128)(2,1)}, u32[]{:S(2)}) copy-start(bf16[32,1152]{1,0:T(8,128)(2,1)} %attention.1.refs_0_.tagged) | copy-start | bytes 221188
  19.8 11.4 %copy-start.2 = (bf16[4,64,2048]{2,1,0:T(8,128)(2,1)S(1)}, bf16[4,64,2048]{2,1,0:T(8,128)(2,1)}, u32[]{:S(2)}) copy-start(bf16[4,64,2048]{2,1,0:T(8,128)(2,1)} %param.20) | copy-start | bytes 3145732
  19.9 11.4 %copy-start.4 = (f32[32,2048]{1,0:T(8,128)S(1)}, f32[32,2048]{1,0:T(8,128)}, u32[]{:S(2)}) copy-start(f32[32,2048]{1,0:T(8,128)} %get-tuple-element.13.refs_9_) | copy-start | bytes 786436
  19.9 11.3 %collective-permute-start.3 = (bf16[64,128]{1,0:T(8,128)(2,1)S(1)}, bf16[64,128]{1,0:T(8,128)(2,1)S(1)}, u32[]{:S(2)}, u32[]{:S(2)}) collective-permute-start(bf16[64,128]{1,0:T(8,128)(2,1)S(1)} %shrink.1.refs_4_), channel_id=1, source_target_pairs={{0,4},{4,8},{8,12},{12,0},{1,5},{5,9},{9,13},{13,1},{2,6},{6,10},{... | collective-permute-start | bytes 49160 | tf_op jit(solution)/shard_map/ppermute | solution.py:19
  19.9 11.3 %collective-permute-start.4 = (bf16[64,128]{1,0:T(8,128)(2,1)S(1)}, bf16[64,128]{1,0:T(8,128)(2,1)S(1)}, u32[]{:S(2)}, u32[]{:S(2)}) collective-permute-start(bf16[64,128]{1,0:T(8,128)(2,1)S(1)} %shrink.1.refs_4_), channel_id=1, source_target_pairs={{0,8},{4,12},{8,0},{12,4},{1,9},{5,13},{9,1},{13,5},{2,10},{6,14},... | collective-permute-start | bytes 49160 | tf_op jit(solution)/shard_map/ppermute | solution.py:19
  20.9 10.3 %collective-permute-start.5 = (bf16[64,128]{1,0:T(8,128)(2,1)S(1)}, bf16[64,128]{1,0:T(8,128)(2,1)S(1)}, u32[]{:S(2)}, u32[]{:S(2)}) collective-permute-start(bf16[64,128]{1,0:T(8,128)(2,1)S(1)} %shrink.1.refs_4_), channel_id=1, source_target_pairs={{0,12},{4,0},{8,4},{12,8},{1,13},{5,1},{9,5},{13,9},{2,14},{6,2},{... | collective-permute-start | bytes 49160 | tf_op jit(solution)/shard_map/ppermute | solution.py:19
  29.1 10.5 %collective-permute-start.6 = (bf16[32,2048]{1,0:T(8,128)(2,1)}, bf16[32,2048]{1,0:T(8,128)(2,1)S(1)}, u32[]{:S(2)}, u32[]{:S(2)}) collective-permute-start(bf16[32,2048]{1,0:T(8,128)(2,1)} %get-tuple-element.15), channel_id=1, source_target_pairs={{0,8},{4,12},{8,0},{12,4},{1,9},{5,13},{9,1},{13,5},{2,10},{6,14},... | collective-permute-start | bytes 393224 | tf_op jit(solution)/shard_map/ppermute | solution.py:19
  31.2 8.4 %collective-permute-start.7 = (bf16[32,2048]{1,0:T(8,128)(2,1)}, bf16[32,2048]{1,0:T(8,128)(2,1)S(1)}, u32[]{:S(2)}, u32[]{:S(2)}) collective-permute-start(bf16[32,2048]{1,0:T(8,128)(2,1)} %get-tuple-element.16), channel_id=1, source_target_pairs={{0,4},{4,8},{8,12},{12,0},{1,5},{5,9},{9,13},{13,1},{2,6},{6,10},{... | collective-permute-start | bytes 393224 | tf_op jit(solution)/shard_map/ppermute | solution.py:19
  31.6 8.0 %collective-permute-start.10 = (bf16[32,2048]{1,0:T(8,128)(2,1)S(1)}, bf16[32,2048]{1,0:T(8,128)(2,1)S(1)}, u32[]{:S(2)}, u32[]{:S(2)}) collective-permute-start(bf16[32,2048]{1,0:T(8,128)(2,1)S(1)} %get-tuple-element.19), channel_id=1, source_target_pairs={{0,2},{1,3},{2,0},{3,1},{4,6},{5,7},{6,4},{7,5},{8,10},{9,11},{10,... | collective-permute-start | bytes 393224 | tf_op jit(solution)/shard_map/ppermute | solution.py:19
  32.2 7.4 %collective-permute-start.11 = (bf16[32,2048]{1,0:T(8,128)(2,1)S(1)}, bf16[32,2048]{1,0:T(8,128)(2,1)S(1)}, u32[]{:S(2)}, u32[]{:S(2)}) collective-permute-start(bf16[32,2048]{1,0:T(8,128)(2,1)S(1)} %get-tuple-element.20), channel_id=1, source_target_pairs={{0,1},{1,2},{2,3},{3,0},{4,5},{5,6},{6,7},{7,4},{8,9},{9,10},{10,1... | collective-permute-start | bytes 393224 | tf_op jit(solution)/shard_map/ppermute | solution.py:19
  32.2 7.4 %collective-permute-start.9 = (bf16[32,2048]{1,0:T(8,128)(2,1)S(1)}, bf16[32,2048]{1,0:T(8,128)(2,1)S(1)}, u32[]{:S(2)}, u32[]{:S(2)}) collective-permute-start(bf16[32,2048]{1,0:T(8,128)(2,1)S(1)} %get-tuple-element.18), channel_id=1, source_target_pairs={{0,3},{1,0},{2,1},{3,2},{4,7},{5,4},{6,5},{7,6},{8,11},{9,8},{10,9... | collective-permute-start | bytes 393224 | tf_op jit(solution)/shard_map/ppermute | solution.py:19

commit v4 on v3

v4 whole, which is shorter than its diff:
```python
import functools

import jax
import jax.numpy as jnp
from jax import lax
from jax.experimental import pallas as pl
from jax.experimental.pallas import tpu as pltpu
from jax.sharding import PartitionSpec as P

HQ = 32
KVH = 4
LANES = 128
VMEM = pltpu.VMEM
GRANT = 56 << 20
F32, BF16 = jnp.float32, jnp.bfloat16


def exchanged(blocks, axis):
    return lax.all_to_all(blocks, axis, 0, 0, tiled=True)


def lane_of(shape):
    return lax.broadcasted_iota(jnp.int32, shape, len(shape) - 1)


def attend_kernel(parts, copies_out, group_at, *refs):
    given, (tagged, *scratch) = refs[:8], refs[8:]
    held, (spread_out, small_sems, key_sems, value_sems) = scratch[:8], scratch[8:]
    key_cache, value_cache = given[:2]
    keys, values, queries, new_key, new_value, lengths, row_adapter, adapter_list = held
    rows, heads, width = queries.shape
    positions = key_cache.shape[2]
    group = group_at[0]
    some = rows // parts

    def cache_copies(part):
        at = pl.ds(part * some, some)
        return (
            pltpu.make_async_copy(key_cache.at[at, group], keys.at[at], key_sems.at[part]),
            pltpu.make_async_copy(value_cache.at[at, group], values.at[at], value_sems.at[part]),
        )

    small = [
        pltpu.make_async_copy(given[i], held[i], small_sems.at[i - 2]) for i in range(2, 8)
    ]
    for copy in small:
        copy.start()
    for part in range(parts):
        for copy in cache_copies(part):
            copy.start()
    for copy in small:
        copy.wait()
    at_row = lax.broadcasted_iota(jnp.int32, (rows, LANES), 0)
    tag = jnp.zeros((rows, LANES), jnp.int32)
    for row in range(rows):
        tag = jnp.where(at_row == row, adapter_list[row_adapter[row]], tag)
    tag = tag.astype(F32).astype(BF16)

    group_row = lax.broadcasted_iota(jnp.int32, new_key.shape, 1) == group
    fresh_key = jnp.sum(
        jnp.where(group_row, new_key[...].astype(F32), F32(0.0)), axis=1, keepdims=True
    )
    fresh_value = jnp.sum(
        jnp.where(group_row, new_value[...].astype(F32), F32(0.0)), axis=1, keepdims=True
    )
    score_scale = width ** (-0.5)
    fresh = jnp.sum(queries[...].astype(F32) * fresh_key, axis=-1, keepdims=True) * score_scale
    for part in range(parts):
        at = slice(part * some, (part + 1) * some)
        key_copy, value_copy = cache_copies(part)
        key_copy.wait()
        scores = (
            lax.dot_general(
                queries[at], keys[at], (((2,), (2,)), ((0,), (0,))), preferred_element_type=F32
            )
            * score_scale
        )
        length = jnp.stack(
            [
                jnp.full((heads, positions), lengths[row], jnp.int32)
                for row in range(part * some, (part + 1) * some)
            ]
        )
        valid = lane_of(scores.shape) < length
        masked = jnp.where(valid, scores, F32(-1e30))
        highest = jnp.maximum(jnp.max(masked, axis=-1, keepdims=True), fresh[at])
        cached_exp = jnp.where(valid, jnp.exp(masked - highest), F32(0.0))
        fresh_exp = jnp.exp(fresh[at] - highest)
        totals = jnp.sum(cached_exp, axis=-1, keepdims=True) + fresh_exp
        cached_w = (cached_exp / totals).astype(BF16)
        fresh_w = (fresh_exp / totals).astype(BF16).astype(F32)
        value_copy.wait()
        attended = lax.dot_general(
            cached_w, values[at], (((2,), (1,)), ((0,), (0,))), preferred_element_type=F32
        )
        attended = attended + fresh_w * fresh_value[at]
        spread_out[pl.ds(part * some * heads, some * heads)] = attended.reshape(
            some * heads, width
        )
    for copy in range(copies_out):
        tagged[copy * rows : (copy + 1) * rows, heads * width :] = tag
    for head in range(heads):
        block = spread_out[pl.ds(head, rows, stride=heads)].astype(BF16)
        for copy in range(copies_out):
            tagged[copy * rows : (copy + 1) * rows, head * width : (head + 1) * width] = block


def attend(
    copies_out,
    queries,
    key_cache,
    value_cache,
    new_key,
    new_value,
    lengths,
    adapter_list,
    row_adapter,
):
    rows, heads, width = queries.shape
    positions = key_cache.shape[2]
    per_group = HQ // KVH
    group_at = (lax.axis_index("tensor") * heads // per_group).reshape(1).astype(jnp.int32)
    full = -(-heads // 8) * 8
    if full != heads:
        queries = jnp.pad(queries, ((0, 0), (0, full - heads), (0, 0)))
    parts = 2
    smem = pl.BlockSpec(memory_space=pltpu.SMEM)
    away = pl.BlockSpec(memory_space=pl.ANY)
    tagged = pl.pallas_call(
        functools.partial(attend_kernel, parts, copies_out),
        out_shape=jax.ShapeDtypeStruct((copies_out * rows, full * width + LANES), BF16),
        in_specs=[smem] + [away] * 8,
        out_specs=pl.BlockSpec(memory_space=VMEM),
        scratch_shapes=[
            VMEM((rows, positions, width), BF16),
            VMEM((rows, positions, width), BF16),
            VMEM(queries.shape, BF16),
            VMEM(new_key.shape, BF16),
            VMEM(new_value.shape, BF16),
            pltpu.SMEM(lengths.shape, jnp.int32),
            pltpu.SMEM(row_adapter.shape, jnp.int32),
            pltpu.SMEM(adapter_list.shape, jnp.int32),
            VMEM((rows * full, width), F32),
            pltpu.SemaphoreType.DMA((6,)),
            pltpu.SemaphoreType.DMA((parts,)),
            pltpu.SemaphoreType.DMA((parts,)),
        ],
        compiler_params=pltpu.CompilerParams(vmem_limit_bytes=GRANT),
        cost_estimate=pl.CostEstimate(
            flops=4 * rows * heads * positions * width,
            bytes_accessed=4 * rows * positions * width,
            transcendentals=rows * heads * positions,
        ),
        name="attention",
    )(
        group_at,
        key_cache,
        value_cache,
        queries,
        new_key,
        new_value,
        lengths,
        row_adapter,
        adapter_list,
    )
    if full != heads:
        tagged = jnp.concatenate([tagged[:, : heads * width], tagged[:, full * width :]], axis=1)
    return tagged


def base_kernel(starts, rows, piece, deep, tagged, out_weight, out, held, sems):
    width = out_weight.shape[0]
    count = len(starts)

    def copy(at):
        return pltpu.make_async_copy(
            out_weight.at[:, pl.ds(starts[at], piece)], held.at[at % deep], sems.at[at % deep]
        )

    for at in range(min(deep, count)):
        copy(at).start()
    per = out.shape[1] // piece
    for at in range(count):
        copy(at).wait()
        term = jnp.dot(tagged[:rows, :width], held[at % deep], preferred_element_type=F32)
        to, column = at // per * rows, at % per * piece
        out[to : to + rows, column : column + piece] = term.astype(out.dtype)
        if at + deep < count:
            copy(at + deep).start()


def base_blocks(tagged, out_weight, rows, tensor_size, block, first, last):
    width = out_weight.shape[0]
    piece = min(last - first, 256)
    starts = [
        to * block + column for to in range(tensor_size) for column in range(first, last, piece)
    ]
    deep = 6
    whole = pl.BlockSpec(memory_space=VMEM)
    return pl.pallas_call(
        functools.partial(base_kernel, starts, rows, piece, deep),
        out_shape=jax.ShapeDtypeStruct((tensor_size * rows, last - first), BF16),
        in_specs=[whole, pl.BlockSpec(memory_space=pl.ANY)],
        out_specs=whole,
        scratch_shapes=[VMEM((deep, width, piece), BF16), pltpu.SemaphoreType.DMA((deep,))],
        compiler_params=pltpu.CompilerParams(vmem_limit_bytes=GRANT),
        cost_estimate=pl.CostEstimate(
            flops=2 * rows * width * (last - first) * tensor_size,
            bytes_accessed=2 * width * (last - first) * tensor_size,
            transcendentals=0,
        ),
        name="base_terms",
    )(tagged, out_weight)


def slots_of(tags, first):
    return tags.astype(F32).astype(jnp.int32) - first


def shrink_kernel(copies_out, first_at, rank, everyone, factors, out):
    pool, rank_width, width = factors.shape
    slot = slots_of(everyone[:, width:], first_at[0])
    terms = lax.dot_general(
        everyone[:, :width],
        factors[...].reshape(pool * rank_width, width),
        (((1,), (1,)), ((), ())),
        preferred_element_type=F32,
    )
    lane = lane_of(slot.shape)
    per = LANES // rank_width
    kept = jnp.zeros(slot.shape, F32)
    for tile in range(pool // per):
        mine, limit = tile * per + lane // rank_width, jnp.zeros_like(lane)
        for n in range(tile * per, (tile + 1) * per):
            limit = jnp.where(mine == n, rank[n], limit)
        keep = (slot == mine) & (lane % rank_width < limit)
        kept = kept + jnp.where(keep, terms[:, tile * LANES : (tile + 1) * LANES], F32(0.0))
    both = kept + pltpu.roll(kept, rank_width, 1)
    half = both.shape[0] // 2
    packed = jnp.where(lane[:half] < rank_width, both[:half], both[half:]).astype(out.dtype)
    for copy in range(copies_out):
        out[copy * half : (copy + 1) * half] = packed


def shrink_part(copies_out, everyone, shrink_weight, adapter_rank, first_at):
    pool, width, rank_width = shrink_weight.shape
    rows = everyone.shape[0]
    smem = pl.BlockSpec(memory_space=pltpu.SMEM)
    whole = pl.BlockSpec(memory_space=VMEM)
    return pl.pallas_call(
        functools.partial(shrink_kernel, copies_out),
        out_shape=jax.ShapeDtypeStruct((copies_out * rows // 2, LANES), BF16),
        in_specs=[smem, smem, whole, whole],
        out_specs=whole,
        compiler_params=pltpu.CompilerParams(vmem_limit_bytes=8 << 20),
        cost_estimate=pl.CostEstimate(
            flops=2 * rows * width * pool * rank_width,
            bytes_accessed=2 * width * (rows + pool * rank_width),
            transcendentals=0,
        ),
        name="shrink",
    )(first_at, adapter_rank, everyone, jnp.swapaxes(shrink_weight, 1, 2))


def expand_kernel(sums, rank_width, first_at, everyone, parts, factors, out):
    slot = slots_of(everyone[...], first_at[0])
    half = parts.shape[0] // sums
    total = parts[:half].astype(F32)
    for at in range(1, sums):
        total = total + parts[at * half : (at + 1) * half].astype(F32)
    total = total.astype(BF16).astype(F32)
    other = pltpu.roll(total, rank_width, 1)
    low = lane_of(total.shape) < rank_width
    shrink = jnp.concatenate(
        [jnp.where(low, total, other), jnp.where(low, other, total)], axis=0
    )
    lane = lane_of(slot.shape)
    per = LANES // rank_width
    spread = jnp.concatenate(
        [
            jnp.where(slot == tile * per + lane // rank_width, shrink, F32(0.0)).astype(BF16)
            for tile in range(factors.shape[0] // LANES)
        ],
        axis=1,
    )
    block = out.shape[1]
    piece = min(block, 512)
    for at in range(0, block, piece):
        out[:, at : at + piece] = jnp.dot(
            spread, factors[:, at : at + piece], preferred_element_type=F32
        ).astype(BF16)


def expand(sums, everyone, parts, expand_weight, first_at):
    pool, rank_width, block = expand_weight.shape
    rows, tagged_width = everyone.shape
    tag = pl.BlockSpec((rows, LANES), lambda i: (0, tagged_width // LANES - 1))
    full = pl.BlockSpec((pool * rank_width, block), lambda i: (0, 0))
    return pl.pallas_call(
        functools.partial(expand_kernel, sums, rank_width),
        grid=(1,),
        out_shape=jax.ShapeDtypeStruct((rows, block), BF16),
        in_specs=[
            pl.BlockSpec(memory_space=pltpu.SMEM),
            tag,
            pl.BlockSpec(parts.shape, lambda i: (0, 0)),
            full,
        ],
        out_specs=pl.BlockSpec((rows, block), lambda i: (0, 0)),
        compiler_params=pltpu.CompilerParams(vmem_limit_bytes=16 << 20),
        cost_estimate=pl.CostEstimate(
            flops=2 * rows * pool * rank_width * block,
            bytes_accessed=2 * pool * rank_width * block,
            transcendentals=0,
        ),
        name="expand",
    )(first_at, everyone, parts, expand_weight.reshape(pool * rank_width, block))


def local(
    tensor_size,
    batch_size,
    queries,
    key_cache,
    value_cache,
    new_key,
    new_value,
    lengths,
    out_weight,
    shrink_weight,
    expand_weight,
    adapter_rank,
    adapter_list,
    row_adapter,
):
    rows = queries.shape[0]
    pool = shrink_weight.shape[0]
    block = expand_weight.shape[2]
    first_at = (lax.axis_index("batch") * pool).reshape(1).astype(jnp.int32)
    tagged = attend(
        batch_size,
        queries,
        key_cache,
        value_cache,
        new_key,
        new_value,
        lengths,
        adapter_list,
        row_adapter,
    )
    everyone = exchanged(tagged, "batch")
    base_in = [
        exchanged(
            base_blocks(tagged, out_weight, rows, tensor_size, block, at, at + block // 2),
            "tensor",
        )
        for at in (0, block // 2)
    ]
    part = shrink_part(tensor_size, everyone, shrink_weight, adapter_rank, first_at)
    parts = exchanged(part, "tensor")
    homes = exchanged(expand(tensor_size, everyone, parts, expand_weight, first_at), "batch")

    def total(arrived, count):
        return jnp.sum(arrived.reshape(count, rows, -1).astype(F32), axis=0)

    base = jnp.concatenate([total(half, tensor_size) for half in base_in], axis=1)
    return (base + total(homes, batch_size)).astype(BF16)


def solution(mesh):
    placed = (
        P(("groups", "batch"), "tensor", None),
        P(("groups", "batch"), None, None, None),
        P(("groups", "batch"), None, None, None),
        P(("groups", "batch"), None, None),
        P(("groups", "batch"), None, None),
        P(("groups", "batch")),
        P("tensor", None),
        P("batch", "tensor", None),
        P("batch", None, "tensor"),
        P("batch"),
        P(("groups", "batch")),
        P(("groups", "batch")),
    )

    def placed_local(*arrays):
        return local(mesh.shape["tensor"], mesh.shape["batch"], *arrays)

    return jax.shard_map(
        placed_local,
        mesh=mesh,
        in_specs=placed,
        out_specs=P(("groups", "batch"), "tensor"),
        check_vma=False,
    )
```

time: 40.6 us -> 65.8 us (1.62)
  waiting for transfers between devices: 5.65 us -> 22.2 us
  starting transfers between devices: 16.4 us -> 22.2 us
  Pallas kernels: 16.1 us -> 19.9 us
  other arithmetic: 2.03 us -> 0.84 us
    all_to_all x0 -> x5, waiting for transfers between devices: none -> 22.2 us  [exchanged(): return lax.all_to_all(blocks, axis, 0, 0, tiled=True)]
    all_to_all x0 -> x5, starting transfers between devices: none -> 22.2 us  [exchanged(): return lax.all_to_all(blocks, axis, 0, 0, tiled=True)]
    ppermute x12 -> x0, starting transfers between devices: 16.4 us -> none  [shifted(): lax.ppermute(array, axis, [(i, (i + shift) % size) for i in range(size)])]
    ppermute x12 -> x0, waiting for transfers between devices: 5.65 us -> none  [shifted(): lax.ppermute(array, axis, [(i, (i + shift) % size) for i in range(size)])]
    pallas_call x5, Pallas kernels: 16.1 us -> 19.9 us  [the longest x2 13.8 us: base_blocks(): pl.pallas_call(functools.partial(base_kernel, starts, rows, piece, deep),...]
    another operation x2 -> x0, other arithmetic: 1.26 us -> none  [base_blocks(): jnp.stack([(here + shift) % tensor_size for shift in shifts])]
  transfers between devices with their start and end apart: 12 -> 5, of which waited for: 1 -> 4; matrix products, arithmetic and copies ran while one was open for 3% -> 0% of each run, Pallas kernels for 30% -> 23%
where the time goes in v4:
time: 65.8 us; the launch traced here: 65.2 us
  starting transfers between devices  22.2 us (34%)
  waiting for transfers between devices  22.2 us (34%)
  Pallas kernels  19.9 us (30%)
  other arithmetic  0.84 us (1%)
    all_to_all x5, waiting for transfers between devices, exchanged(): return lax.all_to_all(blocks, axis, 0, 0, tiled=True)  22.2 us
    all_to_all x5, starting transfers between devices, exchanged(): return lax.all_to_all(blocks, axis, 0, 0, tiled=True)  22.2 us
    pallas_call x2, Pallas kernels, base_blocks(): pl.pallas_call(functools.partial(base_kernel, starts, rows, piece, deep),...  13.8 us
    pallas_call x1, Pallas kernels, attend(): pl.pallas_call(functools.partial(attend_kernel, parts, copies_out), out_s...  3.37 us
    pallas_call x1, Pallas kernels, shrink_part(): pl.pallas_call(functools.partial(shrink_kernel, copies_out), out_shape=ja...  1.55 us
  transfers between devices with their start and end apart: 5, of which 4 were waited for; matrix products, arithmetic and copies ran while one was open for 0% of the time, Pallas kernels for 23%

profile of v4, /device:TPU:0, one launch (start us, length us, event | category | flops | bytes accessed | tf_op | source)
XLA Modules:
  0.0 65.2 jit_solution(14393305630196139058)
XLA Ops:
  0.0 0.0 copy-start.1
  0.0 0.0 copy-start.2
  0.0 3.4 %attention.1.tagged = bf16[128,1152]{1,0:T(8,128)(2,1)} custom-call(s32[1]{0:T(128)} %bitcast.group_at, bf16[32,4,96,128]{3,2,1,0:T(8,128)(2,1)} %refs_0_.1, bf16[32,4,96,128]{3,2,1,0:T(8,128)(2,1)} %refs_1_.1, bf16[32,8,128]{2,1,0:T(8,128)(2,1)} %refs_2_.1, bf16[32,4,128]{2,1,0:T(4,128)(2,1)} %refs_3_.1, bf16[32,4,128]{2,1,0:T(4,128)(2,1)} %refs_4_.1, ...), custom_call_target="tpu_custom_call" | custom-call | flops 12582912 | bytes 1572864 | tf_op jit(solution)/shard_map/attention/pallas_call | solution.py:129
  3.4 4.2 %all-to-all-start.2 = ((bf16[4,32,1152]{2,1,0:T(8,128)(2,1)}), bf16[4,32,1152]{2,1,0:T(8,128)(2,1)S(1)}, u32[]{:S(2)}, u32[]{:S(2)}) async-start(bf16[4,32,1152]{2,1,0:T(8,128)(2,1)} %bitcast.16), calls=%async_computation.2 | async-start | bytes 589824 | tf_op jit(solution)/shard_map/all_to_all | solution.py:19
  7.6 6.4 %all-to-all-done.2 = bf16[4,32,1152]{2,1,0:T(8,128)(2,1)S(1)} async-done(((bf16[4,32,1152]{2,1,0:T(8,128)(2,1)}), bf16[4,32,1152]{2,1,0:T(8,128)(2,1)S(1)}, u32[]{:S(2)}, u32[]{:S(2)}) %all-to-all-start.2) | async-done | bytes 294944 | tf_op jit(solution)/shard_map/all_to_all | solution.py:19
  14.0 0.0 copy-done.1
  14.0 0.0 copy-done.2
  14.0 1.6 %shrink.1 = bf16[256,128]{1,0:T(8,128)(2,1)} custom-call(s32[1]{0:T(128)} %bitcast.3.first_at, s32[4]{0:T(128)S(1)} %copy-done.2, bf16[128,1152]{1,0:T(8,128)(2,1)S(1)} %bitcast.11, bf16[4,64,1024]{2,1,0:T(8,128)(2,1)S(1)} %bitcast.14), custom_call_target="tpu_custom_call" | custom-call | flops 67108864 | bytes 786432 | tf_op jit(solution)/shard_map/shrink/pallas_call | solution.py:250
  15.5 5.5 %all-to-all-start.3 = ((bf16[4,64,128]{2,1,0:T(8,128)(2,1)}), bf16[4,64,128]{2,1,0:T(8,128)(2,1)S(1)}, u32[]{:S(2)}, u32[]{:S(2)}) async-start(bf16[4,64,128]{2,1,0:T(8,128)(2,1)} %bitcast.7), calls=%async_computation.3 | async-start | bytes 131072 | tf_op jit(solution)/shard_map/all_to_all | solution.py:19
  21.1 6.9 %base_terms.3 = bf16[128,1024]{1,0:T(8,128)(2,1)} custom-call(bf16[128,1152]{1,0:T(8,128)(2,1)} %attention.1.tagged, bf16[1024,8192]{1,0:T(8,128)(2,1)} %out_weight.3), custom_call_target="tpu_custom_call" | custom-call | flops 268435456 | bytes 8388608 | tf_op jit(solution)/shard_map/base_terms/pallas_call | solution.py:200
  27.9 0.0 all-to-all-done.3
  28.0 5.1 %all-to-all-start.1 = ((bf16[4,32,1024]{2,1,0:T(8,128)(2,1)}), bf16[4,32,1024]{2,1,0:T(8,128)(2,1)S(1)}, u32[]{:S(2)}, u32[]{:S(2)}) async-start(bf16[4,32,1024]{2,1,0:T(8,128)(2,1)} %bitcast.18), calls=%async_computation.1 | async-start | bytes 524288 | tf_op jit(solution)/shard_map/all_to_all | solution.py:19
  33.1 0.0 copy-start
  33.1 6.9 %base_terms.2 = bf16[128,1024]{1,0:T(8,128)(2,1)} custom-call(bf16[128,1152]{1,0:T(8,128)(2,1)} %attention.1.tagged, bf16[1024,8192]{1,0:T(8,128)(2,1)} %out_weight.3), custom_call_target="tpu_custom_call" | custom-call | flops 268435456 | bytes 8388608 | tf_op jit(solution)/shard_map/base_terms/pallas_call | solution.py:200
  40.0 1.2 %all-to-all-done.1 = bf16[4,32,1024]{2,1,0:T(8,128)(2,1)S(1)} async-done(((bf16[4,32,1024]{2,1,0:T(8,128)(2,1)}), bf16[4,32,1024]{2,1,0:T(8,128)(2,1)S(1)}, u32[]{:S(2)}, u32[]{:S(2)}) %all-to-all-start.1) | async-done | bytes 262176 | tf_op jit(solution)/shard_map/all_to_all | solution.py:19
  41.2 3.9 %all-to-all-start = ((bf16[4,32,1024]{2,1,0:T(8,128)(2,1)}), bf16[4,32,1024]{2,1,0:T(8,128)(2,1)S(1)}, u32[]{:S(2)}, u32[]{:S(2)}) async-start(bf16[4,32,1024]{2,1,0:T(8,128)(2,1)} %bitcast.17), calls=%async_computation | async-start | bytes 524288 | tf_op jit(solution)/shard_map/all_to_all | solution.py:19
  45.1 0.0 copy-done
  45.1 1.2 %expand.1 = bf16[128,2048]{1,0:T(8,128)(2,1)} custom-call(s32[1]{0:T(128)} %bitcast.3.first_at, bf16[128,1152]{1,0:T(8,128)(2,1)S(1)} %bitcast.12, bf16[256,128]{1,0:T(8,128)(2,1)S(1)} %bitcast.15, bf16[256,2048]{1,0:T(8,128)(2,1)S(1)} %bitcast.13), custom_call_target="tpu_custom_call" | custom-call | flops 134217728 | bytes 1048576 | tf_op jit(solution)/shard_map/expand/pallas_call | solution.py:299
  46.3 5.9 %all-to-all-done = bf16[4,32,1024]{2,1,0:T(8,128)(2,1)S(1)} async-done(((bf16[4,32,1024]{2,1,0:T(8,128)(2,1)}), bf16[4,32,1024]{2,1,0:T(8,128)(2,1)S(1)}, u32[]{:S(2)}, u32[]{:S(2)}) %all-to-all-start) | async-done | bytes 262176 | tf_op jit(solution)/shard_map/all_to_all | solution.py:19
  52.2 3.5 %all-to-all-start.4 = ((bf16[4,32,2048]{2,1,0:T(8,128)(2,1)}), bf16[4,32,2048]{2,1,0:T(8,128)(2,1)S(1)}, u32[]{:S(2)}, u32[]{:S(2)}) async-start(bf16[4,32,2048]{2,1,0:T(8,128)(2,1)} %bitcast.10), calls=%async_computation.4 | async-start | bytes 1048576 | tf_op jit(solution)/shard_map/all_to_all | solution.py:19
  55.8 8.7 %all-to-all-done.4 = bf16[4,32,2048]{2,1,0:T(8,128)(2,1)S(1)} async-done(((bf16[4,32,2048]{2,1,0:T(8,128)(2,1)}), bf16[4,32,2048]{2,1,0:T(8,128)(2,1)S(1)}, u32[]{:S(2)}, u32[]{:S(2)}) %all-to-all-start.4) | async-done | bytes 524320 | tf_op jit(solution)/shard_map/all_to_all | solution.py:19
  64.5 0.1 convert_reduce_fusion
  64.6 0.7 %fusion = bf16[32,2048]{1,0:T(8,128)(2,1)} fusion(f32[32,2048]{1,0:T(8,128)S(1)} %convert_reduce_fusion, f32[32,1024]{1,0:T(8,128)S(1)} %convert_reduce_fusion.1, f32[32,1024]{1,0:T(8,128)S(1)} %convert_reduce_fusion.2), kind=kLoop, calls=%fused_computation.4 | loop fusion | flops 196608 | bytes 655360 | tf_op jit(solution)/shard_map/convert_element_type | solution.py:367
  (2 shorter events, 0.1 us)
Async XLA Ops:
  0.0 14.0 %copy-start.1 = (bf16[4,1024,64]{1,2,0:T(8,128)(2,1)S(1)}, bf16[4,1024,64]{1,2,0:T(8,128)(2,1)}, u32[]{:S(2)}) copy-start(bf16[4,1024,64]{1,2,0:T(8,128)(2,1)} %param.19) | copy-start | bytes 1572868
  0.0 14.0 %copy-start.2 = (s32[4]{0:T(128)S(1)}, s32[4]{0:T(128)}, u32[]{:S(2)}) copy-start(s32[4]{0:T(128)} %rank.1) | copy-start | bytes 52
  3.4 10.6 %all-to-all-start.2 = ((bf16[4,32,1152]{2,1,0:T(8,128)(2,1)}), bf16[4,32,1152]{2,1,0:T(8,128)(2,1)S(1)}, u32[]{:S(2)}, u32[]{:S(2)}) async-start(bf16[4,32,1152]{2,1,0:T(8,128)(2,1)} %bitcast.16), calls=%async_computation.2 | async-start | bytes 589824 | tf_op jit(solution)/shard_map/all_to_all | solution.py:19
  15.5 12.4 %all-to-all-start.3 = ((bf16[4,64,128]{2,1,0:T(8,128)(2,1)}), bf16[4,64,128]{2,1,0:T(8,128)(2,1)S(1)}, u32[]{:S(2)}, u32[]{:S(2)}) async-start(bf16[4,64,128]{2,1,0:T(8,128)(2,1)} %bitcast.7), calls=%async_computation.3 | async-start | bytes 131072 | tf_op jit(solution)/shard_map/all_to_all | solution.py:19
  28.0 13.3 %all-to-all-start.1 = ((bf16[4,32,1024]{2,1,0:T(8,128)(2,1)}), bf16[4,32,1024]{2,1,0:T(8,128)(2,1)S(1)}, u32[]{:S(2)}, u32[]{:S(2)}) async-start(bf16[4,32,1024]{2,1,0:T(8,128)(2,1)} %bitcast.18), calls=%async_computation.1 | async-start | bytes 524288 | tf_op jit(solution)/shard_map/all_to_all | solution.py:19
  33.1 12.1 %copy-start = (bf16[4,64,2048]{2,1,0:T(8,128)(2,1)S(1)}, bf16[4,64,2048]{2,1,0:T(8,128)(2,1)}, u32[]{:S(2)}) copy-start(bf16[4,64,2048]{2,1,0:T(8,128)(2,1)} %param.20) | copy-start | bytes 3145732
  41.2 10.9 %all-to-all-start = ((bf16[4,32,1024]{2,1,0:T(8,128)(2,1)}), bf16[4,32,1024]{2,1,0:T(8,128)(2,1)S(1)}, u32[]{:S(2)}, u32[]{:S(2)}) async-start(bf16[4,32,1024]{2,1,0:T(8,128)(2,1)} %bitcast.17), calls=%async_computation | async-start | bytes 524288 | tf_op jit(solution)/shard_map/all_to_all | solution.py:19
  52.2 12.3 %all-to-all-start.4 = ((bf16[4,32,2048]{2,1,0:T(8,128)(2,1)}), bf16[4,32,2048]{2,1,0:T(8,128)(2,1)S(1)}, u32[]{:S(2)}, u32[]{:S(2)}) async-start(bf16[4,32,2048]{2,1,0:T(8,128)(2,1)} %bitcast.10), calls=%async_computation.4 | async-start | bytes 1048576 | tf_op jit(solution)/shard_map/all_to_all | solution.py:19

commit v5 on v4

--- a/solution.py
+++ b/solution.py
@@ -15,15 +15,19 @@
 F32, BF16 = jnp.float32, jnp.bfloat16
 
 
-def exchanged(blocks, axis):
-    return lax.all_to_all(blocks, axis, 0, 0, tiled=True)
+def permuted(array, axis, size, partner):
+    return lax.ppermute(array, axis, [(i, partner(i)) for i in range(size)])
+
+
+def in_hbm(*arrays):
+    return [pltpu.with_memory_space_constraint(array, pltpu.HBM) for array in arrays]
 
 
 def lane_of(shape):
     return lax.broadcasted_iota(jnp.int32, shape, len(shape) - 1)
 
 
-def attend_kernel(parts, copies_out, group_at, *refs):
+def attend_kernel(parts, group_at, *refs):
     given, (tagged, *scratch) = refs[:8], refs[8:]
     held, (spread_out, small_sems, key_sems, value_sems) = scratch[:8], scratch[8:]
     key_cache, value_cache = given[:2]
@@ -97,16 +101,14 @@
         spread_out[pl.ds(part * some * heads, some * heads)] = attended.reshape(
             some * heads, width
         )
-    for copy in range(copies_out):
-        tagged[copy * rows : (copy + 1) * rows, heads * width :] = tag
+    tagged[:, heads * width :] = tag
     for head in range(heads):
-        block = spread_out[pl.ds(head, rows, stride=heads)].astype(BF16)
-        for copy in range(copies_out):
-            tagged[copy * rows : (copy + 1) * rows, head * width : (head + 1) * width] = block
+        tagged[:, head * width : (head + 1) * width] = spread_out[
+            pl.ds(head, rows, stride=heads)
+        ].astype(BF16)
 
 
 def attend(
-    copies_out,
     queries,
     key_cache,
     value_cache,
@@ -127,8 +129,8 @@
     smem = pl.BlockSpec(memory_space=pltpu.SMEM)
     away = pl.BlockSpec(memory_space=pl.ANY)
     tagged = pl.pallas_call(
-        functools.partial(attend_kernel, parts, copies_out),
-        out_shape=jax.ShapeDtypeStruct((copies_out * rows, full * width + LANES), BF16),
+        functools.partial(attend_kernel, parts),
+        out_shape=jax.ShapeDtypeStruct((rows, full * width + LANES), BF16),
         in_specs=[smem] + [away] * 8,
         out_specs=pl.BlockSpec(memory_space=VMEM),
         scratch_shapes=[
@@ -145,7 +147,7 @@
             pltpu.SemaphoreType.DMA((parts,)),
             pltpu.SemaphoreType.DMA((parts,)),
         ],
-        compiler_params=pltpu.CompilerParams(vmem_limit_bytes=GRANT),
+        compiler_params=pltpu.CompilerParams(vmem_limit_bytes=8 << 20),
         cost_estimate=pl.CostEstimate(
             flops=4 * rows * heads * positions * width,
             bytes_accessed=4 * rows * positions * width,
@@ -154,71 +156,95 @@
         name="attention",
     )(
         group_at,
-        key_cache,
-        value_cache,
-        queries,
-        new_key,
-        new_value,
-        lengths,
-        row_adapter,
-        adapter_list,
+        *in_hbm(
+            key_cache,
+            value_cache,
+            queries,
+            new_key,
+            new_value,
+            lengths,
+            row_adapter,
+            adapter_list,
+        ),
     )
     if full != heads:
         tagged = jnp.concatenate([tagged[:, : heads * width], tagged[:, full * width :]], axis=1)
     return tagged
 
 
-def base_kernel(starts, rows, piece, deep, tagged, out_weight, out, held, sems):
-    width = out_weight.shape[0]
-    count = len(starts)
+def base_kernel(ahead, deep, tensor_at, tagged, out_weight, *refs):
+    before, (out, held, sums, sems) = refs[:-4], refs[-4:]
+    _, deep_rows, block = held.shape
+    rows, width = tagged.shape[0], out_weight.shape[0]
+    count = width // deep_rows
+    column = pl.ds(pl.multiple_of((tensor_at[0] ^ ahead) * block, block), block)
 
     def copy(at):
         return pltpu.make_async_copy(
-            out_weight.at[:, pl.ds(starts[at], piece)], held.at[at % deep], sems.at[at % deep]
+            out_weight.at[pl.ds(at * deep_rows, deep_rows), column],
+            held.at[at % deep],
+            sems.at[at % deep],
         )
 
     for at in range(min(deep, count)):
         copy(at).start()
-    per = out.shape[1] // piece
+    if before:
+        out[: before[0].shape[0]] = before[0][...]
+    first = out.shape[0] - rows
+    piece = min(block, 512)
     for at in range(count):
         copy(at).wait()
-        term = jnp.dot(tagged[:rows, :width], held[at % deep], preferred_element_type=F32)
-        to, column = at // per * rows, at % per * piece
-        out[to : to + rows, column : column + piece] = term.astype(out.dtype)
+        inputs = slice(at * deep_rows, (at + 1) * deep_rows)
+        for start in range(0, block, piece):
+            columns = slice(start, start + piece)
+            term = jnp.dot(
+                tagged[:, inputs], held[at % deep, :, columns], preferred_element_type=F32
+            )
+            if at:
+                term = term + sums[:, columns]
+            if at < count - 1:
+                sums[:, columns] = term
+            else:
+                out[first:, columns] = term.astype(out.dtype)
         if at + deep < count:
             copy(at + deep).start()
 
 
-def base_blocks(tagged, out_weight, rows, tensor_size, block, first, last):
+def base_block(tensor_at, tagged, out_weight, block, ahead, dtype, *before):
+    rows = tagged.shape[0]
     width = out_weight.shape[0]
-    piece = min(last - first, 256)
-    starts = [
-        to * block + column for to in range(tensor_size) for column in range(first, last, piece)
-    ]
-    deep = 6
+    deep, deep_rows = 4, min(width, 256)
     whole = pl.BlockSpec(memory_space=VMEM)
+    out_rows = rows + sum(each.shape[0] for each in before)
     return pl.pallas_call(
-        functools.partial(base_kernel, starts, rows, piece, deep),
-        out_shape=jax.ShapeDtypeStruct((tensor_size * rows, last - first), BF16),
-        in_specs=[whole, pl.BlockSpec(memory_space=pl.ANY)],
+        functools.partial(base_kernel, ahead, deep),
+        out_shape=jax.ShapeDtypeStruct((out_rows, block), dtype),
+        in_specs=[pl.BlockSpec(memory_space=pltpu.SMEM), whole, pl.BlockSpec(memory_space=pl.ANY)]
+        + [whole] * len(before),
         out_specs=whole,
-        scratch_shapes=[VMEM((deep, width, piece), BF16), pltpu.SemaphoreType.DMA((deep,))],
-        compiler_params=pltpu.CompilerParams(vmem_limit_bytes=GRANT),
+        scratch_shapes=[
+            VMEM((deep, deep_rows, block), BF16),
+            VMEM((rows, block), F32),
+            pltpu.SemaphoreType.DMA((deep,)),
+        ],
+        compiler_params=pltpu.CompilerParams(vmem_limit_bytes=12 << 20),
         cost_estimate=pl.CostEstimate(
-            flops=2 * rows * width * (last - first) * tensor_size,
-            bytes_accessed=2 * width * (last - first) * tensor_size,
+            flops=2 * rows * width * block,
+            bytes_accessed=2 * width * block,
             transcendentals=0,
         ),
         name="base_terms",
-    )(tagged, out_weight)
+    )(tensor_at, tagged, *in_hbm(out_weight), *before)
 
 
 def slots_of(tags, first):
     return tags.astype(F32).astype(jnp.int32) - first
 
 
-def shrink_kernel(copies_out, first_at, rank, everyone, factors, out):
+def shrink_kernel(first_at, rank, *refs):
+    blocks, (factors, out) = refs[:-2], refs[-2:]
     pool, rank_width, width = factors.shape
+    everyone = jnp.concatenate([block[...] for block in blocks], axis=0)
     slot = slots_of(everyone[:, width:], first_at[0])
     terms = lax.dot_general(
         everyone[:, :width],
@@ -237,20 +263,18 @@
         kept = kept + jnp.where(keep, terms[:, tile * LANES : (tile + 1) * LANES], F32(0.0))
     both = kept + pltpu.roll(kept, rank_width, 1)
     half = both.shape[0] // 2
-    packed = jnp.where(lane[:half] < rank_width, both[:half], both[half:]).astype(out.dtype)
-    for copy in range(copies_out):
-        out[copy * half : (copy + 1) * half] = packed
-
-
-def shrink_part(copies_out, everyone, shrink_weight, adapter_rank, first_at):
+    out[...] = jnp.where(lane[:half] < rank_width, both[:half], both[half:]).astype(out.dtype)
+
+
+def shrink_part(blocks, shrink_weight, adapter_rank, first_at):
     pool, width, rank_width = shrink_weight.shape
-    rows = everyone.shape[0]
+    rows = len(blocks) * blocks[0].shape[0]
     smem = pl.BlockSpec(memory_space=pltpu.SMEM)
     whole = pl.BlockSpec(memory_space=VMEM)
     return pl.pallas_call(
-        functools.partial(shrink_kernel, copies_out),
-        out_shape=jax.ShapeDtypeStruct((copies_out * rows // 2, LANES), BF16),
-        in_specs=[smem, smem, whole, whole],
+        shrink_kernel,
+        out_shape=jax.ShapeDtypeStruct((rows // 2, LANES), BF16),
+        in_specs=[smem, smem] + [whole] * (len(blocks) + 1),
         out_specs=whole,
         compiler_params=pltpu.CompilerParams(vmem_limit_bytes=8 << 20),
         cost_estimate=pl.CostEstimate(
@@ -259,15 +283,15 @@
             transcendentals=0,
         ),
         name="shrink",
-    )(first_at, adapter_rank, everyone, jnp.swapaxes(shrink_weight, 1, 2))
-
-
-def expand_kernel(sums, rank_width, first_at, everyone, parts, factors, out):
-    slot = slots_of(everyone[...], first_at[0])
-    half = parts.shape[0] // sums
-    total = parts[:half].astype(F32)
-    for at in range(1, sums):
-        total = total + parts[at * half : (at + 1) * half].astype(F32)
+    )(first_at, adapter_rank, *blocks, jnp.swapaxes(shrink_weight, 1, 2))
+
+
+def expand_kernel(count, sums, rank_width, first_at, *refs):
+    tags, parts, (factors, kept, given) = refs[:count], refs[count : count + sums], refs[-3:]
+    slot = slots_of(jnp.concatenate([tag[...] for tag in tags], axis=0), first_at[0])
+    total = parts[0][...].astype(F32)
+    for part in parts[1:]:
+        total = total + part[...].astype(F32)
     total = total.astype(BF16).astype(F32)
     other = pltpu.roll(total, rank_width, 1)
     low = lane_of(total.shape) < rank_width
@@ -283,38 +307,40 @@
         ],
         axis=1,
     )
-    block = out.shape[1]
+    half, block = kept.shape
     piece = min(block, 512)
     for at in range(0, block, piece):
-        out[:, at : at + piece] = jnp.dot(
-            spread, factors[:, at : at + piece], preferred_element_type=F32
-        ).astype(BF16)
-
-
-def expand(sums, everyone, parts, expand_weight, first_at):
+        delta = jnp.dot(spread, factors[:, at : at + piece], preferred_element_type=F32)
+        kept[:, at : at + piece] = delta[:half].astype(kept.dtype)
+        given[:, at : at + piece] = delta[half:].astype(given.dtype)
+
+
+def expand(blocks, parts, expand_weight, first_at):
     pool, rank_width, block = expand_weight.shape
-    rows, tagged_width = everyone.shape
+    rows, tagged_width = blocks[0].shape
+    count = len(blocks)
+    half = rows * count // 2
     tag = pl.BlockSpec((rows, LANES), lambda i: (0, tagged_width // LANES - 1))
     full = pl.BlockSpec((pool * rank_width, block), lambda i: (0, 0))
+    part = pl.BlockSpec(parts[0].shape, lambda i: (0, 0))
+    out = pl.BlockSpec((half, block), lambda i: (0, 0))
     return pl.pallas_call(
-        functools.partial(expand_kernel, sums, rank_width),
+        functools.partial(expand_kernel, count, len(parts), rank_width),
         grid=(1,),
-        out_shape=jax.ShapeDtypeStruct((rows, block), BF16),
-        in_specs=[
-            pl.BlockSpec(memory_space=pltpu.SMEM),
-            tag,
-            pl.BlockSpec(parts.shape, lambda i: (0, 0)),
-            full,
-        ],
-        out_specs=pl.BlockSpec((rows, block), lambda i: (0, 0)),
+        out_shape=[jax.ShapeDtypeStruct((half, block), BF16)] * 2,
+        in_specs=[pl.BlockSpec(memory_space=pltpu.SMEM)]
+        + [tag] * count
+        + [part] * len(parts)
+        + [full],
+        out_specs=[out, out],
         compiler_params=pltpu.CompilerParams(vmem_limit_bytes=16 << 20),
         cost_estimate=pl.CostEstimate(
-            flops=2 * rows * pool * rank_width * block,
+            flops=2 * rows * count * pool * rank_width * block,
             bytes_accessed=2 * pool * rank_width * block,
             transcendentals=0,
         ),
         name="expand",
-    )(first_at, everyone, parts, expand_weight.reshape(pool * rank_width, block))
+    )(first_at, *blocks, *parts, expand_weight.reshape(pool * rank_width, block))
 
 
 def local(
@@ -336,35 +362,70 @@
     rows = queries.shape[0]
     pool = shrink_weight.shape[0]
     block = expand_weight.shape[2]
+    chips = batch_size // 2
     first_at = (lax.axis_index("batch") * pool).reshape(1).astype(jnp.int32)
+    tensor_at = lax.axis_index("tensor").reshape(1).astype(jnp.int32)
+
+    def to_sibling(array):
+        return permuted(array, "batch", batch_size, lambda i: i ^ 1)
+
+    def to_chip(array, shift):
+        return permuted(array, "batch", batch_size, lambda i: (i + 2 * shift) % batch_size)
+
+    def across(array, bit):
+        return permuted(array, "tensor", tensor_size, lambda i: i ^ bit)
+
+    def wide(array):
+        return array.astype(F32)
+
+    def terms(ahead, dtype, *before):
+        return base_block(tensor_at, tagged, out_weight, block, ahead, dtype, *before)
+
     tagged = attend(
-        batch_size,
-        queries,
-        key_cache,
-        value_cache,
-        new_key,
-        new_value,
-        lengths,
-        adapter_list,
-        row_adapter,
-    )
-    everyone = exchanged(tagged, "batch")
-    base_in = [
-        exchanged(
-            base_blocks(tagged, out_weight, rows, tensor_size, block, at, at + block // 2),
-            "tensor",
-        )
-        for at in (0, block // 2)
-    ]
-    part = shrink_part(tensor_size, everyone, shrink_weight, adapter_rank, first_at)
-    parts = exchanged(part, "tensor")
-    homes = exchanged(expand(tensor_size, everyone, parts, expand_weight, first_at), "batch")
-
-    def total(arrived, count):
-        return jnp.sum(arrived.reshape(count, rows, -1).astype(F32), axis=0)
-
-    base = jnp.concatenate([total(half, tensor_size) for half in base_in], axis=1)
-    return (base + total(homes, batch_size)).astype(BF16)
+        queries, key_cache, value_cache, new_key, new_value, lengths, adapter_list, row_adapter
+    )
+    beside = to_sibling(tagged)
+    visiting = [to_chip(tagged, shift) for shift in range(1, chips)]
+    odd = terms(1, BF16)
+    visiting, odd = lax.optimization_barrier((visiting, odd))
+    mine = [tagged] + visiting
+    blocks = mine + [beside] + [to_sibling(each) for each in visiting]
+    for ahead in range(3, tensor_size, 2):
+        odd = terms(ahead, BF16, odd)
+    blocks, odd = lax.optimization_barrier((blocks, odd))
+
+    part = shrink_part(blocks, shrink_weight, adapter_rank, first_at)
+    parts = [part, across(part, 1)]
+    arrived = across(odd, 1)
+    base = {ahead: terms(ahead, BF16 if ahead else F32) for ahead in range(2, tensor_size, 2)}
+    bit = 2
+    while bit < tensor_size:
+        part = (wide(parts[0]) + wide(parts[1])).astype(BF16)
+        parts = [part, across(part, bit)]
+        bit *= 2
+    base[0] = terms(0, F32)
+    kept, given = expand(blocks, parts, expand_weight, first_at)
+    given = to_sibling(given)
+
+    bit, sent = 1, range(1, tensor_size, 2)
+    while True:
+        for place, ahead in enumerate(sent):
+            base[ahead ^ bit] = wide(base[ahead ^ bit]) + wide(
+                arrived[place * rows : (place + 1) * rows]
+            )
+        bit *= 2
+        if bit >= tensor_size:
+            break
+        sent = [ahead for ahead in sorted(base) if ahead & bit]
+        message = [base.pop(ahead).astype(BF16) for ahead in sent]
+        arrived = across(jnp.concatenate(message, axis=0), bit)
+
+    result = base[0] + wide(kept[:rows]) + wide(given[:rows])
+    for shift in range(1, chips):
+        at = slice(shift * rows, (shift + 1) * rows)
+        home = (wide(kept[at]) + wide(given[at])).astype(BF16)
+        result = result + wide(to_chip(home, -shift))
+    return result.astype(BF16)
 
 
 def solution(mesh):

time: 65.8 us -> 31.2 us (0.47)
  waiting for transfers between devices: 22.2 us -> 3.64 us
  starting transfers between devices: 22.2 us -> 12.4 us
  Pallas kernels: 19.9 us -> 13.9 us
    all_to_all x5 -> x0, waiting for transfers between devices: 22.2 us -> none  [exchanged(): return lax.all_to_all(blocks, axis, 0, 0, tiled=True)]
    all_to_all x5 -> x0, starting transfers between devices: 22.2 us -> none  [exchanged(): return lax.all_to_all(blocks, axis, 0, 0, tiled=True)]
    ppermute x0 -> x9, starting transfers between devices: none -> 12.4 us  [permuted(): return lax.ppermute(array, axis, [(i, partner(i)) for i in range(size)])]
    pallas_call x5 -> x7, Pallas kernels: 19.9 us -> 13.9 us  [the longest x4 10.1 us: base_block(): pl.pallas_call(functools.partial(base_kernel, ahead, deep), out_shape=jax...]
    ppermute x0 -> x9, waiting for transfers between devices: none -> 3.64 us  [permuted(): return lax.ppermute(array, axis, [(i, partner(i)) for i in range(size)])]
  transfers between devices with their start and end apart: 5 -> 9, of which waited for: 4 -> 3; matrix products, arithmetic and copies ran while one was open for 0% -> 0% of each run, Pallas kernels for 23% -> 34%
where the time goes in v5:
time: 31.2 us; the launch traced here: 31 us
  Pallas kernels  13.9 us (45%)
  starting transfers between devices  12.4 us (40%)
  waiting for transfers between devices  3.64 us (12%)
  other arithmetic  0.82 us (3%)
    ppermute x9, starting transfers between devices, permuted(): return lax.ppermute(array, axis, [(i, partner(i)) for i in range(size)])  12.4 us
    pallas_call x4, Pallas kernels, base_block(): pl.pallas_call(functools.partial(base_kernel, ahead, deep), out_shape=jax...  10.1 us
    ppermute x9, waiting for transfers between devices, permuted(): return lax.ppermute(array, axis, [(i, partner(i)) for i in range(size)])  3.64 us
    pallas_call x1, Pallas kernels, attend(): pl.pallas_call(functools.partial(attend_kernel, parts), out_shape=jax.Sha...  2.61 us
    pallas_call x1, Pallas kernels, shrink_part(): pl.pallas_call(shrink_kernel, out_shape=jax.ShapeDtypeStruct((rows // 2,...  0.92 us
    convert_element_type x1, other arithmetic, local(): return result.astype(BF16)  0.75 us
  transfers between devices with their start and end apart: 9, of which 3 were waited for; matrix products, arithmetic and copies ran while one was open for 0% of the time, Pallas kernels for 34%

profile of v5, /device:TPU:0, one launch (start us, length us, event | category | flops | bytes accessed | tf_op | source)
XLA Modules:
  0.0 31.0 jit_solution(3294379795839328586)
XLA Ops:
  0.0 2.6 %attention.1.tagged.refs_0_ = bf16[32,1152]{1,0:T(8,128)(2,1)S(1)} custom-call(s32[1]{0:T(128)} %bitcast.1.group_at, bf16[32,4,96,128]{3,2,1,0:T(8,128)(2,1)} %refs_0_.1, bf16[32,4,96,128]{3,2,1,0:T(8,128)(2,1)} %refs_1_.1, bf16[32,8,128]{2,1,0:T(8,128)(2,1)} %refs_2_.1, bf16[32,4,128]{2,1,0:T(4,128)(2,1)} %refs_3_.1, bf16[32,4,128]{2,1,0:T(4,128)(2,1)} %refs_4_.1, ...), custom_call_target="tpu_custom_call" | custom-call | flops 12582912 | bytes 1572864 | tf_op jit(solution)/shard_map/attention/pallas_call | solution.py:131
  2.6 3.0 %collective-permute-start = (bf16[32,1152]{1,0:T(8,128)(2,1)S(1)}, bf16[32,1152]{1,0:T(8,128)(2,1)S(1)}, u32[]{:S(2)}, u32[]{:S(2)}) collective-permute-start(bf16[32,1152]{1,0:T(8,128)(2,1)S(1)} %attention.1.tagged.refs_0_), channel_id=1, source_target_pairs={{0,2},{1,3},{2,0},{3,1},{4,6},{5,7},{6,4},{7,5},{8,10},{9,11},{10,... | collective-permute-start | bytes 221192 | tf_op jit(solution)/shard_map/ppermute | solution.py:19
  5.6 0.0 collective-permute-start.1
  5.6 2.5 %base_terms.5.refs_0_ = bf16[32,2048]{1,0:T(8,128)(2,1)S(1)} custom-call(s32[1]{0:T(128)} %bitcast.tensor_at, bf16[32,1152]{1,0:T(8,128)(2,1)S(1)} %attention.1.tagged.refs_0_, bf16[1024,8192]{1,0:T(8,128)(2,1)} %out_weight.7), custom_call_target="tpu_custom_call" | custom-call | flops 134217728 | bytes 4194304 | tf_op jit(solution)/shard_map/base_terms/pallas_call | solution.py:219
  8.1 0.0 collective-permute-done.refs_1_
  8.1 0.6 %collective-permute-start.2 = (bf16[32,1152]{1,0:T(8,128)(2,1)S(1)}, bf16[32,1152]{1,0:T(8,128)(2,1)S(1)}, u32[]{:S(2)}, u32[]{:S(2)}) collective-permute-start(bf16[32,1152]{1,0:T(8,128)(2,1)S(1)} %collective-permute-done.refs_1_), channel_id=1, source_target_pairs={{0,1},{1,0},{2,3},{3,2},{4,5},{5,4},{6,7},{7,6},{8,9},{9,8},{10,11... | collective-permute-start | bytes 221192 | tf_op jit(solution)/shard_map/ppermute | solution.py:19
  8.7 0.0 copy-start.1
  8.7 0.0 copy-start.2
  8.7 2.6 %base_terms.6 = bf16[64,2048]{1,0:T(8,128)(2,1)S(1)} custom-call(s32[1]{0:T(128)} %bitcast.tensor_at, bf16[32,1152]{1,0:T(8,128)(2,1)S(1)} %attention.1.tagged.refs_0_, bf16[1024,8192]{1,0:T(8,128)(2,1)} %out_weight.7, bf16[32,2048]{1,0:T(8,128)(2,1)S(1)} %base_terms.5.refs_0_), custom_call_target="tpu_custom_call" | custom-call | flops 134217728 | bytes 4194304 | tf_op jit(solution)/shard_map/base_terms/pallas_call | solution.py:219
  11.3 0.0 collective-permute-done.1.refs_2_
  11.3 0.0 collective-permute-done.2.refs_3_
  11.3 0.0 copy-done.1
  11.3 0.0 copy-done.2
  11.3 0.9 %shrink.1 = bf16[64,128]{1,0:T(8,128)(2,1)S(1)} custom-call(s32[1]{0:T(128)} %bitcast.2.first_at, s32[4]{0:T(128)S(1)} %copy-done.2, bf16[32,1152]{1,0:T(8,128)(2,1)S(1)} %attention.1.tagged.refs_0_, bf16[32,1152]{1,0:T(8,128)(2,1)S(1)} %collective-permute-done.refs_1_, bf16[32,1152]{1,0:T(8,128)(2,1)S(1)} %collective-permute-done.1.refs_2_, ...), custom_call_target="tpu_custom_call" | custom-call | flops 67108864 | bytes 786432 | tf_op jit(solution)/shard_map/shrink/pallas_call | solution.py:274
  12.3 1.6 %collective-permute-start.5 = (bf16[64,128]{1,0:T(8,128)(2,1)S(1)}, bf16[64,128]{1,0:T(8,128)(2,1)S(1)}, u32[]{:S(2)}, u32[]{:S(2)}) collective-permute-start(bf16[64,128]{1,0:T(8,128)(2,1)S(1)} %shrink.1), channel_id=1, source_target_pairs={{0,4},{4,0},{8,12},{12,8},{1,5},{5,1},{9,13},{13,9},{2,6},{6,2},{1... | collective-permute-start | bytes 49160 | tf_op jit(solution)/shard_map/ppermute | solution.py:19
  13.9 0.4 %collective-permute-start.3 = (bf16[64,2048]{1,0:T(8,128)(2,1)S(1)}, bf16[64,2048]{1,0:T(8,128)(2,1)S(1)}, u32[]{:S(2)}, u32[]{:S(2)}) collective-permute-start(bf16[64,2048]{1,0:T(8,128)(2,1)S(1)} %base_terms.6), channel_id=1, source_target_pairs={{0,4},{4,0},{8,12},{12,8},{1,5},{5,1},{9,13},{13,9},{2,6},{6,2},{1... | collective-permute-start | bytes 786440 | tf_op jit(solution)/shard_map/ppermute | solution.py:19
  14.3 1.7 %collective-permute-done.5 = bf16[64,128]{1,0:T(8,128)(2,1)S(1)} collective-permute-done((bf16[64,128]{1,0:T(8,128)(2,1)S(1)}, bf16[64,128]{1,0:T(8,128)(2,1)S(1)}, u32[]{:S(2)}, u32[]{:S(2)}) %collective-permute-start.5) | collective-permute-done | bytes 16416 | tf_op jit(solution)/shard_map/ppermute | solution.py:19
  16.1 0.0 copy-start
  16.1 2.7 %collective-permute-start.6 = (bf16[64,128]{1,0:T(8,128)(2,1)S(1)}, bf16[64,128]{1,0:T(8,128)(2,1)S(1)}, u32[]{:S(2)}, u32[]{:S(2)}) collective-permute-start(bf16[64,128]{1,0:T(8,128)(2,1)S(1)} %add_convert_fusion.3.refs_4_), channel_id=1, source_target_pairs={{0,8},{4,12},{8,0},{12,4},{1,9},{5,13},{9,1},{13,5},{2,10},{6,14},... | collective-permute-start | bytes 49160 | tf_op jit(solution)/shard_map/ppermute | solution.py:19
  18.7 2.5 %base_terms.7 = bf16[32,2048]{1,0:T(8,128)(2,1)S(1)} custom-call(s32[1]{0:T(128)} %bitcast.tensor_at, bf16[32,1152]{1,0:T(8,128)(2,1)S(1)} %attention.1.tagged.refs_0_, bf16[1024,8192]{1,0:T(8,128)(2,1)} %out_weight.7), custom_call_target="tpu_custom_call" | custom-call | flops 134217728 | bytes 4194304 | tf_op jit(solution)/shard_map/base_terms/pallas_call | solution.py:219
  21.3 0.0 collective-permute-done.6.refs_5_
  21.3 0.0 copy-done
  21.3 0.3 %expand.1 = (bf16[64,2048]{1,0:T(8,128)(2,1)S(1)}, bf16[64,2048]{1,0:T(8,128)(2,1)S(1)}) custom-call(s32[1]{0:T(128)} %bitcast.2.first_at, bf16[32,1152]{1,0:T(8,128)(2,1)S(1)} %attention.1.tagged.refs_0_, bf16[32,1152]{1,0:T(8,128)(2,1)S(1)} %collective-permute-done.refs_1_, bf16[32,1152]{1,0:T(8,128)(2,1)S(1)} %collective-permute-done.1.refs_2_, ...), custom_call_target="tpu_custom_call" | custom-call | flops 134217728 | bytes 1048576 | tf_op jit(solution)/shard_map/expand/pallas_call | solution.py:327
  21.6 0.1 collective-permute-start.7
  21.7 0.7 %collective-permute-done.3 = bf16[64,2048]{1,0:T(8,128)(2,1)S(1)} collective-permute-done((bf16[64,2048]{1,0:T(8,128)(2,1)S(1)}, bf16[64,2048]{1,0:T(8,128)(2,1)S(1)}, u32[]{:S(2)}, u32[]{:S(2)}) %collective-permute-start.3) | collective-permute-done | bytes 262176 | tf_op jit(solution)/shard_map/ppermute | solution.py:19
  22.5 2.5 %collective-permute-start.4 = (bf16[32,2048]{1,0:T(8,128)(2,1)S(1)}, bf16[32,2048]{1,0:T(8,128)(2,1)S(1)}, u32[]{:S(2)}, u32[]{:S(2)}) collective-permute-start(bf16[32,2048]{1,0:T(8,128)(2,1)S(1)} %add_convert_fusion.2), channel_id=1, source_target_pairs={{0,8},{4,12},{8,0},{12,4},{1,9},{5,13},{9,1},{13,5},{2,10},{6,14},... | collective-permute-start | bytes 393224 | tf_op jit(solution)/shard_map/ppermute | solution.py:19
  25.0 0.0 collective-permute-done.7
  25.0 1.6 %collective-permute-start.8 = (bf16[32,2048]{1,0:T(8,128)(2,1)S(1)}, bf16[32,2048]{1,0:T(8,128)(2,1)S(1)}, u32[]{:S(2)}, u32[]{:S(2)}) collective-permute-start(bf16[32,2048]{1,0:T(8,128)(2,1)S(1)} %add_convert_fusion.1), channel_id=1, source_target_pairs={{0,2},{1,3},{2,0},{3,1},{4,6},{5,7},{6,4},{7,5},{8,10},{9,11},{10,... | collective-permute-start | bytes 393224 | tf_op jit(solution)/shard_map/ppermute | solution.py:19
  26.6 2.5 %base_terms.4 = f32[32,2048]{1,0:T(8,128)S(1)} custom-call(s32[1]{0:T(128)} %bitcast.tensor_at, bf16[32,1152]{1,0:T(8,128)(2,1)S(1)} %attention.1.tagged.refs_0_, bf16[1024,8192]{1,0:T(8,128)(2,1)} %out_weight.7), custom_call_target="tpu_custom_call" | custom-call | flops 134217728 | bytes 4194304 | tf_op jit(solution)/shard_map/base_terms/pallas_call | solution.py:219
  29.1 0.0 collective-permute-done.4
  29.1 1.2 %collective-permute-done.8 = bf16[32,2048]{1,0:T(8,128)(2,1)S(1)} collective-permute-done((bf16[32,2048]{1,0:T(8,128)(2,1)S(1)}, bf16[32,2048]{1,0:T(8,128)(2,1)S(1)}, u32[]{:S(2)}, u32[]{:S(2)}) %collective-permute-start.8) | collective-permute-done | bytes 131104 | tf_op jit(solution)/shard_map/ppermute | solution.py:19
  30.3 0.8 %add_convert_fusion = bf16[32,2048]{1,0:T(8,128)(2,1)} fusion(bf16[32,2048]{1,0:T(8,128)(2,1)S(1)} %collective-permute-done.8, bf16[32,2048]{1,0:T(8,128)(2,1)S(1)} %collective-permute-done.4, f32[32,2048]{1,0:T(8,128)S(1)} %base_terms.4, bf16[64,2048]{1,0:T(8,128)(2,1)S(1)} %collective-permute-done.7, bf16[64,2048]{1,0:T(8,128)(2,1)S(1)} %collective-permute-done.3, ...), kind=kLoop, calls=%fused_computation | loop fusion | flops 720896 | bytes 1048576 | tf_op jit(solution)/shard_map/convert_element_type | solution.py:428
  (3 shorter events, 0.1 us)
Async XLA Ops:
  2.6 5.5 %collective-permute-start = (bf16[32,1152]{1,0:T(8,128)(2,1)S(1)}, bf16[32,1152]{1,0:T(8,128)(2,1)S(1)}, u32[]{:S(2)}, u32[]{:S(2)}) collective-permute-start(bf16[32,1152]{1,0:T(8,128)(2,1)S(1)} %attention.1.tagged.refs_0_), channel_id=1, source_target_pairs={{0,2},{1,3},{2,0},{3,1},{4,6},{5,7},{6,4},{7,5},{8,10},{9,11},{10,... | collective-permute-start | bytes 221192 | tf_op jit(solution)/shard_map/ppermute | solution.py:19
  5.6 5.7 %collective-permute-start.1 = (bf16[32,1152]{1,0:T(8,128)(2,1)S(1)}, bf16[32,1152]{1,0:T(8,128)(2,1)S(1)}, u32[]{:S(2)}, u32[]{:S(2)}) collective-permute-start(bf16[32,1152]{1,0:T(8,128)(2,1)S(1)} %attention.1.tagged.refs_0_), channel_id=1, source_target_pairs={{0,1},{1,0},{2,3},{3,2},{4,5},{5,4},{6,7},{7,6},{8,9},{9,8},{10,11... | collective-permute-start | bytes 221192 | tf_op jit(solution)/shard_map/ppermute | solution.py:19
  8.1 3.2 %collective-permute-start.2 = (bf16[32,1152]{1,0:T(8,128)(2,1)S(1)}, bf16[32,1152]{1,0:T(8,128)(2,1)S(1)}, u32[]{:S(2)}, u32[]{:S(2)}) collective-permute-start(bf16[32,1152]{1,0:T(8,128)(2,1)S(1)} %collective-permute-done.refs_1_), channel_id=1, source_target_pairs={{0,1},{1,0},{2,3},{3,2},{4,5},{5,4},{6,7},{7,6},{8,9},{9,8},{10,11... | collective-permute-start | bytes 221192 | tf_op jit(solution)/shard_map/ppermute | solution.py:19
  8.7 2.6 %copy-start.1 = (bf16[4,1024,64]{1,2,0:T(8,128)(2,1)S(1)}, bf16[4,1024,64]{1,2,0:T(8,128)(2,1)}, u32[]{:S(2)}) copy-start(bf16[4,1024,64]{1,2,0:T(8,128)(2,1)} %param.19) | copy-start | bytes 1572868
  8.7 2.6 %copy-start.2 = (s32[4]{0:T(128)S(1)}, s32[4]{0:T(128)}, u32[]{:S(2)}) copy-start(s32[4]{0:T(128)} %rank.1) | copy-start | bytes 52
  12.3 3.8 %collective-permute-start.5 = (bf16[64,128]{1,0:T(8,128)(2,1)S(1)}, bf16[64,128]{1,0:T(8,128)(2,1)S(1)}, u32[]{:S(2)}, u32[]{:S(2)}) collective-permute-start(bf16[64,128]{1,0:T(8,128)(2,1)S(1)} %shrink.1), channel_id=1, source_target_pairs={{0,4},{4,0},{8,12},{12,8},{1,5},{5,1},{9,13},{13,9},{2,6},{6,2},{1... | collective-permute-start | bytes 49160 | tf_op jit(solution)/shard_map/ppermute | solution.py:19
  13.9 8.6 %collective-permute-start.3 = (bf16[64,2048]{1,0:T(8,128)(2,1)S(1)}, bf16[64,2048]{1,0:T(8,128)(2,1)S(1)}, u32[]{:S(2)}, u32[]{:S(2)}) collective-permute-start(bf16[64,2048]{1,0:T(8,128)(2,1)S(1)} %base_terms.6), channel_id=1, source_target_pairs={{0,4},{4,0},{8,12},{12,8},{1,5},{5,1},{9,13},{13,9},{2,6},{6,2},{1... | collective-permute-start | bytes 786440 | tf_op jit(solution)/shard_map/ppermute | solution.py:19
  16.1 5.2 %copy-start = (bf16[4,64,2048]{2,1,0:T(8,128)(2,1)S(1)}, bf16[4,64,2048]{2,1,0:T(8,128)(2,1)}, u32[]{:S(2)}) copy-start(bf16[4,64,2048]{2,1,0:T(8,128)(2,1)} %param.20) | copy-start | bytes 3145732
  16.1 5.2 %collective-permute-start.6 = (bf16[64,128]{1,0:T(8,128)(2,1)S(1)}, bf16[64,128]{1,0:T(8,128)(2,1)S(1)}, u32[]{:S(2)}, u32[]{:S(2)}) collective-permute-start(bf16[64,128]{1,0:T(8,128)(2,1)S(1)} %add_convert_fusion.3.refs_4_), channel_id=1, source_target_pairs={{0,8},{4,12},{8,0},{12,4},{1,9},{5,13},{9,1},{13,5},{2,10},{6,14},... | collective-permute-start | bytes 49160 | tf_op jit(solution)/shard_map/ppermute | solution.py:19
  21.6 3.3 %collective-permute-start.7 = (bf16[64,2048]{1,0:T(8,128)(2,1)S(1)}, bf16[64,2048]{1,0:T(8,128)(2,1)S(1)}, u32[]{:S(2)}, u32[]{:S(2)}) collective-permute-start(bf16[64,2048]{1,0:T(8,128)(2,1)S(1)} %get-tuple-element.22), channel_id=1, source_target_pairs={{0,1},{1,0},{2,3},{3,2},{4,5},{5,4},{6,7},{7,6},{8,9},{9,8},{10,11... | collective-permute-start | bytes 786440 | tf_op jit(solution)/shard_map/ppermute | solution.py:19
  22.5 6.6 %collective-permute-start.4 = (bf16[32,2048]{1,0:T(8,128)(2,1)S(1)}, bf16[32,2048]{1,0:T(8,128)(2,1)S(1)}, u32[]{:S(2)}, u32[]{:S(2)}) collective-permute-start(bf16[32,2048]{1,0:T(8,128)(2,1)S(1)} %add_convert_fusion.2), channel_id=1, source_target_pairs={{0,8},{4,12},{8,0},{12,4},{1,9},{5,13},{9,1},{13,5},{2,10},{6,14},... | collective-permute-start | bytes 393224 | tf_op jit(solution)/shard_map/ppermute | solution.py:19
  25.0 5.2 %collective-permute-start.8 = (bf16[32,2048]{1,0:T(8,128)(2,1)S(1)}, bf16[32,2048]{1,0:T(8,128)(2,1)S(1)}, u32[]{:S(2)}, u32[]{:S(2)}) collective-permute-start(bf16[32,2048]{1,0:T(8,128)(2,1)S(1)} %add_convert_fusion.1), channel_id=1, source_target_pairs={{0,2},{1,3},{2,0},{3,1},{4,6},{5,7},{6,4},{7,5},{8,10},{9,11},{10,... | collective-permute-start | bytes 393224 | tf_op jit(solution)/shard_map/ppermute | solution.py:19

commit v6 on v5

--- a/solution.py
+++ b/solution.py
@@ -27,9 +27,9 @@
     return lax.broadcasted_iota(jnp.int32, shape, len(shape) - 1)
 
 
-def attend_kernel(parts, group_at, *refs):
-    given, (tagged, *scratch) = refs[:8], refs[8:]
-    held, (spread_out, small_sems, key_sems, value_sems) = scratch[:8], scratch[8:]
+def attend_kernel(parts, group_at, early_at, *refs):
+    given, (out_weight, tagged, early, *scratch) = refs[:8], refs[8:]
+    held, (spread_out, small_sems, key_sems, value_sems, early_sem) = scratch[:8], scratch[8:]
     key_cache, value_cache = given[:2]
     keys, values, queries, new_key, new_value, lengths, row_adapter, adapter_list = held
     rows, heads, width = queries.shape
@@ -52,6 +52,10 @@
     for part in range(parts):
         for copy in cache_copies(part):
             copy.start()
+    block = early.shape[1]
+    start = pl.multiple_of(early_at[0] * block, block)
+    early_copy = pltpu.make_async_copy(out_weight.at[:, pl.ds(start, block)], early, early_sem)
+    early_copy.start()
     for copy in small:
         copy.wait()
     at_row = lax.broadcasted_iota(jnp.int32, (rows, LANES), 0)
@@ -106,9 +110,13 @@
         tagged[:, head * width : (head + 1) * width] = spread_out[
             pl.ds(head, rows, stride=heads)
         ].astype(BF16)
+    early_copy.wait()
 
 
 def attend(
+    early_at,
+    block,
+    out_weight,
     queries,
     key_cache,
     value_cache,
@@ -128,11 +136,14 @@
     parts = 2
     smem = pl.BlockSpec(memory_space=pltpu.SMEM)
     away = pl.BlockSpec(memory_space=pl.ANY)
-    tagged = pl.pallas_call(
+    tagged, early = pl.pallas_call(
         functools.partial(attend_kernel, parts),
-        out_shape=jax.ShapeDtypeStruct((rows, full * width + LANES), BF16),
-        in_specs=[smem] + [away] * 8,
-        out_specs=pl.BlockSpec(memory_space=VMEM),
+        out_shape=[
+            jax.ShapeDtypeStruct((rows, full * width + LANES), BF16),
+            VMEM((out_weight.shape[0], block), BF16),
+        ],
+        in_specs=[smem, smem] + [away] * 9,
+        out_specs=[pl.BlockSpec(memory_space=VMEM)] * 2,
         scratch_shapes=[
             VMEM((rows, positions, width), BF16),
             VMEM((rows, positions, width), BF16),
@@ -146,6 +157,7 @@
             pltpu.SemaphoreType.DMA((6,)),
             pltpu.SemaphoreType.DMA((parts,)),
             pltpu.SemaphoreType.DMA((parts,)),
+            pltpu.SemaphoreType.DMA,
         ],
         compiler_params=pltpu.CompilerParams(vmem_limit_bytes=8 << 20),
         cost_estimate=pl.CostEstimate(
@@ -156,6 +168,7 @@
         name="attention",
     )(
         group_at,
+        early_at,
         *in_hbm(
             key_cache,
             value_cache,
@@ -165,17 +178,25 @@
             lengths,
             row_adapter,
             adapter_list,
+            out_weight,
         ),
     )
     if full != heads:
         tagged = jnp.concatenate([tagged[:, : heads * width], tagged[:, full * width :]], axis=1)
-    return tagged
+    return tagged, early
+
+
+def put_stacked(out, start, term, first=0):
+    rows = term.shape[0]
+    for column in range(0, term.shape[1], LANES):
+        at = first + (start + column) // LANES * rows
+        out[at : at + rows] = term[:, column : column + LANES].astype(out.dtype)
 
 
 def base_kernel(ahead, deep, tensor_at, tagged, out_weight, *refs):
-    before, (out, held, sums, sems) = refs[:-4], refs[-4:]
+    *near, out, held, sums, sems = refs
     _, deep_rows, block = held.shape
-    rows, width = tagged.shape[0], out_weight.shape[0]
+    width = out_weight.shape[0]
     count = width // deep_rows
     column = pl.ds(pl.multiple_of((tensor_at[0] ^ ahead) * block, block), block)
 
@@ -188,10 +209,13 @@
 
     for at in range(min(deep, count)):
         copy(at).start()
-    if before:
-        out[: before[0].shape[0]] = before[0][...]
-    first = out.shape[0] - rows
     piece = min(block, 512)
+    if near:
+        early, early_out = near
+        for start in range(0, block, piece):
+            columns = slice(start, start + piece)
+            term = jnp.dot(tagged[:, :width], early[:, columns], preferred_element_type=F32)
+            put_stacked(early_out, start, term)
     for at in range(count):
         copy(at).wait()
         inputs = slice(at * deep_rows, (at + 1) * deep_rows)
@@ -205,23 +229,23 @@
             if at < count - 1:
                 sums[:, columns] = term
             else:
-                out[first:, columns] = term.astype(out.dtype)
+                put_stacked(out, start, term)
         if at + deep < count:
             copy(at + deep).start()
 
 
-def base_block(tensor_at, tagged, out_weight, block, ahead, dtype, *before):
+def base_block(tensor_at, tagged, out_weight, block, ahead, *early):
     rows = tagged.shape[0]
     width = out_weight.shape[0]
     deep, deep_rows = 4, min(width, 256)
     whole = pl.BlockSpec(memory_space=VMEM)
-    out_rows = rows + sum(each.shape[0] for each in before)
+    count = 1 + len(early)
     return pl.pallas_call(
         functools.partial(base_kernel, ahead, deep),
-        out_shape=jax.ShapeDtypeStruct((out_rows, block), dtype),
+        out_shape=[jax.ShapeDtypeStruct((block // LANES * rows, LANES), BF16)] * count,
         in_specs=[pl.BlockSpec(memory_space=pltpu.SMEM), whole, pl.BlockSpec(memory_space=pl.ANY)]
-        + [whole] * len(before),
-        out_specs=whole,
+        + [whole] * len(early),
+        out_specs=[whole] * count,
         scratch_shapes=[
             VMEM((deep, deep_rows, block), BF16),
             VMEM((rows, block), F32),
@@ -229,12 +253,12 @@
         ],
         compiler_params=pltpu.CompilerParams(vmem_limit_bytes=12 << 20),
         cost_estimate=pl.CostEstimate(
-            flops=2 * rows * width * block,
-            bytes_accessed=2 * width * block,
+            flops=2 * rows * width * block * count,
+            bytes_accessed=2 * width * block * count,
             transcendentals=0,
         ),
         name="base_terms",
-    )(tensor_at, tagged, *in_hbm(out_weight), *before)
+    )(tensor_at, tagged, *in_hbm(out_weight), *early)
 
 
 def slots_of(tags, first):
@@ -242,7 +266,9 @@
 
 
 def shrink_kernel(first_at, rank, *refs):
-    blocks, (factors, out) = refs[:-2], refs[-2:]
+    blocks, (factors, terms_ahead, out) = refs[:-3], refs[-3:]
+    above = terms_ahead.shape[0]
+    out[:above] = terms_ahead[...]
     pool, rank_width, width = factors.shape
     everyone = jnp.concatenate([block[...] for block in blocks], axis=0)
     slot = slots_of(everyone[:, width:], first_at[0])
@@ -263,18 +289,19 @@
         kept = kept + jnp.where(keep, terms[:, tile * LANES : (tile + 1) * LANES], F32(0.0))
     both = kept + pltpu.roll(kept, rank_width, 1)
     half = both.shape[0] // 2
-    out[...] = jnp.where(lane[:half] < rank_width, both[:half], both[half:]).astype(out.dtype)
-
-
-def shrink_part(blocks, shrink_weight, adapter_rank, first_at):
+    packed = jnp.where(lane[:half] < rank_width, both[:half], both[half:])
+    out[above:] = packed.astype(out.dtype)
+
+
+def shrink_part(blocks, shrink_weight, adapter_rank, first_at, terms_ahead):
     pool, width, rank_width = shrink_weight.shape
     rows = len(blocks) * blocks[0].shape[0]
     smem = pl.BlockSpec(memory_space=pltpu.SMEM)
     whole = pl.BlockSpec(memory_space=VMEM)
     return pl.pallas_call(
         shrink_kernel,
-        out_shape=jax.ShapeDtypeStruct((rows // 2, LANES), BF16),
-        in_specs=[smem, smem] + [whole] * (len(blocks) + 1),
+        out_shape=jax.ShapeDtypeStruct((terms_ahead.shape[0] + rows // 2, LANES), BF16),
+        in_specs=[smem, smem] + [whole] * (len(blocks) + 2),
         out_specs=whole,
         compiler_params=pltpu.CompilerParams(vmem_limit_bytes=8 << 20),
         cost_estimate=pl.CostEstimate(
@@ -283,7 +310,7 @@
             transcendentals=0,
         ),
         name="shrink",
-    )(first_at, adapter_rank, *blocks, jnp.swapaxes(shrink_weight, 1, 2))
+    )(first_at, adapter_rank, *blocks, jnp.swapaxes(shrink_weight, 1, 2), terms_ahead)
 
 
 def expand_kernel(count, sums, rank_width, first_at, *refs):
@@ -307,27 +334,32 @@
         ],
         axis=1,
     )
-    half, block = kept.shape
+    block = factors.shape[1]
+    rows = tags[0].shape[0]
     piece = min(block, 512)
+    stack = block // LANES * rows
     for at in range(0, block, piece):
         delta = jnp.dot(spread, factors[:, at : at + piece], preferred_element_type=F32)
-        kept[:, at : at + piece] = delta[:half].astype(kept.dtype)
-        given[:, at : at + piece] = delta[half:].astype(given.dtype)
+        for which in range(count):
+            out = kept if which < count // 2 else given
+            put_stacked(
+                out, at, delta[which * rows : (which + 1) * rows], which % (count // 2) * stack
+            )
 
 
 def expand(blocks, parts, expand_weight, first_at):
     pool, rank_width, block = expand_weight.shape
     rows, tagged_width = blocks[0].shape
     count = len(blocks)
-    half = rows * count // 2
+    half = rows * count // 2 * block // LANES
     tag = pl.BlockSpec((rows, LANES), lambda i: (0, tagged_width // LANES - 1))
     full = pl.BlockSpec((pool * rank_width, block), lambda i: (0, 0))
     part = pl.BlockSpec(parts[0].shape, lambda i: (0, 0))
-    out = pl.BlockSpec((half, block), lambda i: (0, 0))
+    out = pl.BlockSpec((half, LANES), lambda i: (0, 0))
     return pl.pallas_call(
         functools.partial(expand_kernel, count, len(parts), rank_width),
         grid=(1,),
-        out_shape=[jax.ShapeDtypeStruct((half, block), BF16)] * 2,
+        out_shape=[jax.ShapeDtypeStruct((half, LANES), BF16)] * 2,
         in_specs=[pl.BlockSpec(memory_space=pltpu.SMEM)]
         + [tag] * count
         + [part] * len(parts)
@@ -341,6 +373,34 @@
         ),
         name="expand",
     )(first_at, *blocks, *parts, expand_weight.reshape(pool * rank_width, block))
+
+
+def total_kernel(kept, given, *refs):
+    terms, out = refs[:-1], refs[-1]
+    rows = out.shape[0]
+    for column in range(0, out.shape[1], LANES):
+        at = slice(column // LANES * rows, (column // LANES + 1) * rows)
+        total = kept[at].astype(F32) + given[at].astype(F32)
+        for term in terms:
+            total = total + term[at].astype(F32)
+        out[:, column : column + LANES] = total.astype(out.dtype)
+
+
+def total(rows, block, kept, given, terms):
+    whole = pl.BlockSpec(memory_space=VMEM)
+    return pl.pallas_call(
+        total_kernel,
+        out_shape=jax.ShapeDtypeStruct((rows, block), BF16),
+        in_specs=[whole] * (2 + len(terms)),
+        out_specs=whole,
+        compiler_params=pltpu.CompilerParams(vmem_limit_bytes=8 << 20),
+        cost_estimate=pl.CostEstimate(
+            flops=rows * block * (2 + len(terms)),
+            bytes_accessed=2 * rows * block * (3 + len(terms)),
+            transcendentals=0,
+        ),
+        name="total",
+    )(kept, given, *terms)
 
 
 def local(
@@ -378,54 +438,54 @@
     def wide(array):
         return array.astype(F32)
 
-    def terms(ahead, dtype, *before):
-        return base_block(tensor_at, tagged, out_weight, block, ahead, dtype, *before)
-
-    tagged = attend(
-        queries, key_cache, value_cache, new_key, new_value, lengths, adapter_list, row_adapter
-    )
+    stack = block // LANES * rows
+    tagged, early = attend(
+        tensor_at ^ 3,
+        block,
+        out_weight,
+        queries,
+        key_cache,
+        value_cache,
+        new_key,
+        new_value,
+        lengths,
+        adapter_list,
+        row_adapter,
+    )
+    visiting = [to_chip(tagged, shift) for shift in range(1, chips)]
     beside = to_sibling(tagged)
-    visiting = [to_chip(tagged, shift) for shift in range(1, chips)]
-    odd = terms(1, BF16)
-    visiting, odd = lax.optimization_barrier((visiting, odd))
-    mine = [tagged] + visiting
-    blocks = mine + [beside] + [to_sibling(each) for each in visiting]
-    for ahead in range(3, tensor_size, 2):
-        odd = terms(ahead, BF16, odd)
-    blocks, odd = lax.optimization_barrier((blocks, odd))
-
-    part = shrink_part(blocks, shrink_weight, adapter_rank, first_at)
-    parts = [part, across(part, 1)]
-    arrived = across(odd, 1)
-    base = {ahead: terms(ahead, BF16 if ahead else F32) for ahead in range(2, tensor_size, 2)}
-    bit = 2
+    third, next_door = base_block(tensor_at, tagged, out_weight, block, 1, early)
+    visiting, third, next_door = lax.optimization_barrier((visiting, third, next_door))
+    blocks = [tagged] + visiting + [beside] + [to_sibling(each) for each in visiting]
+
+    message = shrink_part(blocks, shrink_weight, adapter_rank, first_at, third)
+    arrived = across(message, 1)
+    (second,) = base_block(tensor_at, tagged, out_weight, block, 2)
+    arrived, second = lax.optimization_barrier((arrived, second))
+    part = (wide(message[stack:]) + wide(arrived[stack:])).astype(BF16)
+    parts, bit = [part], 2
     while bit < tensor_size:
-        part = (wide(parts[0]) + wide(parts[1])).astype(BF16)
+        if len(parts) > 1:
+            part = (wide(parts[0]) + wide(parts[1])).astype(BF16)
         parts = [part, across(part, bit)]
         bit *= 2
-    base[0] = terms(0, F32)
+    terms = [across((wide(second) + wide(arrived[:stack])).astype(BF16), 2)]
+    for ahead in range(4, tensor_size, 2):
+        (near,) = base_block(tensor_at, tagged, out_weight, block, ahead)
+        (far,) = base_block(tensor_at, tagged, out_weight, block, ahead + 1)
+        terms.append(across((wide(near) + wide(across(far, 1))).astype(BF16), ahead))
+
     kept, given = expand(blocks, parts, expand_weight, first_at)
     given = to_sibling(given)
-
-    bit, sent = 1, range(1, tensor_size, 2)
-    while True:
-        for place, ahead in enumerate(sent):
-            base[ahead ^ bit] = wide(base[ahead ^ bit]) + wide(
-                arrived[place * rows : (place + 1) * rows]
-            )
-        bit *= 2
-        if bit >= tensor_size:
-            break
-        sent = [ahead for ahead in sorted(base) if ahead & bit]
-        message = [base.pop(ahead).astype(BF16) for ahead in sent]
-        arrived = across(jnp.concatenate(message, axis=0), bit)
-
-    result = base[0] + wide(kept[:rows]) + wide(given[:rows])
-    for shift in range(1, chips):
-        at = slice(shift * rows, (shift + 1) * rows)
-        home = (wide(kept[at]) + wide(given[at])).astype(BF16)
-        result = result + wide(to_chip(home, -shift))
-    return result.astype(BF16)
+    homes = [
+        (wide(kept[at : at + stack]) + wide(given[at : at + stack])).astype(BF16)
+        for at in range(stack, chips * stack, stack)
+    ]
+    homes, next_door, late_tagged = lax.optimization_barrier((homes, next_door, tagged))
+    terms += [to_chip(home, -shift) for shift, home in enumerate(homes, 1)]
+    terms.append(across(next_door, 1))
+    terms += base_block(tensor_at, late_tagged, out_weight, block, 0)
+    return total(rows, block, kept, given, terms)
 
 
 def solution(mesh):

time: 31.2 us -> 34.3 us (1.099)
  waiting for transfers between devices: 3.64 us -> 7.82 us
  Pallas kernels: 13.9 us -> 12.5 us
  starting transfers between devices: 12.4 us -> 13.7 us
  other arithmetic: 0.82 us -> 0.09 us
    ppermute x9, waiting for transfers between devices: 3.64 us -> 7.82 us  [permuted(): return lax.ppermute(array, axis, [(i, partner(i)) for i in range(size)])]
    pallas_call x6, Pallas kernels: 13.6 us -> 12.1 us  [the longest x3 7.59 us: base_block(): pl.pallas_call(functools.partial(base_kernel, ahead, deep), out_shape=[ja...]
    ppermute x9, starting transfers between devices: 12.4 us -> 13.7 us  [permuted(): return lax.ppermute(array, axis, [(i, partner(i)) for i in range(size)])]
    convert_element_type x4 -> x3, other arithmetic: 0.82 us -> 0.09 us  [the longest x1 0.04 us: local(): terms = [across((wide(second) + wide(arrived[:stack])).astype(BF16), 2)]]
  transfers between devices with their start and end apart: 9 -> 9, of which waited for: 3 -> 5; matrix products, arithmetic and copies ran while one was open for 0% -> 0% of each run, Pallas kernels for 34% -> 22%
where the time goes in v6:
time: 34.3 us; the launch traced here: 34.1 us
  starting transfers between devices  13.7 us (40%)
  Pallas kernels  12.5 us (36%)
  waiting for transfers between devices  7.82 us (23%)
    ppermute x9, starting transfers between devices, permuted(): return lax.ppermute(array, axis, [(i, partner(i)) for i in range(size)])  13.7 us
    ppermute x9, waiting for transfers between devices, permuted(): return lax.ppermute(array, axis, [(i, partner(i)) for i in range(size)])  7.82 us
    pallas_call x3, Pallas kernels, base_block(): pl.pallas_call(functools.partial(base_kernel, ahead, deep), out_shape=[ja...  7.59 us
    pallas_call x1, Pallas kernels, attend(): pl.pallas_call(functools.partial(attend_kernel, parts), out_shape=[jax.Sh...  2.84 us
    pallas_call x1, Pallas kernels, shrink_part(): pl.pallas_call(shrink_kernel, out_shape=jax.ShapeDtypeStruct((terms_ahead...  0.92 us
    pallas_call x1, Pallas kernels, total(): pl.pallas_call(total_kernel, out_shape=jax.ShapeDtypeStruct((rows, block)...  0.76 us
  transfers between devices with their start and end apart: 9, of which 5 were waited for; matrix products, arithmetic and copies ran while one was open for 0% of the time, Pallas kernels for 22%

profile of v6, /device:TPU:0, one launch (start us, length us, event | category | flops | bytes accessed | tf_op | source)
XLA Modules:
  0.0 34.1 jit_solution(6509465982140071861)
XLA Ops:
  0.0 2.8 %attention.1 = (bf16[32,1152]{1,0:T(8,128)(2,1)S(1)}, bf16[1024,2048]{1,0:T(8,128)(2,1)S(1)}) custom-call(s32[1]{0:T(128)} %bitcast.1.group_at, s32[1]{0:T(128)S(6)} %xor.3.early_at, bf16[32,4,96,128]{3,2,1,0:T(8,128)(2,1)} %refs_0_.1, bf16[32,4,96,128]{3,2,1,0:T(8,128)(2,1)} %refs_1_.1, bf16[32,8,128]{2,1,0:T(8,128)(2,1)} %refs_2_.1, ...), custom_call_target="tpu_custom_call" | custom-call | flops 12582912 | bytes 1572864 | tf_op jit(solution)/shard_map/attention/pallas_call | solution.py:139
  2.8 3.0 %collective-permute-start = (bf16[32,1152]{1,0:T(8,128)(2,1)S(1)}, bf16[32,1152]{1,0:T(8,128)(2,1)S(1)}, u32[]{:S(2)}, u32[]{:S(2)}) collective-permute-start(bf16[32,1152]{1,0:T(8,128)(2,1)S(1)} %get-tuple-element.32.tagged.refs_0_), channel_id=1, source_target_pairs={{0,2},{1,3},{2,0},{3,1},{4,6},{5,7},{6,4},{7,5},{8,10},{9,11},{10,... | collective-permute-start | bytes 221192 | tf_op jit(solution)/shard_map/ppermute | solution.py:19
  5.9 0.0 collective-permute-start.1
  5.9 0.0 copy-start.1
  5.9 0.0 copy-start.2
  5.9 2.6 %base_terms.3 = (bf16[512,128]{1,0:T(8,128)(2,1)S(1)}, bf16[512,128]{1,0:T(8,128)(2,1)S(1)}) custom-call(s32[1]{0:T(128)} %bitcast.2.tensor_at, bf16[32,1152]{1,0:T(8,128)(2,1)S(1)} %get-tuple-element.32.tagged.refs_0_, bf16[1024,8192]{1,0:T(8,128)(2,1)} %out_weight.5, bf16[1024,2048]{1,0:T(8,128)(2,1)S(1)} %get-tuple-element.20.refs_0_), custom_call_target="tpu_custom_call" | custom-call | flops 268435456 | bytes 8388608 | tf_op jit(solution)/shard_map/base_terms/pallas_call | solution.py:243
  8.5 0.0 collective-permute-done.refs_1_
  8.5 0.6 %collective-permute-start.2 = (bf16[32,1152]{1,0:T(8,128)(2,1)S(1)}, bf16[32,1152]{1,0:T(8,128)(2,1)S(1)}, u32[]{:S(2)}, u32[]{:S(2)}) collective-permute-start(bf16[32,1152]{1,0:T(8,128)(2,1)S(1)} %collective-permute-done.refs_1_), channel_id=1, source_target_pairs={{0,1},{1,0},{2,3},{3,2},{4,5},{5,4},{6,7},{7,6},{8,9},{9,8},{10,11... | collective-permute-start | bytes 221192 | tf_op jit(solution)/shard_map/ppermute | solution.py:19
  9.0 0.0 collective-permute-done.1.refs_2_
  9.0 0.9 %collective-permute-done.2.refs_3_ = bf16[32,1152]{1,0:T(8,128)(2,1)S(1)} collective-permute-done((bf16[32,1152]{1,0:T(8,128)(2,1)S(1)}, bf16[32,1152]{1,0:T(8,128)(2,1)S(1)}, u32[]{:S(2)}, u32[]{:S(2)}) %collective-permute-start.2) | collective-permute-done | bytes 73760 | tf_op jit(solution)/shard_map/ppermute | solution.py:19
  9.9 0.0 copy-done.1
  10.0 0.0 copy-done.2
  10.0 0.9 %shrink.1 = bf16[576,128]{1,0:T(8,128)(2,1)S(1)} custom-call(s32[1]{0:T(128)} %bitcast.first_at, s32[4]{0:T(128)S(1)} %copy-done.2, bf16[32,1152]{1,0:T(8,128)(2,1)S(1)} %get-tuple-element.32.tagged.refs_0_, bf16[32,1152]{1,0:T(8,128)(2,1)S(1)} %collective-permute-done.refs_1_, bf16[32,1152]{1,0:T(8,128)(2,1)S(1)} %collective-permute-done.1.refs_2_, ...), custom_call_target="tpu_custom_call" | custom-call | flops 67108864 | bytes 786432 | tf_op jit(solution)/shard_map/shrink/pallas_call | solution.py:301
  10.9 0.0 copy-start
  10.9 1.7 %collective-permute-start.3 = (bf16[576,128]{1,0:T(8,128)(2,1)S(1)}, bf16[576,128]{1,0:T(8,128)(2,1)S(1)}, u32[]{:S(2)}, u32[]{:S(2)}) collective-permute-start(bf16[576,128]{1,0:T(8,128)(2,1)S(1)} %shrink.1), channel_id=1, source_target_pairs={{0,4},{4,0},{8,12},{12,8},{1,5},{5,1},{9,13},{13,9},{2,6},{6,2},{1... | collective-permute-start | bytes 442376 | tf_op jit(solution)/shard_map/ppermute | solution.py:19
  12.6 2.5 %base_terms.4 = bf16[512,128]{1,0:T(8,128)(2,1)S(1)} custom-call(s32[1]{0:T(128)} %bitcast.2.tensor_at, bf16[32,1152]{1,0:T(8,128)(2,1)S(1)} %get-tuple-element.32.tagged.refs_0_, bf16[1024,8192]{1,0:T(8,128)(2,1)} %out_weight.5), custom_call_target="tpu_custom_call" | custom-call | flops 134217728 | bytes 4194304 | tf_op jit(solution)/shard_map/base_terms/pallas_call | solution.py:243
  15.1 2.0 %collective-permute-done.3 = bf16[576,128]{1,0:T(8,128)(2,1)S(1)} collective-permute-done((bf16[576,128]{1,0:T(8,128)(2,1)S(1)}, bf16[576,128]{1,0:T(8,128)(2,1)S(1)}, u32[]{:S(2)}, u32[]{:S(2)}) %collective-permute-start.3) | collective-permute-done | bytes 147488 | tf_op jit(solution)/shard_map/ppermute | solution.py:19
  17.1 2.7 %collective-permute-start.4 = (bf16[64,128]{1,0:T(8,128)(2,1)S(1)}, bf16[64,128]{1,0:T(8,128)(2,1)S(1)}, u32[]{:S(2)}, u32[]{:S(2)}) collective-permute-start(bf16[64,128]{1,0:T(8,128)(2,1)S(1)} %add_convert_fusion.2.refs_4_), channel_id=1, source_target_pairs={{0,8},{4,12},{8,0},{12,4},{1,9},{5,13},{9,1},{13,5},{2,10},{6,14},... | collective-permute-start | bytes 49160 | tf_op jit(solution)/shard_map/ppermute | solution.py:19
  19.7 2.0 %collective-permute-done.4.refs_5_ = bf16[64,128]{1,0:T(8,128)(2,1)S(1)} collective-permute-done((bf16[64,128]{1,0:T(8,128)(2,1)S(1)}, bf16[64,128]{1,0:T(8,128)(2,1)S(1)}, u32[]{:S(2)}, u32[]{:S(2)}) %collective-permute-start.4) | collective-permute-done | bytes 16416 | tf_op jit(solution)/shard_map/ppermute | solution.py:19
  21.8 0.0 copy-done
  21.8 0.3 %expand.1 = (bf16[1024,128]{1,0:T(8,128)(2,1)S(1)}, bf16[1024,128]{1,0:T(8,128)(2,1)S(1)}) custom-call(s32[1]{0:T(128)} %bitcast.first_at, bf16[32,1152]{1,0:T(8,128)(2,1)S(1)} %get-tuple-element.32.tagged.refs_0_, bf16[32,1152]{1,0:T(8,128)(2,1)S(1)} %collective-permute-done.refs_1_, bf16[32,1152]{1,0:T(8,128)(2,1)S(1)} %collective-permute-done.1.refs_2_, ...), custom_call_target="tpu_custom_call" | custom-call | flops 134217728 | bytes 1048576 | tf_op jit(solution)/shard_map/expand/pallas_call | solution.py:359
  22.1 0.1 collective-permute-start.5
  22.3 2.7 %collective-permute-start.6 = (bf16[512,128]{1,0:T(8,128)(2,1)S(1)}, bf16[512,128]{1,0:T(8,128)(2,1)S(1)}, u32[]{:S(2)}, u32[]{:S(2)}) collective-permute-start(bf16[512,128]{1,0:T(8,128)(2,1)S(1)} %add_convert_fusion.1), channel_id=1, source_target_pairs={{0,8},{4,12},{8,0},{12,4},{1,9},{5,13},{9,1},{13,5},{2,10},{6,14},... | collective-permute-start | bytes 393224 | tf_op jit(solution)/shard_map/ppermute | solution.py:19
  24.9 0.0 collective-permute-done.5.given
  25.0 1.4 %collective-permute-start.7 = (bf16[512,128]{1,0:T(8,128)(2,1)S(1)}, bf16[512,128]{1,0:T(8,128)(2,1)S(1)}, u32[]{:S(2)}, u32[]{:S(2)}) collective-permute-start(bf16[512,128]{1,0:T(8,128)(2,1)S(1)} %add_convert_fusion), channel_id=1, source_target_pairs={{0,2},{1,3},{2,0},{3,1},{4,6},{5,7},{6,4},{7,5},{8,10},{9,11},{10,... | collective-permute-start | bytes 393224 | tf_op jit(solution)/shard_map/ppermute | solution.py:19
  26.4 1.6 %collective-permute-start.8 = (bf16[512,128]{1,0:T(8,128)(2,1)S(1)}, bf16[512,128]{1,0:T(8,128)(2,1)S(1)}, u32[]{:S(2)}, u32[]{:S(2)}) collective-permute-start(bf16[512,128]{1,0:T(8,128)(2,1)S(1)} %get-tuple-element.31), channel_id=1, source_target_pairs={{0,4},{4,0},{8,12},{12,8},{1,5},{5,1},{9,13},{13,9},{2,6},{6,2},{1... | collective-permute-start | bytes 393224 | tf_op jit(solution)/shard_map/ppermute | solution.py:19
  28.0 2.5 %base_terms.5.refs_3_ = bf16[512,128]{1,0:T(8,128)(2,1)S(1)} custom-call(s32[1]{0:T(128)} %bitcast.2.tensor_at, bf16[32,1152]{1,0:T(8,128)(2,1)S(1)} %get-tuple-element.32.tagged.refs_0_, bf16[1024,8192]{1,0:T(8,128)(2,1)} %out_weight.5), custom_call_target="tpu_custom_call" | custom-call | flops 134217728 | bytes 4194304 | tf_op jit(solution)/shard_map/base_terms/pallas_call | solution.py:243
  30.5 1.5 %collective-permute-done.6.refs_0_ = bf16[512,128]{1,0:T(8,128)(2,1)S(1)} collective-permute-done((bf16[512,128]{1,0:T(8,128)(2,1)S(1)}, bf16[512,128]{1,0:T(8,128)(2,1)S(1)}, u32[]{:S(2)}, u32[]{:S(2)}) %collective-permute-start.6) | collective-permute-done | bytes 131104 | tf_op jit(solution)/shard_map/ppermute | solution.py:19
  32.0 0.0 collective-permute-done.7.refs_1_
  32.0 1.3 %collective-permute-done.8.refs_2_ = bf16[512,128]{1,0:T(8,128)(2,1)S(1)} collective-permute-done((bf16[512,128]{1,0:T(8,128)(2,1)S(1)}, bf16[512,128]{1,0:T(8,128)(2,1)S(1)}, u32[]{:S(2)}, u32[]{:S(2)}) %collective-permute-start.8) | collective-permute-done | bytes 131104 | tf_op jit(solution)/shard_map/ppermute | solution.py:19
  33.4 0.8 %total.1 = bf16[32,2048]{1,0:T(8,128)(2,1)} custom-call(bf16[1024,128]{1,0:T(8,128)(2,1)S(1)} %get-tuple-element.26.kept, bf16[1024,128]{1,0:T(8,128)(2,1)S(1)} %collective-permute-done.5.given, bf16[512,128]{1,0:T(8,128)(2,1)S(1)} %collective-permute-done.6.refs_0_, bf16[512,128]{1,0:T(8,128)(2,1)S(1)} %collective-permute-done.7.refs_1_, ...), custom_call_target="tpu_custom_call" | custom-call | flops 393216 | bytes 917504 | tf_op jit(solution)/shard_map/total/pallas_call | solution.py:391
  (3 shorter events, 0.1 us)
Async XLA Ops:
  2.8 5.6 %collective-permute-start = (bf16[32,1152]{1,0:T(8,128)(2,1)S(1)}, bf16[32,1152]{1,0:T(8,128)(2,1)S(1)}, u32[]{:S(2)}, u32[]{:S(2)}) collective-permute-start(bf16[32,1152]{1,0:T(8,128)(2,1)S(1)} %get-tuple-element.32.tagged.refs_0_), channel_id=1, source_target_pairs={{0,2},{1,3},{2,0},{3,1},{4,6},{5,7},{6,4},{7,5},{8,10},{9,11},{10,... | collective-permute-start | bytes 221192 | tf_op jit(solution)/shard_map/ppermute | solution.py:19
  5.9 3.2 %collective-permute-start.1 = (bf16[32,1152]{1,0:T(8,128)(2,1)S(1)}, bf16[32,1152]{1,0:T(8,128)(2,1)S(1)}, u32[]{:S(2)}, u32[]{:S(2)}) collective-permute-start(bf16[32,1152]{1,0:T(8,128)(2,1)S(1)} %get-tuple-element.32.tagged.refs_0_), channel_id=1, source_target_pairs={{0,1},{1,0},{2,3},{3,2},{4,5},{5,4},{6,7},{7,6},{8,9},{9,8},{10,11... | collective-permute-start | bytes 221192 | tf_op jit(solution)/shard_map/ppermute | solution.py:19
  5.9 4.1 %copy-start.1 = (bf16[4,1024,64]{1,2,0:T(8,128)(2,1)S(1)}, bf16[4,1024,64]{1,2,0:T(8,128)(2,1)}, u32[]{:S(2)}) copy-start(bf16[4,1024,64]{1,2,0:T(8,128)(2,1)} %param.19) | copy-start | bytes 1572868
  5.9 4.1 %copy-start.2 = (s32[4]{0:T(128)S(1)}, s32[4]{0:T(128)}, u32[]{:S(2)}) copy-start(s32[4]{0:T(128)} %rank.1) | copy-start | bytes 52
  8.5 1.5 %collective-permute-start.2 = (bf16[32,1152]{1,0:T(8,128)(2,1)S(1)}, bf16[32,1152]{1,0:T(8,128)(2,1)S(1)}, u32[]{:S(2)}, u32[]{:S(2)}) collective-permute-start(bf16[32,1152]{1,0:T(8,128)(2,1)S(1)} %collective-permute-done.refs_1_), channel_id=1, source_target_pairs={{0,1},{1,0},{2,3},{3,2},{4,5},{5,4},{6,7},{7,6},{8,9},{9,8},{10,11... | collective-permute-start | bytes 221192 | tf_op jit(solution)/shard_map/ppermute | solution.py:19
  10.9 10.9 %copy-start = (bf16[4,64,2048]{2,1,0:T(8,128)(2,1)S(1)}, bf16[4,64,2048]{2,1,0:T(8,128)(2,1)}, u32[]{:S(2)}) copy-start(bf16[4,64,2048]{2,1,0:T(8,128)(2,1)} %param.20) | copy-start | bytes 3145732
  10.9 6.2 %collective-permute-start.3 = (bf16[576,128]{1,0:T(8,128)(2,1)S(1)}, bf16[576,128]{1,0:T(8,128)(2,1)S(1)}, u32[]{:S(2)}, u32[]{:S(2)}) collective-permute-start(bf16[576,128]{1,0:T(8,128)(2,1)S(1)} %shrink.1), channel_id=1, source_target_pairs={{0,4},{4,0},{8,12},{12,8},{1,5},{5,1},{9,13},{13,9},{2,6},{6,2},{1... | collective-permute-start | bytes 442376 | tf_op jit(solution)/shard_map/ppermute | solution.py:19
  17.1 4.7 %collective-permute-start.4 = (bf16[64,128]{1,0:T(8,128)(2,1)S(1)}, bf16[64,128]{1,0:T(8,128)(2,1)S(1)}, u32[]{:S(2)}, u32[]{:S(2)}) collective-permute-start(bf16[64,128]{1,0:T(8,128)(2,1)S(1)} %add_convert_fusion.2.refs_4_), channel_id=1, source_target_pairs={{0,8},{4,12},{8,0},{12,4},{1,9},{5,13},{9,1},{13,5},{2,10},{6,14},... | collective-permute-start | bytes 49160 | tf_op jit(solution)/shard_map/ppermute | solution.py:19
  22.1 2.8 %collective-permute-start.5 = (bf16[1024,128]{1,0:T(8,128)(2,1)S(1)}, bf16[1024,128]{1,0:T(8,128)(2,1)S(1)}, u32[]{:S(2)}, u32[]{:S(2)}) collective-permute-start(bf16[1024,128]{1,0:T(8,128)(2,1)S(1)} %get-tuple-element.27), channel_id=1, source_target_pairs={{0,1},{1,0},{2,3},{3,2},{4,5},{5,4},{6,7},{7,6},{8,9},{9,8},{10,11... | collective-permute-start | bytes 786440 | tf_op jit(solution)/shard_map/ppermute | solution.py:19
  22.3 9.8 %collective-permute-start.6 = (bf16[512,128]{1,0:T(8,128)(2,1)S(1)}, bf16[512,128]{1,0:T(8,128)(2,1)S(1)}, u32[]{:S(2)}, u32[]{:S(2)}) collective-permute-start(bf16[512,128]{1,0:T(8,128)(2,1)S(1)} %add_convert_fusion.1), channel_id=1, source_target_pairs={{0,8},{4,12},{8,0},{12,4},{1,9},{5,13},{9,1},{13,5},{2,10},{6,14},... | collective-permute-start | bytes 393224 | tf_op jit(solution)/shard_map/ppermute | solution.py:19
  25.0 7.1 %collective-permute-start.7 = (bf16[512,128]{1,0:T(8,128)(2,1)S(1)}, bf16[512,128]{1,0:T(8,128)(2,1)S(1)}, u32[]{:S(2)}, u32[]{:S(2)}) collective-permute-start(bf16[512,128]{1,0:T(8,128)(2,1)S(1)} %add_convert_fusion), channel_id=1, source_target_pairs={{0,2},{1,3},{2,0},{3,1},{4,6},{5,7},{6,4},{7,5},{8,10},{9,11},{10,... | collective-permute-start | bytes 393224 | tf_op jit(solution)/shard_map/ppermute | solution.py:19
  26.4 7.0 %collective-permute-start.8 = (bf16[512,128]{1,0:T(8,128)(2,1)S(1)}, bf16[512,128]{1,0:T(8,128)(2,1)S(1)}, u32[]{:S(2)}, u32[]{:S(2)}) collective-permute-start(bf16[512,128]{1,0:T(8,128)(2,1)S(1)} %get-tuple-element.31), channel_id=1, source_target_pairs={{0,4},{4,0},{8,12},{12,8},{1,5},{5,1},{9,13},{13,9},{2,6},{6,2},{1... | collective-permute-start | bytes 393224 | tf_op jit(solution)/shard_map/ppermute | solution.py:19

commit v7 on v6

--- a/solution.py
+++ b/solution.py
@@ -186,15 +186,18 @@
     return tagged, early
 
 
-def put_stacked(out, start, term, first=0):
+def put_stacked(out, start, term, first=0, others=()):
     rows = term.shape[0]
     for column in range(0, term.shape[1], LANES):
         at = first + (start + column) // LANES * rows
-        out[at : at + rows] = term[:, column : column + LANES].astype(out.dtype)
-
-
-def base_kernel(ahead, deep, tensor_at, tagged, out_weight, *refs):
-    *near, out, held, sums, sems = refs
+        part = term[:, column : column + LANES]
+        for other in others:
+            part = part + other[at : at + rows].astype(F32)
+        out[at : at + rows] = part.astype(out.dtype)
+
+
+def base_kernel(ahead, deep, arriving, tensor_at, tagged, out_weight, *refs):
+    arrived, (*near, out, held, sums, sems) = refs[:arriving], refs[arriving:]
     _, deep_rows, block = held.shape
     width = out_weight.shape[0]
     count = width // deep_rows
@@ -229,22 +232,23 @@
             if at < count - 1:
                 sums[:, columns] = term
             else:
-                put_stacked(out, start, term)
+                put_stacked(out, start, term, 0, arrived)
         if at + deep < count:
             copy(at + deep).start()
 
 
-def base_block(tensor_at, tagged, out_weight, block, ahead, *early):
+def base_block(tensor_at, tagged, out_weight, block, ahead, early=(), arrived=()):
     rows = tagged.shape[0]
     width = out_weight.shape[0]
     deep, deep_rows = 4, min(width, 256)
     whole = pl.BlockSpec(memory_space=VMEM)
     count = 1 + len(early)
     return pl.pallas_call(
-        functools.partial(base_kernel, ahead, deep),
-        out_shape=[jax.ShapeDtypeStruct((block // LANES * rows, LANES), BF16)] * count,
+        functools.partial(base_kernel, ahead, deep, len(arrived)),
+        out_shape=[jax.ShapeDtypeStruct((block // LANES * rows, LANES), BF16 if ahead else F32)]
+        * count,
         in_specs=[pl.BlockSpec(memory_space=pltpu.SMEM), whole, pl.BlockSpec(memory_space=pl.ANY)]
-        + [whole] * len(early),
+        + [whole] * (len(arrived) + len(early)),
         out_specs=[whole] * count,
         scratch_shapes=[
             VMEM((deep, deep_rows, block), BF16),
@@ -254,68 +258,70 @@
         compiler_params=pltpu.CompilerParams(vmem_limit_bytes=12 << 20),
         cost_estimate=pl.CostEstimate(
             flops=2 * rows * width * block * count,
-            bytes_accessed=2 * width * block * count,
+            bytes_accessed=2 * width * block * (2 if arrived else count),
             transcendentals=0,
         ),
         name="base_terms",
-    )(tensor_at, tagged, *in_hbm(out_weight), *early)
-
-
-def slots_of(tags, first):
-    return tags.astype(F32).astype(jnp.int32) - first
-
-
-def shrink_kernel(first_at, rank, *refs):
-    blocks, (factors, terms_ahead, out) = refs[:-3], refs[-3:]
-    above = terms_ahead.shape[0]
-    out[:above] = terms_ahead[...]
-    pool, rank_width, width = factors.shape
+    )(tensor_at, tagged, *in_hbm(out_weight), *arrived, *early)
+
+
+def slots_of(tags, batch_at, pool, tile, per):
+    lane = lane_of(tags.shape)
+    ids = tags.astype(F32).astype(jnp.int32)
+    mine = tile * per + lane // (LANES // per)
+    held = tile * per // pool
+    return ids - (batch_at[0] ^ held) * pool + held * pool, mine
+
+
+def shrink_kernel(batch_at, *refs):
+    blocks, factors, out = refs[:-3], refs[-3:-1], refs[-1]
+    pool, rank_width, width = factors[0].shape
     everyone = jnp.concatenate([block[...] for block in blocks], axis=0)
-    slot = slots_of(everyone[:, width:], first_at[0])
-    terms = lax.dot_general(
-        everyone[:, :width],
-        factors[...].reshape(pool * rank_width, width),
-        (((1,), (1,)), ((), ())),
-        preferred_element_type=F32,
-    )
-    lane = lane_of(slot.shape)
     per = LANES // rank_width
-    kept = jnp.zeros(slot.shape, F32)
-    for tile in range(pool // per):
-        mine, limit = tile * per + lane // rank_width, jnp.zeros_like(lane)
-        for n in range(tile * per, (tile + 1) * per):
-            limit = jnp.where(mine == n, rank[n], limit)
-        keep = (slot == mine) & (lane % rank_width < limit)
-        kept = kept + jnp.where(keep, terms[:, tile * LANES : (tile + 1) * LANES], F32(0.0))
+    lane = lane_of((everyone.shape[0], LANES))
+    kept = jnp.zeros(lane.shape, F32)
+    for held, weights in enumerate(factors):
+        terms = lax.dot_general(
+            everyone[:, :width],
+            weights[...].reshape(pool * rank_width, width),
+            (((1,), (1,)), ((), ())),
+            preferred_element_type=F32,
+        )
+        for tile in range(pool // per):
+            slot, mine = slots_of(everyone[:, width:], batch_at, pool, held * pool // per + tile, per)
+            kept = kept + jnp.where(
+                slot == mine, terms[:, tile * LANES : (tile + 1) * LANES], F32(0.0)
+            )
     both = kept + pltpu.roll(kept, rank_width, 1)
     half = both.shape[0] // 2
     packed = jnp.where(lane[:half] < rank_width, both[:half], both[half:])
-    out[above:] = packed.astype(out.dtype)
-
-
-def shrink_part(blocks, shrink_weight, adapter_rank, first_at, terms_ahead):
-    pool, width, rank_width = shrink_weight.shape
+    out[...] = packed.astype(out.dtype)
+
+
+def shrink_part(blocks, factors, batch_at):
+    pool, rank_width, width = factors[0].shape
     rows = len(blocks) * blocks[0].shape[0]
     smem = pl.BlockSpec(memory_space=pltpu.SMEM)
     whole = pl.BlockSpec(memory_space=VMEM)
     return pl.pallas_call(
         shrink_kernel,
-        out_shape=jax.ShapeDtypeStruct((terms_ahead.shape[0] + rows // 2, LANES), BF16),
-        in_specs=[smem, smem] + [whole] * (len(blocks) + 2),
+        out_shape=jax.ShapeDtypeStruct((rows // 2, LANES), BF16),
+        in_specs=[smem] + [whole] * (len(blocks) + 2),
         out_specs=whole,
         compiler_params=pltpu.CompilerParams(vmem_limit_bytes=8 << 20),
         cost_estimate=pl.CostEstimate(
-            flops=2 * rows * width * pool * rank_width,
-            bytes_accessed=2 * width * (rows + pool * rank_width),
+            flops=4 * rows * width * pool * rank_width,
+            bytes_accessed=2 * width * (rows + 2 * pool * rank_width),
             transcendentals=0,
         ),
         name="shrink",
-    )(first_at, adapter_rank, *blocks, jnp.swapaxes(shrink_weight, 1, 2), terms_ahead)
-
-
-def expand_kernel(count, sums, rank_width, first_at, *refs):
-    tags, parts, (factors, kept, given) = refs[:count], refs[count : count + sums], refs[-3:]
-    slot = slots_of(jnp.concatenate([tag[...] for tag in tags], axis=0), first_at[0])
+    )(batch_at, *blocks, *factors)
+
+
+def expand_kernel(count, sums, rank_width, batch_at, rank, sibling_rank, *refs):
+    tags, parts = refs[:count], refs[count : count + sums]
+    factors, outs = refs[count + sums : count + sums + 2], refs[count + sums + 2 :]
+    tags = jnp.concatenate([tag[...] for tag in tags], axis=0)
     total = parts[0][...].astype(F32)
     for part in parts[1:]:
         total = total + part[...].astype(F32)
@@ -325,82 +331,107 @@
     shrink = jnp.concatenate(
         [jnp.where(low, total, other), jnp.where(low, other, total)], axis=0
     )
-    lane = lane_of(slot.shape)
     per = LANES // rank_width
-    spread = jnp.concatenate(
-        [
-            jnp.where(slot == tile * per + lane // rank_width, shrink, F32(0.0)).astype(BF16)
-            for tile in range(factors.shape[0] // LANES)
-        ],
-        axis=1,
-    )
-    block = factors.shape[1]
-    rows = tags[0].shape[0]
+    inputs, block = factors[0].shape
+    pool = inputs // rank_width
+    tiles = []
+    for tile in range(2 * pool // per):
+        slot, mine = slots_of(tags, batch_at, pool, tile, per)
+        lane, limit = lane_of(tags.shape) % rank_width, jnp.zeros_like(mine)
+        for n in range(tile * per, (tile + 1) * per):
+            limit = jnp.where(mine == n, (rank, sibling_rank)[n // pool][n % pool], limit)
+        tiles.append(jnp.where((slot == mine) & (lane < limit), shrink, F32(0.0)).astype(BF16))
+    half = len(tiles) // 2
+    spreads = [jnp.concatenate(tiles[:half], axis=1), jnp.concatenate(tiles[half:], axis=1)]
+    rows = tags.shape[0] // count
     piece = min(block, 512)
-    stack = block // LANES * rows
     for at in range(0, block, piece):
-        delta = jnp.dot(spread, factors[:, at : at + piece], preferred_element_type=F32)
-        for which in range(count):
-            out = kept if which < count // 2 else given
-            put_stacked(
-                out, at, delta[which * rows : (which + 1) * rows], which % (count // 2) * stack
-            )
-
-
-def expand(blocks, parts, expand_weight, first_at):
-    pool, rank_width, block = expand_weight.shape
+        delta = sum(
+            jnp.dot(spread, each[:, at : at + piece], preferred_element_type=F32)
+            for spread, each in zip(spreads, factors)
+        )
+        for which, out in enumerate(outs):
+            put_stacked(out, at, delta[which * rows : (which + 1) * rows])
+
+
+def expand(blocks, parts, factors, ranks, batch_at):
+    pool, rank_width, block = factors[0].shape
     rows, tagged_width = blocks[0].shape
     count = len(blocks)
-    half = rows * count // 2 * block // LANES
+    stack = rows * block // LANES
     tag = pl.BlockSpec((rows, LANES), lambda i: (0, tagged_width // LANES - 1))
     full = pl.BlockSpec((pool * rank_width, block), lambda i: (0, 0))
     part = pl.BlockSpec(parts[0].shape, lambda i: (0, 0))
-    out = pl.BlockSpec((half, LANES), lambda i: (0, 0))
     return pl.pallas_call(
         functools.partial(expand_kernel, count, len(parts), rank_width),
         grid=(1,),
-        out_shape=[jax.ShapeDtypeStruct((half, LANES), BF16)] * 2,
-        in_specs=[pl.BlockSpec(memory_space=pltpu.SMEM)]
+        out_shape=[jax.ShapeDtypeStruct((stack, LANES), BF16) for _ in blocks],
+        in_specs=[pl.BlockSpec(memory_space=pltpu.SMEM)] * 3
         + [tag] * count
         + [part] * len(parts)
-        + [full],
-        out_specs=[out, out],
+        + [full] * 2,
+        out_specs=[pl.BlockSpec((stack, LANES), lambda i: (0, 0)) for _ in blocks],
         compiler_params=pltpu.CompilerParams(vmem_limit_bytes=16 << 20),
         cost_estimate=pl.CostEstimate(
-            flops=2 * rows * count * pool * rank_width * block,
+            flops=4 * rows * count * pool * rank_width * block,
             bytes_accessed=2 * pool * rank_width * block,
             transcendentals=0,
         ),
         name="expand",
-    )(first_at, *blocks, *parts, expand_weight.reshape(pool * rank_width, block))
-
-
-def total_kernel(kept, given, *refs):
+    )(batch_at, *ranks, *blocks, *parts, *[each.reshape(pool * rank_width, block) for each in factors])
+
+
+def total_kernel(*refs):
     terms, out = refs[:-1], refs[-1]
     rows = out.shape[0]
     for column in range(0, out.shape[1], LANES):
         at = slice(column // LANES * rows, (column // LANES + 1) * rows)
-        total = kept[at].astype(F32) + given[at].astype(F32)
-        for term in terms:
+        total = terms[0][at].astype(F32)
+        for term in terms[1:]:
             total = total + term[at].astype(F32)
         out[:, column : column + LANES] = total.astype(out.dtype)
 
 
-def total(rows, block, kept, given, terms):
+def total(rows, block, terms):
     whole = pl.BlockSpec(memory_space=VMEM)
     return pl.pallas_call(
         total_kernel,
         out_shape=jax.ShapeDtypeStruct((rows, block), BF16),
-        in_specs=[whole] * (2 + len(terms)),
+        in_specs=[whole] * len(terms),
         out_specs=whole,
         compiler_params=pltpu.CompilerParams(vmem_limit_bytes=8 << 20),
         cost_estimate=pl.CostEstimate(
-            flops=rows * block * (2 + len(terms)),
-            bytes_accessed=2 * rows * block * (3 + len(terms)),
+            flops=rows * block * len(terms),
+            bytes_accessed=2 * rows * block * (1 + len(terms)),
             transcendentals=0,
         ),
         name="total",
-    )(kept, given, *terms)
+    )(*terms)
+
+
+def partial_kernel(*refs):
+    terms, out = refs[:-1], refs[-1]
+    total = terms[0][...].astype(F32)
+    for term in terms[1:]:
+        total = total + term[...].astype(F32)
+    out[...] = total
+
+
+def partial_total(terms):
+    whole = pl.BlockSpec(memory_space=VMEM)
+    return pl.pallas_call(
+        partial_kernel,
+        out_shape=jax.ShapeDtypeStruct(terms[0].shape, F32),
+        in_specs=[whole] * len(terms),
+        out_specs=whole,
+        compiler_params=pltpu.CompilerParams(vmem_limit_bytes=8 << 20),
+        cost_estimate=pl.CostEstimate(
+            flops=terms[0].size * len(terms),
+            bytes_accessed=8 << 20,
+            transcendentals=0,
+        ),
+        name="partial_total",
+    )(*terms)
 
 
 def local(
@@ -420,10 +451,9 @@
     row_adapter,
 ):
     rows = queries.shape[0]
-    pool = shrink_weight.shape[0]
     block = expand_weight.shape[2]
     chips = batch_size // 2
-    first_at = (lax.axis_index("batch") * pool).reshape(1).astype(jnp.int32)
+    batch_at = lax.axis_index("batch").reshape(1).astype(jnp.int32)
     tensor_at = lax.axis_index("tensor").reshape(1).astype(jnp.int32)
 
     def to_sibling(array):
@@ -452,40 +482,39 @@
         adapter_list,
         row_adapter,
     )
+    ranks = [adapter_rank, to_sibling(adapter_rank)]
+    shrink_weight = jnp.swapaxes(shrink_weight, 1, 2)
+    shrink_factors = [shrink_weight, to_sibling(shrink_weight)]
+    expand_factors = [expand_weight, to_sibling(expand_weight)]
     visiting = [to_chip(tagged, shift) for shift in range(1, chips)]
-    beside = to_sibling(tagged)
-    third, next_door = base_block(tensor_at, tagged, out_weight, block, 1, early)
+    third, next_door = base_block(tensor_at, tagged, out_weight, block, 1, [early])
     visiting, third, next_door = lax.optimization_barrier((visiting, third, next_door))
-    blocks = [tagged] + visiting + [beside] + [to_sibling(each) for each in visiting]
-
-    message = shrink_part(blocks, shrink_weight, adapter_rank, first_at, third)
-    arrived = across(message, 1)
-    (second,) = base_block(tensor_at, tagged, out_weight, block, 2)
-    arrived, second = lax.optimization_barrier((arrived, second))
-    part = (wide(message[stack:]) + wide(arrived[stack:])).astype(BF16)
-    parts, bit = [part], 2
+    blocks = [tagged] + visiting
+    third = across(third, 1)
+
+    part = shrink_part(blocks, shrink_factors, batch_at)
+    parts = [part, across(part, 1)]
+    part, later_tagged = lax.optimization_barrier((part, tagged))
+    (second,) = base_block(tensor_at, later_tagged, out_weight, block, 2)
+    second = (wide(second) + wide(third)).astype(BF16)
+    parts, second = lax.optimization_barrier((parts, second))
+    bit = 2
     while bit < tensor_size:
-        if len(parts) > 1:
-            part = (wide(parts[0]) + wide(parts[1])).astype(BF16)
+        part = (wide(parts[0]) + wide(parts[1])).astype(BF16)
         parts = [part, across(part, bit)]
         bit *= 2
-    terms = [across((wide(second) + wide(arrived[:stack])).astype(BF16), 2)]
+    arrived = [across(second, 2), across(next_door, 1)]
     for ahead in range(4, tensor_size, 2):
         (near,) = base_block(tensor_at, tagged, out_weight, block, ahead)
         (far,) = base_block(tensor_at, tagged, out_weight, block, ahead + 1)
-        terms.append(across((wide(near) + wide(across(far, 1))).astype(BF16), ahead))
-
-    kept, given = expand(blocks, parts, expand_weight, first_at)
-    given = to_sibling(given)
-    homes = [
-        (wide(kept[at : at + stack]) + wide(given[at : at + stack])).astype(BF16)
-        for at in range(stack, chips * stack, stack)
-    ]
-    homes, next_door, late_tagged = lax.optimization_barrier((homes, next_door, tagged))
-    terms += [to_chip(home, -shift) for shift, home in enumerate(homes, 1)]
-    terms.append(across(next_door, 1))
-    terms += base_block(tensor_at, late_tagged, out_weight, block, 0)
-    return total(rows, block, kept, given, terms)
+        arrived.append(across((wide(near) + wide(across(far, 1))).astype(BF16), ahead))
+
+    deltas = expand(blocks, parts, expand_factors, ranks, batch_at)
+    deltas, late_tagged = lax.optimization_barrier((deltas, tagged))
+    (own,) = base_block(tensor_at, late_tagged, out_weight, block, 0)
+    terms = [partial_total([own, deltas[0], *arrived])]
+    terms += [to_chip(home, -shift) for shift, home in enumerate(deltas[1:], 1)]
+    return total(rows, block, terms)
 
 
 def solution(mesh):

time: 34.3 us -> 28.9 us (0.84)
  waiting for transfers between devices: 7.82 us -> 4.7 us
  starting transfers between devices: 13.7 us -> 11.2 us
    ppermute x9 -> x10, waiting for transfers between devices: 7.82 us -> 4.7 us  [permuted(): return lax.ppermute(array, axis, [(i, partner(i)) for i in range(size)])]
    ppermute x9 -> x10, starting transfers between devices: 13.7 us -> 11.2 us  [permuted(): return lax.ppermute(array, axis, [(i, partner(i)) for i in range(size)])]
    pallas_call x1, Pallas kernels: 0.35 us -> 1.07 us  [expand(): pl.pallas_call(functools.partial(expand_kernel, count, len(parts), rank_w...]
    pallas_call x4 -> x5, Pallas kernels: 8.51 us -> 8.16 us  [the longest x3 7.59 us: base_block(): pl.pallas_call(functools.partial(base_kernel, ahead, deep, len(arrived)),...]
  transfers between devices with their start and end apart: 9 -> 10, of which waited for: 5 -> 4; matrix products, arithmetic and copies ran while one was open for 0% -> 0% of each run, Pallas kernels for 22% -> 42%
where the time goes in v7:
time: 28.9 us; the launch traced here: 28.8 us
  Pallas kernels  12.8 us (44%)
  starting transfers between devices  11.2 us (39%)
  waiting for transfers between devices  4.7 us (16%)
    ppermute x10, starting transfers between devices, permuted(): return lax.ppermute(array, axis, [(i, partner(i)) for i in range(size)])  11.2 us
    pallas_call x3, Pallas kernels, base_block(): pl.pallas_call(functools.partial(base_kernel, ahead, deep, len(arrived)),...  7.59 us
    ppermute x10, waiting for transfers between devices, permuted(): return lax.ppermute(array, axis, [(i, partner(i)) for i in range(size)])  4.7 us
    pallas_call x1, Pallas kernels, attend(): pl.pallas_call(functools.partial(attend_kernel, parts), out_shape=[jax.Sh...  2.84 us
    pallas_call x1, Pallas kernels, expand(): pl.pallas_call(functools.partial(expand_kernel, count, len(parts), rank_w...  1.07 us
    pallas_call x1, Pallas kernels, total(): pl.pallas_call(total_kernel, out_shape=jax.ShapeDtypeStruct((rows, block)...  0.69 us
  transfers between devices with their start and end apart: 10, of which 4 were waited for; matrix products, arithmetic and copies ran while one was open for 0% of the time, Pallas kernels for 42%

profile of v7, /device:TPU:0, one launch (start us, length us, event | category | flops | bytes accessed | tf_op | source)
XLA Modules:
  0.0 28.8 jit_solution(12931901297367130292)
XLA Ops:
  0.0 0.5 %collective-permute-start.6 = (bf16[4,64,2048]{2,1,0:T(8,128)(2,1)}, bf16[4,64,2048]{2,1,0:T(8,128)(2,1)S(1)}, u32[]{:S(2)}, u32[]{:S(2)}) collective-permute-start(bf16[4,64,2048]{2,1,0:T(8,128)(2,1)} %param.20), channel_id=1, source_target_pairs={{0,1},{1,0},{2,3},{3,2},{4,5},{5,4},{6,7},{7,6},{8,9},{9,8},{10,11... | collective-permute-start | bytes 3145736 | tf_op jit(solution)/shard_map/ppermute | solution.py:19
  0.5 0.1 collective-permute-start.2
  0.5 2.8 %attention.1 = (bf16[32,1152]{1,0:T(8,128)(2,1)S(1)}, bf16[1024,2048]{1,0:T(8,128)(2,1)S(1)}) custom-call(s32[1]{0:T(128)} %bitcast.2.group_at, s32[1]{0:T(128)S(6)} %xor.3.early_at, bf16[32,4,96,128]{3,2,1,0:T(8,128)(2,1)} %refs_0_.1, bf16[32,4,96,128]{3,2,1,0:T(8,128)(2,1)} %refs_1_.1, bf16[32,8,128]{2,1,0:T(8,128)(2,1)} %refs_2_.1, ...), custom_call_target="tpu_custom_call" | custom-call | flops 12582912 | bytes 1572864 | tf_op jit(solution)/shard_map/attention/pallas_call | solution.py:139
  3.4 3.0 %collective-permute-start.1 = (bf16[32,1152]{1,0:T(8,128)(2,1)S(1)}, bf16[32,1152]{1,0:T(8,128)(2,1)S(1)}, u32[]{:S(2)}, u32[]{:S(2)}) collective-permute-start(bf16[32,1152]{1,0:T(8,128)(2,1)S(1)} %get-tuple-element.32.tagged.refs_0_), channel_id=1, source_target_pairs={{0,2},{1,3},{2,0},{3,1},{4,6},{5,7},{6,4},{7,5},{8,10},{9,11},{10,... | collective-permute-start | bytes 221192 | tf_op jit(solution)/shard_map/ppermute | solution.py:19
  6.4 0.0 copy-start.1
  6.4 2.6 %base_terms.3 = (bf16[512,128]{1,0:T(8,128)(2,1)S(1)}, bf16[512,128]{1,0:T(8,128)(2,1)S(1)}) custom-call(s32[1]{0:T(128)} %bitcast.tensor_at, bf16[32,1152]{1,0:T(8,128)(2,1)S(1)} %get-tuple-element.32.tagged.refs_0_, bf16[1024,8192]{1,0:T(8,128)(2,1)} %out_weight.5, bf16[1024,2048]{1,0:T(8,128)(2,1)S(1)} %get-tuple-element.22.refs_0_), custom_call_target="tpu_custom_call" | custom-call | flops 268435456 | bytes 8388608 | tf_op jit(solution)/shard_map/base_terms/pallas_call | solution.py:246
  9.0 0.0 collective-permute-done.1.refs_1_
  9.0 1.8 %collective-permute-start.4 = (bf16[512,128]{1,0:T(8,128)(2,1)S(1)}, bf16[512,128]{1,0:T(8,128)(2,1)S(1)}, u32[]{:S(2)}, u32[]{:S(2)}) collective-permute-start(bf16[512,128]{1,0:T(8,128)(2,1)S(1)} %get-tuple-element.27), channel_id=1, source_target_pairs={{0,4},{4,0},{8,12},{12,8},{1,5},{5,1},{9,13},{13,9},{2,6},{6,2},{1... | collective-permute-start | bytes 393224 | tf_op jit(solution)/shard_map/ppermute | solution.py:19
  10.8 0.0 collective-permute-done.2.refs_3_
  10.8 0.0 copy-done.1
  10.8 0.5 %shrink.1 = bf16[32,128]{1,0:T(8,128)(2,1)S(1)} custom-call(s32[1]{0:T(128)} %bitcast.1.batch_at, bf16[32,1152]{1,0:T(8,128)(2,1)S(1)} %get-tuple-element.32.tagged.refs_0_, bf16[32,1152]{1,0:T(8,128)(2,1)S(1)} %collective-permute-done.1.refs_1_, bf16[4,64,1024]{2,1,0:T(8,128)(2,1)S(1)} %bitcast.9, bf16[4,64,1024]{2,1,0:T(8,128)(2,1)S(1)} %collective-permute-done.2.refs_3_), custom_call_target="tpu_custom_call" | custom-call | flops 67108864 | bytes 1179648 | tf_op jit(solution)/shard_map/shrink/pallas_call | solution.py:306
  11.3 0.0 copy-start.2
  11.3 0.0 copy-start
  11.3 0.3 %collective-permute-start.3 = (bf16[32,128]{1,0:T(8,128)(2,1)S(1)}, bf16[32,128]{1,0:T(8,128)(2,1)S(1)}, u32[]{:S(2)}, u32[]{:S(2)}) collective-permute-start(bf16[32,128]{1,0:T(8,128)(2,1)S(1)} %shrink.1), channel_id=1, source_target_pairs={{0,4},{4,0},{8,12},{12,8},{1,5},{5,1},{9,13},{13,9},{2,6},{6,2},{1... | collective-permute-start | bytes 24584 | tf_op jit(solution)/shard_map/ppermute | solution.py:19
  11.7 2.5 %base_terms.4 = bf16[512,128]{1,0:T(8,128)(2,1)S(1)} custom-call(s32[1]{0:T(128)} %bitcast.tensor_at, bf16[32,1152]{1,0:T(8,128)(2,1)S(1)} %get-tuple-element.32.tagged.refs_0_, bf16[1024,8192]{1,0:T(8,128)(2,1)} %out_weight.5), custom_call_target="tpu_custom_call" | custom-call | flops 134217728 | bytes 4194304 | tf_op jit(solution)/shard_map/base_terms/pallas_call | solution.py:246
  14.2 0.1 collective-permute-done.4
  14.3 0.8 %collective-permute-done.3 = bf16[32,128]{1,0:T(8,128)(2,1)S(1)} collective-permute-done((bf16[32,128]{1,0:T(8,128)(2,1)S(1)}, bf16[32,128]{1,0:T(8,128)(2,1)S(1)}, u32[]{:S(2)}, u32[]{:S(2)}) %collective-permute-start.3) | collective-permute-done | bytes 8224 | tf_op jit(solution)/shard_map/ppermute | solution.py:19
  15.1 2.6 %collective-permute-start.5 = (bf16[32,128]{1,0:T(8,128)(2,1)S(1)}, bf16[32,128]{1,0:T(8,128)(2,1)S(1)}, u32[]{:S(2)}, u32[]{:S(2)}) collective-permute-start(bf16[32,128]{1,0:T(8,128)(2,1)S(1)} %add_convert_fusion.1.refs_2_), channel_id=1, source_target_pairs={{0,8},{4,12},{8,0},{12,4},{1,9},{5,13},{9,1},{13,5},{2,10},{6,14},... | collective-permute-start | bytes 24584 | tf_op jit(solution)/shard_map/ppermute | solution.py:19
  17.7 0.0 copy-done.2
  17.7 0.0 collective-permute-start
  17.7 1.0 %collective-permute-start.8 = (bf16[512,128]{1,0:T(8,128)(2,1)S(1)}, bf16[512,128]{1,0:T(8,128)(2,1)S(1)}, u32[]{:S(2)}, u32[]{:S(2)}) collective-permute-start(bf16[512,128]{1,0:T(8,128)(2,1)S(1)} %get-tuple-element.35), channel_id=1, source_target_pairs={{0,4},{4,0},{8,12},{12,8},{1,5},{5,1},{9,13},{13,9},{2,6},{6,2},{1... | collective-permute-start | bytes 393224 | tf_op jit(solution)/shard_map/ppermute | solution.py:19
  18.7 0.3 %collective-permute-start.7 = (bf16[512,128]{1,0:T(8,128)(2,1)S(1)}, bf16[512,128]{1,0:T(8,128)(2,1)S(1)}, u32[]{:S(2)}, u32[]{:S(2)}) collective-permute-start(bf16[512,128]{1,0:T(8,128)(2,1)S(1)} %add_convert_fusion), channel_id=1, source_target_pairs={{0,8},{4,12},{8,0},{12,4},{1,9},{5,13},{9,1},{13,5},{2,10},{6,14},... | collective-permute-start | bytes 393224 | tf_op jit(solution)/shard_map/ppermute | solution.py:19
  19.0 0.0 collective-permute-done.sibling_rank
  19.0 0.6 %collective-permute-done.5.refs_3_ = bf16[32,128]{1,0:T(8,128)(2,1)S(1)} collective-permute-done((bf16[32,128]{1,0:T(8,128)(2,1)S(1)}, bf16[32,128]{1,0:T(8,128)(2,1)S(1)}, u32[]{:S(2)}, u32[]{:S(2)}) %collective-permute-start.5) | collective-permute-done | bytes 8224 | tf_op jit(solution)/shard_map/ppermute | solution.py:19
  19.6 0.0 collective-permute-done.6
  19.6 0.0 copy-done
  19.6 1.1 %expand.1 = (bf16[512,128]{1,0:T(8,128)(2,1)S(1)}, bf16[512,128]{1,0:T(8,128)(2,1)S(1)}) custom-call(s32[1]{0:T(128)} %bitcast.1.batch_at, s32[4]{0:T(128)S(1)} %copy-done.2, s32[4]{0:T(128)S(1)} %collective-permute-done.sibling_rank, bf16[32,1152]{1,0:T(8,128)(2,1)S(1)} %get-tuple-element.32.tagged.refs_0_, ...), custom_call_target="tpu_custom_call" | custom-call | flops 134217728 | bytes 1048576 | tf_op jit(solution)/shard_map/expand/pallas_call | solution.py:365
  20.7 1.6 %collective-permute-start.9 = (bf16[512,128]{1,0:T(8,128)(2,1)S(1)}, bf16[512,128]{1,0:T(8,128)(2,1)S(1)}, u32[]{:S(2)}, u32[]{:S(2)}) collective-permute-start(bf16[512,128]{1,0:T(8,128)(2,1)S(1)} %get-tuple-element.36), channel_id=1, source_target_pairs={{0,2},{1,3},{2,0},{3,1},{4,6},{5,7},{6,4},{7,5},{8,10},{9,11},{10,... | collective-permute-start | bytes 393224 | tf_op jit(solution)/shard_map/ppermute | solution.py:19
  22.3 2.5 %base_terms.5.refs_0_ = f32[512,128]{1,0:T(8,128)S(1)} custom-call(s32[1]{0:T(128)} %bitcast.tensor_at, bf16[32,1152]{1,0:T(8,128)(2,1)S(1)} %get-tuple-element.32.tagged.refs_0_, bf16[1024,8192]{1,0:T(8,128)(2,1)} %out_weight.5), custom_call_target="tpu_custom_call" | custom-call | flops 134217728 | bytes 4194304 | tf_op jit(solution)/shard_map/base_terms/pallas_call | solution.py:246
  24.8 0.0 collective-permute-done.8.refs_3_
  24.8 3.3 %collective-permute-done.7.refs_2_ = bf16[512,128]{1,0:T(8,128)(2,1)S(1)} collective-permute-done((bf16[512,128]{1,0:T(8,128)(2,1)S(1)}, bf16[512,128]{1,0:T(8,128)(2,1)S(1)}, u32[]{:S(2)}, u32[]{:S(2)}) %collective-permute-start.7) | collective-permute-done | bytes 131104 | tf_op jit(solution)/shard_map/ppermute | solution.py:19
  28.0 0.1 partial_total.1.refs_0_
  28.1 0.0 collective-permute-done.9.refs_1_
  28.1 0.7 %total.1 = bf16[32,2048]{1,0:T(8,128)(2,1)} custom-call(f32[512,128]{1,0:T(8,128)S(1)} %partial_total.1.refs_0_, bf16[512,128]{1,0:T(8,128)(2,1)S(1)} %collective-permute-done.9.refs_1_), custom_call_target="tpu_custom_call" | custom-call | flops 131072 | bytes 393216 | tf_op jit(solution)/shard_map/total/pallas_call | solution.py:397
  (2 shorter events, 0.0 us)
Async XLA Ops:
  0.0 19.6 %collective-permute-start.6 = (bf16[4,64,2048]{2,1,0:T(8,128)(2,1)}, bf16[4,64,2048]{2,1,0:T(8,128)(2,1)S(1)}, u32[]{:S(2)}, u32[]{:S(2)}) collective-permute-start(bf16[4,64,2048]{2,1,0:T(8,128)(2,1)} %param.20), channel_id=1, source_target_pairs={{0,1},{1,0},{2,3},{3,2},{4,5},{5,4},{6,7},{7,6},{8,9},{9,8},{10,11... | collective-permute-start | bytes 3145736 | tf_op jit(solution)/shard_map/ppermute | solution.py:19
  0.5 10.4 %collective-permute-start.2 = (bf16[4,64,1024]{2,1,0:T(8,128)(2,1)}, bf16[4,64,1024]{2,1,0:T(8,128)(2,1)S(1)}, u32[]{:S(2)}, u32[]{:S(2)}) collective-permute-start(bf16[4,64,1024]{2,1,0:T(8,128)(2,1)} %bitcast.8), channel_id=1, source_target_pairs={{0,1},{1,0},{2,3},{3,2},{4,5},{5,4},{6,7},{7,6},{8,9},{9,8},{10,11... | collective-permute-start | bytes 1572872 | tf_op jit(solution)/shard_map/ppermute | solution.py:19
  3.4 5.6 %collective-permute-start.1 = (bf16[32,1152]{1,0:T(8,128)(2,1)S(1)}, bf16[32,1152]{1,0:T(8,128)(2,1)S(1)}, u32[]{:S(2)}, u32[]{:S(2)}) collective-permute-start(bf16[32,1152]{1,0:T(8,128)(2,1)S(1)} %get-tuple-element.32.tagged.refs_0_), channel_id=1, source_target_pairs={{0,2},{1,3},{2,0},{3,1},{4,6},{5,7},{6,4},{7,5},{8,10},{9,11},{10,... | collective-permute-start | bytes 221192 | tf_op jit(solution)/shard_map/ppermute | solution.py:19
  6.4 4.4 %copy-start.1 = (bf16[4,1024,64]{1,2,0:T(8,128)(2,1)S(1)}, bf16[4,1024,64]{1,2,0:T(8,128)(2,1)}, u32[]{:S(2)}) copy-start(bf16[4,1024,64]{1,2,0:T(8,128)(2,1)} %param.19) | copy-start | bytes 1572868
  9.0 5.3 %collective-permute-start.4 = (bf16[512,128]{1,0:T(8,128)(2,1)S(1)}, bf16[512,128]{1,0:T(8,128)(2,1)S(1)}, u32[]{:S(2)}, u32[]{:S(2)}) collective-permute-start(bf16[512,128]{1,0:T(8,128)(2,1)S(1)} %get-tuple-element.27), channel_id=1, source_target_pairs={{0,4},{4,0},{8,12},{12,8},{1,5},{5,1},{9,13},{13,9},{2,6},{6,2},{1... | collective-permute-start | bytes 393224 | tf_op jit(solution)/shard_map/ppermute | solution.py:19
  11.3 6.3 %copy-start.2 = (s32[4]{0:T(128)S(1)}, s32[4]{0:T(128)}, u32[]{:S(2)}) copy-start(s32[4]{0:T(128)} %rank.1) | copy-start | bytes 52
  11.3 8.3 %copy-start = (bf16[4,64,2048]{2,1,0:T(8,128)(2,1)S(1)}, bf16[4,64,2048]{2,1,0:T(8,128)(2,1)}, u32[]{:S(2)}) copy-start(bf16[4,64,2048]{2,1,0:T(8,128)(2,1)} %param.20) | copy-start | bytes 3145732
  11.3 3.7 %collective-permute-start.3 = (bf16[32,128]{1,0:T(8,128)(2,1)S(1)}, bf16[32,128]{1,0:T(8,128)(2,1)S(1)}, u32[]{:S(2)}, u32[]{:S(2)}) collective-permute-start(bf16[32,128]{1,0:T(8,128)(2,1)S(1)} %shrink.1), channel_id=1, source_target_pairs={{0,4},{4,0},{8,12},{12,8},{1,5},{5,1},{9,13},{13,9},{2,6},{6,2},{1... | collective-permute-start | bytes 24584 | tf_op jit(solution)/shard_map/ppermute | solution.py:19
  15.1 4.5 %collective-permute-start.5 = (bf16[32,128]{1,0:T(8,128)(2,1)S(1)}, bf16[32,128]{1,0:T(8,128)(2,1)S(1)}, u32[]{:S(2)}, u32[]{:S(2)}) collective-permute-start(bf16[32,128]{1,0:T(8,128)(2,1)S(1)} %add_convert_fusion.1.refs_2_), channel_id=1, source_target_pairs={{0,8},{4,12},{8,0},{12,4},{1,9},{5,13},{9,1},{13,5},{2,10},{6,14},... | collective-permute-start | bytes 24584 | tf_op jit(solution)/shard_map/ppermute | solution.py:19
  17.7 1.4 %collective-permute-start = (s32[4]{0:T(128)S(1)}, s32[4]{0:T(128)S(1)}, u32[]{:S(2)}, u32[]{:S(2)}) collective-permute-start(s32[4]{0:T(128)S(1)} %copy-done.2), channel_id=1, source_target_pairs={{0,1},{1,0},{2,3},{3,2},{4,5},{5,4},{6,7},{7,6},{8,9},{9,8},{10,11... | collective-permute-start | bytes 56 | tf_op jit(solution)/shard_map/ppermute | solution.py:19
  17.7 7.1 %collective-permute-start.8 = (bf16[512,128]{1,0:T(8,128)(2,1)S(1)}, bf16[512,128]{1,0:T(8,128)(2,1)S(1)}, u32[]{:S(2)}, u32[]{:S(2)}) collective-permute-start(bf16[512,128]{1,0:T(8,128)(2,1)S(1)} %get-tuple-element.35), channel_id=1, source_target_pairs={{0,4},{4,0},{8,12},{12,8},{1,5},{5,1},{9,13},{13,9},{2,6},{6,2},{1... | collective-permute-start | bytes 393224 | tf_op jit(solution)/shard_map/ppermute | solution.py:19
  18.7 9.3 %collective-permute-start.7 = (bf16[512,128]{1,0:T(8,128)(2,1)S(1)}, bf16[512,128]{1,0:T(8,128)(2,1)S(1)}, u32[]{:S(2)}, u32[]{:S(2)}) collective-permute-start(bf16[512,128]{1,0:T(8,128)(2,1)S(1)} %add_convert_fusion), channel_id=1, source_target_pairs={{0,8},{4,12},{8,0},{12,4},{1,9},{5,13},{9,1},{13,5},{2,10},{6,14},... | collective-permute-start | bytes 393224 | tf_op jit(solution)/shard_map/ppermute | solution.py:19
  20.7 7.4 %collective-permute-start.9 = (bf16[512,128]{1,0:T(8,128)(2,1)S(1)}, bf16[512,128]{1,0:T(8,128)(2,1)S(1)}, u32[]{:S(2)}, u32[]{:S(2)}) collective-permute-start(bf16[512,128]{1,0:T(8,128)(2,1)S(1)} %get-tuple-element.36), channel_id=1, source_target_pairs={{0,2},{1,3},{2,0},{3,1},{4,6},{5,7},{6,4},{7,5},{8,10},{9,11},{10,... | collective-permute-start | bytes 393224 | tf_op jit(solution)/shard_map/ppermute | solution.py:19

commit v8 on v7

--- a/solution.py
+++ b/solution.py
@@ -27,11 +27,11 @@
     return lax.broadcasted_iota(jnp.int32, shape, len(shape) - 1)
 
 
-def attend_kernel(parts, group_at, early_at, *refs):
-    given, (out_weight, tagged, early, *scratch) = refs[:8], refs[8:]
-    held, (spread_out, small_sems, key_sems, value_sems, early_sem) = scratch[:8], scratch[8:]
+def attend_kernel(parts, rank_width, group_at, early_at, *refs):
+    given, (out_weight, tagged, early, limits, *scratch) = refs[:9], refs[9:]
+    held, (spread_out, small_sems, key_sems, value_sems, early_sem) = scratch[:9], scratch[9:]
     key_cache, value_cache = given[:2]
-    keys, values, queries, new_key, new_value, lengths, row_adapter, adapter_list = held
+    keys, values, queries, new_key, new_value, lengths, row_adapter, adapter_list, ranks = held
     rows, heads, width = queries.shape
     positions = key_cache.shape[2]
     group = group_at[0]
@@ -45,7 +45,7 @@
         )
 
     small = [
-        pltpu.make_async_copy(given[i], held[i], small_sems.at[i - 2]) for i in range(2, 8)
+        pltpu.make_async_copy(given[i], held[i], small_sems.at[i - 2]) for i in range(2, 9)
     ]
     for copy in small:
         copy.start()
@@ -63,6 +63,12 @@
     for row in range(rows):
         tag = jnp.where(at_row == row, adapter_list[row_adapter[row]], tag)
     tag = tag.astype(F32).astype(BF16)
+    slot = lax.broadcasted_iota(jnp.int32, limits.shape, 0) * (LANES // rank_width)
+    slot = slot + lane_of(limits.shape) // rank_width
+    limit = jnp.zeros(limits.shape, jnp.int32)
+    for held_at in range(ranks.shape[0]):
+        limit = jnp.where(slot == held_at, ranks[held_at], limit)
+    limits[...] = limit
 
     group_row = lax.broadcasted_iota(jnp.int32, new_key.shape, 1) == group
     fresh_key = jnp.sum(
@@ -125,6 +131,8 @@
     lengths,
     adapter_list,
     row_adapter,
+    adapter_rank,
+    rank_width,
 ):
     rows, heads, width = queries.shape
     positions = key_cache.shape[2]
@@ -136,14 +144,15 @@
     parts = 2
     smem = pl.BlockSpec(memory_space=pltpu.SMEM)
     away = pl.BlockSpec(memory_space=pl.ANY)
-    tagged, early = pl.pallas_call(
-        functools.partial(attend_kernel, parts),
+    tagged, early, limits = pl.pallas_call(
+        functools.partial(attend_kernel, parts, rank_width),
         out_shape=[
             jax.ShapeDtypeStruct((rows, full * width + LANES), BF16),
             VMEM((out_weight.shape[0], block), BF16),
+            jax.ShapeDtypeStruct((8, LANES), jnp.int32),
         ],
-        in_specs=[smem, smem] + [away] * 9,
-        out_specs=[pl.BlockSpec(memory_space=VMEM)] * 2,
+        in_specs=[smem, smem] + [away] * 10,
+        out_specs=[pl.BlockSpec(memory_space=VMEM)] * 3,
         scratch_shapes=[
             VMEM((rows, positions, width), BF16),
             VMEM((rows, positions, width), BF16),
@@ -153,8 +162,9 @@
             pltpu.SMEM(lengths.shape, jnp.int32),
             pltpu.SMEM(row_adapter.shape, jnp.int32),
             pltpu.SMEM(adapter_list.shape, jnp.int32),
+            pltpu.SMEM(adapter_rank.shape, jnp.int32),
             VMEM((rows * full, width), F32),
-            pltpu.SemaphoreType.DMA((6,)),
+            pltpu.SemaphoreType.DMA((7,)),
             pltpu.SemaphoreType.DMA((parts,)),
             pltpu.SemaphoreType.DMA((parts,)),
             pltpu.SemaphoreType.DMA,
@@ -178,12 +188,13 @@
             lengths,
             row_adapter,
             adapter_list,
+            adapter_rank,
             out_weight,
         ),
     )
     if full != heads:
         tagged = jnp.concatenate([tagged[:, : heads * width], tagged[:, full * width :]], axis=1)
-    return tagged, early
+    return tagged, early, limits
 
 
 def put_stacked(out, start, term, first=0, others=()):
@@ -318,7 +329,8 @@
     )(batch_at, *blocks, *factors)
 
 
-def expand_kernel(count, sums, rank_width, batch_at, rank, sibling_rank, *refs):
+def expand_kernel(count, sums, rank_width, batch_at, *refs):
+    limits, refs = refs[:2], refs[2:]
     tags, parts = refs[:count], refs[count : count + sums]
     factors, outs = refs[count + sums : count + sums + 2], refs[count + sums + 2 :]
     tags = jnp.concatenate([tag[...] for tag in tags], axis=0)
@@ -337,10 +349,10 @@
     tiles = []
     for tile in range(2 * pool // per):
         slot, mine = slots_of(tags, batch_at, pool, tile, per)
-        lane, limit = lane_of(tags.shape) % rank_width, jnp.zeros_like(mine)
-        for n in range(tile * per, (tile + 1) * per):
-            limit = jnp.where(mine == n, (rank, sibling_rank)[n // pool][n % pool], limit)
-        tiles.append(jnp.where((slot == mine) & (lane < limit), shrink, F32(0.0)).astype(BF16))
+        held, at = divmod(tile * per, pool)
+        limit = limits[held][at // per : at // per + 1]
+        keep = (slot == mine) & (lane_of(tags.shape) % rank_width < limit)
+        tiles.append(jnp.where(keep, shrink, F32(0.0)).astype(BF16))
     half = len(tiles) // 2
     spreads = [jnp.concatenate(tiles[:half], axis=1), jnp.concatenate(tiles[half:], axis=1)]
     rows = tags.shape[0] // count
@@ -354,7 +366,7 @@
             put_stacked(out, at, delta[which * rows : (which + 1) * rows])
 
 
-def expand(blocks, parts, factors, ranks, batch_at):
+def expand(blocks, parts, factors, limits, batch_at):
     pool, rank_width, block = factors[0].shape
     rows, tagged_width = blocks[0].shape
     count = len(blocks)
@@ -366,7 +378,8 @@
         functools.partial(expand_kernel, count, len(parts), rank_width),
         grid=(1,),
         out_shape=[jax.ShapeDtypeStruct((stack, LANES), BF16) for _ in blocks],
-        in_specs=[pl.BlockSpec(memory_space=pltpu.SMEM)] * 3
+        in_specs=[pl.BlockSpec(memory_space=pltpu.SMEM)]
+        + [pl.BlockSpec(each.shape, lambda i: (0, 0)) for each in limits]
         + [tag] * count
         + [part] * len(parts)
         + [full] * 2,
@@ -378,7 +391,7 @@
             transcendentals=0,
         ),
         name="expand",
-    )(batch_at, *ranks, *blocks, *parts, *[each.reshape(pool * rank_width, block) for each in factors])
+    )(batch_at, *limits, *blocks, *parts, *[each.reshape(pool * rank_width, block) for each in factors])
 
 
 def total_kernel(*refs):
@@ -417,7 +430,7 @@
     out[...] = total
 
 
-def partial_total(terms):
+def partial_total(terms, weight):
     whole = pl.BlockSpec(memory_space=VMEM)
     return pl.pallas_call(
         partial_kernel,
@@ -427,7 +440,7 @@
         compiler_params=pltpu.CompilerParams(vmem_limit_bytes=8 << 20),
         cost_estimate=pl.CostEstimate(
             flops=terms[0].size * len(terms),
-            bytes_accessed=8 << 20,
+            bytes_accessed=4 * terms[0].size + weight,
             transcendentals=0,
         ),
         name="partial_total",
@@ -469,7 +482,7 @@
         return array.astype(F32)
 
     stack = block // LANES * rows
-    tagged, early = attend(
+    tagged, early, limits = attend(
         tensor_at ^ 3,
         block,
         out_weight,
@@ -481,14 +494,18 @@
         lengths,
         adapter_list,
         row_adapter,
-    )
-    ranks = [adapter_rank, to_sibling(adapter_rank)]
+        adapter_rank,
+        shrink_weight.shape[2],
+    )
+    limits = [limits, to_sibling(limits)]
     shrink_weight = jnp.swapaxes(shrink_weight, 1, 2)
     shrink_factors = [shrink_weight, to_sibling(shrink_weight)]
     expand_factors = [expand_weight, to_sibling(expand_weight)]
     visiting = [to_chip(tagged, shift) for shift in range(1, chips)]
     third, next_door = base_block(tensor_at, tagged, out_weight, block, 1, [early])
-    visiting, third, next_door = lax.optimization_barrier((visiting, third, next_door))
+    visiting, third, next_door, limits = lax.optimization_barrier(
+        (visiting, third, next_door, limits)
+    )
     blocks = [tagged] + visiting
     third = across(third, 1)
 
@@ -501,6 +518,7 @@
     bit = 2
     while bit < tensor_size:
         part = (wide(parts[0]) + wide(parts[1])).astype(BF16)
+        part, next_door = lax.optimization_barrier((part, next_door))
         parts = [part, across(part, bit)]
         bit *= 2
     arrived = [across(second, 2), across(next_door, 1)]
@@ -509,10 +527,11 @@
         (far,) = base_block(tensor_at, tagged, out_weight, block, ahead + 1)
         arrived.append(across((wide(near) + wide(across(far, 1))).astype(BF16), ahead))
 
-    deltas = expand(blocks, parts, expand_factors, ranks, batch_at)
+    deltas = expand(blocks, parts, expand_factors, limits, batch_at)
     deltas, late_tagged = lax.optimization_barrier((deltas, tagged))
     (own,) = base_block(tensor_at, late_tagged, out_weight, block, 0)
-    terms = [partial_total([own, deltas[0], *arrived])]
+    so_far = partial_total([own, deltas[0], arrived[0], *arrived[2:]], 0)
+    terms = [partial_total([so_far, arrived[1]], 8 << 20)]
     terms += [to_chip(home, -shift) for shift, home in enumerate(deltas[1:], 1)]
     return total(rows, block, terms)
 

time: 28.9 us -> 27.1 us (0.938)
  waiting for transfers between devices: 4.7 us -> 2.76 us
  Pallas kernels: 12.8 us -> 12.2 us
  starting transfers between devices: 11.2 us -> 11.8 us
    ppermute x10, waiting for transfers between devices: 4.7 us -> 2.76 us  [permuted(): return lax.ppermute(array, axis, [(i, partner(i)) for i in range(size)])]
    ppermute x10, starting transfers between devices: 11.2 us -> 11.8 us  [permuted(): return lax.ppermute(array, axis, [(i, partner(i)) for i in range(size)])]
    pallas_call x1, Pallas kernels: 1.07 us -> 0.52 us  [expand(): pl.pallas_call(functools.partial(expand_kernel, count, len(parts), rank_w...]
  transfers between devices with their start and end apart: 10 -> 10, of which waited for: 4 -> 2; matrix products, arithmetic and copies ran while one was open for 0% -> 0% of each run, Pallas kernels for 42% -> 43%
where the time goes in v8:
time: 27.1 us; the launch traced here: 27 us
  Pallas kernels  12.2 us (45%)
  starting transfers between devices  11.8 us (44%)
  waiting for transfers between devices  2.76 us (10%)
    ppermute x10, starting transfers between devices, permuted(): return lax.ppermute(array, axis, [(i, partner(i)) for i in range(size)])  11.8 us
    pallas_call x3, Pallas kernels, base_block(): pl.pallas_call(functools.partial(base_kernel, ahead, deep, len(arrived)),...  7.59 us
    pallas_call x1, Pallas kernels, attend(): pl.pallas_call(functools.partial(attend_kernel, parts, rank_width), out_s...  2.85 us
    ppermute x10, waiting for transfers between devices, permuted(): return lax.ppermute(array, axis, [(i, partner(i)) for i in range(size)])  2.76 us
    pallas_call x1, Pallas kernels, total(): pl.pallas_call(total_kernel, out_shape=jax.ShapeDtypeStruct((rows, block)...  0.69 us
  transfers between devices with their start and end apart: 10, of which 2 were waited for; matrix products, arithmetic and copies ran while one was open for 0% of the time, Pallas kernels for 43%

profile of v8, /device:TPU:0, one launch (start us, length us, event | category | flops | bytes accessed | tf_op | source)
XLA Modules:
  0.0 27.0 jit_solution(2470691358549732624)
XLA Ops:
  0.0 0.5 %collective-permute-start.6 = (bf16[4,64,2048]{2,1,0:T(8,128)(2,1)}, bf16[4,64,2048]{2,1,0:T(8,128)(2,1)S(1)}, u32[]{:S(2)}, u32[]{:S(2)}) collective-permute-start(bf16[4,64,2048]{2,1,0:T(8,128)(2,1)} %param.20), channel_id=1, source_target_pairs={{0,1},{1,0},{2,3},{3,2},{4,5},{5,4},{6,7},{7,6},{8,9},{9,8},{10,11... | collective-permute-start | bytes 3145736 | tf_op jit(solution)/shard_map/ppermute | solution.py:19
  0.5 0.1 collective-permute-start.2
  0.5 2.8 %attention.1 = (bf16[32,1152]{1,0:T(8,128)(2,1)S(1)}, bf16[1024,2048]{1,0:T(8,128)(2,1)S(1)}, s32[8,128]{1,0:T(8,128)S(1)}) custom-call(s32[1]{0:T(128)} %bitcast.2.group_at, s32[1]{0:T(128)S(6)} %xor.3.early_at, bf16[32,4,96,128]{3,2,1,0:T(8,128)(2,1)} %refs_0_.1, bf16[32,4,96,128]{3,2,1,0:T(8,128)(2,1)} %refs_1_.1, bf16[32,8,128]{2,1,0:T(8,128)(2,1)} %refs_2_.1, ...), custom_call_target="tpu_custom_call" | custom-call | flops 12582912 | bytes 1572864 | tf_op jit(solution)/shard_map/attention/pallas_call | solution.py:147
  3.4 3.0 %collective-permute-start = (bf16[32,1152]{1,0:T(8,128)(2,1)S(1)}, bf16[32,1152]{1,0:T(8,128)(2,1)S(1)}, u32[]{:S(2)}, u32[]{:S(2)}) collective-permute-start(bf16[32,1152]{1,0:T(8,128)(2,1)S(1)} %get-tuple-element.42.tagged.refs_0_.refs_2_), channel_id=1, source_target_pairs={{0,2},{1,3},{2,0},{3,1},{4,6},{5,7},{6,4},{7,5},{8,10},{9,11},{10,... | collective-permute-start | bytes 221192 | tf_op jit(solution)/shard_map/ppermute | solution.py:19
  6.4 0.0 collective-permute-start.1
  6.4 0.0 copy-start.1
  6.4 2.6 %base_terms.3 = (bf16[512,128]{1,0:T(8,128)(2,1)S(1)}, bf16[512,128]{1,0:T(8,128)(2,1)S(1)}) custom-call(s32[1]{0:T(128)} %bitcast.tensor_at, bf16[32,1152]{1,0:T(8,128)(2,1)S(1)} %get-tuple-element.42.tagged.refs_0_.refs_2_, bf16[1024,8192]{1,0:T(8,128)(2,1)} %out_weight.5, bf16[1024,2048]{1,0:T(8,128)(2,1)S(1)} %get-tuple-element.27.refs_0_), custom_call_target="tpu_custom_call" | custom-call | flops 268435456 | bytes 8388608 | tf_op jit(solution)/shard_map/base_terms/pallas_call | solution.py:257
  9.0 0.0 collective-permute-done.1.refs_1_
  9.0 0.0 collective-permute-done.refs_1_.refs_3_
  9.0 1.8 %collective-permute-start.4 = (bf16[512,128]{1,0:T(8,128)(2,1)S(1)}, bf16[512,128]{1,0:T(8,128)(2,1)S(1)}, u32[]{:S(2)}, u32[]{:S(2)}) collective-permute-start(bf16[512,128]{1,0:T(8,128)(2,1)S(1)} %get-tuple-element.35), channel_id=1, source_target_pairs={{0,4},{4,0},{8,12},{12,8},{1,5},{5,1},{9,13},{13,9},{2,6},{6,2},{1... | collective-permute-start | bytes 393224 | tf_op jit(solution)/shard_map/ppermute | solution.py:19
  10.8 0.0 collective-permute-done.2.refs_3_
  10.8 0.0 copy-done.1
  10.8 0.5 %shrink.1 = bf16[32,128]{1,0:T(8,128)(2,1)S(1)} custom-call(s32[1]{0:T(128)} %bitcast.1.batch_at, bf16[32,1152]{1,0:T(8,128)(2,1)S(1)} %get-tuple-element.42.tagged.refs_0_.refs_2_, bf16[32,1152]{1,0:T(8,128)(2,1)S(1)} %collective-permute-done.refs_1_.refs_3_, bf16[4,64,1024]{2,1,0:T(8,128)(2,1)S(1)} %bitcast.9, ...), custom_call_target="tpu_custom_call" | custom-call | flops 67108864 | bytes 1179648 | tf_op jit(solution)/shard_map/shrink/pallas_call | solution.py:317
  11.3 0.0 copy-start
  11.3 0.3 %collective-permute-start.3 = (bf16[32,128]{1,0:T(8,128)(2,1)S(1)}, bf16[32,128]{1,0:T(8,128)(2,1)S(1)}, u32[]{:S(2)}, u32[]{:S(2)}) collective-permute-start(bf16[32,128]{1,0:T(8,128)(2,1)S(1)} %shrink.1), channel_id=1, source_target_pairs={{0,4},{4,0},{8,12},{12,8},{1,5},{5,1},{9,13},{13,9},{2,6},{6,2},{1... | collective-permute-start | bytes 24584 | tf_op jit(solution)/shard_map/ppermute | solution.py:19
  11.7 2.5 %base_terms.4 = bf16[512,128]{1,0:T(8,128)(2,1)S(1)} custom-call(s32[1]{0:T(128)} %bitcast.tensor_at, bf16[32,1152]{1,0:T(8,128)(2,1)S(1)} %get-tuple-element.42.tagged.refs_0_.refs_2_, bf16[1024,8192]{1,0:T(8,128)(2,1)} %out_weight.5), custom_call_target="tpu_custom_call" | custom-call | flops 134217728 | bytes 4194304 | tf_op jit(solution)/shard_map/base_terms/pallas_call | solution.py:257
  14.2 0.9 %collective-permute-done.4 = bf16[512,128]{1,0:T(8,128)(2,1)S(1)} collective-permute-done((bf16[512,128]{1,0:T(8,128)(2,1)S(1)}, bf16[512,128]{1,0:T(8,128)(2,1)S(1)}, u32[]{:S(2)}, u32[]{:S(2)}) %collective-permute-start.4) | collective-permute-done | bytes 131104 | tf_op jit(solution)/shard_map/ppermute | solution.py:19
  15.1 0.0 collective-permute-done.3
  15.2 2.6 %collective-permute-start.5 = (bf16[32,128]{1,0:T(8,128)(2,1)S(1)}, bf16[32,128]{1,0:T(8,128)(2,1)S(1)}, u32[]{:S(2)}, u32[]{:S(2)}) collective-permute-start(bf16[32,128]{1,0:T(8,128)(2,1)S(1)} %add_convert_fusion.1.refs_4_), channel_id=1, source_target_pairs={{0,8},{4,12},{8,0},{12,4},{1,9},{5,13},{9,1},{13,5},{2,10},{6,14},... | collective-permute-start | bytes 24584 | tf_op jit(solution)/shard_map/ppermute | solution.py:19
  17.8 0.3 %collective-permute-start.7 = (bf16[512,128]{1,0:T(8,128)(2,1)S(1)}, bf16[512,128]{1,0:T(8,128)(2,1)S(1)}, u32[]{:S(2)}, u32[]{:S(2)}) collective-permute-start(bf16[512,128]{1,0:T(8,128)(2,1)S(1)} %add_convert_fusion), channel_id=1, source_target_pairs={{0,8},{4,12},{8,0},{12,4},{1,9},{5,13},{9,1},{13,5},{2,10},{6,14},... | collective-permute-start | bytes 393224 | tf_op jit(solution)/shard_map/ppermute | solution.py:19
  18.1 1.6 %collective-permute-start.8 = (bf16[512,128]{1,0:T(8,128)(2,1)S(1)}, bf16[512,128]{1,0:T(8,128)(2,1)S(1)}, u32[]{:S(2)}, u32[]{:S(2)}) collective-permute-start(bf16[512,128]{1,0:T(8,128)(2,1)S(1)} %get-tuple-element.45), channel_id=1, source_target_pairs={{0,4},{4,0},{8,12},{12,8},{1,5},{5,1},{9,13},{13,9},{2,6},{6,2},{1... | collective-permute-start | bytes 393224 | tf_op jit(solution)/shard_map/ppermute | solution.py:19
  19.7 0.0 collective-permute-done.5.refs_5_
  19.7 0.0 collective-permute-done.6
  19.7 0.0 copy-done
  19.7 0.5 %expand.1 = (bf16[512,128]{1,0:T(8,128)(2,1)S(1)}, bf16[512,128]{1,0:T(8,128)(2,1)S(1)}) custom-call(s32[1]{0:T(128)} %bitcast.1.batch_at, s32[8,128]{1,0:T(8,128)S(1)} %get-tuple-element.31.refs_0_, s32[8,128]{1,0:T(8,128)S(1)} %collective-permute-done.1.refs_1_, bf16[32,1152]{1,0:T(8,128)(2,1)S(1)} %get-tuple-element.42.tagged.refs_0_.refs_2_, ...), custom_call_target="tpu_custom_call" | custom-call | flops 134217728 | bytes 1048576 | tf_op jit(solution)/shard_map/expand/pallas_call | solution.py:377
  20.3 1.6 %collective-permute-start.9 = (bf16[512,128]{1,0:T(8,128)(2,1)S(1)}, bf16[512,128]{1,0:T(8,128)(2,1)S(1)}, u32[]{:S(2)}, u32[]{:S(2)}) collective-permute-start(bf16[512,128]{1,0:T(8,128)(2,1)S(1)} %get-tuple-element.46), channel_id=1, source_target_pairs={{0,2},{1,3},{2,0},{3,1},{4,6},{5,7},{6,4},{7,5},{8,10},{9,11},{10,... | collective-permute-start | bytes 393224 | tf_op jit(solution)/shard_map/ppermute | solution.py:19
  21.9 2.5 %base_terms.5.refs_0_ = f32[512,128]{1,0:T(8,128)S(1)} custom-call(s32[1]{0:T(128)} %bitcast.tensor_at, bf16[32,1152]{1,0:T(8,128)(2,1)S(1)} %get-tuple-element.42.tagged.refs_0_.refs_2_, bf16[1024,8192]{1,0:T(8,128)(2,1)} %out_weight.5), custom_call_target="tpu_custom_call" | custom-call | flops 134217728 | bytes 4194304 | tf_op jit(solution)/shard_map/base_terms/pallas_call | solution.py:257
  24.4 1.8 %collective-permute-done.7.refs_2_ = bf16[512,128]{1,0:T(8,128)(2,1)S(1)} collective-permute-done((bf16[512,128]{1,0:T(8,128)(2,1)S(1)}, bf16[512,128]{1,0:T(8,128)(2,1)S(1)}, u32[]{:S(2)}, u32[]{:S(2)}) %collective-permute-start.7) | collective-permute-done | bytes 131104 | tf_op jit(solution)/shard_map/ppermute | solution.py:19
  26.2 0.0 collective-permute-done.8.refs_1_
  26.3 0.0 collective-permute-done.9.refs_1_
  26.3 0.7 %total.1 = bf16[32,2048]{1,0:T(8,128)(2,1)} custom-call(f32[512,128]{1,0:T(8,128)S(1)} %partial_total.3.refs_0_, bf16[512,128]{1,0:T(8,128)(2,1)S(1)} %collective-permute-done.9.refs_1_), custom_call_target="tpu_custom_call" | custom-call | flops 131072 | bytes 393216 | tf_op jit(solution)/shard_map/total/pallas_call | solution.py:410
  (4 shorter events, 0.1 us)
Async XLA Ops:
  0.0 19.7 %collective-permute-start.6 = (bf16[4,64,2048]{2,1,0:T(8,128)(2,1)}, bf16[4,64,2048]{2,1,0:T(8,128)(2,1)S(1)}, u32[]{:S(2)}, u32[]{:S(2)}) collective-permute-start(bf16[4,64,2048]{2,1,0:T(8,128)(2,1)} %param.20), channel_id=1, source_target_pairs={{0,1},{1,0},{2,3},{3,2},{4,5},{5,4},{6,7},{7,6},{8,9},{9,8},{10,11... | collective-permute-start | bytes 3145736 | tf_op jit(solution)/shard_map/ppermute | solution.py:19
  0.5 10.4 %collective-permute-start.2 = (bf16[4,64,1024]{2,1,0:T(8,128)(2,1)}, bf16[4,64,1024]{2,1,0:T(8,128)(2,1)S(1)}, u32[]{:S(2)}, u32[]{:S(2)}) collective-permute-start(bf16[4,64,1024]{2,1,0:T(8,128)(2,1)} %bitcast.8), channel_id=1, source_target_pairs={{0,1},{1,0},{2,3},{3,2},{4,5},{5,4},{6,7},{7,6},{8,9},{9,8},{10,11... | collective-permute-start | bytes 1572872 | tf_op jit(solution)/shard_map/ppermute | solution.py:19
  3.4 5.6 %collective-permute-start = (bf16[32,1152]{1,0:T(8,128)(2,1)S(1)}, bf16[32,1152]{1,0:T(8,128)(2,1)S(1)}, u32[]{:S(2)}, u32[]{:S(2)}) collective-permute-start(bf16[32,1152]{1,0:T(8,128)(2,1)S(1)} %get-tuple-element.42.tagged.refs_0_.refs_2_), channel_id=1, source_target_pairs={{0,2},{1,3},{2,0},{3,1},{4,6},{5,7},{6,4},{7,5},{8,10},{9,11},{10,... | collective-permute-start | bytes 221192 | tf_op jit(solution)/shard_map/ppermute | solution.py:19
  6.4 2.6 %collective-permute-start.1 = (s32[8,128]{1,0:T(8,128)S(1)}, s32[8,128]{1,0:T(8,128)S(1)}, u32[]{:S(2)}, u32[]{:S(2)}) collective-permute-start(s32[8,128]{1,0:T(8,128)S(1)} %get-tuple-element.31.refs_0_), channel_id=1, source_target_pairs={{0,1},{1,0},{2,3},{3,2},{4,5},{5,4},{6,7},{7,6},{8,9},{9,8},{10,11... | collective-permute-start | bytes 12296 | tf_op jit(solution)/shard_map/ppermute | solution.py:19
  6.4 4.4 %copy-start.1 = (bf16[4,1024,64]{1,2,0:T(8,128)(2,1)S(1)}, bf16[4,1024,64]{1,2,0:T(8,128)(2,1)}, u32[]{:S(2)}) copy-start(bf16[4,1024,64]{1,2,0:T(8,128)(2,1)} %param.19) | copy-start | bytes 1572868
  9.0 6.1 %collective-permute-start.4 = (bf16[512,128]{1,0:T(8,128)(2,1)S(1)}, bf16[512,128]{1,0:T(8,128)(2,1)S(1)}, u32[]{:S(2)}, u32[]{:S(2)}) collective-permute-start(bf16[512,128]{1,0:T(8,128)(2,1)S(1)} %get-tuple-element.35), channel_id=1, source_target_pairs={{0,4},{4,0},{8,12},{12,8},{1,5},{5,1},{9,13},{13,9},{2,6},{6,2},{1... | collective-permute-start | bytes 393224 | tf_op jit(solution)/shard_map/ppermute | solution.py:19
  11.3 8.4 %copy-start = (bf16[4,64,2048]{2,1,0:T(8,128)(2,1)S(1)}, bf16[4,64,2048]{2,1,0:T(8,128)(2,1)}, u32[]{:S(2)}) copy-start(bf16[4,64,2048]{2,1,0:T(8,128)(2,1)} %param.20) | copy-start | bytes 3145732
  11.3 3.8 %collective-permute-start.3 = (bf16[32,128]{1,0:T(8,128)(2,1)S(1)}, bf16[32,128]{1,0:T(8,128)(2,1)S(1)}, u32[]{:S(2)}, u32[]{:S(2)}) collective-permute-start(bf16[32,128]{1,0:T(8,128)(2,1)S(1)} %shrink.1), channel_id=1, source_target_pairs={{0,4},{4,0},{8,12},{12,8},{1,5},{5,1},{9,13},{13,9},{2,6},{6,2},{1... | collective-permute-start | bytes 24584 | tf_op jit(solution)/shard_map/ppermute | solution.py:19
  15.2 4.6 %collective-permute-start.5 = (bf16[32,128]{1,0:T(8,128)(2,1)S(1)}, bf16[32,128]{1,0:T(8,128)(2,1)S(1)}, u32[]{:S(2)}, u32[]{:S(2)}) collective-permute-start(bf16[32,128]{1,0:T(8,128)(2,1)S(1)} %add_convert_fusion.1.refs_4_), channel_id=1, source_target_pairs={{0,8},{4,12},{8,0},{12,4},{1,9},{5,13},{9,1},{13,5},{2,10},{6,14},... | collective-permute-start | bytes 24584 | tf_op jit(solution)/shard_map/ppermute | solution.py:19
  17.8 8.4 %collective-permute-start.7 = (bf16[512,128]{1,0:T(8,128)(2,1)S(1)}, bf16[512,128]{1,0:T(8,128)(2,1)S(1)}, u32[]{:S(2)}, u32[]{:S(2)}) collective-permute-start(bf16[512,128]{1,0:T(8,128)(2,1)S(1)} %add_convert_fusion), channel_id=1, source_target_pairs={{0,8},{4,12},{8,0},{12,4},{1,9},{5,13},{9,1},{13,5},{2,10},{6,14},... | collective-permute-start | bytes 393224 | tf_op jit(solution)/shard_map/ppermute | solution.py:19
  18.1 8.1 %collective-permute-start.8 = (bf16[512,128]{1,0:T(8,128)(2,1)S(1)}, bf16[512,128]{1,0:T(8,128)(2,1)S(1)}, u32[]{:S(2)}, u32[]{:S(2)}) collective-permute-start(bf16[512,128]{1,0:T(8,128)(2,1)S(1)} %get-tuple-element.45), channel_id=1, source_target_pairs={{0,4},{4,0},{8,12},{12,8},{1,5},{5,1},{9,13},{13,9},{2,6},{6,2},{1... | collective-permute-start | bytes 393224 | tf_op jit(solution)/shard_map/ppermute | solution.py:19
  20.3 6.0 %collective-permute-start.9 = (bf16[512,128]{1,0:T(8,128)(2,1)S(1)}, bf16[512,128]{1,0:T(8,128)(2,1)S(1)}, u32[]{:S(2)}, u32[]{:S(2)}) collective-permute-start(bf16[512,128]{1,0:T(8,128)(2,1)S(1)} %get-tuple-element.46), channel_id=1, source_target_pairs={{0,2},{1,3},{2,0},{3,1},{4,6},{5,7},{6,4},{7,5},{8,10},{9,11},{10,... | collective-permute-start | bytes 393224 | tf_op jit(solution)/shard_map/ppermute | solution.py:19

commit v9 on v7

--- a/solution.py
+++ b/solution.py
@@ -28,10 +28,10 @@
 
 
 def attend_kernel(parts, group_at, early_at, *refs):
-    given, (out_weight, tagged, early, *scratch) = refs[:8], refs[8:]
-    held, (spread_out, small_sems, key_sems, value_sems, early_sem) = scratch[:8], scratch[8:]
+    given, (out_weight, tagged, early, kept_factors, *scratch) = refs[:10], refs[10:]
+    held, (spread_out, small_sems, key_sems, value_sems, early_sem) = scratch[:10], scratch[10:]
     key_cache, value_cache = given[:2]
-    keys, values, queries, new_key, new_value, lengths, row_adapter, adapter_list = held
+    keys, values, queries, new_key, new_value, lengths, row_adapter, adapter_list, ranks, factors = held
     rows, heads, width = queries.shape
     positions = key_cache.shape[2]
     group = group_at[0]
@@ -45,16 +45,20 @@
         )
 
     small = [
-        pltpu.make_async_copy(given[i], held[i], small_sems.at[i - 2]) for i in range(2, 8)
+        pltpu.make_async_copy(given[i], held[i], small_sems.at[i - 2]) for i in range(2, 10)
     ]
+    factors_copy = small.pop()
     for copy in small:
         copy.start()
     for part in range(parts):
         for copy in cache_copies(part):
             copy.start()
-    block = early.shape[1]
+    early_rows, block = early.shape
     start = pl.multiple_of(early_at[0] * block, block)
-    early_copy = pltpu.make_async_copy(out_weight.at[:, pl.ds(start, block)], early, early_sem)
+    early_copy = pltpu.make_async_copy(
+        out_weight.at[pl.ds(0, early_rows), pl.ds(start, block)], early, early_sem
+    )
+    factors_copy.start()
     early_copy.start()
     for copy in small:
         copy.wait()
@@ -63,7 +67,6 @@
     for row in range(rows):
         tag = jnp.where(at_row == row, adapter_list[row_adapter[row]], tag)
     tag = tag.astype(F32).astype(BF16)
-
     group_row = lax.broadcasted_iota(jnp.int32, new_key.shape, 1) == group
     fresh_key = jnp.sum(
         jnp.where(group_row, new_key[...].astype(F32), F32(0.0)), axis=1, keepdims=True
@@ -110,6 +113,12 @@
         tagged[:, head * width : (head + 1) * width] = spread_out[
             pl.ds(head, rows, stride=heads)
         ].astype(BF16)
+    factors_copy.wait()
+    for held_at in range(factors.shape[0]):
+        factor = factors[held_at].astype(F32)
+        column = lax.broadcasted_iota(jnp.int32, factor.shape, 0)
+        kept = jnp.where(column < ranks[held_at], factor, F32(0.0))
+        kept_factors[held_at] = kept.astype(kept_factors.dtype)
     early_copy.wait()
 
 
@@ -125,6 +134,8 @@
     lengths,
     adapter_list,
     row_adapter,
+    adapter_rank,
+    factors,
 ):
     rows, heads, width = queries.shape
     positions = key_cache.shape[2]
@@ -133,17 +144,18 @@
     full = -(-heads // 8) * 8
     if full != heads:
         queries = jnp.pad(queries, ((0, 0), (0, full - heads), (0, 0)))
-    parts = 2
+    parts = 4
     smem = pl.BlockSpec(memory_space=pltpu.SMEM)
     away = pl.BlockSpec(memory_space=pl.ANY)
-    tagged, early = pl.pallas_call(
+    tagged, early, masked = pl.pallas_call(
         functools.partial(attend_kernel, parts),
         out_shape=[
             jax.ShapeDtypeStruct((rows, full * width + LANES), BF16),
-            VMEM((out_weight.shape[0], block), BF16),
+            VMEM((out_weight.shape[0] // 2, block), BF16),
+            VMEM(factors.shape, BF16),
         ],
-        in_specs=[smem, smem] + [away] * 9,
-        out_specs=[pl.BlockSpec(memory_space=VMEM)] * 2,
+        in_specs=[smem, smem] + [away] * 11,
+        out_specs=[pl.BlockSpec(memory_space=VMEM)] * 3,
         scratch_shapes=[
             VMEM((rows, positions, width), BF16),
             VMEM((rows, positions, width), BF16),
@@ -153,13 +165,15 @@
             pltpu.SMEM(lengths.shape, jnp.int32),
             pltpu.SMEM(row_adapter.shape, jnp.int32),
             pltpu.SMEM(adapter_list.shape, jnp.int32),
+            pltpu.SMEM(adapter_rank.shape, jnp.int32),
+            VMEM(factors.shape, BF16),
             VMEM((rows * full, width), F32),
-            pltpu.SemaphoreType.DMA((6,)),
+            pltpu.SemaphoreType.DMA((8,)),
             pltpu.SemaphoreType.DMA((parts,)),
             pltpu.SemaphoreType.DMA((parts,)),
             pltpu.SemaphoreType.DMA,
         ],
-        compiler_params=pltpu.CompilerParams(vmem_limit_bytes=8 << 20),
+        compiler_params=pltpu.CompilerParams(vmem_limit_bytes=12 << 20),
         cost_estimate=pl.CostEstimate(
             flops=4 * rows * heads * positions * width,
             bytes_accessed=4 * rows * positions * width,
@@ -178,12 +192,14 @@
             lengths,
             row_adapter,
             adapter_list,
+            adapter_rank,
+            factors,
             out_weight,
         ),
     )
     if full != heads:
         tagged = jnp.concatenate([tagged[:, : heads * width], tagged[:, full * width :]], axis=1)
-    return tagged, early
+    return tagged, early, masked
 
 
 def put_stacked(out, start, term, first=0, others=()):
@@ -196,59 +212,69 @@
         out[at : at + rows] = part.astype(out.dtype)
 
 
-def base_kernel(ahead, deep, arriving, tensor_at, tagged, out_weight, *refs):
-    arrived, (*near, out, held, sums, sems) = refs[:arriving], refs[arriving:]
+def base_kernel(aheads, early_rows, deep, tensor_at, tagged, out_weight, *refs):
+    early = refs[0] if early_rows else None
+    outs, (held, sums, sems) = refs[bool(early_rows) : -3], refs[-3:]
     _, deep_rows, block = held.shape
     width = out_weight.shape[0]
-    count = width // deep_rows
-    column = pl.ds(pl.multiple_of((tensor_at[0] ^ ahead) * block, block), block)
+    pieces = [
+        (which, row)
+        for which in range(len(aheads))
+        for row in range(0 if which else early_rows, width, deep_rows)
+    ]
 
     def copy(at):
+        which, row = pieces[at]
+        start = pl.multiple_of((tensor_at[0] ^ aheads[which]) * block, block)
         return pltpu.make_async_copy(
-            out_weight.at[pl.ds(at * deep_rows, deep_rows), column],
+            out_weight.at[pl.ds(row, deep_rows), pl.ds(start, block)],
             held.at[at % deep],
             sems.at[at % deep],
         )
 
-    for at in range(min(deep, count)):
+    for at in range(min(deep, len(pieces))):
         copy(at).start()
     piece = min(block, 512)
-    if near:
-        early, early_out = near
+    if early_rows:
         for start in range(0, block, piece):
             columns = slice(start, start + piece)
-            term = jnp.dot(tagged[:, :width], early[:, columns], preferred_element_type=F32)
-            put_stacked(early_out, start, term)
-    for at in range(count):
+            sums[:, columns] = jnp.dot(
+                tagged[:, :early_rows], early[:, columns], preferred_element_type=F32
+            )
+    for at, (which, row) in enumerate(pieces):
         copy(at).wait()
-        inputs = slice(at * deep_rows, (at + 1) * deep_rows)
         for start in range(0, block, piece):
             columns = slice(start, start + piece)
             term = jnp.dot(
-                tagged[:, inputs], held[at % deep, :, columns], preferred_element_type=F32
+                tagged[:, row : row + deep_rows],
+                held[at % deep, :, columns],
+                preferred_element_type=F32,
             )
-            if at:
+            if row:
                 term = term + sums[:, columns]
-            if at < count - 1:
+            if row + deep_rows < width:
                 sums[:, columns] = term
             else:
-                put_stacked(out, start, term, 0, arrived)
-        if at + deep < count:
+                put_stacked(outs[which], start, term)
+        if at + deep < len(pieces):
             copy(at + deep).start()
 
 
-def base_block(tensor_at, tagged, out_weight, block, ahead, early=(), arrived=()):
+def base_terms(tensor_at, tagged, out_weight, block, aheads, early=None):
     rows = tagged.shape[0]
     width = out_weight.shape[0]
-    deep, deep_rows = 4, min(width, 256)
+    deep, deep_rows = 4, min(width // 2, 256)
+    early_rows = 0 if early is None else early.shape[0]
     whole = pl.BlockSpec(memory_space=VMEM)
-    count = 1 + len(early)
+    count = len(aheads)
     return pl.pallas_call(
-        functools.partial(base_kernel, ahead, deep, len(arrived)),
-        out_shape=[jax.ShapeDtypeStruct((block // LANES * rows, LANES), BF16 if ahead else F32)]
-        * count,
+        functools.partial(base_kernel, aheads, early_rows, deep),
+        out_shape=[
+            jax.ShapeDtypeStruct((block // LANES * rows, LANES), BF16 if ahead else F32)
+            for ahead in aheads
+        ],
         in_specs=[pl.BlockSpec(memory_space=pltpu.SMEM), whole, pl.BlockSpec(memory_space=pl.ANY)]
-        + [whole] * (len(arrived) + len(early)),
+        + [whole] * bool(early_rows),
         out_specs=[whole] * count,
         scratch_shapes=[
             VMEM((deep, deep_rows, block), BF16),
@@ -258,11 +284,11 @@
         compiler_params=pltpu.CompilerParams(vmem_limit_bytes=12 << 20),
         cost_estimate=pl.CostEstimate(
             flops=2 * rows * width * block * count,
-            bytes_accessed=2 * width * block * (2 if arrived else count),
+            bytes_accessed=2 * width * block * count,
             transcendentals=0,
         ),
         name="base_terms",
-    )(tensor_at, tagged, *in_hbm(out_weight), *arrived, *early)
+    )(tensor_at, tagged, *in_hbm(out_weight), *([early] if early_rows else []))
 
 
 def slots_of(tags, batch_at, pool, tile, per):
@@ -318,7 +344,7 @@
     )(batch_at, *blocks, *factors)
 
 
-def expand_kernel(count, sums, rank_width, batch_at, rank, sibling_rank, *refs):
+def expand_kernel(count, sums, rank_width, batch_at, *refs):
     tags, parts = refs[:count], refs[count : count + sums]
     factors, outs = refs[count + sums : count + sums + 2], refs[count + sums + 2 :]
     tags = jnp.concatenate([tag[...] for tag in tags], axis=0)
@@ -337,10 +363,7 @@
     tiles = []
     for tile in range(2 * pool // per):
         slot, mine = slots_of(tags, batch_at, pool, tile, per)
-        lane, limit = lane_of(tags.shape) % rank_width, jnp.zeros_like(mine)
-        for n in range(tile * per, (tile + 1) * per):
-            limit = jnp.where(mine == n, (rank, sibling_rank)[n // pool][n % pool], limit)
-        tiles.append(jnp.where((slot == mine) & (lane < limit), shrink, F32(0.0)).astype(BF16))
+        tiles.append(jnp.where(slot == mine, shrink, F32(0.0)).astype(BF16))
     half = len(tiles) // 2
     spreads = [jnp.concatenate(tiles[:half], axis=1), jnp.concatenate(tiles[half:], axis=1)]
     rows = tags.shape[0] // count
@@ -354,7 +377,7 @@
             put_stacked(out, at, delta[which * rows : (which + 1) * rows])
 
 
-def expand(blocks, parts, factors, ranks, batch_at):
+def expand(blocks, parts, factors, batch_at):
     pool, rank_width, block = factors[0].shape
     rows, tagged_width = blocks[0].shape
     count = len(blocks)
@@ -366,7 +389,7 @@
         functools.partial(expand_kernel, count, len(parts), rank_width),
         grid=(1,),
         out_shape=[jax.ShapeDtypeStruct((stack, LANES), BF16) for _ in blocks],
-        in_specs=[pl.BlockSpec(memory_space=pltpu.SMEM)] * 3
+        in_specs=[pl.BlockSpec(memory_space=pltpu.SMEM)]
         + [tag] * count
         + [part] * len(parts)
         + [full] * 2,
@@ -378,7 +401,7 @@
             transcendentals=0,
         ),
         name="expand",
-    )(batch_at, *ranks, *blocks, *parts, *[each.reshape(pool * rank_width, block) for each in factors])
+    )(batch_at, *blocks, *parts, *[each.reshape(pool * rank_width, block) for each in factors])
 
 
 def total_kernel(*refs):
@@ -417,7 +440,7 @@
     out[...] = total
 
 
-def partial_total(terms):
+def partial_total(terms, weight):
     whole = pl.BlockSpec(memory_space=VMEM)
     return pl.pallas_call(
         partial_kernel,
@@ -427,7 +450,7 @@
         compiler_params=pltpu.CompilerParams(vmem_limit_bytes=8 << 20),
         cost_estimate=pl.CostEstimate(
             flops=terms[0].size * len(terms),
-            bytes_accessed=8 << 20,
+            bytes_accessed=4 * terms[0].size + weight,
             transcendentals=0,
         ),
         name="partial_total",
@@ -469,7 +492,7 @@
         return array.astype(F32)
 
     stack = block // LANES * rows
-    tagged, early = attend(
+    tagged, early, masked = attend(
         tensor_at ^ 3,
         block,
         out_weight,
@@ -481,13 +504,13 @@
         lengths,
         adapter_list,
         row_adapter,
-    )
-    ranks = [adapter_rank, to_sibling(adapter_rank)]
-    shrink_weight = jnp.swapaxes(shrink_weight, 1, 2)
-    shrink_factors = [shrink_weight, to_sibling(shrink_weight)]
+        adapter_rank,
+        jnp.swapaxes(shrink_weight, 1, 2),
+    )
+    shrink_factors = [masked, to_sibling(masked)]
     expand_factors = [expand_weight, to_sibling(expand_weight)]
     visiting = [to_chip(tagged, shift) for shift in range(1, chips)]
-    third, next_door = base_block(tensor_at, tagged, out_weight, block, 1, [early])
+    third, next_door = base_terms(tensor_at, tagged, out_weight, block, [3, 1], early)
     visiting, third, next_door = lax.optimization_barrier((visiting, third, next_door))
     blocks = [tagged] + visiting
     third = across(third, 1)
@@ -495,24 +518,25 @@
     part = shrink_part(blocks, shrink_factors, batch_at)
     parts = [part, across(part, 1)]
     part, later_tagged = lax.optimization_barrier((part, tagged))
-    (second,) = base_block(tensor_at, later_tagged, out_weight, block, 2)
+    (second,) = base_terms(tensor_at, later_tagged, out_weight, block, [2])
     second = (wide(second) + wide(third)).astype(BF16)
     parts, second = lax.optimization_barrier((parts, second))
     bit = 2
     while bit < tensor_size:
         part = (wide(parts[0]) + wide(parts[1])).astype(BF16)
+        part, next_door = lax.optimization_barrier((part, next_door))
         parts = [part, across(part, bit)]
         bit *= 2
     arrived = [across(second, 2), across(next_door, 1)]
     for ahead in range(4, tensor_size, 2):
-        (near,) = base_block(tensor_at, tagged, out_weight, block, ahead)
-        (far,) = base_block(tensor_at, tagged, out_weight, block, ahead + 1)
+        near, far = base_terms(tensor_at, tagged, out_weight, block, [ahead, ahead + 1])
         arrived.append(across((wide(near) + wide(across(far, 1))).astype(BF16), ahead))
 
-    deltas = expand(blocks, parts, expand_factors, ranks, batch_at)
+    deltas = expand(blocks, parts, expand_factors, batch_at)
     deltas, late_tagged = lax.optimization_barrier((deltas, tagged))
-    (own,) = base_block(tensor_at, late_tagged, out_weight, block, 0)
-    terms = [partial_total([own, deltas[0], *arrived])]
+    (own,) = base_terms(tensor_at, late_tagged, out_weight, block, [0])
+    so_far = partial_total([own, deltas[0], arrived[0], *arrived[2:]], 0)
+    terms = [partial_total([so_far, arrived[1]], 8 << 20)]
     terms += [to_chip(home, -shift) for shift, home in enumerate(deltas[1:], 1)]
     return total(rows, block, terms)
 

time: 28.9 us -> 27.6 us (0.955)
  waiting for transfers between devices: 4.7 us -> 2.78 us
  Pallas kernels: 12.8 us -> 13.8 us
  starting transfers between devices: 11.2 us -> 10.8 us
    ppermute x10 -> x9, waiting for transfers between devices: 4.7 us -> 2.78 us  [permuted(): return lax.ppermute(array, axis, [(i, partner(i)) for i in range(size)])]
    pallas_call x3, Pallas kernels: 7.59 us -> 8.42 us  [base_terms(): pl.pallas_call(functools.partial(base_kernel, aheads, early_rows, deep),...]
    pallas_call x1, Pallas kernels: 2.84 us -> 3.53 us  [attend(): pl.pallas_call(functools.partial(attend_kernel, parts), out_shape=[jax.Sh...]
    pallas_call x1, Pallas kernels: 1.07 us -> 0.52 us  [expand(): pl.pallas_call(functools.partial(expand_kernel, count, len(parts), rank_w...]
    ppermute x10 -> x9, starting transfers between devices: 11.2 us -> 10.8 us  [permuted(): return lax.ppermute(array, axis, [(i, partner(i)) for i in range(size)])]
  transfers between devices with their start and end apart: 10 -> 9, of which waited for: 4 -> 4; matrix products, arithmetic and copies ran while one was open for 0% -> 0% of each run, Pallas kernels for 42% -> 48%
where the time goes in v9:
time: 27.6 us; the launch traced here: 27.4 us
  Pallas kernels  13.8 us (50%)
  starting transfers between devices  10.8 us (39%)
  waiting for transfers between devices  2.78 us (10%)
    ppermute x9, starting transfers between devices, permuted(): return lax.ppermute(array, axis, [(i, partner(i)) for i in range(size)])  10.8 us
    pallas_call x3, Pallas kernels, base_terms(): pl.pallas_call(functools.partial(base_kernel, aheads, early_rows, deep),...  8.42 us
    pallas_call x1, Pallas kernels, attend(): pl.pallas_call(functools.partial(attend_kernel, parts), out_shape=[jax.Sh...  3.53 us
    ppermute x9, waiting for transfers between devices, permuted(): return lax.ppermute(array, axis, [(i, partner(i)) for i in range(size)])  2.78 us
    pallas_call x1, Pallas kernels, total(): pl.pallas_call(total_kernel, out_shape=jax.ShapeDtypeStruct((rows, block)...  0.69 us
  transfers between devices with their start and end apart: 9, of which 4 were waited for; matrix products, arithmetic and copies ran while one was open for 0% of the time, Pallas kernels for 48%

profile of v9, /device:TPU:0, one launch (start us, length us, event | category | flops | bytes accessed | tf_op | source)
XLA Modules:
  0.0 27.4 jit_solution(8097777196243715561)
XLA Ops:
  0.0 0.5 %collective-permute-start.5 = (bf16[4,64,2048]{2,1,0:T(8,128)(2,1)}, bf16[4,64,2048]{2,1,0:T(8,128)(2,1)S(1)}, u32[]{:S(2)}, u32[]{:S(2)}) collective-permute-start(bf16[4,64,2048]{2,1,0:T(8,128)(2,1)} %param.20), channel_id=1, source_target_pairs={{0,1},{1,0},{2,3},{3,2},{4,5},{5,4},{6,7},{7,6},{8,9},{9,8},{10,11... | collective-permute-start | bytes 3145736 | tf_op jit(solution)/shard_map/ppermute | solution.py:19
  0.5 3.5 %attention.1 = (bf16[32,1152]{1,0:T(8,128)(2,1)S(1)}, bf16[512,2048]{1,0:T(8,128)(2,1)S(1)}, bf16[4,64,1024]{2,1,0:T(8,128)(2,1)S(1)}) custom-call(s32[1]{0:T(128)} %bitcast.2.group_at, s32[1]{0:T(128)S(6)} %xor.3.early_at, bf16[32,4,96,128]{3,2,1,0:T(8,128)(2,1)} %refs_0_.1, bf16[32,4,96,128]{3,2,1,0:T(8,128)(2,1)} %refs_1_.1, bf16[32,8,128]{2,1,0:T(8,128)(2,1)} %refs_2_.1, ...), custom_call_target="tpu_custom_call" | custom-call | flops 12582912 | bytes 1572864 | tf_op jit(solution)/shard_map/attention/pallas_call | solution.py:150
  4.0 0.1 collective-permute-start.1
  4.1 2.9 %collective-permute-start = (bf16[32,1152]{1,0:T(8,128)(2,1)S(1)}, bf16[32,1152]{1,0:T(8,128)(2,1)S(1)}, u32[]{:S(2)}, u32[]{:S(2)}) collective-permute-start(bf16[32,1152]{1,0:T(8,128)(2,1)S(1)} %get-tuple-element.38.tagged.refs_0_), channel_id=1, source_target_pairs={{0,2},{1,3},{2,0},{3,1},{4,6},{5,7},{6,4},{7,5},{8,10},{9,11},{10,... | collective-permute-start | bytes 221192 | tf_op jit(solution)/shard_map/ppermute | solution.py:19
  7.1 3.4 %base_terms.3 = (bf16[512,128]{1,0:T(8,128)(2,1)S(1)}, bf16[512,128]{1,0:T(8,128)(2,1)S(1)}) custom-call(s32[1]{0:T(128)} %bitcast.tensor_at, bf16[32,1152]{1,0:T(8,128)(2,1)S(1)} %get-tuple-element.38.tagged.refs_0_, bf16[1024,8192]{1,0:T(8,128)(2,1)} %out_weight.5, bf16[512,2048]{1,0:T(8,128)(2,1)S(1)} %get-tuple-element.25.refs_0_), custom_call_target="tpu_custom_call" | custom-call | flops 268435456 | bytes 8388608 | tf_op jit(solution)/shard_map/base_terms/pallas_call | solution.py:270
  10.5 0.0 collective-permute-done.refs_1_
  10.5 1.6 %collective-permute-start.3 = (bf16[512,128]{1,0:T(8,128)(2,1)S(1)}, bf16[512,128]{1,0:T(8,128)(2,1)S(1)}, u32[]{:S(2)}, u32[]{:S(2)}) collective-permute-start(bf16[512,128]{1,0:T(8,128)(2,1)S(1)} %get-tuple-element.31), channel_id=1, source_target_pairs={{0,4},{4,0},{8,12},{12,8},{1,5},{5,1},{9,13},{13,9},{2,6},{6,2},{1... | collective-permute-start | bytes 393224 | tf_op jit(solution)/shard_map/ppermute | solution.py:19
  12.1 0.0 collective-permute-done.1.refs_3_
  12.1 0.5 %shrink.1 = bf16[32,128]{1,0:T(8,128)(2,1)S(1)} custom-call(s32[1]{0:T(128)} %bitcast.1.batch_at, bf16[32,1152]{1,0:T(8,128)(2,1)S(1)} %get-tuple-element.38.tagged.refs_0_, bf16[32,1152]{1,0:T(8,128)(2,1)S(1)} %collective-permute-done.refs_1_, bf16[4,64,1024]{2,1,0:T(8,128)(2,1)S(1)} %get-tuple-element.29.refs_2_, ...), custom_call_target="tpu_custom_call" | custom-call | flops 67108864 | bytes 1179648 | tf_op jit(solution)/shard_map/shrink/pallas_call | solution.py:332
  12.6 0.0 copy-start
  12.6 0.5 %collective-permute-start.2 = (bf16[32,128]{1,0:T(8,128)(2,1)S(1)}, bf16[32,128]{1,0:T(8,128)(2,1)S(1)}, u32[]{:S(2)}, u32[]{:S(2)}) collective-permute-start(bf16[32,128]{1,0:T(8,128)(2,1)S(1)} %shrink.1), channel_id=1, source_target_pairs={{0,4},{4,0},{8,12},{12,8},{1,5},{5,1},{9,13},{13,9},{2,6},{6,2},{1... | collective-permute-start | bytes 24584 | tf_op jit(solution)/shard_map/ppermute | solution.py:19
  13.2 2.5 %base_terms.4 = bf16[512,128]{1,0:T(8,128)(2,1)S(1)} custom-call(s32[1]{0:T(128)} %bitcast.tensor_at, bf16[32,1152]{1,0:T(8,128)(2,1)S(1)} %get-tuple-element.38.tagged.refs_0_, bf16[1024,8192]{1,0:T(8,128)(2,1)} %out_weight.5), custom_call_target="tpu_custom_call" | custom-call | flops 134217728 | bytes 4194304 | tf_op jit(solution)/shard_map/base_terms/pallas_call | solution.py:270
  15.7 0.2 collective-permute-done.3
  15.9 0.5 %collective-permute-done.2 = bf16[32,128]{1,0:T(8,128)(2,1)S(1)} collective-permute-done((bf16[32,128]{1,0:T(8,128)(2,1)S(1)}, bf16[32,128]{1,0:T(8,128)(2,1)S(1)}, u32[]{:S(2)}, u32[]{:S(2)}) %collective-permute-start.2) | collective-permute-done | bytes 8224 | tf_op jit(solution)/shard_map/ppermute | solution.py:19
  16.4 2.6 %collective-permute-start.4 = (bf16[32,128]{1,0:T(8,128)(2,1)S(1)}, bf16[32,128]{1,0:T(8,128)(2,1)S(1)}, u32[]{:S(2)}, u32[]{:S(2)}) collective-permute-start(bf16[32,128]{1,0:T(8,128)(2,1)S(1)} %add_convert_fusion.1.refs_2_), channel_id=1, source_target_pairs={{0,8},{4,12},{8,0},{12,4},{1,9},{5,13},{9,1},{13,5},{2,10},{6,14},... | collective-permute-start | bytes 24584 | tf_op jit(solution)/shard_map/ppermute | solution.py:19
  19.0 0.3 %collective-permute-start.6 = (bf16[512,128]{1,0:T(8,128)(2,1)S(1)}, bf16[512,128]{1,0:T(8,128)(2,1)S(1)}, u32[]{:S(2)}, u32[]{:S(2)}) collective-permute-start(bf16[512,128]{1,0:T(8,128)(2,1)S(1)} %add_convert_fusion), channel_id=1, source_target_pairs={{0,8},{4,12},{8,0},{12,4},{1,9},{5,13},{9,1},{13,5},{2,10},{6,14},... | collective-permute-start | bytes 393224 | tf_op jit(solution)/shard_map/ppermute | solution.py:19
  19.3 1.2 %collective-permute-start.7 = (bf16[512,128]{1,0:T(8,128)(2,1)S(1)}, bf16[512,128]{1,0:T(8,128)(2,1)S(1)}, u32[]{:S(2)}, u32[]{:S(2)}) collective-permute-start(bf16[512,128]{1,0:T(8,128)(2,1)S(1)} %get-tuple-element.41), channel_id=1, source_target_pairs={{0,4},{4,0},{8,12},{12,8},{1,5},{5,1},{9,13},{13,9},{2,6},{6,2},{1... | collective-permute-start | bytes 393224 | tf_op jit(solution)/shard_map/ppermute | solution.py:19
  20.5 0.6 %collective-permute-done.4.refs_3_ = bf16[32,128]{1,0:T(8,128)(2,1)S(1)} collective-permute-done((bf16[32,128]{1,0:T(8,128)(2,1)S(1)}, bf16[32,128]{1,0:T(8,128)(2,1)S(1)}, u32[]{:S(2)}, u32[]{:S(2)}) %collective-permute-start.4) | collective-permute-done | bytes 8224 | tf_op jit(solution)/shard_map/ppermute | solution.py:19
  21.0 0.0 collective-permute-done.5
  21.0 0.0 copy-done
  21.0 0.5 %expand.1 = (bf16[512,128]{1,0:T(8,128)(2,1)S(1)}, bf16[512,128]{1,0:T(8,128)(2,1)S(1)}) custom-call(s32[1]{0:T(128)} %bitcast.1.batch_at, bf16[32,1152]{1,0:T(8,128)(2,1)S(1)} %get-tuple-element.38.tagged.refs_0_, bf16[32,1152]{1,0:T(8,128)(2,1)S(1)} %collective-permute-done.refs_1_, bf16[32,128]{1,0:T(8,128)(2,1)S(1)} %add_convert_fusion.1.refs_2_, ...), custom_call_target="tpu_custom_call" | custom-call | flops 134217728 | bytes 1048576 | tf_op jit(solution)/shard_map/expand/pallas_call | solution.py:388
  21.6 1.0 %collective-permute-start.8 = (bf16[512,128]{1,0:T(8,128)(2,1)S(1)}, bf16[512,128]{1,0:T(8,128)(2,1)S(1)}, u32[]{:S(2)}, u32[]{:S(2)}) collective-permute-start(bf16[512,128]{1,0:T(8,128)(2,1)S(1)} %get-tuple-element.42), channel_id=1, source_target_pairs={{0,2},{1,3},{2,0},{3,1},{4,6},{5,7},{6,4},{7,5},{8,10},{9,11},{10,... | collective-permute-start | bytes 393224 | tf_op jit(solution)/shard_map/ppermute | solution.py:19
  22.6 2.5 %base_terms.5.refs_0_ = f32[512,128]{1,0:T(8,128)S(1)} custom-call(s32[1]{0:T(128)} %bitcast.tensor_at, bf16[32,1152]{1,0:T(8,128)(2,1)S(1)} %get-tuple-element.38.tagged.refs_0_, bf16[1024,8192]{1,0:T(8,128)(2,1)} %out_weight.5), custom_call_target="tpu_custom_call" | custom-call | flops 134217728 | bytes 4194304 | tf_op jit(solution)/shard_map/base_terms/pallas_call | solution.py:270
  25.1 1.6 %collective-permute-done.6.refs_2_ = bf16[512,128]{1,0:T(8,128)(2,1)S(1)} collective-permute-done((bf16[512,128]{1,0:T(8,128)(2,1)S(1)}, bf16[512,128]{1,0:T(8,128)(2,1)S(1)}, u32[]{:S(2)}, u32[]{:S(2)}) %collective-permute-start.6) | collective-permute-done | bytes 131104 | tf_op jit(solution)/shard_map/ppermute | solution.py:19
  26.6 0.1 partial_total.2.refs_0_
  26.7 0.0 collective-permute-done.7.refs_1_
  26.7 0.0 collective-permute-done.8.refs_1_
  26.8 0.7 %total.1 = bf16[32,2048]{1,0:T(8,128)(2,1)} custom-call(f32[512,128]{1,0:T(8,128)S(1)} %partial_total.3.refs_0_, bf16[512,128]{1,0:T(8,128)(2,1)S(1)} %collective-permute-done.8.refs_1_), custom_call_target="tpu_custom_call" | custom-call | flops 131072 | bytes 393216 | tf_op jit(solution)/shard_map/total/pallas_call | solution.py:420
  (3 shorter events, 0.1 us)
Async XLA Ops:
  0.0 21.0 %collective-permute-start.5 = (bf16[4,64,2048]{2,1,0:T(8,128)(2,1)}, bf16[4,64,2048]{2,1,0:T(8,128)(2,1)S(1)}, u32[]{:S(2)}, u32[]{:S(2)}) collective-permute-start(bf16[4,64,2048]{2,1,0:T(8,128)(2,1)} %param.20), channel_id=1, source_target_pairs={{0,1},{1,0},{2,3},{3,2},{4,5},{5,4},{6,7},{7,6},{8,9},{9,8},{10,11... | collective-permute-start | bytes 3145736 | tf_op jit(solution)/shard_map/ppermute | solution.py:19
  4.0 8.1 %collective-permute-start.1 = (bf16[4,64,1024]{2,1,0:T(8,128)(2,1)S(1)}, bf16[4,64,1024]{2,1,0:T(8,128)(2,1)S(1)}, u32[]{:S(2)}, u32[]{:S(2)}) collective-permute-start(bf16[4,64,1024]{2,1,0:T(8,128)(2,1)S(1)} %get-tuple-element.29.refs_2_), channel_id=1, source_target_pairs={{0,1},{1,0},{2,3},{3,2},{4,5},{5,4},{6,7},{7,6},{8,9},{9,8},{10,11... | collective-permute-start | bytes 1572872 | tf_op jit(solution)/shard_map/ppermute | solution.py:19
  4.1 6.4 %collective-permute-start = (bf16[32,1152]{1,0:T(8,128)(2,1)S(1)}, bf16[32,1152]{1,0:T(8,128)(2,1)S(1)}, u32[]{:S(2)}, u32[]{:S(2)}) collective-permute-start(bf16[32,1152]{1,0:T(8,128)(2,1)S(1)} %get-tuple-element.38.tagged.refs_0_), channel_id=1, source_target_pairs={{0,2},{1,3},{2,0},{3,1},{4,6},{5,7},{6,4},{7,5},{8,10},{9,11},{10,... | collective-permute-start | bytes 221192 | tf_op jit(solution)/shard_map/ppermute | solution.py:19
  10.5 5.4 %collective-permute-start.3 = (bf16[512,128]{1,0:T(8,128)(2,1)S(1)}, bf16[512,128]{1,0:T(8,128)(2,1)S(1)}, u32[]{:S(2)}, u32[]{:S(2)}) collective-permute-start(bf16[512,128]{1,0:T(8,128)(2,1)S(1)} %get-tuple-element.31), channel_id=1, source_target_pairs={{0,4},{4,0},{8,12},{12,8},{1,5},{5,1},{9,13},{13,9},{2,6},{6,2},{1... | collective-permute-start | bytes 393224 | tf_op jit(solution)/shard_map/ppermute | solution.py:19
  12.6 8.4 %copy-start = (bf16[4,64,2048]{2,1,0:T(8,128)(2,1)S(1)}, bf16[4,64,2048]{2,1,0:T(8,128)(2,1)}, u32[]{:S(2)}) copy-start(bf16[4,64,2048]{2,1,0:T(8,128)(2,1)} %param.20) | copy-start | bytes 3145732
  12.6 3.7 %collective-permute-start.2 = (bf16[32,128]{1,0:T(8,128)(2,1)S(1)}, bf16[32,128]{1,0:T(8,128)(2,1)S(1)}, u32[]{:S(2)}, u32[]{:S(2)}) collective-permute-start(bf16[32,128]{1,0:T(8,128)(2,1)S(1)} %shrink.1), channel_id=1, source_target_pairs={{0,4},{4,0},{8,12},{12,8},{1,5},{5,1},{9,13},{13,9},{2,6},{6,2},{1... | collective-permute-start | bytes 24584 | tf_op jit(solution)/shard_map/ppermute | solution.py:19
  16.4 4.7 %collective-permute-start.4 = (bf16[32,128]{1,0:T(8,128)(2,1)S(1)}, bf16[32,128]{1,0:T(8,128)(2,1)S(1)}, u32[]{:S(2)}, u32[]{:S(2)}) collective-permute-start(bf16[32,128]{1,0:T(8,128)(2,1)S(1)} %add_convert_fusion.1.refs_2_), channel_id=1, source_target_pairs={{0,8},{4,12},{8,0},{12,4},{1,9},{5,13},{9,1},{13,5},{2,10},{6,14},... | collective-permute-start | bytes 24584 | tf_op jit(solution)/shard_map/ppermute | solution.py:19
  19.0 7.7 %collective-permute-start.6 = (bf16[512,128]{1,0:T(8,128)(2,1)S(1)}, bf16[512,128]{1,0:T(8,128)(2,1)S(1)}, u32[]{:S(2)}, u32[]{:S(2)}) collective-permute-start(bf16[512,128]{1,0:T(8,128)(2,1)S(1)} %add_convert_fusion), channel_id=1, source_target_pairs={{0,8},{4,12},{8,0},{12,4},{1,9},{5,13},{9,1},{13,5},{2,10},{6,14},... | collective-permute-start | bytes 393224 | tf_op jit(solution)/shard_map/ppermute | solution.py:19
  19.3 7.4 %collective-permute-start.7 = (bf16[512,128]{1,0:T(8,128)(2,1)S(1)}, bf16[512,128]{1,0:T(8,128)(2,1)S(1)}, u32[]{:S(2)}, u32[]{:S(2)}) collective-permute-start(bf16[512,128]{1,0:T(8,128)(2,1)S(1)} %get-tuple-element.41), channel_id=1, source_target_pairs={{0,4},{4,0},{8,12},{12,8},{1,5},{5,1},{9,13},{13,9},{2,6},{6,2},{1... | collective-permute-start | bytes 393224 | tf_op jit(solution)/shard_map/ppermute | solution.py:19
  21.6 5.2 %collective-permute-start.8 = (bf16[512,128]{1,0:T(8,128)(2,1)S(1)}, bf16[512,128]{1,0:T(8,128)(2,1)S(1)}, u32[]{:S(2)}, u32[]{:S(2)}) collective-permute-start(bf16[512,128]{1,0:T(8,128)(2,1)S(1)} %get-tuple-element.42), channel_id=1, source_target_pairs={{0,2},{1,3},{2,0},{3,1},{4,6},{5,7},{6,4},{7,5},{8,10},{9,11},{10,... | collective-permute-start | bytes 393224 | tf_op jit(solution)/shard_map/ppermute | solution.py:19

commit v10 on v8

--- a/solution.py
+++ b/solution.py
@@ -141,7 +141,7 @@
     full = -(-heads // 8) * 8
     if full != heads:
         queries = jnp.pad(queries, ((0, 0), (0, full - heads), (0, 0)))
-    parts = 2
+    parts = 1
     smem = pl.BlockSpec(memory_space=pltpu.SMEM)
     away = pl.BlockSpec(memory_space=pl.ANY)
     tagged, early, limits = pl.pallas_call(
@@ -500,7 +500,6 @@
     limits = [limits, to_sibling(limits)]
     shrink_weight = jnp.swapaxes(shrink_weight, 1, 2)
     shrink_factors = [shrink_weight, to_sibling(shrink_weight)]
-    expand_factors = [expand_weight, to_sibling(expand_weight)]
     visiting = [to_chip(tagged, shift) for shift in range(1, chips)]
     third, next_door = base_block(tensor_at, tagged, out_weight, block, 1, [early])
     visiting, third, next_door, limits = lax.optimization_barrier(
@@ -511,7 +510,8 @@
 
     part = shrink_part(blocks, shrink_factors, batch_at)
     parts = [part, across(part, 1)]
-    part, later_tagged = lax.optimization_barrier((part, tagged))
+    part, later_tagged, expand_weight = lax.optimization_barrier((part, tagged, expand_weight))
+    expand_factors = [expand_weight, to_sibling(expand_weight)]
     (second,) = base_block(tensor_at, later_tagged, out_weight, block, 2)
     second = (wide(second) + wide(third)).astype(BF16)
     parts, second = lax.optimization_barrier((parts, second))

time: 27.1 us -> 27.8 us (1.026)
  waiting for transfers between devices: 2.76 us -> 3.36 us
    ppermute x10, waiting for transfers between devices: 2.76 us -> 3.36 us  [permuted(): return lax.ppermute(array, axis, [(i, partner(i)) for i in range(size)])]
  transfers between devices with their start and end apart: 10 -> 10, of which waited for: 2 -> 2; matrix products, arithmetic and copies ran while one was open for 0% -> 0% of each run, Pallas kernels for 43% -> 40%
where the time goes in v10:
time: 27.8 us; the launch traced here: 27.7 us
  Pallas kernels  12.3 us (44%)
  starting transfers between devices  11.9 us (43%)
  waiting for transfers between devices  3.36 us (12%)
    ppermute x10, starting transfers between devices, permuted(): return lax.ppermute(array, axis, [(i, partner(i)) for i in range(size)])  11.9 us
    pallas_call x3, Pallas kernels, base_block(): pl.pallas_call(functools.partial(base_kernel, ahead, deep, len(arrived)),...  7.65 us
    ppermute x10, waiting for transfers between devices, permuted(): return lax.ppermute(array, axis, [(i, partner(i)) for i in range(size)])  3.36 us
    pallas_call x1, Pallas kernels, attend(): pl.pallas_call(functools.partial(attend_kernel, parts, rank_width), out_s...  2.83 us
    pallas_call x1, Pallas kernels, total(): pl.pallas_call(total_kernel, out_shape=jax.ShapeDtypeStruct((rows, block)...  0.69 us
  transfers between devices with their start and end apart: 10, of which 2 were waited for; matrix products, arithmetic and copies ran while one was open for 0% of the time, Pallas kernels for 40%

profile of v10, /device:TPU:0, one launch (start us, length us, event | category | flops | bytes accessed | tf_op | source)
XLA Modules:
  0.0 27.7 jit_solution(7793056081727268250)
XLA Ops:
  0.0 0.5 %collective-permute-start.2 = (bf16[4,64,1024]{2,1,0:T(8,128)(2,1)}, bf16[4,64,1024]{2,1,0:T(8,128)(2,1)S(1)}, u32[]{:S(2)}, u32[]{:S(2)}) collective-permute-start(bf16[4,64,1024]{2,1,0:T(8,128)(2,1)} %bitcast.8), channel_id=1, source_target_pairs={{0,1},{1,0},{2,3},{3,2},{4,5},{5,4},{6,7},{7,6},{8,9},{9,8},{10,11... | collective-permute-start | bytes 1572872 | tf_op jit(solution)/shard_map/ppermute | solution.py:19
  0.5 2.8 %attention.1 = (bf16[32,1152]{1,0:T(8,128)(2,1)S(1)}, bf16[1024,2048]{1,0:T(8,128)(2,1)S(1)}, s32[8,128]{1,0:T(8,128)S(1)}) custom-call(s32[1]{0:T(128)} %bitcast.2.group_at, s32[1]{0:T(128)S(6)} %xor.3.early_at, bf16[32,4,96,128]{3,2,1,0:T(8,128)(2,1)} %refs_0_.1, bf16[32,4,96,128]{3,2,1,0:T(8,128)(2,1)} %refs_1_.1, bf16[32,8,128]{2,1,0:T(8,128)(2,1)} %refs_2_.1, ...), custom_call_target="tpu_custom_call" | custom-call | flops 12582912 | bytes 1572864 | tf_op jit(solution)/shard_map/attention/pallas_call | solution.py:147
  3.3 2.6 %collective-permute-start = (bf16[32,1152]{1,0:T(8,128)(2,1)S(1)}, bf16[32,1152]{1,0:T(8,128)(2,1)S(1)}, u32[]{:S(2)}, u32[]{:S(2)}) collective-permute-start(bf16[32,1152]{1,0:T(8,128)(2,1)S(1)} %get-tuple-element.44.tagged.refs_0_.refs_2_), channel_id=1, source_target_pairs={{0,2},{1,3},{2,0},{3,1},{4,6},{5,7},{6,4},{7,5},{8,10},{9,11},{10,... | collective-permute-start | bytes 221192 | tf_op jit(solution)/shard_map/ppermute | solution.py:19
  5.8 0.2 collective-permute-start.1
  6.1 0.0 copy-start.1
  6.1 0.0 copy-start
  6.1 2.6 %base_terms.3 = (bf16[512,128]{1,0:T(8,128)(2,1)S(1)}, bf16[512,128]{1,0:T(8,128)(2,1)S(1)}) custom-call(s32[1]{0:T(128)} %bitcast.tensor_at, bf16[32,1152]{1,0:T(8,128)(2,1)S(1)} %get-tuple-element.44.tagged.refs_0_.refs_2_, bf16[1024,8192]{1,0:T(8,128)(2,1)} %out_weight.5, bf16[1024,2048]{1,0:T(8,128)(2,1)S(1)} %get-tuple-element.28.refs_0_), custom_call_target="tpu_custom_call" | custom-call | flops 268435456 | bytes 8388608 | tf_op jit(solution)/shard_map/base_terms/pallas_call | solution.py:257
  8.7 0.0 collective-permute-done.1.refs_1_
  8.7 0.0 collective-permute-done.refs_1_.refs_3_
  8.8 0.0 collective-permute-done.2.refs_3_
  8.8 0.0 copy-done.1
  8.8 0.5 %shrink.1 = bf16[32,128]{1,0:T(8,128)(2,1)S(1)} custom-call(s32[1]{0:T(128)} %bitcast.1.batch_at, bf16[32,1152]{1,0:T(8,128)(2,1)S(1)} %get-tuple-element.44.tagged.refs_0_.refs_2_, bf16[32,1152]{1,0:T(8,128)(2,1)S(1)} %collective-permute-done.refs_1_.refs_3_, bf16[4,64,1024]{2,1,0:T(8,128)(2,1)S(1)} %bitcast.9, ...), custom_call_target="tpu_custom_call" | custom-call | flops 67108864 | bytes 1179648 | tf_op jit(solution)/shard_map/shrink/pallas_call | solution.py:317
  9.3 0.0 copy-done
  9.3 0.3 %collective-permute-start.6 = (bf16[4,64,2048]{2,1,0:T(8,128)(2,1)S(1)}, bf16[4,64,2048]{2,1,0:T(8,128)(2,1)S(1)}, u32[]{:S(2)}, u32[]{:S(2)}) collective-permute-start(bf16[4,64,2048]{2,1,0:T(8,128)(2,1)S(1)} %copy-done), channel_id=1, source_target_pairs={{0,1},{1,0},{2,3},{3,2},{4,5},{5,4},{6,7},{7,6},{8,9},{9,8},{10,11... | collective-permute-start | bytes 3145736 | tf_op jit(solution)/shard_map/ppermute | solution.py:19
  9.6 1.6 %collective-permute-start.4 = (bf16[512,128]{1,0:T(8,128)(2,1)S(1)}, bf16[512,128]{1,0:T(8,128)(2,1)S(1)}, u32[]{:S(2)}, u32[]{:S(2)}) collective-permute-start(bf16[512,128]{1,0:T(8,128)(2,1)S(1)} %get-tuple-element.36), channel_id=1, source_target_pairs={{0,4},{4,0},{8,12},{12,8},{1,5},{5,1},{9,13},{13,9},{2,6},{6,2},{1... | collective-permute-start | bytes 393224 | tf_op jit(solution)/shard_map/ppermute | solution.py:19
  11.3 0.4 %collective-permute-start.3 = (bf16[32,128]{1,0:T(8,128)(2,1)S(1)}, bf16[32,128]{1,0:T(8,128)(2,1)S(1)}, u32[]{:S(2)}, u32[]{:S(2)}) collective-permute-start(bf16[32,128]{1,0:T(8,128)(2,1)S(1)} %shrink.1), channel_id=1, source_target_pairs={{0,4},{4,0},{8,12},{12,8},{1,5},{5,1},{9,13},{13,9},{2,6},{6,2},{1... | collective-permute-start | bytes 24584 | tf_op jit(solution)/shard_map/ppermute | solution.py:19
  11.7 2.5 %base_terms.4 = bf16[512,128]{1,0:T(8,128)(2,1)S(1)} custom-call(s32[1]{0:T(128)} %bitcast.tensor_at, bf16[32,1152]{1,0:T(8,128)(2,1)S(1)} %get-tuple-element.44.tagged.refs_0_.refs_2_, bf16[1024,8192]{1,0:T(8,128)(2,1)} %out_weight.5), custom_call_target="tpu_custom_call" | custom-call | flops 134217728 | bytes 4194304 | tf_op jit(solution)/shard_map/base_terms/pallas_call | solution.py:257
  14.2 1.3 %collective-permute-done.4 = bf16[512,128]{1,0:T(8,128)(2,1)S(1)} collective-permute-done((bf16[512,128]{1,0:T(8,128)(2,1)S(1)}, bf16[512,128]{1,0:T(8,128)(2,1)S(1)}, u32[]{:S(2)}, u32[]{:S(2)}) %collective-permute-start.4) | collective-permute-done | bytes 131104 | tf_op jit(solution)/shard_map/ppermute | solution.py:19
  15.5 0.0 collective-permute-done.3
  15.6 2.8 %collective-permute-start.5 = (bf16[32,128]{1,0:T(8,128)(2,1)S(1)}, bf16[32,128]{1,0:T(8,128)(2,1)S(1)}, u32[]{:S(2)}, u32[]{:S(2)}) collective-permute-start(bf16[32,128]{1,0:T(8,128)(2,1)S(1)} %add_convert_fusion.1.refs_4_), channel_id=1, source_target_pairs={{0,8},{4,12},{8,0},{12,4},{1,9},{5,13},{9,1},{13,5},{2,10},{6,14},... | collective-permute-start | bytes 24584 | tf_op jit(solution)/shard_map/ppermute | solution.py:19
  18.4 0.2 collective-permute-start.7
  18.5 1.8 %collective-permute-start.8 = (bf16[512,128]{1,0:T(8,128)(2,1)S(1)}, bf16[512,128]{1,0:T(8,128)(2,1)S(1)}, u32[]{:S(2)}, u32[]{:S(2)}) collective-permute-start(bf16[512,128]{1,0:T(8,128)(2,1)S(1)} %get-tuple-element.47), channel_id=1, source_target_pairs={{0,4},{4,0},{8,12},{12,8},{1,5},{5,1},{9,13},{13,9},{2,6},{6,2},{1... | collective-permute-start | bytes 393224 | tf_op jit(solution)/shard_map/ppermute | solution.py:19
  20.3 0.0 collective-permute-done.5.refs_5_
  20.3 0.0 collective-permute-done.6
  20.3 0.5 %expand.1 = (bf16[512,128]{1,0:T(8,128)(2,1)S(1)}, bf16[512,128]{1,0:T(8,128)(2,1)S(1)}) custom-call(s32[1]{0:T(128)} %bitcast.1.batch_at, s32[8,128]{1,0:T(8,128)S(1)} %get-tuple-element.32.refs_0_, s32[8,128]{1,0:T(8,128)S(1)} %collective-permute-done.1.refs_1_, bf16[32,1152]{1,0:T(8,128)(2,1)S(1)} %get-tuple-element.44.tagged.refs_0_.refs_2_, ...), custom_call_target="tpu_custom_call" | custom-call | flops 134217728 | bytes 1048576 | tf_op jit(solution)/shard_map/expand/pallas_call | solution.py:377
  20.8 1.6 %collective-permute-start.9 = (bf16[512,128]{1,0:T(8,128)(2,1)S(1)}, bf16[512,128]{1,0:T(8,128)(2,1)S(1)}, u32[]{:S(2)}, u32[]{:S(2)}) collective-permute-start(bf16[512,128]{1,0:T(8,128)(2,1)S(1)} %get-tuple-element.48), channel_id=1, source_target_pairs={{0,2},{1,3},{2,0},{3,1},{4,6},{5,7},{6,4},{7,5},{8,10},{9,11},{10,... | collective-permute-start | bytes 393224 | tf_op jit(solution)/shard_map/ppermute | solution.py:19
  22.4 2.5 %base_terms.5.refs_0_ = f32[512,128]{1,0:T(8,128)S(1)} custom-call(s32[1]{0:T(128)} %bitcast.tensor_at, bf16[32,1152]{1,0:T(8,128)(2,1)S(1)} %get-tuple-element.44.tagged.refs_0_.refs_2_, bf16[1024,8192]{1,0:T(8,128)(2,1)} %out_weight.5), custom_call_target="tpu_custom_call" | custom-call | flops 134217728 | bytes 4194304 | tf_op jit(solution)/shard_map/base_terms/pallas_call | solution.py:257
  24.9 2.0 %collective-permute-done.7.refs_2_ = bf16[512,128]{1,0:T(8,128)(2,1)S(1)} collective-permute-done((bf16[512,128]{1,0:T(8,128)(2,1)S(1)}, bf16[512,128]{1,0:T(8,128)(2,1)S(1)}, u32[]{:S(2)}, u32[]{:S(2)}) %collective-permute-start.7) | collective-permute-done | bytes 131104 | tf_op jit(solution)/shard_map/ppermute | solution.py:19
  26.9 0.0 collective-permute-done.8.refs_1_
  27.0 0.0 collective-permute-done.9.refs_1_
  27.0 0.7 %total.1 = bf16[32,2048]{1,0:T(8,128)(2,1)} custom-call(f32[512,128]{1,0:T(8,128)S(1)} %partial_total.3.refs_0_, bf16[512,128]{1,0:T(8,128)(2,1)S(1)} %collective-permute-done.9.refs_1_), custom_call_target="tpu_custom_call" | custom-call | flops 131072 | bytes 393216 | tf_op jit(solution)/shard_map/total/pallas_call | solution.py:410
  (4 shorter events, 0.1 us)
Async XLA Ops:
  0.0 8.8 %collective-permute-start.2 = (bf16[4,64,1024]{2,1,0:T(8,128)(2,1)}, bf16[4,64,1024]{2,1,0:T(8,128)(2,1)S(1)}, u32[]{:S(2)}, u32[]{:S(2)}) collective-permute-start(bf16[4,64,1024]{2,1,0:T(8,128)(2,1)} %bitcast.8), channel_id=1, source_target_pairs={{0,1},{1,0},{2,3},{3,2},{4,5},{5,4},{6,7},{7,6},{8,9},{9,8},{10,11... | collective-permute-start | bytes 1572872 | tf_op jit(solution)/shard_map/ppermute | solution.py:19
  3.3 5.5 %collective-permute-start = (bf16[32,1152]{1,0:T(8,128)(2,1)S(1)}, bf16[32,1152]{1,0:T(8,128)(2,1)S(1)}, u32[]{:S(2)}, u32[]{:S(2)}) collective-permute-start(bf16[32,1152]{1,0:T(8,128)(2,1)S(1)} %get-tuple-element.44.tagged.refs_0_.refs_2_), channel_id=1, source_target_pairs={{0,2},{1,3},{2,0},{3,1},{4,6},{5,7},{6,4},{7,5},{8,10},{9,11},{10,... | collective-permute-start | bytes 221192 | tf_op jit(solution)/shard_map/ppermute | solution.py:19
  5.8 2.9 %collective-permute-start.1 = (s32[8,128]{1,0:T(8,128)S(1)}, s32[8,128]{1,0:T(8,128)S(1)}, u32[]{:S(2)}, u32[]{:S(2)}) collective-permute-start(s32[8,128]{1,0:T(8,128)S(1)} %get-tuple-element.32.refs_0_), channel_id=1, source_target_pairs={{0,1},{1,0},{2,3},{3,2},{4,5},{5,4},{6,7},{7,6},{8,9},{9,8},{10,11... | collective-permute-start | bytes 12296 | tf_op jit(solution)/shard_map/ppermute | solution.py:19
  6.1 2.7 %copy-start.1 = (bf16[4,1024,64]{1,2,0:T(8,128)(2,1)S(1)}, bf16[4,1024,64]{1,2,0:T(8,128)(2,1)}, u32[]{:S(2)}) copy-start(bf16[4,1024,64]{1,2,0:T(8,128)(2,1)} %param.19) | copy-start | bytes 1572868
  6.1 3.2 %copy-start = (bf16[4,64,2048]{2,1,0:T(8,128)(2,1)S(1)}, bf16[4,64,2048]{2,1,0:T(8,128)(2,1)}, u32[]{:S(2)}) copy-start(bf16[4,64,2048]{2,1,0:T(8,128)(2,1)} %param.20) | copy-start | bytes 3145732
  9.3 11.0 %collective-permute-start.6 = (bf16[4,64,2048]{2,1,0:T(8,128)(2,1)S(1)}, bf16[4,64,2048]{2,1,0:T(8,128)(2,1)S(1)}, u32[]{:S(2)}, u32[]{:S(2)}) collective-permute-start(bf16[4,64,2048]{2,1,0:T(8,128)(2,1)S(1)} %copy-done), channel_id=1, source_target_pairs={{0,1},{1,0},{2,3},{3,2},{4,5},{5,4},{6,7},{7,6},{8,9},{9,8},{10,11... | collective-permute-start | bytes 3145736 | tf_op jit(solution)/shard_map/ppermute | solution.py:19
  9.6 5.8 %collective-permute-start.4 = (bf16[512,128]{1,0:T(8,128)(2,1)S(1)}, bf16[512,128]{1,0:T(8,128)(2,1)S(1)}, u32[]{:S(2)}, u32[]{:S(2)}) collective-permute-start(bf16[512,128]{1,0:T(8,128)(2,1)S(1)} %get-tuple-element.36), channel_id=1, source_target_pairs={{0,4},{4,0},{8,12},{12,8},{1,5},{5,1},{9,13},{13,9},{2,6},{6,2},{1... | collective-permute-start | bytes 393224 | tf_op jit(solution)/shard_map/ppermute | solution.py:19
  11.3 4.3 %collective-permute-start.3 = (bf16[32,128]{1,0:T(8,128)(2,1)S(1)}, bf16[32,128]{1,0:T(8,128)(2,1)S(1)}, u32[]{:S(2)}, u32[]{:S(2)}) collective-permute-start(bf16[32,128]{1,0:T(8,128)(2,1)S(1)} %shrink.1), channel_id=1, source_target_pairs={{0,4},{4,0},{8,12},{12,8},{1,5},{5,1},{9,13},{13,9},{2,6},{6,2},{1... | collective-permute-start | bytes 24584 | tf_op jit(solution)/shard_map/ppermute | solution.py:19
  15.6 4.7 %collective-permute-start.5 = (bf16[32,128]{1,0:T(8,128)(2,1)S(1)}, bf16[32,128]{1,0:T(8,128)(2,1)S(1)}, u32[]{:S(2)}, u32[]{:S(2)}) collective-permute-start(bf16[32,128]{1,0:T(8,128)(2,1)S(1)} %add_convert_fusion.1.refs_4_), channel_id=1, source_target_pairs={{0,8},{4,12},{8,0},{12,4},{1,9},{5,13},{9,1},{13,5},{2,10},{6,14},... | collective-permute-start | bytes 24584 | tf_op jit(solution)/shard_map/ppermute | solution.py:19
  18.4 8.5 %collective-permute-start.7 = (bf16[512,128]{1,0:T(8,128)(2,1)S(1)}, bf16[512,128]{1,0:T(8,128)(2,1)S(1)}, u32[]{:S(2)}, u32[]{:S(2)}) collective-permute-start(bf16[512,128]{1,0:T(8,128)(2,1)S(1)} %add_convert_fusion), channel_id=1, source_target_pairs={{0,8},{4,12},{8,0},{12,4},{1,9},{5,13},{9,1},{13,5},{2,10},{6,14},... | collective-permute-start | bytes 393224 | tf_op jit(solution)/shard_map/ppermute | solution.py:19
  18.5 8.4 %collective-permute-start.8 = (bf16[512,128]{1,0:T(8,128)(2,1)S(1)}, bf16[512,128]{1,0:T(8,128)(2,1)S(1)}, u32[]{:S(2)}, u32[]{:S(2)}) collective-permute-start(bf16[512,128]{1,0:T(8,128)(2,1)S(1)} %get-tuple-element.47), channel_id=1, source_target_pairs={{0,4},{4,0},{8,12},{12,8},{1,5},{5,1},{9,13},{13,9},{2,6},{6,2},{1... | collective-permute-start | bytes 393224 | tf_op jit(solution)/shard_map/ppermute | solution.py:19
  20.8 6.2 %collective-permute-start.9 = (bf16[512,128]{1,0:T(8,128)(2,1)S(1)}, bf16[512,128]{1,0:T(8,128)(2,1)S(1)}, u32[]{:S(2)}, u32[]{:S(2)}) collective-permute-start(bf16[512,128]{1,0:T(8,128)(2,1)S(1)} %get-tuple-element.48), channel_id=1, source_target_pairs={{0,2},{1,3},{2,0},{3,1},{4,6},{5,7},{6,4},{7,5},{8,10},{9,11},{10,... | collective-permute-start | bytes 393224 | tf_op jit(solution)/shard_map/ppermute | solution.py:19

commit v11 on v10

--- a/solution.py
+++ b/solution.py
@@ -510,11 +510,11 @@
 
     part = shrink_part(blocks, shrink_factors, batch_at)
     parts = [part, across(part, 1)]
-    part, later_tagged, expand_weight = lax.optimization_barrier((part, tagged, expand_weight))
-    expand_factors = [expand_weight, to_sibling(expand_weight)]
+    part, later_tagged = lax.optimization_barrier((part, tagged))
     (second,) = base_block(tensor_at, later_tagged, out_weight, block, 2)
     second = (wide(second) + wide(third)).astype(BF16)
-    parts, second = lax.optimization_barrier((parts, second))
+    parts, second, expand_weight = lax.optimization_barrier((parts, second, expand_weight))
+    expand_factors = [expand_weight, to_sibling(expand_weight)]
     bit = 2
     while bit < tensor_size:
         part = (wide(parts[0]) + wide(parts[1])).astype(BF16)

time: 27.8 us -> 27.7 us (level)
  starting transfers between devices: 11.9 us -> 11.3 us
  waiting for transfers between devices: 3.36 us -> 3.9 us
    ppermute x10, starting transfers between devices: 11.9 us -> 11.3 us  [permuted(): return lax.ppermute(array, axis, [(i, partner(i)) for i in range(size)])]
    ppermute x10, waiting for transfers between devices: 3.36 us -> 3.9 us  [permuted(): return lax.ppermute(array, axis, [(i, partner(i)) for i in range(size)])]
  transfers between devices with their start and end apart: 10 -> 10, of which waited for: 2 -> 5; matrix products, arithmetic and copies ran while one was open for 0% -> 0% of each run, Pallas kernels for 40% -> 42%
where the time goes in v11:
time: 27.7 us; the launch traced here: 27.6 us
  Pallas kernels  12.3 us (44%)
  starting transfers between devices  11.3 us (41%)
  waiting for transfers between devices  3.9 us (14%)
    ppermute x10, starting transfers between devices, permuted(): return lax.ppermute(array, axis, [(i, partner(i)) for i in range(size)])  11.3 us
    pallas_call x3, Pallas kernels, base_block(): pl.pallas_call(functools.partial(base_kernel, ahead, deep, len(arrived)),...  7.64 us
    ppermute x10, waiting for transfers between devices, permuted(): return lax.ppermute(array, axis, [(i, partner(i)) for i in range(size)])  3.9 us
    pallas_call x1, Pallas kernels, attend(): pl.pallas_call(functools.partial(attend_kernel, parts, rank_width), out_s...  2.83 us
    pallas_call x1, Pallas kernels, total(): pl.pallas_call(total_kernel, out_shape=jax.ShapeDtypeStruct((rows, block)...  0.69 us
  transfers between devices with their start and end apart: 10, of which 5 were waited for; matrix products, arithmetic and copies ran while one was open for 0% of the time, Pallas kernels for 42%

profile of v11, /device:TPU:0, one launch (start us, length us, event | category | flops | bytes accessed | tf_op | source)
XLA Modules:
  0.0 27.6 jit_solution(10567070357410960182)
XLA Ops:
  0.0 0.5 %collective-permute-start.2 = (bf16[4,64,1024]{2,1,0:T(8,128)(2,1)}, bf16[4,64,1024]{2,1,0:T(8,128)(2,1)S(1)}, u32[]{:S(2)}, u32[]{:S(2)}) collective-permute-start(bf16[4,64,1024]{2,1,0:T(8,128)(2,1)} %bitcast.8), channel_id=1, source_target_pairs={{0,1},{1,0},{2,3},{3,2},{4,5},{5,4},{6,7},{7,6},{8,9},{9,8},{10,11... | collective-permute-start | bytes 1572872 | tf_op jit(solution)/shard_map/ppermute | solution.py:19
  0.5 2.8 %attention.1 = (bf16[32,1152]{1,0:T(8,128)(2,1)S(1)}, bf16[1024,2048]{1,0:T(8,128)(2,1)S(1)}, s32[8,128]{1,0:T(8,128)S(1)}) custom-call(s32[1]{0:T(128)} %bitcast.2.group_at, s32[1]{0:T(128)S(6)} %xor.3.early_at, bf16[32,4,96,128]{3,2,1,0:T(8,128)(2,1)} %refs_0_.1, bf16[32,4,96,128]{3,2,1,0:T(8,128)(2,1)} %refs_1_.1, bf16[32,8,128]{2,1,0:T(8,128)(2,1)} %refs_2_.1, ...), custom_call_target="tpu_custom_call" | custom-call | flops 12582912 | bytes 1572864 | tf_op jit(solution)/shard_map/attention/pallas_call | solution.py:147
  3.3 2.6 %collective-permute-start = (bf16[32,1152]{1,0:T(8,128)(2,1)S(1)}, bf16[32,1152]{1,0:T(8,128)(2,1)S(1)}, u32[]{:S(2)}, u32[]{:S(2)}) collective-permute-start(bf16[32,1152]{1,0:T(8,128)(2,1)S(1)} %get-tuple-element.44.tagged.refs_0_.refs_2_), channel_id=1, source_target_pairs={{0,2},{1,3},{2,0},{3,1},{4,6},{5,7},{6,4},{7,5},{8,10},{9,11},{10,... | collective-permute-start | bytes 221192 | tf_op jit(solution)/shard_map/ppermute | solution.py:19
  5.8 0.2 collective-permute-start.1
  6.1 0.0 copy-start.1
  6.1 2.6 %base_terms.3 = (bf16[512,128]{1,0:T(8,128)(2,1)S(1)}, bf16[512,128]{1,0:T(8,128)(2,1)S(1)}) custom-call(s32[1]{0:T(128)} %bitcast.tensor_at, bf16[32,1152]{1,0:T(8,128)(2,1)S(1)} %get-tuple-element.44.tagged.refs_0_.refs_2_, bf16[1024,8192]{1,0:T(8,128)(2,1)} %out_weight.5, bf16[1024,2048]{1,0:T(8,128)(2,1)S(1)} %get-tuple-element.28.refs_0_), custom_call_target="tpu_custom_call" | custom-call | flops 268435456 | bytes 8388608 | tf_op jit(solution)/shard_map/base_terms/pallas_call | solution.py:257
  8.7 0.0 collective-permute-done.1.refs_1_
  8.7 0.1 collective-permute-done.refs_1_.refs_3_
  8.8 1.8 %collective-permute-start.4 = (bf16[512,128]{1,0:T(8,128)(2,1)S(1)}, bf16[512,128]{1,0:T(8,128)(2,1)S(1)}, u32[]{:S(2)}, u32[]{:S(2)}) collective-permute-start(bf16[512,128]{1,0:T(8,128)(2,1)S(1)} %get-tuple-element.36), channel_id=1, source_target_pairs={{0,4},{4,0},{8,12},{12,8},{1,5},{5,1},{9,13},{13,9},{2,6},{6,2},{1... | collective-permute-start | bytes 393224 | tf_op jit(solution)/shard_map/ppermute | solution.py:19
  10.6 0.0 collective-permute-done.2.refs_3_
  10.6 0.0 copy-done.1
  10.6 0.5 %shrink.1 = bf16[32,128]{1,0:T(8,128)(2,1)S(1)} custom-call(s32[1]{0:T(128)} %bitcast.1.batch_at, bf16[32,1152]{1,0:T(8,128)(2,1)S(1)} %get-tuple-element.44.tagged.refs_0_.refs_2_, bf16[32,1152]{1,0:T(8,128)(2,1)S(1)} %collective-permute-done.refs_1_.refs_3_, bf16[4,64,1024]{2,1,0:T(8,128)(2,1)S(1)} %bitcast.9, ...), custom_call_target="tpu_custom_call" | custom-call | flops 67108864 | bytes 1179648 | tf_op jit(solution)/shard_map/shrink/pallas_call | solution.py:317
  11.1 0.0 copy-start
  11.1 0.3 collective-permute-start.3
  11.4 2.6 %base_terms.4 = bf16[512,128]{1,0:T(8,128)(2,1)S(1)} custom-call(s32[1]{0:T(128)} %bitcast.tensor_at, bf16[32,1152]{1,0:T(8,128)(2,1)S(1)} %get-tuple-element.44.tagged.refs_0_.refs_2_, bf16[1024,8192]{1,0:T(8,128)(2,1)} %out_weight.5), custom_call_target="tpu_custom_call" | custom-call | flops 134217728 | bytes 4194304 | tf_op jit(solution)/shard_map/base_terms/pallas_call | solution.py:257
  14.0 0.6 %collective-permute-done.4 = bf16[512,128]{1,0:T(8,128)(2,1)S(1)} collective-permute-done((bf16[512,128]{1,0:T(8,128)(2,1)S(1)}, bf16[512,128]{1,0:T(8,128)(2,1)S(1)}, u32[]{:S(2)}, u32[]{:S(2)}) %collective-permute-start.4) | collective-permute-done | bytes 131104 | tf_op jit(solution)/shard_map/ppermute | solution.py:19
  14.6 0.3 %collective-permute-done.3 = bf16[32,128]{1,0:T(8,128)(2,1)S(1)} collective-permute-done((bf16[32,128]{1,0:T(8,128)(2,1)S(1)}, bf16[32,128]{1,0:T(8,128)(2,1)S(1)}, u32[]{:S(2)}, u32[]{:S(2)}) %collective-permute-start.3) | collective-permute-done | bytes 8224 | tf_op jit(solution)/shard_map/ppermute | solution.py:19
  14.9 0.0 copy-done
  14.9 0.0 collective-permute-start.6
  14.9 2.7 %collective-permute-start.5 = (bf16[32,128]{1,0:T(8,128)(2,1)S(1)}, bf16[32,128]{1,0:T(8,128)(2,1)S(1)}, u32[]{:S(2)}, u32[]{:S(2)}) collective-permute-start(bf16[32,128]{1,0:T(8,128)(2,1)S(1)} %add_convert_fusion.1.refs_4_), channel_id=1, source_target_pairs={{0,8},{4,12},{8,0},{12,4},{1,9},{5,13},{9,1},{13,5},{2,10},{6,14},... | collective-permute-start | bytes 24584 | tf_op jit(solution)/shard_map/ppermute | solution.py:19
  17.5 0.3 %collective-permute-start.7 = (bf16[512,128]{1,0:T(8,128)(2,1)S(1)}, bf16[512,128]{1,0:T(8,128)(2,1)S(1)}, u32[]{:S(2)}, u32[]{:S(2)}) collective-permute-start(bf16[512,128]{1,0:T(8,128)(2,1)S(1)} %add_convert_fusion), channel_id=1, source_target_pairs={{0,8},{4,12},{8,0},{12,4},{1,9},{5,13},{9,1},{13,5},{2,10},{6,14},... | collective-permute-start | bytes 393224 | tf_op jit(solution)/shard_map/ppermute | solution.py:19
  17.9 1.4 %collective-permute-start.8 = (bf16[512,128]{1,0:T(8,128)(2,1)S(1)}, bf16[512,128]{1,0:T(8,128)(2,1)S(1)}, u32[]{:S(2)}, u32[]{:S(2)}) collective-permute-start(bf16[512,128]{1,0:T(8,128)(2,1)S(1)} %get-tuple-element.47), channel_id=1, source_target_pairs={{0,4},{4,0},{8,12},{12,8},{1,5},{5,1},{9,13},{13,9},{2,6},{6,2},{1... | collective-permute-start | bytes 393224 | tf_op jit(solution)/shard_map/ppermute | solution.py:19
  19.3 0.2 collective-permute-done.5.refs_5_
  19.5 0.0 collective-permute-done.6
  19.5 0.5 %expand.1 = (bf16[512,128]{1,0:T(8,128)(2,1)S(1)}, bf16[512,128]{1,0:T(8,128)(2,1)S(1)}) custom-call(s32[1]{0:T(128)} %bitcast.1.batch_at, s32[8,128]{1,0:T(8,128)S(1)} %get-tuple-element.32.refs_0_, s32[8,128]{1,0:T(8,128)S(1)} %collective-permute-done.1.refs_1_, bf16[32,1152]{1,0:T(8,128)(2,1)S(1)} %get-tuple-element.44.tagged.refs_0_.refs_2_, ...), custom_call_target="tpu_custom_call" | custom-call | flops 134217728 | bytes 1048576 | tf_op jit(solution)/shard_map/expand/pallas_call | solution.py:377
  20.0 1.6 %collective-permute-start.9 = (bf16[512,128]{1,0:T(8,128)(2,1)S(1)}, bf16[512,128]{1,0:T(8,128)(2,1)S(1)}, u32[]{:S(2)}, u32[]{:S(2)}) collective-permute-start(bf16[512,128]{1,0:T(8,128)(2,1)S(1)} %get-tuple-element.48), channel_id=1, source_target_pairs={{0,2},{1,3},{2,0},{3,1},{4,6},{5,7},{6,4},{7,5},{8,10},{9,11},{10,... | collective-permute-start | bytes 393224 | tf_op jit(solution)/shard_map/ppermute | solution.py:19
  21.6 2.5 %base_terms.5.refs_0_ = f32[512,128]{1,0:T(8,128)S(1)} custom-call(s32[1]{0:T(128)} %bitcast.tensor_at, bf16[32,1152]{1,0:T(8,128)(2,1)S(1)} %get-tuple-element.44.tagged.refs_0_.refs_2_, bf16[1024,8192]{1,0:T(8,128)(2,1)} %out_weight.5), custom_call_target="tpu_custom_call" | custom-call | flops 134217728 | bytes 4194304 | tf_op jit(solution)/shard_map/base_terms/pallas_call | solution.py:257
  24.1 2.7 %collective-permute-done.7.refs_2_ = bf16[512,128]{1,0:T(8,128)(2,1)S(1)} collective-permute-done((bf16[512,128]{1,0:T(8,128)(2,1)S(1)}, bf16[512,128]{1,0:T(8,128)(2,1)S(1)}, u32[]{:S(2)}, u32[]{:S(2)}) %collective-permute-start.7) | collective-permute-done | bytes 131104 | tf_op jit(solution)/shard_map/ppermute | solution.py:19
  26.8 0.0 collective-permute-done.8.refs_1_
  26.9 0.0 collective-permute-done.9.refs_1_
  26.9 0.7 %total.1 = bf16[32,2048]{1,0:T(8,128)(2,1)} custom-call(f32[512,128]{1,0:T(8,128)S(1)} %partial_total.3.refs_0_, bf16[512,128]{1,0:T(8,128)(2,1)S(1)} %collective-permute-done.9.refs_1_), custom_call_target="tpu_custom_call" | custom-call | flops 131072 | bytes 393216 | tf_op jit(solution)/shard_map/total/pallas_call | solution.py:410
  (4 shorter events, 0.1 us)
Async XLA Ops:
  0.0 10.6 %collective-permute-start.2 = (bf16[4,64,1024]{2,1,0:T(8,128)(2,1)}, bf16[4,64,1024]{2,1,0:T(8,128)(2,1)S(1)}, u32[]{:S(2)}, u32[]{:S(2)}) collective-permute-start(bf16[4,64,1024]{2,1,0:T(8,128)(2,1)} %bitcast.8), channel_id=1, source_target_pairs={{0,1},{1,0},{2,3},{3,2},{4,5},{5,4},{6,7},{7,6},{8,9},{9,8},{10,11... | collective-permute-start | bytes 1572872 | tf_op jit(solution)/shard_map/ppermute | solution.py:19
  3.3 5.5 %collective-permute-start = (bf16[32,1152]{1,0:T(8,128)(2,1)S(1)}, bf16[32,1152]{1,0:T(8,128)(2,1)S(1)}, u32[]{:S(2)}, u32[]{:S(2)}) collective-permute-start(bf16[32,1152]{1,0:T(8,128)(2,1)S(1)} %get-tuple-element.44.tagged.refs_0_.refs_2_), channel_id=1, source_target_pairs={{0,2},{1,3},{2,0},{3,1},{4,6},{5,7},{6,4},{7,5},{8,10},{9,11},{10,... | collective-permute-start | bytes 221192 | tf_op jit(solution)/shard_map/ppermute | solution.py:19
  5.8 2.8 %collective-permute-start.1 = (s32[8,128]{1,0:T(8,128)S(1)}, s32[8,128]{1,0:T(8,128)S(1)}, u32[]{:S(2)}, u32[]{:S(2)}) collective-permute-start(s32[8,128]{1,0:T(8,128)S(1)} %get-tuple-element.32.refs_0_), channel_id=1, source_target_pairs={{0,1},{1,0},{2,3},{3,2},{4,5},{5,4},{6,7},{7,6},{8,9},{9,8},{10,11... | collective-permute-start | bytes 12296 | tf_op jit(solution)/shard_map/ppermute | solution.py:19
  6.1 4.5 %copy-start.1 = (bf16[4,1024,64]{1,2,0:T(8,128)(2,1)S(1)}, bf16[4,1024,64]{1,2,0:T(8,128)(2,1)}, u32[]{:S(2)}) copy-start(bf16[4,1024,64]{1,2,0:T(8,128)(2,1)} %param.19) | copy-start | bytes 1572868
  8.8 5.7 %collective-permute-start.4 = (bf16[512,128]{1,0:T(8,128)(2,1)S(1)}, bf16[512,128]{1,0:T(8,128)(2,1)S(1)}, u32[]{:S(2)}, u32[]{:S(2)}) collective-permute-start(bf16[512,128]{1,0:T(8,128)(2,1)S(1)} %get-tuple-element.36), channel_id=1, source_target_pairs={{0,4},{4,0},{8,12},{12,8},{1,5},{5,1},{9,13},{13,9},{2,6},{6,2},{1... | collective-permute-start | bytes 393224 | tf_op jit(solution)/shard_map/ppermute | solution.py:19
  11.1 3.7 %copy-start = (bf16[4,64,2048]{2,1,0:T(8,128)(2,1)S(1)}, bf16[4,64,2048]{2,1,0:T(8,128)(2,1)}, u32[]{:S(2)}) copy-start(bf16[4,64,2048]{2,1,0:T(8,128)(2,1)} %param.20) | copy-start | bytes 3145732
  11.1 3.7 %collective-permute-start.3 = (bf16[32,128]{1,0:T(8,128)(2,1)S(1)}, bf16[32,128]{1,0:T(8,128)(2,1)S(1)}, u32[]{:S(2)}, u32[]{:S(2)}) collective-permute-start(bf16[32,128]{1,0:T(8,128)(2,1)S(1)} %shrink.1), channel_id=1, source_target_pairs={{0,4},{4,0},{8,12},{12,8},{1,5},{5,1},{9,13},{13,9},{2,6},{6,2},{1... | collective-permute-start | bytes 24584 | tf_op jit(solution)/shard_map/ppermute | solution.py:19
  14.9 4.6 %collective-permute-start.6 = (bf16[4,64,2048]{2,1,0:T(8,128)(2,1)S(1)}, bf16[4,64,2048]{2,1,0:T(8,128)(2,1)S(1)}, u32[]{:S(2)}, u32[]{:S(2)}) collective-permute-start(bf16[4,64,2048]{2,1,0:T(8,128)(2,1)S(1)} %copy-done), channel_id=1, source_target_pairs={{0,1},{1,0},{2,3},{3,2},{4,5},{5,4},{6,7},{7,6},{8,9},{9,8},{10,11... | collective-permute-start | bytes 3145736 | tf_op jit(solution)/shard_map/ppermute | solution.py:19
  14.9 4.6 %collective-permute-start.5 = (bf16[32,128]{1,0:T(8,128)(2,1)S(1)}, bf16[32,128]{1,0:T(8,128)(2,1)S(1)}, u32[]{:S(2)}, u32[]{:S(2)}) collective-permute-start(bf16[32,128]{1,0:T(8,128)(2,1)S(1)} %add_convert_fusion.1.refs_4_), channel_id=1, source_target_pairs={{0,8},{4,12},{8,0},{12,4},{1,9},{5,13},{9,1},{13,5},{2,10},{6,14},... | collective-permute-start | bytes 24584 | tf_op jit(solution)/shard_map/ppermute | solution.py:19
  17.5 9.3 %collective-permute-start.7 = (bf16[512,128]{1,0:T(8,128)(2,1)S(1)}, bf16[512,128]{1,0:T(8,128)(2,1)S(1)}, u32[]{:S(2)}, u32[]{:S(2)}) collective-permute-start(bf16[512,128]{1,0:T(8,128)(2,1)S(1)} %add_convert_fusion), channel_id=1, source_target_pairs={{0,8},{4,12},{8,0},{12,4},{1,9},{5,13},{9,1},{13,5},{2,10},{6,14},... | collective-permute-start | bytes 393224 | tf_op jit(solution)/shard_map/ppermute | solution.py:19
  17.9 9.0 %collective-permute-start.8 = (bf16[512,128]{1,0:T(8,128)(2,1)S(1)}, bf16[512,128]{1,0:T(8,128)(2,1)S(1)}, u32[]{:S(2)}, u32[]{:S(2)}) collective-permute-start(bf16[512,128]{1,0:T(8,128)(2,1)S(1)} %get-tuple-element.47), channel_id=1, source_target_pairs={{0,4},{4,0},{8,12},{12,8},{1,5},{5,1},{9,13},{13,9},{2,6},{6,2},{1... | collective-permute-start | bytes 393224 | tf_op jit(solution)/shard_map/ppermute | solution.py:19
  20.0 6.9 %collective-permute-start.9 = (bf16[512,128]{1,0:T(8,128)(2,1)S(1)}, bf16[512,128]{1,0:T(8,128)(2,1)S(1)}, u32[]{:S(2)}, u32[]{:S(2)}) collective-permute-start(bf16[512,128]{1,0:T(8,128)(2,1)S(1)} %get-tuple-element.48), channel_id=1, source_target_pairs={{0,2},{1,3},{2,0},{3,1},{4,6},{5,7},{6,4},{7,5},{8,10},{9,11},{10,... | collective-permute-start | bytes 393224 | tf_op jit(solution)/shard_map/ppermute | solution.py:19

commit v12 on v8

--- a/solution.py
+++ b/solution.py
@@ -207,6 +207,47 @@
         out[at : at + rows] = part.astype(out.dtype)
 
 
+def fetch_kernel(ahead, tensor_at, tagged, early, out_weight, out, fetched, sem):
+    width, block = fetched.shape
+    column = pl.ds(pl.multiple_of((tensor_at[0] ^ ahead) * block, block), block)
+    copy = pltpu.make_async_copy(out_weight.at[:, column], fetched, sem)
+    copy.start()
+    piece = min(block, 512)
+    for start in range(0, block, piece):
+        columns = slice(start, start + piece)
+        term = jnp.dot(tagged[:, :width], early[:, columns], preferred_element_type=F32)
+        put_stacked(out, start, term)
+    copy.wait()
+
+
+def base_and_fetch(tensor_at, tagged, early, out_weight, ahead):
+    rows = tagged.shape[0]
+    width, block = early.shape
+    whole = pl.BlockSpec(memory_space=VMEM)
+    return pl.pallas_call(
+        functools.partial(fetch_kernel, ahead),
+        out_shape=[
+            jax.ShapeDtypeStruct((block // LANES * rows, LANES), BF16),
+            VMEM((width, block), BF16),
+        ],
+        in_specs=[
+            pl.BlockSpec(memory_space=pltpu.SMEM),
+            whole,
+            whole,
+            pl.BlockSpec(memory_space=pl.ANY),
+        ],
+        out_specs=[whole] * 2,
+        scratch_shapes=[pltpu.SemaphoreType.DMA],
+        compiler_params=pltpu.CompilerParams(vmem_limit_bytes=8 << 20),
+        cost_estimate=pl.CostEstimate(
+            flops=2 * rows * width * block,
+            bytes_accessed=4 * width * block,
+            transcendentals=0,
+        ),
+        name="base_and_fetch",
+    )(tensor_at, tagged, early, *in_hbm(out_weight))
+
+
 def base_kernel(ahead, deep, arriving, tensor_at, tagged, out_weight, *refs):
     arrived, (*near, out, held, sums, sems) = refs[:arriving], refs[arriving:]
     _, deep_rows, block = held.shape
@@ -248,7 +289,7 @@
             copy(at + deep).start()
 
 
-def base_block(tensor_at, tagged, out_weight, block, ahead, early=(), arrived=()):
+def base_block(tensor_at, tagged, out_weight, block, ahead, early=(), arrived=(), weight=1):
     rows = tagged.shape[0]
     width = out_weight.shape[0]
     deep, deep_rows = 4, min(width, 256)
@@ -268,8 +309,8 @@
         ],
         compiler_params=pltpu.CompilerParams(vmem_limit_bytes=12 << 20),
         cost_estimate=pl.CostEstimate(
-            flops=2 * rows * width * block * count,
-            bytes_accessed=2 * width * block * (2 if arrived else count),
+            flops=2 * rows * width * block * count * weight,
+            bytes_accessed=2 * width * block * count,
             transcendentals=0,
         ),
         name="base_terms",
@@ -502,17 +543,17 @@
     shrink_factors = [shrink_weight, to_sibling(shrink_weight)]
     expand_factors = [expand_weight, to_sibling(expand_weight)]
     visiting = [to_chip(tagged, shift) for shift in range(1, chips)]
-    third, next_door = base_block(tensor_at, tagged, out_weight, block, 1, [early])
-    visiting, third, next_door, limits = lax.optimization_barrier(
-        (visiting, third, next_door, limits)
-    )
+    third, fetched = base_and_fetch(tensor_at, tagged, early, out_weight, 2)
+    visiting, fetched, limits = lax.optimization_barrier((visiting, fetched, limits))
     blocks = [tagged] + visiting
     third = across(third, 1)
 
     part = shrink_part(blocks, shrink_factors, batch_at)
     parts = [part, across(part, 1)]
     part, later_tagged = lax.optimization_barrier((part, tagged))
-    (second,) = base_block(tensor_at, later_tagged, out_weight, block, 2)
+    second, next_door = base_block(
+        tensor_at, later_tagged, out_weight, block, 1, [fetched], (), 12
+    )
     second = (wide(second) + wide(third)).astype(BF16)
     parts, second = lax.optimization_barrier((parts, second))
     bit = 2

time: 27.1 us -> 31.2 us (1.15)
  local copies, waits for them, and re-layouts: 0.01 us -> 4.15 us
  starting transfers between devices: 11.8 us -> 10.7 us
  waiting for transfers between devices: 2.76 us -> 3.39 us
  Pallas kernels: 12.2 us -> 12.7 us
    unnamed x4 -> x8, local copies, waits for them, and re-layouts: 0.01 us -> 4.15 us
    pallas_call x0 -> x1, Pallas kernels: none -> 2.89 us  [base_and_fetch(): pl.pallas_call(functools.partial(fetch_kernel, ahead), out_shape=[jax.Sha...]
    pallas_call x3 -> x2, Pallas kernels: 7.59 us -> 5.12 us  [base_block(): pl.pallas_call(functools.partial(base_kernel, ahead, deep, len(arrived)),...]
    ppermute x10, starting transfers between devices: 11.8 us -> 10.7 us  [permuted(): return lax.ppermute(array, axis, [(i, partner(i)) for i in range(size)])]
    ppermute x10, waiting for transfers between devices: 2.76 us -> 3.39 us  [permuted(): return lax.ppermute(array, axis, [(i, partner(i)) for i in range(size)])]
  transfers between devices with their start and end apart: 10 -> 10, of which waited for: 2 -> 2; matrix products, arithmetic and copies ran while one was open for 0% -> 0% of each run, Pallas kernels for 43% -> 39%
where the time goes in v12:
time: 31.2 us; the launch traced here: 31 us
  Pallas kernels  12.7 us (41%)
  starting transfers between devices  10.7 us (34%)
  local copies, waits for them, and re-layouts  4.15 us (13%)
  waiting for transfers between devices  3.39 us (11%)
    ppermute x10, starting transfers between devices, permuted(): return lax.ppermute(array, axis, [(i, partner(i)) for i in range(size)])  10.7 us
    pallas_call x2, Pallas kernels, base_block(): pl.pallas_call(functools.partial(base_kernel, ahead, deep, len(arrived)),...  5.12 us
    unnamed x8, local copies, waits for them, and re-layouts  4.15 us
    ppermute x10, waiting for transfers between devices, permuted(): return lax.ppermute(array, axis, [(i, partner(i)) for i in range(size)])  3.39 us
    pallas_call x1, Pallas kernels, base_and_fetch(): pl.pallas_call(functools.partial(fetch_kernel, ahead), out_shape=[jax.Sha...  2.89 us
    pallas_call x1, Pallas kernels, attend(): pl.pallas_call(functools.partial(attend_kernel, parts, rank_width), out_s...  2.85 us
    pallas_call x1, Pallas kernels, total(): pl.pallas_call(total_kernel, out_shape=jax.ShapeDtypeStruct((rows, block)...  0.69 us
  transfers between devices with their start and end apart: 10, of which 2 were waited for; matrix products, arithmetic and copies ran while one was open for 0% of the time, Pallas kernels for 39%

profile of v12, /device:TPU:0, one launch (start us, length us, event | category | flops | bytes accessed | tf_op | source)
XLA Modules:
  0.0 31.0 jit_solution(13808546818990533146)
XLA Ops:
  0.0 0.5 %collective-permute-start.2 = (bf16[4,64,1024]{2,1,0:T(8,128)(2,1)}, bf16[4,64,1024]{2,1,0:T(8,128)(2,1)S(1)}, u32[]{:S(2)}, u32[]{:S(2)}) collective-permute-start(bf16[4,64,1024]{2,1,0:T(8,128)(2,1)} %bitcast.8), channel_id=1, source_target_pairs={{0,1},{1,0},{2,3},{3,2},{4,5},{5,4},{6,7},{7,6},{8,9},{9,8},{10,11... | collective-permute-start | bytes 1572872 | tf_op jit(solution)/shard_map/ppermute | solution.py:19
  0.5 0.1 collective-permute-start.6
  0.5 2.8 %attention.1 = (bf16[32,1152]{1,0:T(8,128)(2,1)S(1)}, bf16[1024,2048]{1,0:T(8,128)(2,1)S(1)}, s32[8,128]{1,0:T(8,128)S(1)}) custom-call(s32[1]{0:T(128)} %bitcast.2.group_at, s32[1]{0:T(128)S(6)} %xor.3.early_at, bf16[32,4,96,128]{3,2,1,0:T(8,128)(2,1)} %refs_0_.1, bf16[32,4,96,128]{3,2,1,0:T(8,128)(2,1)} %refs_1_.1, bf16[32,8,128]{2,1,0:T(8,128)(2,1)} %refs_2_.1, ...), custom_call_target="tpu_custom_call" | custom-call | flops 12582912 | bytes 1572864 | tf_op jit(solution)/shard_map/attention/pallas_call | solution.py:147
  3.4 3.0 %collective-permute-start = (bf16[32,1152]{1,0:T(8,128)(2,1)S(1)}, bf16[32,1152]{1,0:T(8,128)(2,1)S(1)}, u32[]{:S(2)}, u32[]{:S(2)}) collective-permute-start(bf16[32,1152]{1,0:T(8,128)(2,1)S(1)} %get-tuple-element.44.tagged.refs_0_.refs_2_), channel_id=1, source_target_pairs={{0,2},{1,3},{2,0},{3,1},{4,6},{5,7},{6,4},{7,5},{8,10},{9,11},{10,... | collective-permute-start | bytes 221192 | tf_op jit(solution)/shard_map/ppermute | solution.py:19
  6.4 0.0 collective-permute-start.1
  6.4 0.0 copy-start.3
  6.4 2.9 %base_and_fetch.1 = (bf16[512,128]{1,0:T(8,128)(2,1)S(1)}, bf16[1024,2048]{1,0:T(8,128)(2,1)S(1)}) custom-call(s32[1]{0:T(128)} %bitcast.tensor_at, bf16[32,1152]{1,0:T(8,128)(2,1)S(1)} %get-tuple-element.44.tagged.refs_0_.refs_2_, bf16[1024,2048]{1,0:T(8,128)(2,1)S(1)} %get-tuple-element.28.early, bf16[1024,8192]{1,0:T(8,128)(2,1)} %out_weight.5), custom_call_target="tpu_custom_call" | custom-call | flops 134217728 | bytes 8388608 | tf_op jit(solution)/shard_map/base_and_fetch/pallas_call | solution.py:227
  9.3 0.0 copy-start
  9.3 2.0 %copy-done = bf16[1024,2048]{1,0:T(8,128)(2,1)} copy-done((bf16[1024,2048]{1,0:T(8,128)(2,1)}, bf16[1024,2048]{1,0:T(8,128)(2,1)S(1)}, u32[]{:S(2)}) %copy-start) | copy-done | bytes 4194328
  11.2 1.6 %collective-permute-start.4 = (bf16[512,128]{1,0:T(8,128)(2,1)S(1)}, bf16[512,128]{1,0:T(8,128)(2,1)S(1)}, u32[]{:S(2)}, u32[]{:S(2)}) collective-permute-start(bf16[512,128]{1,0:T(8,128)(2,1)S(1)} %get-tuple-element.37), channel_id=1, source_target_pairs={{0,4},{4,0},{8,12},{12,8},{1,5},{5,1},{9,13},{13,9},{2,6},{6,2},{1... | collective-permute-start | bytes 393224 | tf_op jit(solution)/shard_map/ppermute | solution.py:19
  12.8 0.0 collective-permute-done.1.refs_1_
  12.8 0.0 collective-permute-done.refs_1_.refs_3_
  12.8 0.0 collective-permute-done.2.refs_3_
  12.8 0.0 copy-done.3
  12.8 0.5 %shrink.1 = bf16[32,128]{1,0:T(8,128)(2,1)S(1)} custom-call(s32[1]{0:T(128)} %bitcast.1.batch_at, bf16[32,1152]{1,0:T(8,128)(2,1)S(1)} %get-tuple-element.44.tagged.refs_0_.refs_2_, bf16[32,1152]{1,0:T(8,128)(2,1)S(1)} %collective-permute-done.refs_1_.refs_3_, bf16[4,64,1024]{2,1,0:T(8,128)(2,1)S(1)} %bitcast.9, ...), custom_call_target="tpu_custom_call" | custom-call | flops 67108864 | bytes 1179648 | tf_op jit(solution)/shard_map/shrink/pallas_call | solution.py:358
  13.4 0.5 %collective-permute-start.3 = (bf16[32,128]{1,0:T(8,128)(2,1)S(1)}, bf16[32,128]{1,0:T(8,128)(2,1)S(1)}, u32[]{:S(2)}, u32[]{:S(2)}) collective-permute-start(bf16[32,128]{1,0:T(8,128)(2,1)S(1)} %shrink.1), channel_id=1, source_target_pairs={{0,4},{4,0},{8,12},{12,8},{1,5},{5,1},{9,13},{13,9},{2,6},{6,2},{1... | collective-permute-start | bytes 24584 | tf_op jit(solution)/shard_map/ppermute | solution.py:19
  13.9 0.0 copy-start.1
  13.9 2.2 %copy-done.1 = bf16[1024,2048]{1,0:T(8,128)(2,1)S(1)} copy-done((bf16[1024,2048]{1,0:T(8,128)(2,1)S(1)}, bf16[1024,2048]{1,0:T(8,128)(2,1)}, u32[]{:S(2)}) %copy-start.1) | copy-done | bytes 4194328
  16.1 0.0 copy-start.2
  16.1 2.6 %base_terms.2 = (bf16[512,128]{1,0:T(8,128)(2,1)S(1)}, bf16[512,128]{1,0:T(8,128)(2,1)S(1)}) custom-call(s32[1]{0:T(128)} %bitcast.tensor_at, bf16[32,1152]{1,0:T(8,128)(2,1)S(1)} %get-tuple-element.44.tagged.refs_0_.refs_2_, bf16[1024,8192]{1,0:T(8,128)(2,1)} %out_weight.5, bf16[1024,2048]{1,0:T(8,128)(2,1)S(1)} %copy-done.1), custom_call_target="tpu_custom_call" | custom-call | flops 3221225472 | bytes 8388608 | tf_op jit(solution)/shard_map/base_terms/pallas_call | solution.py:298
  18.7 0.0 collective-permute-done.4
  18.7 0.0 collective-permute-done.3
  18.8 2.7 %collective-permute-start.5 = (bf16[32,128]{1,0:T(8,128)(2,1)S(1)}, bf16[32,128]{1,0:T(8,128)(2,1)S(1)}, u32[]{:S(2)}, u32[]{:S(2)}) collective-permute-start(bf16[32,128]{1,0:T(8,128)(2,1)S(1)} %add_convert_fusion.1.refs_4_), channel_id=1, source_target_pairs={{0,8},{4,12},{8,0},{12,4},{1,9},{5,13},{9,1},{13,5},{2,10},{6,14},... | collective-permute-start | bytes 24584 | tf_op jit(solution)/shard_map/ppermute | solution.py:19
  21.4 0.3 %collective-permute-start.7 = (bf16[512,128]{1,0:T(8,128)(2,1)S(1)}, bf16[512,128]{1,0:T(8,128)(2,1)S(1)}, u32[]{:S(2)}, u32[]{:S(2)}) collective-permute-start(bf16[512,128]{1,0:T(8,128)(2,1)S(1)} %add_convert_fusion), channel_id=1, source_target_pairs={{0,8},{4,12},{8,0},{12,4},{1,9},{5,13},{9,1},{13,5},{2,10},{6,14},... | collective-permute-start | bytes 393224 | tf_op jit(solution)/shard_map/ppermute | solution.py:19
  21.8 1.6 %collective-permute-start.8 = (bf16[512,128]{1,0:T(8,128)(2,1)S(1)}, bf16[512,128]{1,0:T(8,128)(2,1)S(1)}, u32[]{:S(2)}, u32[]{:S(2)}) collective-permute-start(bf16[512,128]{1,0:T(8,128)(2,1)S(1)} %get-tuple-element.47), channel_id=1, source_target_pairs={{0,4},{4,0},{8,12},{12,8},{1,5},{5,1},{9,13},{13,9},{2,6},{6,2},{1... | collective-permute-start | bytes 393224 | tf_op jit(solution)/shard_map/ppermute | solution.py:19
  23.3 0.1 collective-permute-done.5.refs_5_
  23.5 0.0 collective-permute-done.6
  23.5 0.0 copy-done.2
  23.5 0.5 %expand.1 = (bf16[512,128]{1,0:T(8,128)(2,1)S(1)}, bf16[512,128]{1,0:T(8,128)(2,1)S(1)}) custom-call(s32[1]{0:T(128)} %bitcast.1.batch_at, s32[8,128]{1,0:T(8,128)S(1)} %get-tuple-element.31.refs_0_, s32[8,128]{1,0:T(8,128)S(1)} %collective-permute-done.1.refs_1_, bf16[32,1152]{1,0:T(8,128)(2,1)S(1)} %get-tuple-element.44.tagged.refs_0_.refs_2_, ...), custom_call_target="tpu_custom_call" | custom-call | flops 134217728 | bytes 1048576 | tf_op jit(solution)/shard_map/expand/pallas_call | solution.py:418
  24.0 0.5 %collective-permute-start.9 = (bf16[512,128]{1,0:T(8,128)(2,1)S(1)}, bf16[512,128]{1,0:T(8,128)(2,1)S(1)}, u32[]{:S(2)}, u32[]{:S(2)}) collective-permute-start(bf16[512,128]{1,0:T(8,128)(2,1)S(1)} %get-tuple-element.48), channel_id=1, source_target_pairs={{0,2},{1,3},{2,0},{3,1},{4,6},{5,7},{6,4},{7,5},{8,10},{9,11},{10,... | collective-permute-start | bytes 393224 | tf_op jit(solution)/shard_map/ppermute | solution.py:19
  24.5 2.5 %base_terms.3.refs_0_ = f32[512,128]{1,0:T(8,128)S(1)} custom-call(s32[1]{0:T(128)} %bitcast.tensor_at, bf16[32,1152]{1,0:T(8,128)(2,1)S(1)} %get-tuple-element.44.tagged.refs_0_.refs_2_, bf16[1024,8192]{1,0:T(8,128)(2,1)} %out_weight.5), custom_call_target="tpu_custom_call" | custom-call | flops 134217728 | bytes 4194304 | tf_op jit(solution)/shard_map/base_terms/pallas_call | solution.py:298
  27.0 3.2 %collective-permute-done.7.refs_2_ = bf16[512,128]{1,0:T(8,128)(2,1)S(1)} collective-permute-done((bf16[512,128]{1,0:T(8,128)(2,1)S(1)}, bf16[512,128]{1,0:T(8,128)(2,1)S(1)}, u32[]{:S(2)}, u32[]{:S(2)}) %collective-permute-start.7) | collective-permute-done | bytes 131104 | tf_op jit(solution)/shard_map/ppermute | solution.py:19
  30.3 0.0 collective-permute-done.8.refs_1_
  30.3 0.0 collective-permute-done.9.refs_1_
  30.3 0.7 %total.1 = bf16[32,2048]{1,0:T(8,128)(2,1)} custom-call(f32[512,128]{1,0:T(8,128)S(1)} %partial_total.3.refs_0_, bf16[512,128]{1,0:T(8,128)(2,1)S(1)} %collective-permute-done.9.refs_1_), custom_call_target="tpu_custom_call" | custom-call | flops 131072 | bytes 393216 | tf_op jit(solution)/shard_map/total/pallas_call | solution.py:451
  (4 shorter events, 0.1 us)
Async XLA Ops:
  0.0 12.8 %collective-permute-start.2 = (bf16[4,64,1024]{2,1,0:T(8,128)(2,1)}, bf16[4,64,1024]{2,1,0:T(8,128)(2,1)S(1)}, u32[]{:S(2)}, u32[]{:S(2)}) collective-permute-start(bf16[4,64,1024]{2,1,0:T(8,128)(2,1)} %bitcast.8), channel_id=1, source_target_pairs={{0,1},{1,0},{2,3},{3,2},{4,5},{5,4},{6,7},{7,6},{8,9},{9,8},{10,11... | collective-permute-start | bytes 1572872 | tf_op jit(solution)/shard_map/ppermute | solution.py:19
  0.5 23.0 %collective-permute-start.6 = (bf16[4,64,2048]{2,1,0:T(8,128)(2,1)}, bf16[4,64,2048]{2,1,0:T(8,128)(2,1)S(1)}, u32[]{:S(2)}, u32[]{:S(2)}) collective-permute-start(bf16[4,64,2048]{2,1,0:T(8,128)(2,1)} %param.20), channel_id=1, source_target_pairs={{0,1},{1,0},{2,3},{3,2},{4,5},{5,4},{6,7},{7,6},{8,9},{9,8},{10,11... | collective-permute-start | bytes 3145736 | tf_op jit(solution)/shard_map/ppermute | solution.py:19
  3.4 9.5 %collective-permute-start = (bf16[32,1152]{1,0:T(8,128)(2,1)S(1)}, bf16[32,1152]{1,0:T(8,128)(2,1)S(1)}, u32[]{:S(2)}, u32[]{:S(2)}) collective-permute-start(bf16[32,1152]{1,0:T(8,128)(2,1)S(1)} %get-tuple-element.44.tagged.refs_0_.refs_2_), channel_id=1, source_target_pairs={{0,2},{1,3},{2,0},{3,1},{4,6},{5,7},{6,4},{7,5},{8,10},{9,11},{10,... | collective-permute-start | bytes 221192 | tf_op jit(solution)/shard_map/ppermute | solution.py:19
  6.4 6.4 %collective-permute-start.1 = (s32[8,128]{1,0:T(8,128)S(1)}, s32[8,128]{1,0:T(8,128)S(1)}, u32[]{:S(2)}, u32[]{:S(2)}) collective-permute-start(s32[8,128]{1,0:T(8,128)S(1)} %get-tuple-element.31.refs_0_), channel_id=1, source_target_pairs={{0,1},{1,0},{2,3},{3,2},{4,5},{5,4},{6,7},{7,6},{8,9},{9,8},{10,11... | collective-permute-start | bytes 12296 | tf_op jit(solution)/shard_map/ppermute | solution.py:19
  6.4 6.5 %copy-start.3 = (bf16[4,1024,64]{1,2,0:T(8,128)(2,1)S(1)}, bf16[4,1024,64]{1,2,0:T(8,128)(2,1)}, u32[]{:S(2)}) copy-start(bf16[4,1024,64]{1,2,0:T(8,128)(2,1)} %param.19) | copy-start | bytes 1572868
  9.3 2.0 %copy-start = (bf16[1024,2048]{1,0:T(8,128)(2,1)}, bf16[1024,2048]{1,0:T(8,128)(2,1)S(1)}, u32[]{:S(2)}) copy-start(bf16[1024,2048]{1,0:T(8,128)(2,1)S(1)} %get-tuple-element.35.refs_0_) | copy-start | bytes 12582916
  11.2 7.4 %collective-permute-start.4 = (bf16[512,128]{1,0:T(8,128)(2,1)S(1)}, bf16[512,128]{1,0:T(8,128)(2,1)S(1)}, u32[]{:S(2)}, u32[]{:S(2)}) collective-permute-start(bf16[512,128]{1,0:T(8,128)(2,1)S(1)} %get-tuple-element.37), channel_id=1, source_target_pairs={{0,4},{4,0},{8,12},{12,8},{1,5},{5,1},{9,13},{13,9},{2,6},{6,2},{1... | collective-permute-start | bytes 393224 | tf_op jit(solution)/shard_map/ppermute | solution.py:19
  13.4 5.4 %collective-permute-start.3 = (bf16[32,128]{1,0:T(8,128)(2,1)S(1)}, bf16[32,128]{1,0:T(8,128)(2,1)S(1)}, u32[]{:S(2)}, u32[]{:S(2)}) collective-permute-start(bf16[32,128]{1,0:T(8,128)(2,1)S(1)} %shrink.1), channel_id=1, source_target_pairs={{0,4},{4,0},{8,12},{12,8},{1,5},{5,1},{9,13},{13,9},{2,6},{6,2},{1... | collective-permute-start | bytes 24584 | tf_op jit(solution)/shard_map/ppermute | solution.py:19
  13.9 2.2 %copy-start.1 = (bf16[1024,2048]{1,0:T(8,128)(2,1)S(1)}, bf16[1024,2048]{1,0:T(8,128)(2,1)}, u32[]{:S(2)}) copy-start(bf16[1024,2048]{1,0:T(8,128)(2,1)} %copy-done) | copy-start | bytes 12582916
  16.1 7.4 %copy-start.2 = (bf16[4,64,2048]{2,1,0:T(8,128)(2,1)S(1)}, bf16[4,64,2048]{2,1,0:T(8,128)(2,1)}, u32[]{:S(2)}) copy-start(bf16[4,64,2048]{2,1,0:T(8,128)(2,1)} %param.20) | copy-start | bytes 3145732
  18.8 4.7 %collective-permute-start.5 = (bf16[32,128]{1,0:T(8,128)(2,1)S(1)}, bf16[32,128]{1,0:T(8,128)(2,1)S(1)}, u32[]{:S(2)}, u32[]{:S(2)}) collective-permute-start(bf16[32,128]{1,0:T(8,128)(2,1)S(1)} %add_convert_fusion.1.refs_4_), channel_id=1, source_target_pairs={{0,8},{4,12},{8,0},{12,4},{1,9},{5,13},{9,1},{13,5},{2,10},{6,14},... | collective-permute-start | bytes 24584 | tf_op jit(solution)/shard_map/ppermute | solution.py:19
  21.4 8.8 %collective-permute-start.7 = (bf16[512,128]{1,0:T(8,128)(2,1)S(1)}, bf16[512,128]{1,0:T(8,128)(2,1)S(1)}, u32[]{:S(2)}, u32[]{:S(2)}) collective-permute-start(bf16[512,128]{1,0:T(8,128)(2,1)S(1)} %add_convert_fusion), channel_id=1, source_target_pairs={{0,8},{4,12},{8,0},{12,4},{1,9},{5,13},{9,1},{13,5},{2,10},{6,14},... | collective-permute-start | bytes 393224 | tf_op jit(solution)/shard_map/ppermute | solution.py:19
  21.8 8.5 %collective-permute-start.8 = (bf16[512,128]{1,0:T(8,128)(2,1)S(1)}, bf16[512,128]{1,0:T(8,128)(2,1)S(1)}, u32[]{:S(2)}, u32[]{:S(2)}) collective-permute-start(bf16[512,128]{1,0:T(8,128)(2,1)S(1)} %get-tuple-element.47), channel_id=1, source_target_pairs={{0,4},{4,0},{8,12},{12,8},{1,5},{5,1},{9,13},{13,9},{2,6},{6,2},{1... | collective-permute-start | bytes 393224 | tf_op jit(solution)/shard_map/ppermute | solution.py:19
  24.0 6.3 %collective-permute-start.9 = (bf16[512,128]{1,0:T(8,128)(2,1)S(1)}, bf16[512,128]{1,0:T(8,128)(2,1)S(1)}, u32[]{:S(2)}, u32[]{:S(2)}) collective-permute-start(bf16[512,128]{1,0:T(8,128)(2,1)S(1)} %get-tuple-element.48), channel_id=1, source_target_pairs={{0,2},{1,3},{2,0},{3,1},{4,6},{5,7},{6,4},{7,5},{8,10},{9,11},{10,... | collective-permute-start | bytes 393224 | tf_op jit(solution)/shard_map/ppermute | solution.py:19

commit v13 on v8

--- a/solution.py
+++ b/solution.py
@@ -197,83 +197,47 @@
     return tagged, early, limits
 
 
-def put_stacked(out, start, term, first=0, others=()):
+def put_stacked(out, start, term):
     rows = term.shape[0]
     for column in range(0, term.shape[1], LANES):
-        at = first + (start + column) // LANES * rows
-        part = term[:, column : column + LANES]
-        for other in others:
-            part = part + other[at : at + rows].astype(F32)
-        out[at : at + rows] = part.astype(out.dtype)
-
-
-def base_kernel(ahead, deep, arriving, tensor_at, tagged, out_weight, *refs):
-    arrived, (*near, out, held, sums, sems) = refs[:arriving], refs[arriving:]
-    _, deep_rows, block = held.shape
-    width = out_weight.shape[0]
-    count = width // deep_rows
-    column = pl.ds(pl.multiple_of((tensor_at[0] ^ ahead) * block, block), block)
-
-    def copy(at):
-        return pltpu.make_async_copy(
-            out_weight.at[pl.ds(at * deep_rows, deep_rows), column],
-            held.at[at % deep],
-            sems.at[at % deep],
-        )
-
-    for at in range(min(deep, count)):
-        copy(at).start()
-    piece = min(block, 512)
-    if near:
-        early, early_out = near
-        for start in range(0, block, piece):
-            columns = slice(start, start + piece)
-            term = jnp.dot(tagged[:, :width], early[:, columns], preferred_element_type=F32)
-            put_stacked(early_out, start, term)
-    for at in range(count):
-        copy(at).wait()
-        inputs = slice(at * deep_rows, (at + 1) * deep_rows)
-        for start in range(0, block, piece):
-            columns = slice(start, start + piece)
+        at = (start + column) // LANES * rows
+        out[at : at + rows] = term[:, column : column + LANES].astype(out.dtype)
+
+
+def base_kernel(apart, piece, tensor_at, tagged, weight, *outs):
+    width = weight.shape[0]
+    for ahead, out in zip(apart, outs):
+        block = out.shape[0] // tagged.shape[0] * LANES
+        for at in range(0, block, piece):
+            start = at
+            if weight.shape[1] > block:
+                start = pl.multiple_of((tensor_at[0] ^ ahead) * block + at, piece)
             term = jnp.dot(
-                tagged[:, inputs], held[at % deep, :, columns], preferred_element_type=F32
+                tagged[:, :width], weight[:, pl.ds(start, piece)], preferred_element_type=F32
             )
-            if at:
-                term = term + sums[:, columns]
-            if at < count - 1:
-                sums[:, columns] = term
-            else:
-                put_stacked(out, start, term, 0, arrived)
-        if at + deep < count:
-            copy(at + deep).start()
-
-
-def base_block(tensor_at, tagged, out_weight, block, ahead, early=(), arrived=()):
+            put_stacked(out, at, term)
+
+
+def base_terms(tensor_at, tagged, weight, block, apart, cost):
     rows = tagged.shape[0]
-    width = out_weight.shape[0]
-    deep, deep_rows = 4, min(width, 256)
+    width = weight.shape[0]
     whole = pl.BlockSpec(memory_space=VMEM)
-    count = 1 + len(early)
     return pl.pallas_call(
-        functools.partial(base_kernel, ahead, deep, len(arrived)),
-        out_shape=[jax.ShapeDtypeStruct((block // LANES * rows, LANES), BF16 if ahead else F32)]
-        * count,
-        in_specs=[pl.BlockSpec(memory_space=pltpu.SMEM), whole, pl.BlockSpec(memory_space=pl.ANY)]
-        + [whole] * (len(arrived) + len(early)),
-        out_specs=[whole] * count,
-        scratch_shapes=[
-            VMEM((deep, deep_rows, block), BF16),
-            VMEM((rows, block), F32),
-            pltpu.SemaphoreType.DMA((deep,)),
+        functools.partial(base_kernel, apart, min(block, 512)),
+        out_shape=[
+            jax.ShapeDtypeStruct((block // LANES * rows, LANES), BF16 if ahead else F32)
+            for ahead in apart
         ],
-        compiler_params=pltpu.CompilerParams(vmem_limit_bytes=12 << 20),
+        in_specs=[pl.BlockSpec(memory_space=pltpu.SMEM), whole, whole],
+        out_specs=[whole] * len(apart),
+        compiler_params=pltpu.CompilerParams(vmem_limit_bytes=6 << 20),
         cost_estimate=pl.CostEstimate(
-            flops=2 * rows * width * block * count,
-            bytes_accessed=2 * width * block * (2 if arrived else count),
+            flops=cost * rows * width * block * len(apart),
+            bytes_accessed=2 * width * block * len(apart),
             transcendentals=0,
         ),
         name="base_terms",
-    )(tensor_at, tagged, *in_hbm(out_weight), *arrived, *early)
+    )(tensor_at, tagged, weight)
 
 
 def slots_of(tags, batch_at, pool, tile, per):
@@ -502,17 +466,16 @@
     shrink_factors = [shrink_weight, to_sibling(shrink_weight)]
     expand_factors = [expand_weight, to_sibling(expand_weight)]
     visiting = [to_chip(tagged, shift) for shift in range(1, chips)]
-    third, next_door = base_block(tensor_at, tagged, out_weight, block, 1, [early])
-    visiting, third, next_door, limits = lax.optimization_barrier(
-        (visiting, third, next_door, limits)
-    )
+    weight = pltpu.with_memory_space_constraint(out_weight, VMEM)
+    (third,) = base_terms(tensor_at, tagged, early, block, [3], 120)
+    visiting, limits = lax.optimization_barrier((visiting, limits))
     blocks = [tagged] + visiting
     third = across(third, 1)
 
     part = shrink_part(blocks, shrink_factors, batch_at)
     parts = [part, across(part, 1)]
     part, later_tagged = lax.optimization_barrier((part, tagged))
-    (second,) = base_block(tensor_at, later_tagged, out_weight, block, 2)
+    second, next_door = base_terms(tensor_at, later_tagged, weight, block, [2, 1], 20)
     second = (wide(second) + wide(third)).astype(BF16)
     parts, second = lax.optimization_barrier((parts, second))
     bit = 2
@@ -523,13 +486,12 @@
         bit *= 2
     arrived = [across(second, 2), across(next_door, 1)]
     for ahead in range(4, tensor_size, 2):
-        (near,) = base_block(tensor_at, tagged, out_weight, block, ahead)
-        (far,) = base_block(tensor_at, tagged, out_weight, block, ahead + 1)
+        near, far = base_terms(tensor_at, tagged, weight, block, [ahead, ahead + 1], 20)
         arrived.append(across((wide(near) + wide(across(far, 1))).astype(BF16), ahead))
 
     deltas = expand(blocks, parts, expand_factors, limits, batch_at)
     deltas, late_tagged = lax.optimization_barrier((deltas, tagged))
-    (own,) = base_block(tensor_at, late_tagged, out_weight, block, 0)
+    (own,) = base_terms(tensor_at, late_tagged, weight, block, [0], 20)
     so_far = partial_total([own, deltas[0], arrived[0], *arrived[2:]], 0)
     terms = [partial_total([so_far, arrived[1]], 8 << 20)]
     terms += [to_chip(home, -shift) for shift, home in enumerate(deltas[1:], 1)]

time: 27.1 us -> 31.6 us (1.17)
  local copies, waits for them, and re-layouts: 0.01 us -> 5.78 us
  Pallas kernels: 12.2 us -> 7.94 us
  other arithmetic: 0.04 us -> 1.59 us
  waiting for transfers between devices: 2.76 us -> 4.22 us
    unnamed x4 -> x8, local copies, waits for them, and re-layouts: 0.01 us -> 5.78 us
    pallas_call x3, Pallas kernels: 7.59 us -> 3.16 us  [base_terms(): pl.pallas_call(functools.partial(base_kernel, apart, min(block, 512)), ou...]
    convert_element_type x1, other arithmetic: 0.04 us -> 1.58 us  [local(): second = (wide(second) + wide(third)).astype(BF16)]
    ppermute x10, waiting for transfers between devices: 2.76 us -> 4.22 us  [permuted(): return lax.ppermute(array, axis, [(i, partner(i)) for i in range(size)])]
  transfers between devices with their start and end apart: 10 -> 10, of which waited for: 2 -> 2; matrix products, arithmetic and copies ran while one was open for 0% -> 5% of each run, Pallas kernels for 43% -> 14%
where the time goes in v13:
time: 31.6 us; the launch traced here: 31.5 us
  starting transfers between devices  11.9 us (38%)
  Pallas kernels  7.94 us (25%)
  local copies, waits for them, and re-layouts  5.78 us (18%)
  waiting for transfers between devices  4.22 us (13%)
  other arithmetic  1.59 us (5%)
    ppermute x10, starting transfers between devices, permuted(): return lax.ppermute(array, axis, [(i, partner(i)) for i in range(size)])  11.9 us
    unnamed x8, local copies, waits for them, and re-layouts  5.78 us
    ppermute x10, waiting for transfers between devices, permuted(): return lax.ppermute(array, axis, [(i, partner(i)) for i in range(size)])  4.22 us
    pallas_call x3, Pallas kernels, base_terms(): pl.pallas_call(functools.partial(base_kernel, apart, min(block, 512)), ou...  3.16 us
    pallas_call x1, Pallas kernels, attend(): pl.pallas_call(functools.partial(attend_kernel, parts, rank_width), out_s...  2.97 us
    convert_element_type x1, other arithmetic, local(): second = (wide(second) + wide(third)).astype(BF16)  1.58 us
    pallas_call x1, Pallas kernels, total(): pl.pallas_call(total_kernel, out_shape=jax.ShapeDtypeStruct((rows, block)...  0.68 us
  transfers between devices with their start and end apart: 10, of which 2 were waited for; matrix products, arithmetic and copies ran while one was open for 5% of the time, Pallas kernels for 14%

profile of v13, /device:TPU:0, one launch (start us, length us, event | category | flops | bytes accessed | tf_op | source)
XLA Modules:
  0.0 31.5 jit_solution(13258821686765527304)
XLA Ops:
  0.0 0.0 copy-start.3
  0.0 0.0 copy-start.2
  0.0 3.0 %attention.1 = (bf16[32,1152]{1,0:T(8,128)(2,1)S(1)}, bf16[1024,2048]{1,0:T(8,128)(2,1)S(1)}, s32[8,128]{1,0:T(8,128)S(1)}) custom-call(s32[1]{0:T(128)} %bitcast.2.group_at, s32[1]{0:T(128)S(6)} %xor.3.early_at, bf16[32,4,96,128]{3,2,1,0:T(8,128)(2,1)} %refs_0_.1, bf16[32,4,96,128]{3,2,1,0:T(8,128)(2,1)} %refs_1_.1, bf16[32,8,128]{2,1,0:T(8,128)(2,1)} %refs_2_.1, ...), custom_call_target="tpu_custom_call" | custom-call | flops 12582912 | bytes 1572864 | tf_op jit(solution)/shard_map/attention/pallas_call | solution.py:147
  3.0 3.0 %collective-permute-start = (bf16[32,1152]{1,0:T(8,128)(2,1)S(1)}, bf16[32,1152]{1,0:T(8,128)(2,1)S(1)}, u32[]{:S(2)}, u32[]{:S(2)}) collective-permute-start(bf16[32,1152]{1,0:T(8,128)(2,1)S(1)} %get-tuple-element.38.refs_0_.tagged.refs_2_), channel_id=1, source_target_pairs={{0,2},{1,3},{2,0},{3,1},{4,6},{5,7},{6,4},{7,5},{8,10},{9,11},{10,... | collective-permute-start | bytes 221192 | tf_op jit(solution)/shard_map/ppermute | solution.py:19
  6.0 0.0 collective-permute-start.1
  6.0 0.0 copy-done.3
  6.0 0.5 %collective-permute-start.2 = (bf16[4,64,1024]{2,1,0:T(8,128)(2,1)S(1)}, bf16[4,64,1024]{2,1,0:T(8,128)(2,1)S(1)}, u32[]{:S(2)}, u32[]{:S(2)}) collective-permute-start(bf16[4,64,1024]{2,1,0:T(8,128)(2,1)S(1)} %bitcast.8), channel_id=1, source_target_pairs={{0,1},{1,0},{2,3},{3,2},{4,5},{5,4},{6,7},{7,6},{8,9},{9,8},{10,11... | collective-permute-start | bytes 1572872 | tf_op jit(solution)/shard_map/ppermute | solution.py:19
  6.5 0.0 copy-done.2
  6.5 0.1 collective-permute-start.6
  6.6 0.8 %base_terms.4 = bf16[512,128]{1,0:T(8,128)(2,1)S(1)} custom-call(s32[1]{0:T(128)} %bitcast.tensor_at, bf16[32,1152]{1,0:T(8,128)(2,1)S(1)} %get-tuple-element.38.refs_0_.tagged.refs_2_, bf16[1024,2048]{1,0:T(8,128)(2,1)S(1)} %get-tuple-element.31.weight), custom_call_target="tpu_custom_call" | custom-call | flops 8053063680 | bytes 4194304 | tf_op jit(solution)/shard_map/base_terms/pallas_call | solution.py:225
  7.4 1.6 %collective-permute-start.4 = (bf16[512,128]{1,0:T(8,128)(2,1)S(1)}, bf16[512,128]{1,0:T(8,128)(2,1)}, u32[]{:S(2)}, u32[]{:S(2)}) collective-permute-start(bf16[512,128]{1,0:T(8,128)(2,1)S(1)} %base_terms.4), channel_id=1, source_target_pairs={{0,4},{4,0},{8,12},{12,8},{1,5},{5,1},{9,13},{13,9},{2,6},{6,2},{1... | collective-permute-start | bytes 393224 | tf_op jit(solution)/shard_map/ppermute | solution.py:19
  9.0 0.0 collective-permute-done.1.refs_1_
  9.0 0.0 collective-permute-done.refs_1_.refs_3_
  9.0 0.0 collective-permute-done.2.refs_3_
  9.0 0.5 %shrink.1 = bf16[32,128]{1,0:T(8,128)(2,1)S(1)} custom-call(s32[1]{0:T(128)} %bitcast.1.batch_at, bf16[32,1152]{1,0:T(8,128)(2,1)S(1)} %get-tuple-element.38.refs_0_.tagged.refs_2_, bf16[32,1152]{1,0:T(8,128)(2,1)S(1)} %collective-permute-done.refs_1_.refs_3_, bf16[4,64,1024]{2,1,0:T(8,128)(2,1)S(1)} %bitcast.9, ...), custom_call_target="tpu_custom_call" | custom-call | flops 67108864 | bytes 1179648 | tf_op jit(solution)/shard_map/shrink/pallas_call | solution.py:281
  9.5 1.5 %collective-permute-start.3 = (bf16[32,128]{1,0:T(8,128)(2,1)S(1)}, bf16[32,128]{1,0:T(8,128)(2,1)S(1)}, u32[]{:S(2)}, u32[]{:S(2)}) collective-permute-start(bf16[32,128]{1,0:T(8,128)(2,1)S(1)} %shrink.1), channel_id=1, source_target_pairs={{0,4},{4,0},{8,12},{12,8},{1,5},{5,1},{9,13},{13,9},{2,6},{6,2},{1... | collective-permute-start | bytes 24584 | tf_op jit(solution)/shard_map/ppermute | solution.py:19
  11.0 0.0 copy-start
  11.0 5.8 %copy-done = bf16[1024,8192]{1,0:T(8,128)(2,1)S(1)} copy-done((bf16[1024,8192]{1,0:T(8,128)(2,1)S(1)}, bf16[1024,8192]{1,0:T(8,128)(2,1)}, u32[]{:S(2)}) %copy-start) | copy-done | bytes 16777240
  16.8 0.0 copy-start.1
  16.8 1.5 %base_terms.3 = (bf16[512,128]{1,0:T(8,128)(2,1)S(1)}, bf16[512,128]{1,0:T(8,128)(2,1)S(1)}) custom-call(s32[1]{0:T(128)} %bitcast.tensor_at, bf16[32,1152]{1,0:T(8,128)(2,1)S(1)} %get-tuple-element.38.refs_0_.tagged.refs_2_, bf16[1024,8192]{1,0:T(8,128)(2,1)S(1)} %copy-done), custom_call_target="tpu_custom_call" | custom-call | flops 2684354560 | bytes 8388608 | tf_op jit(solution)/shard_map/base_terms/pallas_call | solution.py:225
  18.3 0.0 collective-permute-done.4
  18.3 1.6 %add_convert_fusion = bf16[512,128]{1,0:T(8,128)(2,1)S(1)} fusion(bf16[512,128]{1,0:T(8,128)(2,1)} %collective-permute-done.4, bf16[512,128]{1,0:T(8,128)(2,1)S(1)} %get-tuple-element.30), kind=kLoop, calls=%fused_computation | loop fusion | flops 262144 | bytes 393216 | tf_op jit(solution)/shard_map/convert_element_type | solution.py:479
  19.9 0.0 collective-permute-done.3
  19.9 2.7 %collective-permute-start.5 = (bf16[32,128]{1,0:T(8,128)(2,1)S(1)}, bf16[32,128]{1,0:T(8,128)(2,1)S(1)}, u32[]{:S(2)}, u32[]{:S(2)}) collective-permute-start(bf16[32,128]{1,0:T(8,128)(2,1)S(1)} %add_convert_fusion.1.refs_4_), channel_id=1, source_target_pairs={{0,8},{4,12},{8,0},{12,4},{1,9},{5,13},{9,1},{13,5},{2,10},{6,14},... | collective-permute-start | bytes 24584 | tf_op jit(solution)/shard_map/ppermute | solution.py:19
  22.6 0.3 %collective-permute-start.7 = (bf16[512,128]{1,0:T(8,128)(2,1)S(1)}, bf16[512,128]{1,0:T(8,128)(2,1)S(1)}, u32[]{:S(2)}, u32[]{:S(2)}) collective-permute-start(bf16[512,128]{1,0:T(8,128)(2,1)S(1)} %add_convert_fusion), channel_id=1, source_target_pairs={{0,8},{4,12},{8,0},{12,4},{1,9},{5,13},{9,1},{13,5},{2,10},{6,14},... | collective-permute-start | bytes 393224 | tf_op jit(solution)/shard_map/ppermute | solution.py:19
  22.9 0.6 %collective-permute-start.8 = (bf16[512,128]{1,0:T(8,128)(2,1)S(1)}, bf16[512,128]{1,0:T(8,128)(2,1)S(1)}, u32[]{:S(2)}, u32[]{:S(2)}) collective-permute-start(bf16[512,128]{1,0:T(8,128)(2,1)S(1)} %get-tuple-element.41), channel_id=1, source_target_pairs={{0,4},{4,0},{8,12},{12,8},{1,5},{5,1},{9,13},{13,9},{2,6},{6,2},{1... | collective-permute-start | bytes 393224 | tf_op jit(solution)/shard_map/ppermute | solution.py:19
  23.5 1.1 %collective-permute-done.5.refs_5_ = bf16[32,128]{1,0:T(8,128)(2,1)S(1)} collective-permute-done((bf16[32,128]{1,0:T(8,128)(2,1)S(1)}, bf16[32,128]{1,0:T(8,128)(2,1)S(1)}, u32[]{:S(2)}, u32[]{:S(2)}) %collective-permute-start.5) | collective-permute-done | bytes 8224 | tf_op jit(solution)/shard_map/ppermute | solution.py:19
  24.7 0.0 collective-permute-done.6
  24.7 0.5 %expand.1 = (bf16[512,128]{1,0:T(8,128)(2,1)S(1)}, bf16[512,128]{1,0:T(8,128)(2,1)S(1)}) custom-call(s32[1]{0:T(128)} %bitcast.1.batch_at, s32[8,128]{1,0:T(8,128)S(1)} %get-tuple-element.26.refs_0_, s32[8,128]{1,0:T(8,128)S(1)} %collective-permute-done.1.refs_1_, bf16[32,1152]{1,0:T(8,128)(2,1)S(1)} %get-tuple-element.38.refs_0_.tagged.refs_2_, ...), custom_call_target="tpu_custom_call" | custom-call | flops 134217728 | bytes 1048576 | tf_op jit(solution)/shard_map/expand/pallas_call | solution.py:341
  25.2 1.6 %collective-permute-start.9 = (bf16[512,128]{1,0:T(8,128)(2,1)S(1)}, bf16[512,128]{1,0:T(8,128)(2,1)S(1)}, u32[]{:S(2)}, u32[]{:S(2)}) collective-permute-start(bf16[512,128]{1,0:T(8,128)(2,1)S(1)} %get-tuple-element.42), channel_id=1, source_target_pairs={{0,2},{1,3},{2,0},{3,1},{4,6},{5,7},{6,4},{7,5},{8,10},{9,11},{10,... | collective-permute-start | bytes 393224 | tf_op jit(solution)/shard_map/ppermute | solution.py:19
  26.8 0.0 copy-done.1
  26.8 0.8 %base_terms.5.refs_0_ = f32[512,128]{1,0:T(8,128)S(1)} custom-call(s32[1]{0:T(128)} %bitcast.tensor_at, bf16[32,1152]{1,0:T(8,128)(2,1)S(1)} %get-tuple-element.38.refs_0_.tagged.refs_2_, bf16[1024,8192]{1,0:T(8,128)(2,1)S(1)} %copy-done.1), custom_call_target="tpu_custom_call" | custom-call | flops 1342177280 | bytes 4194304 | tf_op jit(solution)/shard_map/base_terms/pallas_call | solution.py:225
  27.7 3.0 %collective-permute-done.7.refs_2_ = bf16[512,128]{1,0:T(8,128)(2,1)S(1)} collective-permute-done((bf16[512,128]{1,0:T(8,128)(2,1)S(1)}, bf16[512,128]{1,0:T(8,128)(2,1)S(1)}, u32[]{:S(2)}, u32[]{:S(2)}) %collective-permute-start.7) | collective-permute-done | bytes 131104 | tf_op jit(solution)/shard_map/ppermute | solution.py:19
  30.7 0.1 partial_total.2.refs_0_
  30.8 0.0 collective-permute-done.8.refs_1_
  30.8 0.0 collective-permute-done.9.refs_1_
  30.8 0.7 %total.1 = bf16[32,2048]{1,0:T(8,128)(2,1)} custom-call(f32[512,128]{1,0:T(8,128)S(1)} %partial_total.3.refs_0_, bf16[512,128]{1,0:T(8,128)(2,1)S(1)} %collective-permute-done.9.refs_1_), custom_call_target="tpu_custom_call" | custom-call | flops 131072 | bytes 393216 | tf_op jit(solution)/shard_map/total/pallas_call | solution.py:374
  (2 shorter events, 0.0 us)
Async XLA Ops:
  0.0 6.0 %copy-start.3 = (bf16[4,1024,64]{1,2,0:T(8,128)(2,1)S(1)}, bf16[4,1024,64]{1,2,0:T(8,128)(2,1)}, u32[]{:S(2)}) copy-start(bf16[4,1024,64]{1,2,0:T(8,128)(2,1)} %param.19) | copy-start | bytes 1572868
  0.0 6.5 %copy-start.2 = (bf16[4,64,2048]{2,1,0:T(8,128)(2,1)S(1)}, bf16[4,64,2048]{2,1,0:T(8,128)(2,1)}, u32[]{:S(2)}) copy-start(bf16[4,64,2048]{2,1,0:T(8,128)(2,1)} %param.20) | copy-start | bytes 3145732
  3.0 6.0 %collective-permute-start = (bf16[32,1152]{1,0:T(8,128)(2,1)S(1)}, bf16[32,1152]{1,0:T(8,128)(2,1)S(1)}, u32[]{:S(2)}, u32[]{:S(2)}) collective-permute-start(bf16[32,1152]{1,0:T(8,128)(2,1)S(1)} %get-tuple-element.38.refs_0_.tagged.refs_2_), channel_id=1, source_target_pairs={{0,2},{1,3},{2,0},{3,1},{4,6},{5,7},{6,4},{7,5},{8,10},{9,11},{10,... | collective-permute-start | bytes 221192 | tf_op jit(solution)/shard_map/ppermute | solution.py:19
  6.0 3.0 %collective-permute-start.1 = (s32[8,128]{1,0:T(8,128)S(1)}, s32[8,128]{1,0:T(8,128)S(1)}, u32[]{:S(2)}, u32[]{:S(2)}) collective-permute-start(s32[8,128]{1,0:T(8,128)S(1)} %get-tuple-element.26.refs_0_), channel_id=1, source_target_pairs={{0,1},{1,0},{2,3},{3,2},{4,5},{5,4},{6,7},{7,6},{8,9},{9,8},{10,11... | collective-permute-start | bytes 12296 | tf_op jit(solution)/shard_map/ppermute | solution.py:19
  6.0 3.0 %collective-permute-start.2 = (bf16[4,64,1024]{2,1,0:T(8,128)(2,1)S(1)}, bf16[4,64,1024]{2,1,0:T(8,128)(2,1)S(1)}, u32[]{:S(2)}, u32[]{:S(2)}) collective-permute-start(bf16[4,64,1024]{2,1,0:T(8,128)(2,1)S(1)} %bitcast.8), channel_id=1, source_target_pairs={{0,1},{1,0},{2,3},{3,2},{4,5},{5,4},{6,7},{7,6},{8,9},{9,8},{10,11... | collective-permute-start | bytes 1572872 | tf_op jit(solution)/shard_map/ppermute | solution.py:19
  6.5 18.2 %collective-permute-start.6 = (bf16[4,64,2048]{2,1,0:T(8,128)(2,1)S(1)}, bf16[4,64,2048]{2,1,0:T(8,128)(2,1)S(1)}, u32[]{:S(2)}, u32[]{:S(2)}) collective-permute-start(bf16[4,64,2048]{2,1,0:T(8,128)(2,1)S(1)} %copy-done.2), channel_id=1, source_target_pairs={{0,1},{1,0},{2,3},{3,2},{4,5},{5,4},{6,7},{7,6},{8,9},{9,8},{10,11... | collective-permute-start | bytes 3145736 | tf_op jit(solution)/shard_map/ppermute | solution.py:19
  7.4 10.9 %collective-permute-start.4 = (bf16[512,128]{1,0:T(8,128)(2,1)S(1)}, bf16[512,128]{1,0:T(8,128)(2,1)}, u32[]{:S(2)}, u32[]{:S(2)}) collective-permute-start(bf16[512,128]{1,0:T(8,128)(2,1)S(1)} %base_terms.4), channel_id=1, source_target_pairs={{0,4},{4,0},{8,12},{12,8},{1,5},{5,1},{9,13},{13,9},{2,6},{6,2},{1... | collective-permute-start | bytes 393224 | tf_op jit(solution)/shard_map/ppermute | solution.py:19
  9.5 10.4 %collective-permute-start.3 = (bf16[32,128]{1,0:T(8,128)(2,1)S(1)}, bf16[32,128]{1,0:T(8,128)(2,1)S(1)}, u32[]{:S(2)}, u32[]{:S(2)}) collective-permute-start(bf16[32,128]{1,0:T(8,128)(2,1)S(1)} %shrink.1), channel_id=1, source_target_pairs={{0,4},{4,0},{8,12},{12,8},{1,5},{5,1},{9,13},{13,9},{2,6},{6,2},{1... | collective-permute-start | bytes 24584 | tf_op jit(solution)/shard_map/ppermute | solution.py:19
  11.0 5.8 %copy-start = (bf16[1024,8192]{1,0:T(8,128)(2,1)S(1)}, bf16[1024,8192]{1,0:T(8,128)(2,1)}, u32[]{:S(2)}) copy-start(bf16[1024,8192]{1,0:T(8,128)(2,1)} %weight.3) | copy-start | bytes 50331652
  16.8 10.1 %copy-start.1 = (bf16[1024,8192]{1,0:T(8,128)(2,1)S(1)}, bf16[1024,8192]{1,0:T(8,128)(2,1)}, u32[]{:S(2)}) copy-start(bf16[1024,8192]{1,0:T(8,128)(2,1)} %weight.3) | copy-start | bytes 50331652
  19.9 4.7 %collective-permute-start.5 = (bf16[32,128]{1,0:T(8,128)(2,1)S(1)}, bf16[32,128]{1,0:T(8,128)(2,1)S(1)}, u32[]{:S(2)}, u32[]{:S(2)}) collective-permute-start(bf16[32,128]{1,0:T(8,128)(2,1)S(1)} %add_convert_fusion.1.refs_4_), channel_id=1, source_target_pairs={{0,8},{4,12},{8,0},{12,4},{1,9},{5,13},{9,1},{13,5},{2,10},{6,14},... | collective-permute-start | bytes 24584 | tf_op jit(solution)/shard_map/ppermute | solution.py:19
  22.6 8.1 %collective-permute-start.7 = (bf16[512,128]{1,0:T(8,128)(2,1)S(1)}, bf16[512,128]{1,0:T(8,128)(2,1)S(1)}, u32[]{:S(2)}, u32[]{:S(2)}) collective-permute-start(bf16[512,128]{1,0:T(8,128)(2,1)S(1)} %add_convert_fusion), channel_id=1, source_target_pairs={{0,8},{4,12},{8,0},{12,4},{1,9},{5,13},{9,1},{13,5},{2,10},{6,14},... | collective-permute-start | bytes 393224 | tf_op jit(solution)/shard_map/ppermute | solution.py:19
  22.9 7.8 %collective-permute-start.8 = (bf16[512,128]{1,0:T(8,128)(2,1)S(1)}, bf16[512,128]{1,0:T(8,128)(2,1)S(1)}, u32[]{:S(2)}, u32[]{:S(2)}) collective-permute-start(bf16[512,128]{1,0:T(8,128)(2,1)S(1)} %get-tuple-element.41), channel_id=1, source_target_pairs={{0,4},{4,0},{8,12},{12,8},{1,5},{5,1},{9,13},{13,9},{2,6},{6,2},{1... | collective-permute-start | bytes 393224 | tf_op jit(solution)/shard_map/ppermute | solution.py:19
  25.2 5.6 %collective-permute-start.9 = (bf16[512,128]{1,0:T(8,128)(2,1)S(1)}, bf16[512,128]{1,0:T(8,128)(2,1)S(1)}, u32[]{:S(2)}, u32[]{:S(2)}) collective-permute-start(bf16[512,128]{1,0:T(8,128)(2,1)S(1)} %get-tuple-element.42), channel_id=1, source_target_pairs={{0,2},{1,3},{2,0},{3,1},{4,6},{5,7},{6,4},{7,5},{8,10},{9,11},{10,... | collective-permute-start | bytes 393224 | tf_op jit(solution)/shard_map/ppermute | solution.py:19

commit v14 on v13

--- a/solution.py
+++ b/solution.py
@@ -10,6 +10,8 @@
 HQ = 32
 KVH = 4
 LANES = 128
+EARLY = (3, 2)
+EARLY_CUTS = 4
 VMEM = pltpu.VMEM
 GRANT = 56 << 20
 F32, BF16 = jnp.float32, jnp.bfloat16
@@ -27,9 +29,10 @@
     return lax.broadcasted_iota(jnp.int32, shape, len(shape) - 1)
 
 
-def attend_kernel(parts, rank_width, group_at, early_at, *refs):
-    given, (out_weight, tagged, early, limits, *scratch) = refs[:9], refs[9:]
-    held, (spread_out, small_sems, key_sems, value_sems, early_sem) = scratch[:9], scratch[9:]
+def attend_kernel(parts, rank_width, count, group_at, early_at, *refs):
+    given, (out_weight, tagged, *early, limits) = refs[:9], refs[9 : 9 + 3 + count]
+    scratch = refs[9 + 3 + count :]
+    held, (spread_out, small_sems, key_sems, value_sems, early_sems) = scratch[:9], scratch[9:]
     key_cache, value_cache = given[:2]
     keys, values, queries, new_key, new_value, lengths, row_adapter, adapter_list, ranks = held
     rows, heads, width = queries.shape
@@ -52,10 +55,21 @@
     for part in range(parts):
         for copy in cache_copies(part):
             copy.start()
-    block = early.shape[1]
-    start = pl.multiple_of(early_at[0] * block, block)
-    early_copy = pltpu.make_async_copy(out_weight.at[:, pl.ds(start, block)], early, early_sem)
-    early_copy.start()
+    early_copies = []
+    for which, out in enumerate(early):
+        rows_each, block = out.shape[0] // EARLY_CUTS, out.shape[1]
+        start = pl.multiple_of((early_at[0] ^ EARLY[which]) * block, block)
+        for cut in range(EARLY_CUTS):
+            at = pl.ds(cut * rows_each, rows_each)
+            early_copies.append(
+                pltpu.make_async_copy(
+                    out_weight.at[at, pl.ds(start, block)],
+                    out.at[at],
+                    early_sems.at[which * EARLY_CUTS + cut],
+                )
+            )
+    for copy in early_copies:
+        copy.start()
     for copy in small:
         copy.wait()
     at_row = lax.broadcasted_iota(jnp.int32, (rows, LANES), 0)
@@ -116,7 +130,8 @@
         tagged[:, head * width : (head + 1) * width] = spread_out[
             pl.ds(head, rows, stride=heads)
         ].astype(BF16)
-    early_copy.wait()
+    for copy in early_copies:
+        copy.wait()
 
 
 def attend(
@@ -144,15 +159,15 @@
     parts = 2
     smem = pl.BlockSpec(memory_space=pltpu.SMEM)
     away = pl.BlockSpec(memory_space=pl.ANY)
-    tagged, early, limits = pl.pallas_call(
-        functools.partial(attend_kernel, parts, rank_width),
+    tagged, *early, limits = pl.pallas_call(
+        functools.partial(attend_kernel, parts, rank_width, len(EARLY)),
         out_shape=[
             jax.ShapeDtypeStruct((rows, full * width + LANES), BF16),
-            VMEM((out_weight.shape[0], block), BF16),
+            *[VMEM((out_weight.shape[0], block), BF16) for _ in EARLY],
             jax.ShapeDtypeStruct((8, LANES), jnp.int32),
         ],
         in_specs=[smem, smem] + [away] * 10,
-        out_specs=[pl.BlockSpec(memory_space=VMEM)] * 3,
+        out_specs=[pl.BlockSpec(memory_space=VMEM)] * (2 + len(EARLY)),
         scratch_shapes=[
             VMEM((rows, positions, width), BF16),
             VMEM((rows, positions, width), BF16),
@@ -167,7 +182,7 @@
             pltpu.SemaphoreType.DMA((7,)),
             pltpu.SemaphoreType.DMA((parts,)),
             pltpu.SemaphoreType.DMA((parts,)),
-            pltpu.SemaphoreType.DMA,
+            pltpu.SemaphoreType.DMA((len(EARLY) * EARLY_CUTS,)),
         ],
         compiler_params=pltpu.CompilerParams(vmem_limit_bytes=8 << 20),
         cost_estimate=pl.CostEstimate(
@@ -238,6 +253,75 @@
         ),
         name="base_terms",
     )(tensor_at, tagged, weight)
+
+
+def stream_kernel(ahead, deep, tensor_at, tagged, out_weight, *refs):
+    *near, out, held, sums, sems = refs
+    _, deep_rows, block = held.shape
+    width = out_weight.shape[0]
+    count = width // deep_rows
+    column = pl.ds(pl.multiple_of((tensor_at[0] ^ ahead) * block, block), block)
+
+    def copy(at):
+        return pltpu.make_async_copy(
+            out_weight.at[pl.ds(at * deep_rows, deep_rows), column],
+            held.at[at % deep],
+            sems.at[at % deep],
+        )
+
+    for at in range(min(deep, count)):
+        copy(at).start()
+    piece = min(block, 512)
+    if near:
+        early, early_out = near
+        for start in range(0, block, piece):
+            columns = slice(start, start + piece)
+            term = jnp.dot(tagged[:, :width], early[:, columns], preferred_element_type=F32)
+            put_stacked(early_out, start, term)
+    for at in range(count):
+        copy(at).wait()
+        inputs = slice(at * deep_rows, (at + 1) * deep_rows)
+        for start in range(0, block, piece):
+            columns = slice(start, start + piece)
+            term = jnp.dot(
+                tagged[:, inputs], held[at % deep, :, columns], preferred_element_type=F32
+            )
+            if at:
+                term = term + sums[:, columns]
+            if at < count - 1:
+                sums[:, columns] = term
+            else:
+                put_stacked(out, start, term)
+        if at + deep < count:
+            copy(at + deep).start()
+
+
+def stream_terms(tensor_at, tagged, out_weight, block, ahead, early=(), cost=2):
+    rows = tagged.shape[0]
+    width = out_weight.shape[0]
+    deep, deep_rows = 4, min(width, 256)
+    whole = pl.BlockSpec(memory_space=VMEM)
+    count = 1 + len(early)
+    return pl.pallas_call(
+        functools.partial(stream_kernel, ahead, deep),
+        out_shape=[jax.ShapeDtypeStruct((block // LANES * rows, LANES), BF16 if ahead else F32)]
+        * count,
+        in_specs=[pl.BlockSpec(memory_space=pltpu.SMEM), whole, pl.BlockSpec(memory_space=pl.ANY)]
+        + [whole] * len(early),
+        out_specs=[whole] * count,
+        scratch_shapes=[
+            VMEM((deep, deep_rows, block), BF16),
+            VMEM((rows, block), F32),
+            pltpu.SemaphoreType.DMA((deep,)),
+        ],
+        compiler_params=pltpu.CompilerParams(vmem_limit_bytes=12 << 20),
+        cost_estimate=pl.CostEstimate(
+            flops=cost * rows * width * block * count,
+            bytes_accessed=2 * width * block * count,
+            transcendentals=0,
+        ),
+        name="base_terms",
+    )(tensor_at, tagged, *in_hbm(out_weight), *early)
 
 
 def slots_of(tags, batch_at, pool, tile, per):
@@ -447,7 +531,7 @@
 
     stack = block // LANES * rows
     tagged, early, limits = attend(
-        tensor_at ^ 3,
+        tensor_at,
         block,
         out_weight,
         queries,
@@ -466,8 +550,7 @@
     shrink_factors = [shrink_weight, to_sibling(shrink_weight)]
     expand_factors = [expand_weight, to_sibling(expand_weight)]
     visiting = [to_chip(tagged, shift) for shift in range(1, chips)]
-    weight = pltpu.with_memory_space_constraint(out_weight, VMEM)
-    (third,) = base_terms(tensor_at, tagged, early, block, [3], 120)
+    (third,) = base_terms(tensor_at, tagged, early[0], block, [3], 60)
     visiting, limits = lax.optimization_barrier((visiting, limits))
     blocks = [tagged] + visiting
     third = across(third, 1)
@@ -475,7 +558,9 @@
     part = shrink_part(blocks, shrink_factors, batch_at)
     parts = [part, across(part, 1)]
     part, later_tagged = lax.optimization_barrier((part, tagged))
-    second, next_door = base_terms(tensor_at, later_tagged, weight, block, [2, 1], 20)
+    second, next_door = stream_terms(
+        tensor_at, later_tagged, out_weight, block, 1, [early[1]], 60
+    )
     second = (wide(second) + wide(third)).astype(BF16)
     parts, second = lax.optimization_barrier((parts, second))
     bit = 2
@@ -486,12 +571,13 @@
         bit *= 2
     arrived = [across(second, 2), across(next_door, 1)]
     for ahead in range(4, tensor_size, 2):
-        near, far = base_terms(tensor_at, tagged, weight, block, [ahead, ahead + 1], 20)
+        (near,) = stream_terms(tensor_at, tagged, out_weight, block, ahead)
+        (far,) = stream_terms(tensor_at, tagged, out_weight, block, ahead + 1)
         arrived.append(across((wide(near) + wide(across(far, 1))).astype(BF16), ahead))
 
     deltas = expand(blocks, parts, expand_factors, limits, batch_at)
     deltas, late_tagged = lax.optimization_barrier((deltas, tagged))
-    (own,) = base_terms(tensor_at, late_tagged, weight, block, [0], 20)
+    (own,) = stream_terms(tensor_at, late_tagged, out_weight, block, 0, (), 60)
     so_far = partial_total([own, deltas[0], arrived[0], *arrived[2:]], 0)
     terms = [partial_total([so_far, arrived[1]], 8 << 20)]
     terms += [to_chip(home, -shift) for shift, home in enumerate(deltas[1:], 1)]

time: 31.6 us -> 30.6 us (0.968)
  Pallas kernels: 7.94 us -> 12.2 us
  local copies, waits for them, and re-layouts: 5.78 us -> 2.21 us
  waiting for transfers between devices: 4.22 us -> 3.39 us
  other arithmetic: 1.59 us -> 0.95 us
  starting transfers between devices: 11.9 us -> 11.5 us
    pallas_call x1 -> x3, Pallas kernels: 2.97 us -> 9.59 us  [the longest x2 5.04 us: stream_terms(): pl.pallas_call(functools.partial(stream_kernel, ahead, deep), out_shape=[...]
    unnamed x8, local copies, waits for them, and re-layouts: 5.78 us -> 2.21 us
    pallas_call x3 -> x1, Pallas kernels: 3.16 us -> 0.81 us  [base_terms(): pl.pallas_call(functools.partial(base_kernel, apart, min(block, 512)), ou...]
    ppermute x10, waiting for transfers between devices: 4.22 us -> 3.39 us  [permuted(): return lax.ppermute(array, axis, [(i, partner(i)) for i in range(size)])]
    convert_element_type x1, other arithmetic: 1.58 us -> 0.95 us  [local(): second = (wide(second) + wide(third)).astype(BF16)]
    ppermute x10, starting transfers between devices: 11.9 us -> 11.5 us  [permuted(): return lax.ppermute(array, axis, [(i, partner(i)) for i in range(size)])]
  transfers between devices with their start and end apart: 10 -> 10, of which waited for: 2 -> 3; matrix products, arithmetic and copies ran while one was open for 5% -> 3% of each run, Pallas kernels for 14% -> 38%
where the time goes in v14:
time: 30.6 us; the launch traced here: 30.4 us
  Pallas kernels  12.2 us (40%)
  starting transfers between devices  11.5 us (38%)
  waiting for transfers between devices  3.39 us (11%)
  local copies, waits for them, and re-layouts  2.21 us (7%)
  other arithmetic  0.95 us (3%)
    ppermute x10, starting transfers between devices, permuted(): return lax.ppermute(array, axis, [(i, partner(i)) for i in range(size)])  11.5 us
    pallas_call x2, Pallas kernels, stream_terms(): pl.pallas_call(functools.partial(stream_kernel, ahead, deep), out_shape=[...  5.04 us
    pallas_call x1, Pallas kernels, attend(): pl.pallas_call(functools.partial(attend_kernel, parts, rank_width, len(EA...  4.56 us
    ppermute x10, waiting for transfers between devices, permuted(): return lax.ppermute(array, axis, [(i, partner(i)) for i in range(size)])  3.39 us
    unnamed x8, local copies, waits for them, and re-layouts  2.21 us
    convert_element_type x1, other arithmetic, local(): second = (wide(second) + wide(third)).astype(BF16)  0.95 us
    pallas_call x1, Pallas kernels, base_terms(): pl.pallas_call(functools.partial(base_kernel, apart, min(block, 512)), ou...  0.81 us
    pallas_call x1, Pallas kernels, total(): pl.pallas_call(total_kernel, out_shape=jax.ShapeDtypeStruct((rows, block)...  0.69 us
  transfers between devices with their start and end apart: 10, of which 3 were waited for; matrix products, arithmetic and copies ran while one was open for 3% of the time, Pallas kernels for 38%

profile of v14, /device:TPU:0, one launch (start us, length us, event | category | flops | bytes accessed | tf_op | source)
XLA Modules:
  0.0 30.4 jit_solution(16108572930827660945)
XLA Ops:
  0.0 0.5 %collective-permute-start.2 = (bf16[4,64,1024]{2,1,0:T(8,128)(2,1)}, bf16[4,64,1024]{2,1,0:T(8,128)(2,1)S(1)}, u32[]{:S(2)}, u32[]{:S(2)}) collective-permute-start(bf16[4,64,1024]{2,1,0:T(8,128)(2,1)} %bitcast.8), channel_id=1, source_target_pairs={{0,1},{1,0},{2,3},{3,2},{4,5},{5,4},{6,7},{7,6},{8,9},{9,8},{10,11... | collective-permute-start | bytes 1572872 | tf_op jit(solution)/shard_map/ppermute | solution.py:21
  0.5 4.6 %attention.1 = (bf16[32,1152]{1,0:T(8,128)(2,1)S(1)}, bf16[1024,2048]{1,0:T(8,128)(2,1)S(1)}, bf16[1024,2048]{1,0:T(8,128)(2,1)S(1)}, s32[8,128]{1,0:T(8,128)S(1)}) custom-call(s32[1]{0:T(128)} %bitcast.2.group_at, s32[1]{0:T(128)} %bitcast.early_at.tensor_at, bf16[32,4,96,128]{3,2,1,0:T(8,128)(2,1)} %refs_0_.1, bf16[32,4,96,128]{3,2,1,0:T(8,128)(2,1)} %refs_1_.1, ...), custom_call_target="tpu_custom_call" | custom-call | flops 12582912 | bytes 1572864 | tf_op jit(solution)/shard_map/attention/pallas_call | solution.py:162
  5.0 0.0 copy-start.2
  5.0 2.6 %collective-permute-start = (bf16[32,1152]{1,0:T(8,128)(2,1)S(1)}, bf16[32,1152]{1,0:T(8,128)(2,1)S(1)}, u32[]{:S(2)}, u32[]{:S(2)}) collective-permute-start(bf16[32,1152]{1,0:T(8,128)(2,1)S(1)} %get-tuple-element.40.refs_0_.tagged.refs_2_), channel_id=1, source_target_pairs={{0,2},{1,3},{2,0},{3,1},{4,6},{5,7},{6,4},{7,5},{8,10},{9,11},{10,... | collective-permute-start | bytes 221192 | tf_op jit(solution)/shard_map/ppermute | solution.py:21
  7.6 0.2 collective-permute-start.1
  7.8 0.0 copy-start
  7.8 0.0 copy-start.1
  7.8 0.8 %base_terms.4 = bf16[512,128]{1,0:T(8,128)(2,1)S(1)} custom-call(s32[1]{0:T(128)} %bitcast.early_at.tensor_at, bf16[32,1152]{1,0:T(8,128)(2,1)S(1)} %get-tuple-element.40.refs_0_.tagged.refs_2_, bf16[1024,2048]{1,0:T(8,128)(2,1)S(1)} %get-tuple-element.33.weight), custom_call_target="tpu_custom_call" | custom-call | flops 4026531840 | bytes 4194304 | tf_op jit(solution)/shard_map/base_terms/pallas_call | solution.py:240
  8.6 0.0 copy-done.2
  8.6 1.6 %collective-permute-start.4 = (bf16[512,128]{1,0:T(8,128)(2,1)S(1)}, bf16[512,128]{1,0:T(8,128)(2,1)}, u32[]{:S(2)}, u32[]{:S(2)}) collective-permute-start(bf16[512,128]{1,0:T(8,128)(2,1)S(1)} %base_terms.4), channel_id=1, source_target_pairs={{0,4},{4,0},{8,12},{12,8},{1,5},{5,1},{9,13},{13,9},{2,6},{6,2},{1... | collective-permute-start | bytes 393224 | tf_op jit(solution)/shard_map/ppermute | solution.py:21
  10.3 0.0 copy-done
  10.3 0.0 collective-permute-start.6
  10.3 0.0 collective-permute-done.1.refs_1_
  10.3 0.2 collective-permute-done.refs_1_.refs_3_
  10.5 0.0 collective-permute-done.2.refs_3_
  10.5 0.0 copy-done.1
  10.5 0.5 %shrink.1 = bf16[32,128]{1,0:T(8,128)(2,1)S(1)} custom-call(s32[1]{0:T(128)} %bitcast.1.batch_at, bf16[32,1152]{1,0:T(8,128)(2,1)S(1)} %get-tuple-element.40.refs_0_.tagged.refs_2_, bf16[32,1152]{1,0:T(8,128)(2,1)S(1)} %collective-permute-done.refs_1_.refs_3_, bf16[4,64,1024]{2,1,0:T(8,128)(2,1)S(1)} %bitcast.9, ...), custom_call_target="tpu_custom_call" | custom-call | flops 67108864 | bytes 1179648 | tf_op jit(solution)/shard_map/shrink/pallas_call | solution.py:365
  11.0 1.9 %collective-permute-start.3 = (bf16[32,128]{1,0:T(8,128)(2,1)S(1)}, bf16[32,128]{1,0:T(8,128)(2,1)S(1)}, u32[]{:S(2)}, u32[]{:S(2)}) collective-permute-start(bf16[32,128]{1,0:T(8,128)(2,1)S(1)} %shrink.1), channel_id=1, source_target_pairs={{0,4},{4,0},{8,12},{12,8},{1,5},{5,1},{9,13},{13,9},{2,6},{6,2},{1... | collective-permute-start | bytes 24584 | tf_op jit(solution)/shard_map/ppermute | solution.py:21
  12.9 0.0 copy-start.3
  12.9 2.2 %copy-done.3 = bf16[1024,2048]{1,0:T(8,128)(2,1)S(1)} copy-done((bf16[1024,2048]{1,0:T(8,128)(2,1)S(1)}, bf16[1024,2048]{1,0:T(8,128)(2,1)}, u32[]{:S(2)}) %copy-start.3) | copy-done | bytes 4194328
  15.1 2.5 %base_terms.3 = (bf16[512,128]{1,0:T(8,128)(2,1)S(1)}, bf16[512,128]{1,0:T(8,128)(2,1)S(1)}) custom-call(s32[1]{0:T(128)} %bitcast.early_at.tensor_at, bf16[32,1152]{1,0:T(8,128)(2,1)S(1)} %get-tuple-element.40.refs_0_.tagged.refs_2_, bf16[1024,8192]{1,0:T(8,128)(2,1)} %out_weight.3, bf16[1024,2048]{1,0:T(8,128)(2,1)S(1)} %copy-done.3), custom_call_target="tpu_custom_call" | custom-call | flops 8053063680 | bytes 8388608 | tf_op jit(solution)/shard_map/base_terms/pallas_call | solution.py:305
  17.7 0.0 collective-permute-done.4
  17.7 0.9 %add_convert_fusion = bf16[512,128]{1,0:T(8,128)(2,1)S(1)} fusion(bf16[512,128]{1,0:T(8,128)(2,1)} %collective-permute-done.4, bf16[512,128]{1,0:T(8,128)(2,1)S(1)} %get-tuple-element.32), kind=kLoop, calls=%fused_computation | loop fusion | flops 262144 | bytes 393216 | tf_op jit(solution)/shard_map/convert_element_type | solution.py:564
  18.6 0.0 collective-permute-done.3
  18.6 2.7 %collective-permute-start.5 = (bf16[32,128]{1,0:T(8,128)(2,1)S(1)}, bf16[32,128]{1,0:T(8,128)(2,1)S(1)}, u32[]{:S(2)}, u32[]{:S(2)}) collective-permute-start(bf16[32,128]{1,0:T(8,128)(2,1)S(1)} %add_convert_fusion.1.refs_4_), channel_id=1, source_target_pairs={{0,8},{4,12},{8,0},{12,4},{1,9},{5,13},{9,1},{13,5},{2,10},{6,14},... | collective-permute-start | bytes 24584 | tf_op jit(solution)/shard_map/ppermute | solution.py:21
  21.3 0.3 %collective-permute-start.7 = (bf16[512,128]{1,0:T(8,128)(2,1)S(1)}, bf16[512,128]{1,0:T(8,128)(2,1)S(1)}, u32[]{:S(2)}, u32[]{:S(2)}) collective-permute-start(bf16[512,128]{1,0:T(8,128)(2,1)S(1)} %add_convert_fusion), channel_id=1, source_target_pairs={{0,8},{4,12},{8,0},{12,4},{1,9},{5,13},{9,1},{13,5},{2,10},{6,14},... | collective-permute-start | bytes 393224 | tf_op jit(solution)/shard_map/ppermute | solution.py:21
  21.6 0.2 collective-permute-start.8
  21.8 1.5 %collective-permute-done.5.refs_5_ = bf16[32,128]{1,0:T(8,128)(2,1)S(1)} collective-permute-done((bf16[32,128]{1,0:T(8,128)(2,1)S(1)}, bf16[32,128]{1,0:T(8,128)(2,1)S(1)}, u32[]{:S(2)}, u32[]{:S(2)}) %collective-permute-start.5) | collective-permute-done | bytes 8224 | tf_op jit(solution)/shard_map/ppermute | solution.py:21
  23.4 0.0 collective-permute-done.6
  23.4 0.5 %expand.1 = (bf16[512,128]{1,0:T(8,128)(2,1)S(1)}, bf16[512,128]{1,0:T(8,128)(2,1)S(1)}) custom-call(s32[1]{0:T(128)} %bitcast.1.batch_at, s32[8,128]{1,0:T(8,128)S(1)} %get-tuple-element.27.refs_0_, s32[8,128]{1,0:T(8,128)S(1)} %collective-permute-done.1.refs_1_, bf16[32,1152]{1,0:T(8,128)(2,1)S(1)} %get-tuple-element.40.refs_0_.tagged.refs_2_, ...), custom_call_target="tpu_custom_call" | custom-call | flops 134217728 | bytes 1048576 | tf_op jit(solution)/shard_map/expand/pallas_call | solution.py:425
  23.9 1.5 %collective-permute-start.9 = (bf16[512,128]{1,0:T(8,128)(2,1)S(1)}, bf16[512,128]{1,0:T(8,128)(2,1)S(1)}, u32[]{:S(2)}, u32[]{:S(2)}) collective-permute-start(bf16[512,128]{1,0:T(8,128)(2,1)S(1)} %get-tuple-element.44), channel_id=1, source_target_pairs={{0,2},{1,3},{2,0},{3,1},{4,6},{5,7},{6,4},{7,5},{8,10},{9,11},{10,... | collective-permute-start | bytes 393224 | tf_op jit(solution)/shard_map/ppermute | solution.py:21
  25.5 2.5 %base_terms.5.refs_0_ = f32[512,128]{1,0:T(8,128)S(1)} custom-call(s32[1]{0:T(128)} %bitcast.early_at.tensor_at, bf16[32,1152]{1,0:T(8,128)(2,1)S(1)} %get-tuple-element.40.refs_0_.tagged.refs_2_, bf16[1024,8192]{1,0:T(8,128)(2,1)} %out_weight.3), custom_call_target="tpu_custom_call" | custom-call | flops 4026531840 | bytes 4194304 | tf_op jit(solution)/shard_map/base_terms/pallas_call | solution.py:305
  28.0 1.6 %collective-permute-done.7.refs_2_ = bf16[512,128]{1,0:T(8,128)(2,1)S(1)} collective-permute-done((bf16[512,128]{1,0:T(8,128)(2,1)S(1)}, bf16[512,128]{1,0:T(8,128)(2,1)S(1)}, u32[]{:S(2)}, u32[]{:S(2)}) %collective-permute-start.7) | collective-permute-done | bytes 131104 | tf_op jit(solution)/shard_map/ppermute | solution.py:21
  29.6 0.0 collective-permute-done.8.refs_1_
  29.7 0.0 collective-permute-done.9.refs_1_
  29.7 0.7 %total.1 = bf16[32,2048]{1,0:T(8,128)(2,1)} custom-call(f32[512,128]{1,0:T(8,128)S(1)} %partial_total.3.refs_0_, bf16[512,128]{1,0:T(8,128)(2,1)S(1)} %collective-permute-done.9.refs_1_), custom_call_target="tpu_custom_call" | custom-call | flops 131072 | bytes 393216 | tf_op jit(solution)/shard_map/total/pallas_call | solution.py:458
  (3 shorter events, 0.1 us)
Async XLA Ops:
  0.0 10.5 %collective-permute-start.2 = (bf16[4,64,1024]{2,1,0:T(8,128)(2,1)}, bf16[4,64,1024]{2,1,0:T(8,128)(2,1)S(1)}, u32[]{:S(2)}, u32[]{:S(2)}) collective-permute-start(bf16[4,64,1024]{2,1,0:T(8,128)(2,1)} %bitcast.8), channel_id=1, source_target_pairs={{0,1},{1,0},{2,3},{3,2},{4,5},{5,4},{6,7},{7,6},{8,9},{9,8},{10,11... | collective-permute-start | bytes 1572872 | tf_op jit(solution)/shard_map/ppermute | solution.py:21
  5.0 3.6 %copy-start.2 = (bf16[1024,2048]{1,0:T(8,128)(2,1)}, bf16[1024,2048]{1,0:T(8,128)(2,1)S(1)}, u32[]{:S(2)}) copy-start(bf16[1024,2048]{1,0:T(8,128)(2,1)S(1)} %get-tuple-element.31.refs_0_) | copy-start | bytes 12582916
  5.0 5.5 %collective-permute-start = (bf16[32,1152]{1,0:T(8,128)(2,1)S(1)}, bf16[32,1152]{1,0:T(8,128)(2,1)S(1)}, u32[]{:S(2)}, u32[]{:S(2)}) collective-permute-start(bf16[32,1152]{1,0:T(8,128)(2,1)S(1)} %get-tuple-element.40.refs_0_.tagged.refs_2_), channel_id=1, source_target_pairs={{0,2},{1,3},{2,0},{3,1},{4,6},{5,7},{6,4},{7,5},{8,10},{9,11},{10,... | collective-permute-start | bytes 221192 | tf_op jit(solution)/shard_map/ppermute | solution.py:21
  7.6 2.7 %collective-permute-start.1 = (s32[8,128]{1,0:T(8,128)S(1)}, s32[8,128]{1,0:T(8,128)S(1)}, u32[]{:S(2)}, u32[]{:S(2)}) collective-permute-start(s32[8,128]{1,0:T(8,128)S(1)} %get-tuple-element.27.refs_0_), channel_id=1, source_target_pairs={{0,1},{1,0},{2,3},{3,2},{4,5},{5,4},{6,7},{7,6},{8,9},{9,8},{10,11... | collective-permute-start | bytes 12296 | tf_op jit(solution)/shard_map/ppermute | solution.py:21
  7.8 2.5 %copy-start = (bf16[4,64,2048]{2,1,0:T(8,128)(2,1)S(1)}, bf16[4,64,2048]{2,1,0:T(8,128)(2,1)}, u32[]{:S(2)}) copy-start(bf16[4,64,2048]{2,1,0:T(8,128)(2,1)} %param.20) | copy-start | bytes 3145732
  7.8 2.7 %copy-start.1 = (bf16[4,1024,64]{1,2,0:T(8,128)(2,1)S(1)}, bf16[4,1024,64]{1,2,0:T(8,128)(2,1)}, u32[]{:S(2)}) copy-start(bf16[4,1024,64]{1,2,0:T(8,128)(2,1)} %param.19) | copy-start | bytes 1572868
  8.6 9.0 %collective-permute-start.4 = (bf16[512,128]{1,0:T(8,128)(2,1)S(1)}, bf16[512,128]{1,0:T(8,128)(2,1)}, u32[]{:S(2)}, u32[]{:S(2)}) collective-permute-start(bf16[512,128]{1,0:T(8,128)(2,1)S(1)} %base_terms.4), channel_id=1, source_target_pairs={{0,4},{4,0},{8,12},{12,8},{1,5},{5,1},{9,13},{13,9},{2,6},{6,2},{1... | collective-permute-start | bytes 393224 | tf_op jit(solution)/shard_map/ppermute | solution.py:21
  10.3 13.1 %collective-permute-start.6 = (bf16[4,64,2048]{2,1,0:T(8,128)(2,1)S(1)}, bf16[4,64,2048]{2,1,0:T(8,128)(2,1)S(1)}, u32[]{:S(2)}, u32[]{:S(2)}) collective-permute-start(bf16[4,64,2048]{2,1,0:T(8,128)(2,1)S(1)} %copy-done), channel_id=1, source_target_pairs={{0,1},{1,0},{2,3},{3,2},{4,5},{5,4},{6,7},{7,6},{8,9},{9,8},{10,11... | collective-permute-start | bytes 3145736 | tf_op jit(solution)/shard_map/ppermute | solution.py:21
  11.0 7.6 %collective-permute-start.3 = (bf16[32,128]{1,0:T(8,128)(2,1)S(1)}, bf16[32,128]{1,0:T(8,128)(2,1)S(1)}, u32[]{:S(2)}, u32[]{:S(2)}) collective-permute-start(bf16[32,128]{1,0:T(8,128)(2,1)S(1)} %shrink.1), channel_id=1, source_target_pairs={{0,4},{4,0},{8,12},{12,8},{1,5},{5,1},{9,13},{13,9},{2,6},{6,2},{1... | collective-permute-start | bytes 24584 | tf_op jit(solution)/shard_map/ppermute | solution.py:21
  12.9 2.2 %copy-start.3 = (bf16[1024,2048]{1,0:T(8,128)(2,1)S(1)}, bf16[1024,2048]{1,0:T(8,128)(2,1)}, u32[]{:S(2)}) copy-start(bf16[1024,2048]{1,0:T(8,128)(2,1)} %copy-done.2) | copy-start | bytes 12582916
  18.6 4.7 %collective-permute-start.5 = (bf16[32,128]{1,0:T(8,128)(2,1)S(1)}, bf16[32,128]{1,0:T(8,128)(2,1)S(1)}, u32[]{:S(2)}, u32[]{:S(2)}) collective-permute-start(bf16[32,128]{1,0:T(8,128)(2,1)S(1)} %add_convert_fusion.1.refs_4_), channel_id=1, source_target_pairs={{0,8},{4,12},{8,0},{12,4},{1,9},{5,13},{9,1},{13,5},{2,10},{6,14},... | collective-permute-start | bytes 24584 | tf_op jit(solution)/shard_map/ppermute | solution.py:21
  21.3 8.3 %collective-permute-start.7 = (bf16[512,128]{1,0:T(8,128)(2,1)S(1)}, bf16[512,128]{1,0:T(8,128)(2,1)S(1)}, u32[]{:S(2)}, u32[]{:S(2)}) collective-permute-start(bf16[512,128]{1,0:T(8,128)(2,1)S(1)} %add_convert_fusion), channel_id=1, source_target_pairs={{0,8},{4,12},{8,0},{12,4},{1,9},{5,13},{9,1},{13,5},{2,10},{6,14},... | collective-permute-start | bytes 393224 | tf_op jit(solution)/shard_map/ppermute | solution.py:21
  21.6 8.0 %collective-permute-start.8 = (bf16[512,128]{1,0:T(8,128)(2,1)S(1)}, bf16[512,128]{1,0:T(8,128)(2,1)S(1)}, u32[]{:S(2)}, u32[]{:S(2)}) collective-permute-start(bf16[512,128]{1,0:T(8,128)(2,1)S(1)} %get-tuple-element.43), channel_id=1, source_target_pairs={{0,4},{4,0},{8,12},{12,8},{1,5},{5,1},{9,13},{13,9},{2,6},{6,2},{1... | collective-permute-start | bytes 393224 | tf_op jit(solution)/shard_map/ppermute | solution.py:21
  23.9 5.8 %collective-permute-start.9 = (bf16[512,128]{1,0:T(8,128)(2,1)S(1)}, bf16[512,128]{1,0:T(8,128)(2,1)S(1)}, u32[]{:S(2)}, u32[]{:S(2)}) collective-permute-start(bf16[512,128]{1,0:T(8,128)(2,1)S(1)} %get-tuple-element.44), channel_id=1, source_target_pairs={{0,2},{1,3},{2,0},{3,1},{4,6},{5,7},{6,4},{7,5},{8,10},{9,11},{10,... | collective-permute-start | bytes 393224 | tf_op jit(solution)/shard_map/ppermute | solution.py:21

commit v15 on v14

--- a/solution.py
+++ b/solution.py
@@ -10,7 +10,7 @@
 HQ = 32
 KVH = 4
 LANES = 128
-EARLY = (3, 2)
+EARLY = (3,)
 EARLY_CUTS = 4
 VMEM = pltpu.VMEM
 GRANT = 56 << 20
@@ -487,8 +487,8 @@
         out_specs=whole,
         compiler_params=pltpu.CompilerParams(vmem_limit_bytes=8 << 20),
         cost_estimate=pl.CostEstimate(
-            flops=terms[0].size * len(terms),
-            bytes_accessed=4 * terms[0].size + weight,
+            flops=weight,
+            bytes_accessed=4 * terms[0].size * len(terms),
             transcendentals=0,
         ),
         name="partial_total",
@@ -558,15 +558,13 @@
     part = shrink_part(blocks, shrink_factors, batch_at)
     parts = [part, across(part, 1)]
     part, later_tagged = lax.optimization_barrier((part, tagged))
-    second, next_door = stream_terms(
-        tensor_at, later_tagged, out_weight, block, 1, [early[1]], 60
-    )
+    (second,) = stream_terms(tensor_at, later_tagged, out_weight, block, 2, (), 60)
     second = (wide(second) + wide(third)).astype(BF16)
-    parts, second = lax.optimization_barrier((parts, second))
+    parts, second, later_tagged = lax.optimization_barrier((parts, second, later_tagged))
+    (next_door,) = stream_terms(tensor_at, later_tagged, out_weight, block, 1, (), 60)
     bit = 2
     while bit < tensor_size:
         part = (wide(parts[0]) + wide(parts[1])).astype(BF16)
-        part, next_door = lax.optimization_barrier((part, next_door))
         parts = [part, across(part, bit)]
         bit *= 2
     arrived = [across(second, 2), across(next_door, 1)]
@@ -578,8 +576,8 @@
     deltas = expand(blocks, parts, expand_factors, limits, batch_at)
     deltas, late_tagged = lax.optimization_barrier((deltas, tagged))
     (own,) = stream_terms(tensor_at, late_tagged, out_weight, block, 0, (), 60)
-    so_far = partial_total([own, deltas[0], arrived[0], *arrived[2:]], 0)
-    terms = [partial_total([so_far, arrived[1]], 8 << 20)]
+    so_far = partial_total([own, deltas[0], arrived[0], *arrived[2:]], 1000)
+    terms = [partial_total([so_far, arrived[1]], 1000)]
     terms += [to_chip(home, -shift) for shift, home in enumerate(deltas[1:], 1)]
     return total(rows, block, terms)
 

time: 30.6 us -> 28.4 us (0.928)
  local copies, waits for them, and re-layouts: 2.21 us -> 0.01 us
  waiting for transfers between devices: 3.39 us -> 1.98 us
  Pallas kernels: 12.2 us -> 13.4 us
    pallas_call x2 -> x3, Pallas kernels: 5.04 us -> 7.51 us  [stream_terms(): pl.pallas_call(functools.partial(stream_kernel, ahead, deep), out_shape=[...]
    unnamed x8 -> x4, local copies, waits for them, and re-layouts: 2.21 us -> 0.01 us
    ppermute x10, waiting for transfers between devices: 3.39 us -> 1.98 us  [permuted(): return lax.ppermute(array, axis, [(i, partner(i)) for i in range(size)])]
    pallas_call x1, Pallas kernels: 4.56 us -> 3.29 us  [attend(): pl.pallas_call(functools.partial(attend_kernel, parts, rank_width, len(EA...]
  transfers between devices with their start and end apart: 10 -> 10, of which waited for: 3 -> 3; matrix products, arithmetic and copies ran while one was open for 3% -> 3% of each run, Pallas kernels for 38% -> 45%
where the time goes in v15:
time: 28.4 us; the launch traced here: 28.2 us
  Pallas kernels  13.4 us (47%)
  starting transfers between devices  11.8 us (42%)
  waiting for transfers between devices  1.98 us (7%)
  other arithmetic  0.95 us (3%)
    ppermute x10, starting transfers between devices, permuted(): return lax.ppermute(array, axis, [(i, partner(i)) for i in range(size)])  11.8 us
    pallas_call x3, Pallas kernels, stream_terms(): pl.pallas_call(functools.partial(stream_kernel, ahead, deep), out_shape=[...  7.51 us
    pallas_call x1, Pallas kernels, attend(): pl.pallas_call(functools.partial(attend_kernel, parts, rank_width, len(EA...  3.29 us
    ppermute x10, waiting for transfers between devices, permuted(): return lax.ppermute(array, axis, [(i, partner(i)) for i in range(size)])  1.98 us
    convert_element_type x1, other arithmetic, local(): second = (wide(second) + wide(third)).astype(BF16)  0.94 us
    pallas_call x1, Pallas kernels, base_terms(): pl.pallas_call(functools.partial(base_kernel, apart, min(block, 512)), ou...  0.81 us
    pallas_call x1, Pallas kernels, total(): pl.pallas_call(total_kernel, out_shape=jax.ShapeDtypeStruct((rows, block)...  0.69 us
  transfers between devices with their start and end apart: 10, of which 3 were waited for; matrix products, arithmetic and copies ran while one was open for 3% of the time, Pallas kernels for 45%

profile of v15, /device:TPU:0, one launch (start us, length us, event | category | flops | bytes accessed | tf_op | source)
XLA Modules:
  0.0 28.2 jit_solution(1114434009464487559)
XLA Ops:
  0.0 0.5 %collective-permute-start.2 = (bf16[4,64,1024]{2,1,0:T(8,128)(2,1)}, bf16[4,64,1024]{2,1,0:T(8,128)(2,1)S(1)}, u32[]{:S(2)}, u32[]{:S(2)}) collective-permute-start(bf16[4,64,1024]{2,1,0:T(8,128)(2,1)} %bitcast.8), channel_id=1, source_target_pairs={{0,1},{1,0},{2,3},{3,2},{4,5},{5,4},{6,7},{7,6},{8,9},{9,8},{10,11... | collective-permute-start | bytes 1572872 | tf_op jit(solution)/shard_map/ppermute | solution.py:21
  0.5 3.3 %attention.1 = (bf16[32,1152]{1,0:T(8,128)(2,1)S(1)}, bf16[1024,2048]{1,0:T(8,128)(2,1)S(1)}, s32[8,128]{1,0:T(8,128)S(1)}) custom-call(s32[1]{0:T(128)} %bitcast.2.group_at, s32[1]{0:T(128)} %bitcast.early_at.tensor_at, bf16[32,4,96,128]{3,2,1,0:T(8,128)(2,1)} %refs_0_.1, bf16[32,4,96,128]{3,2,1,0:T(8,128)(2,1)} %refs_1_.1, bf16[32,8,128]{2,1,0:T(8,128)(2,1)} %refs_2_.1, ...), custom_call_target="tpu_custom_call" | custom-call | flops 12582912 | bytes 1572864 | tf_op jit(solution)/shard_map/attention/pallas_call | solution.py:162
  3.8 2.6 %collective-permute-start = (bf16[32,1152]{1,0:T(8,128)(2,1)S(1)}, bf16[32,1152]{1,0:T(8,128)(2,1)S(1)}, u32[]{:S(2)}, u32[]{:S(2)}) collective-permute-start(bf16[32,1152]{1,0:T(8,128)(2,1)S(1)} %get-tuple-element.35.refs_0_.tagged.refs_2_), channel_id=1, source_target_pairs={{0,2},{1,3},{2,0},{3,1},{4,6},{5,7},{6,4},{7,5},{8,10},{9,11},{10,... | collective-permute-start | bytes 221192 | tf_op jit(solution)/shard_map/ppermute | solution.py:21
  6.3 0.2 collective-permute-start.1
  6.5 0.0 copy-start
  6.5 0.0 copy-start.1
  6.5 0.8 %base_terms.5 = bf16[512,128]{1,0:T(8,128)(2,1)S(1)} custom-call(s32[1]{0:T(128)} %bitcast.early_at.tensor_at, bf16[32,1152]{1,0:T(8,128)(2,1)S(1)} %get-tuple-element.35.refs_0_.tagged.refs_2_, bf16[1024,2048]{1,0:T(8,128)(2,1)S(1)} %get-tuple-element.27.weight), custom_call_target="tpu_custom_call" | custom-call | flops 4026531840 | bytes 4194304 | tf_op jit(solution)/shard_map/base_terms/pallas_call | solution.py:240
  7.4 1.6 %collective-permute-start.4 = (bf16[512,128]{1,0:T(8,128)(2,1)S(1)}, bf16[512,128]{1,0:T(8,128)(2,1)}, u32[]{:S(2)}, u32[]{:S(2)}) collective-permute-start(bf16[512,128]{1,0:T(8,128)(2,1)S(1)} %base_terms.5), channel_id=1, source_target_pairs={{0,4},{4,0},{8,12},{12,8},{1,5},{5,1},{9,13},{13,9},{2,6},{6,2},{1... | collective-permute-start | bytes 393224 | tf_op jit(solution)/shard_map/ppermute | solution.py:21
  8.9 0.0 copy-done
  8.9 0.0 collective-permute-start.6
  9.0 0.0 collective-permute-done.1.refs_1_
  9.0 0.3 %collective-permute-done.refs_1_.refs_3_ = bf16[32,1152]{1,0:T(8,128)(2,1)S(1)} collective-permute-done((bf16[32,1152]{1,0:T(8,128)(2,1)S(1)}, bf16[32,1152]{1,0:T(8,128)(2,1)S(1)}, u32[]{:S(2)}, u32[]{:S(2)}) %collective-permute-start) | collective-permute-done | bytes 73760 | tf_op jit(solution)/shard_map/ppermute | solution.py:21
  9.2 0.0 collective-permute-done.2.refs_3_
  9.2 0.0 copy-done.1
  9.3 0.5 %shrink.1 = bf16[32,128]{1,0:T(8,128)(2,1)S(1)} custom-call(s32[1]{0:T(128)} %bitcast.1.batch_at, bf16[32,1152]{1,0:T(8,128)(2,1)S(1)} %get-tuple-element.35.refs_0_.tagged.refs_2_, bf16[32,1152]{1,0:T(8,128)(2,1)S(1)} %collective-permute-done.refs_1_.refs_3_, bf16[4,64,1024]{2,1,0:T(8,128)(2,1)S(1)} %bitcast.9, ...), custom_call_target="tpu_custom_call" | custom-call | flops 67108864 | bytes 1179648 | tf_op jit(solution)/shard_map/shrink/pallas_call | solution.py:365
  9.8 1.9 %collective-permute-start.3 = (bf16[32,128]{1,0:T(8,128)(2,1)S(1)}, bf16[32,128]{1,0:T(8,128)(2,1)S(1)}, u32[]{:S(2)}, u32[]{:S(2)}) collective-permute-start(bf16[32,128]{1,0:T(8,128)(2,1)S(1)} %shrink.1), channel_id=1, source_target_pairs={{0,4},{4,0},{8,12},{12,8},{1,5},{5,1},{9,13},{13,9},{2,6},{6,2},{1... | collective-permute-start | bytes 24584 | tf_op jit(solution)/shard_map/ppermute | solution.py:21
  11.7 2.5 %base_terms.4 = bf16[512,128]{1,0:T(8,128)(2,1)S(1)} custom-call(s32[1]{0:T(128)} %bitcast.early_at.tensor_at, bf16[32,1152]{1,0:T(8,128)(2,1)S(1)} %get-tuple-element.35.refs_0_.tagged.refs_2_, bf16[1024,8192]{1,0:T(8,128)(2,1)} %out_weight.5), custom_call_target="tpu_custom_call" | custom-call | flops 4026531840 | bytes 4194304 | tf_op jit(solution)/shard_map/base_terms/pallas_call | solution.py:305
  14.2 0.0 collective-permute-done.4
  14.2 0.9 %add_convert_fusion = bf16[512,128]{1,0:T(8,128)(2,1)S(1)} fusion(bf16[512,128]{1,0:T(8,128)(2,1)} %collective-permute-done.4, bf16[512,128]{1,0:T(8,128)(2,1)S(1)} %base_terms.4), kind=kLoop, calls=%fused_computation | loop fusion | flops 262144 | bytes 393216 | tf_op jit(solution)/shard_map/convert_element_type | solution.py:562
  15.1 0.0 collective-permute-done.3
  15.1 2.7 %collective-permute-start.5 = (bf16[32,128]{1,0:T(8,128)(2,1)S(1)}, bf16[32,128]{1,0:T(8,128)(2,1)S(1)}, u32[]{:S(2)}, u32[]{:S(2)}) collective-permute-start(bf16[32,128]{1,0:T(8,128)(2,1)S(1)} %add_convert_fusion.1.refs_4_), channel_id=1, source_target_pairs={{0,8},{4,12},{8,0},{12,4},{1,9},{5,13},{9,1},{13,5},{2,10},{6,14},... | collective-permute-start | bytes 24584 | tf_op jit(solution)/shard_map/ppermute | solution.py:21
  17.8 0.3 %collective-permute-start.7 = (bf16[512,128]{1,0:T(8,128)(2,1)S(1)}, bf16[512,128]{1,0:T(8,128)(2,1)S(1)}, u32[]{:S(2)}, u32[]{:S(2)}) collective-permute-start(bf16[512,128]{1,0:T(8,128)(2,1)S(1)} %add_convert_fusion), channel_id=1, source_target_pairs={{0,8},{4,12},{8,0},{12,4},{1,9},{5,13},{9,1},{13,5},{2,10},{6,14},... | collective-permute-start | bytes 393224 | tf_op jit(solution)/shard_map/ppermute | solution.py:21
  18.1 2.5 %base_terms.7 = bf16[512,128]{1,0:T(8,128)(2,1)S(1)} custom-call(s32[1]{0:T(128)} %bitcast.early_at.tensor_at, bf16[32,1152]{1,0:T(8,128)(2,1)S(1)} %get-tuple-element.35.refs_0_.tagged.refs_2_, bf16[1024,8192]{1,0:T(8,128)(2,1)} %out_weight.5), custom_call_target="tpu_custom_call" | custom-call | flops 4026531840 | bytes 4194304 | tf_op jit(solution)/shard_map/base_terms/pallas_call | solution.py:305
  20.6 0.7 %collective-permute-start.8 = (bf16[512,128]{1,0:T(8,128)(2,1)S(1)}, bf16[512,128]{1,0:T(8,128)(2,1)S(1)}, u32[]{:S(2)}, u32[]{:S(2)}) collective-permute-start(bf16[512,128]{1,0:T(8,128)(2,1)S(1)} %base_terms.7), channel_id=1, source_target_pairs={{0,4},{4,0},{8,12},{12,8},{1,5},{5,1},{9,13},{13,9},{2,6},{6,2},{1... | collective-permute-start | bytes 393224 | tf_op jit(solution)/shard_map/ppermute | solution.py:21
  21.4 0.0 collective-permute-done.5.refs_5_
  21.4 0.0 collective-permute-done.6
  21.4 0.5 %expand.1 = (bf16[512,128]{1,0:T(8,128)(2,1)S(1)}, bf16[512,128]{1,0:T(8,128)(2,1)S(1)}) custom-call(s32[1]{0:T(128)} %bitcast.1.batch_at, s32[8,128]{1,0:T(8,128)S(1)} %get-tuple-element.23.refs_0_, s32[8,128]{1,0:T(8,128)S(1)} %collective-permute-done.1.refs_1_, bf16[32,1152]{1,0:T(8,128)(2,1)S(1)} %get-tuple-element.35.refs_0_.tagged.refs_2_, ...), custom_call_target="tpu_custom_call" | custom-call | flops 134217728 | bytes 1048576 | tf_op jit(solution)/shard_map/expand/pallas_call | solution.py:425
  21.9 1.4 %collective-permute-start.9 = (bf16[512,128]{1,0:T(8,128)(2,1)S(1)}, bf16[512,128]{1,0:T(8,128)(2,1)S(1)}, u32[]{:S(2)}, u32[]{:S(2)}) collective-permute-start(bf16[512,128]{1,0:T(8,128)(2,1)S(1)} %get-tuple-element.36), channel_id=1, source_target_pairs={{0,2},{1,3},{2,0},{3,1},{4,6},{5,7},{6,4},{7,5},{8,10},{9,11},{10,... | collective-permute-start | bytes 393224 | tf_op jit(solution)/shard_map/ppermute | solution.py:21
  23.3 2.5 %base_terms.6.refs_0_ = f32[512,128]{1,0:T(8,128)S(1)} custom-call(s32[1]{0:T(128)} %bitcast.early_at.tensor_at, bf16[32,1152]{1,0:T(8,128)(2,1)S(1)} %get-tuple-element.35.refs_0_.tagged.refs_2_, bf16[1024,8192]{1,0:T(8,128)(2,1)} %out_weight.5), custom_call_target="tpu_custom_call" | custom-call | flops 4026531840 | bytes 4194304 | tf_op jit(solution)/shard_map/base_terms/pallas_call | solution.py:305
  25.8 0.4 %collective-permute-done.7.refs_2_ = bf16[512,128]{1,0:T(8,128)(2,1)S(1)} collective-permute-done((bf16[512,128]{1,0:T(8,128)(2,1)S(1)}, bf16[512,128]{1,0:T(8,128)(2,1)S(1)}, u32[]{:S(2)}, u32[]{:S(2)}) %collective-permute-start.7) | collective-permute-done | bytes 131104 | tf_op jit(solution)/shard_map/ppermute | solution.py:21
  26.2 1.3 %collective-permute-done.8.refs_1_ = bf16[512,128]{1,0:T(8,128)(2,1)S(1)} collective-permute-done((bf16[512,128]{1,0:T(8,128)(2,1)S(1)}, bf16[512,128]{1,0:T(8,128)(2,1)S(1)}, u32[]{:S(2)}, u32[]{:S(2)}) %collective-permute-start.8) | collective-permute-done | bytes 131104 | tf_op jit(solution)/shard_map/ppermute | solution.py:21
  27.5 0.0 collective-permute-done.9.refs_1_
  27.5 0.7 %total.1 = bf16[32,2048]{1,0:T(8,128)(2,1)} custom-call(f32[512,128]{1,0:T(8,128)S(1)} %partial_total.3.refs_0_, bf16[512,128]{1,0:T(8,128)(2,1)S(1)} %collective-permute-done.9.refs_1_), custom_call_target="tpu_custom_call" | custom-call | flops 131072 | bytes 393216 | tf_op jit(solution)/shard_map/total/pallas_call | solution.py:458
  (3 shorter events, 0.1 us)
Async XLA Ops:
  0.0 9.2 %collective-permute-start.2 = (bf16[4,64,1024]{2,1,0:T(8,128)(2,1)}, bf16[4,64,1024]{2,1,0:T(8,128)(2,1)S(1)}, u32[]{:S(2)}, u32[]{:S(2)}) collective-permute-start(bf16[4,64,1024]{2,1,0:T(8,128)(2,1)} %bitcast.8), channel_id=1, source_target_pairs={{0,1},{1,0},{2,3},{3,2},{4,5},{5,4},{6,7},{7,6},{8,9},{9,8},{10,11... | collective-permute-start | bytes 1572872 | tf_op jit(solution)/shard_map/ppermute | solution.py:21
  3.8 5.5 %collective-permute-start = (bf16[32,1152]{1,0:T(8,128)(2,1)S(1)}, bf16[32,1152]{1,0:T(8,128)(2,1)S(1)}, u32[]{:S(2)}, u32[]{:S(2)}) collective-permute-start(bf16[32,1152]{1,0:T(8,128)(2,1)S(1)} %get-tuple-element.35.refs_0_.tagged.refs_2_), channel_id=1, source_target_pairs={{0,2},{1,3},{2,0},{3,1},{4,6},{5,7},{6,4},{7,5},{8,10},{9,11},{10,... | collective-permute-start | bytes 221192 | tf_op jit(solution)/shard_map/ppermute | solution.py:21
  6.3 2.6 %collective-permute-start.1 = (s32[8,128]{1,0:T(8,128)S(1)}, s32[8,128]{1,0:T(8,128)S(1)}, u32[]{:S(2)}, u32[]{:S(2)}) collective-permute-start(s32[8,128]{1,0:T(8,128)S(1)} %get-tuple-element.23.refs_0_), channel_id=1, source_target_pairs={{0,1},{1,0},{2,3},{3,2},{4,5},{5,4},{6,7},{7,6},{8,9},{9,8},{10,11... | collective-permute-start | bytes 12296 | tf_op jit(solution)/shard_map/ppermute | solution.py:21
  6.5 2.4 %copy-start = (bf16[4,64,2048]{2,1,0:T(8,128)(2,1)S(1)}, bf16[4,64,2048]{2,1,0:T(8,128)(2,1)}, u32[]{:S(2)}) copy-start(bf16[4,64,2048]{2,1,0:T(8,128)(2,1)} %param.20) | copy-start | bytes 3145732
  6.5 2.7 %copy-start.1 = (bf16[4,1024,64]{1,2,0:T(8,128)(2,1)S(1)}, bf16[4,1024,64]{1,2,0:T(8,128)(2,1)}, u32[]{:S(2)}) copy-start(bf16[4,1024,64]{1,2,0:T(8,128)(2,1)} %param.19) | copy-start | bytes 1572868
  7.4 6.8 %collective-permute-start.4 = (bf16[512,128]{1,0:T(8,128)(2,1)S(1)}, bf16[512,128]{1,0:T(8,128)(2,1)}, u32[]{:S(2)}, u32[]{:S(2)}) collective-permute-start(bf16[512,128]{1,0:T(8,128)(2,1)S(1)} %base_terms.5), channel_id=1, source_target_pairs={{0,4},{4,0},{8,12},{12,8},{1,5},{5,1},{9,13},{13,9},{2,6},{6,2},{1... | collective-permute-start | bytes 393224 | tf_op jit(solution)/shard_map/ppermute | solution.py:21
  8.9 12.4 %collective-permute-start.6 = (bf16[4,64,2048]{2,1,0:T(8,128)(2,1)S(1)}, bf16[4,64,2048]{2,1,0:T(8,128)(2,1)S(1)}, u32[]{:S(2)}, u32[]{:S(2)}) collective-permute-start(bf16[4,64,2048]{2,1,0:T(8,128)(2,1)S(1)} %copy-done), channel_id=1, source_target_pairs={{0,1},{1,0},{2,3},{3,2},{4,5},{5,4},{6,7},{7,6},{8,9},{9,8},{10,11... | collective-permute-start | bytes 3145736 | tf_op jit(solution)/shard_map/ppermute | solution.py:21
  9.8 5.4 %collective-permute-start.3 = (bf16[32,128]{1,0:T(8,128)(2,1)S(1)}, bf16[32,128]{1,0:T(8,128)(2,1)S(1)}, u32[]{:S(2)}, u32[]{:S(2)}) collective-permute-start(bf16[32,128]{1,0:T(8,128)(2,1)S(1)} %shrink.1), channel_id=1, source_target_pairs={{0,4},{4,0},{8,12},{12,8},{1,5},{5,1},{9,13},{13,9},{2,6},{6,2},{1... | collective-permute-start | bytes 24584 | tf_op jit(solution)/shard_map/ppermute | solution.py:21
  15.1 6.2 %collective-permute-start.5 = (bf16[32,128]{1,0:T(8,128)(2,1)S(1)}, bf16[32,128]{1,0:T(8,128)(2,1)S(1)}, u32[]{:S(2)}, u32[]{:S(2)}) collective-permute-start(bf16[32,128]{1,0:T(8,128)(2,1)S(1)} %add_convert_fusion.1.refs_4_), channel_id=1, source_target_pairs={{0,8},{4,12},{8,0},{12,4},{1,9},{5,13},{9,1},{13,5},{2,10},{6,14},... | collective-permute-start | bytes 24584 | tf_op jit(solution)/shard_map/ppermute | solution.py:21
  17.8 8.4 %collective-permute-start.7 = (bf16[512,128]{1,0:T(8,128)(2,1)S(1)}, bf16[512,128]{1,0:T(8,128)(2,1)S(1)}, u32[]{:S(2)}, u32[]{:S(2)}) collective-permute-start(bf16[512,128]{1,0:T(8,128)(2,1)S(1)} %add_convert_fusion), channel_id=1, source_target_pairs={{0,8},{4,12},{8,0},{12,4},{1,9},{5,13},{9,1},{13,5},{2,10},{6,14},... | collective-permute-start | bytes 393224 | tf_op jit(solution)/shard_map/ppermute | solution.py:21
  20.6 6.8 %collective-permute-start.8 = (bf16[512,128]{1,0:T(8,128)(2,1)S(1)}, bf16[512,128]{1,0:T(8,128)(2,1)S(1)}, u32[]{:S(2)}, u32[]{:S(2)}) collective-permute-start(bf16[512,128]{1,0:T(8,128)(2,1)S(1)} %base_terms.7), channel_id=1, source_target_pairs={{0,4},{4,0},{8,12},{12,8},{1,5},{5,1},{9,13},{13,9},{2,6},{6,2},{1... | collective-permute-start | bytes 393224 | tf_op jit(solution)/shard_map/ppermute | solution.py:21
  21.9 5.6 %collective-permute-start.9 = (bf16[512,128]{1,0:T(8,128)(2,1)S(1)}, bf16[512,128]{1,0:T(8,128)(2,1)S(1)}, u32[]{:S(2)}, u32[]{:S(2)}) collective-permute-start(bf16[512,128]{1,0:T(8,128)(2,1)S(1)} %get-tuple-element.36), channel_id=1, source_target_pairs={{0,2},{1,3},{2,0},{3,1},{4,6},{5,7},{6,4},{7,5},{8,10},{9,11},{10,... | collective-permute-start | bytes 393224 | tf_op jit(solution)/shard_map/ppermute | solution.py:21

commit v16 on v13

--- a/solution.py
+++ b/solution.py
@@ -171,7 +171,7 @@
         ],
         compiler_params=pltpu.CompilerParams(vmem_limit_bytes=8 << 20),
         cost_estimate=pl.CostEstimate(
-            flops=4 * rows * heads * positions * width,
+            flops=3 * 10**9,
             bytes_accessed=4 * rows * positions * width,
             transcendentals=rows * heads * positions,
         ),
@@ -230,7 +230,7 @@
         ],
         in_specs=[pl.BlockSpec(memory_space=pltpu.SMEM), whole, whole],
         out_specs=[whole] * len(apart),
-        compiler_params=pltpu.CompilerParams(vmem_limit_bytes=6 << 20),
+        compiler_params=pltpu.CompilerParams(vmem_limit_bytes=24 << 20),
         cost_estimate=pl.CostEstimate(
             flops=cost * rows * width * block * len(apart),
             bytes_accessed=2 * width * block * len(apart),
@@ -466,8 +466,8 @@
     shrink_factors = [shrink_weight, to_sibling(shrink_weight)]
     expand_factors = [expand_weight, to_sibling(expand_weight)]
     visiting = [to_chip(tagged, shift) for shift in range(1, chips)]
-    weight = pltpu.with_memory_space_constraint(out_weight, VMEM)
-    (third,) = base_terms(tensor_at, tagged, early, block, [3], 120)
+    weight = out_weight
+    (third,) = base_terms(tensor_at, tagged, early, block, [3], 20)
     visiting, limits = lax.optimization_barrier((visiting, limits))
     blocks = [tagged] + visiting
     third = across(third, 1)

time: 31.6 us -> 30.7 us (0.972)
  other arithmetic: 1.59 us -> 0.05 us
  starting transfers between devices: 11.9 us -> 13.1 us
  waiting for transfers between devices: 4.22 us -> 3.71 us
    convert_element_type x1, other arithmetic: 1.58 us -> 0.04 us  [local(): second = (wide(second) + wide(third)).astype(BF16)]
    ppermute x10, starting transfers between devices: 11.9 us -> 13.1 us  [permuted(): return lax.ppermute(array, axis, [(i, partner(i)) for i in range(size)])]
    ppermute x10, waiting for transfers between devices: 4.22 us -> 3.71 us  [permuted(): return lax.ppermute(array, axis, [(i, partner(i)) for i in range(size)])]
    unnamed x8 -> x6, local copies, waits for them, and re-layouts: 5.78 us -> 5.78 us
  transfers between devices with their start and end apart: 10 -> 10, of which waited for: 2 -> 3; matrix products, arithmetic and copies ran while one was open for 5% -> 0% of each run, Pallas kernels for 14% -> 23%
where the time goes in v16:
time: 30.7 us; the launch traced here: 30.5 us
  starting transfers between devices  13.1 us (43%)
  Pallas kernels  7.82 us (25%)
  local copies, waits for them, and re-layouts  5.78 us (19%)
  waiting for transfers between devices  3.71 us (12%)
    ppermute x10, starting transfers between devices, permuted(): return lax.ppermute(array, axis, [(i, partner(i)) for i in range(size)])  13.1 us
    unnamed x6, local copies, waits for them, and re-layouts  5.78 us
    ppermute x10, waiting for transfers between devices, permuted(): return lax.ppermute(array, axis, [(i, partner(i)) for i in range(size)])  3.71 us
    pallas_call x3, Pallas kernels, base_terms(): pl.pallas_call(functools.partial(base_kernel, apart, min(block, 512)), ou...  3.15 us
    pallas_call x1, Pallas kernels, attend(): pl.pallas_call(functools.partial(attend_kernel, parts, rank_width), out_s...  2.85 us
    pallas_call x1, Pallas kernels, total(): pl.pallas_call(total_kernel, out_shape=jax.ShapeDtypeStruct((rows, block)...  0.69 us
  transfers between devices with their start and end apart: 10, of which 3 were waited for; matrix products, arithmetic and copies ran while one was open for 0% of the time, Pallas kernels for 23%

profile of v16, /device:TPU:0, one launch (start us, length us, event | category | flops | bytes accessed | tf_op | source)
XLA Modules:
  0.0 30.5 jit_solution(8006556049140799757)
XLA Ops:
  0.0 0.5 %collective-permute-start.2 = (bf16[4,64,1024]{2,1,0:T(8,128)(2,1)}, bf16[4,64,1024]{2,1,0:T(8,128)(2,1)S(1)}, u32[]{:S(2)}, u32[]{:S(2)}) collective-permute-start(bf16[4,64,1024]{2,1,0:T(8,128)(2,1)} %bitcast.8), channel_id=1, source_target_pairs={{0,1},{1,0},{2,3},{3,2},{4,5},{5,4},{6,7},{7,6},{8,9},{9,8},{10,11... | collective-permute-start | bytes 1572872 | tf_op jit(solution)/shard_map/ppermute | solution.py:19
  0.5 0.1 collective-permute-start.6
  0.5 2.8 %attention.1 = (bf16[32,1152]{1,0:T(8,128)(2,1)S(1)}, bf16[1024,2048]{1,0:T(8,128)(2,1)S(1)}, s32[8,128]{1,0:T(8,128)S(1)}) custom-call(s32[1]{0:T(128)} %bitcast.2.group_at, s32[1]{0:T(128)S(6)} %xor.3.early_at, bf16[32,4,96,128]{3,2,1,0:T(8,128)(2,1)} %refs_0_.1, bf16[32,4,96,128]{3,2,1,0:T(8,128)(2,1)} %refs_1_.1, bf16[32,8,128]{2,1,0:T(8,128)(2,1)} %refs_2_.1, ...), custom_call_target="tpu_custom_call" | custom-call | flops 3000000000 | bytes 1572864 | tf_op jit(solution)/shard_map/attention/pallas_call | solution.py:147
  3.4 0.0 copy-start.2
  3.4 3.0 %collective-permute-start = (bf16[32,1152]{1,0:T(8,128)(2,1)S(1)}, bf16[32,1152]{1,0:T(8,128)(2,1)S(1)}, u32[]{:S(2)}, u32[]{:S(2)}) collective-permute-start(bf16[32,1152]{1,0:T(8,128)(2,1)S(1)} %get-tuple-element.38.refs_0_.tagged.refs_2_), channel_id=1, source_target_pairs={{0,2},{1,3},{2,0},{3,1},{4,6},{5,7},{6,4},{7,5},{8,10},{9,11},{10,... | collective-permute-start | bytes 221192 | tf_op jit(solution)/shard_map/ppermute | solution.py:19
  6.4 0.0 collective-permute-start.1
  6.4 0.8 %base_terms.4 = bf16[512,128]{1,0:T(8,128)(2,1)S(1)} custom-call(s32[1]{0:T(128)} %bitcast.tensor_at, bf16[32,1152]{1,0:T(8,128)(2,1)S(1)} %get-tuple-element.38.refs_0_.tagged.refs_2_, bf16[1024,2048]{1,0:T(8,128)(2,1)S(1)} %get-tuple-element.31.weight), custom_call_target="tpu_custom_call" | custom-call | flops 1342177280 | bytes 4194304 | tf_op jit(solution)/shard_map/base_terms/pallas_call | solution.py:225
  7.2 1.6 %collective-permute-start.4 = (bf16[512,128]{1,0:T(8,128)(2,1)S(1)}, bf16[512,128]{1,0:T(8,128)(2,1)S(1)}, u32[]{:S(2)}, u32[]{:S(2)}) collective-permute-start(bf16[512,128]{1,0:T(8,128)(2,1)S(1)} %base_terms.4), channel_id=1, source_target_pairs={{0,4},{4,0},{8,12},{12,8},{1,5},{5,1},{9,13},{13,9},{2,6},{6,2},{1... | collective-permute-start | bytes 393224 | tf_op jit(solution)/shard_map/ppermute | solution.py:19
  8.8 0.0 collective-permute-done.1.refs_1_
  8.8 0.0 collective-permute-done.refs_1_.refs_3_
  8.8 0.0 collective-permute-done.2.refs_3_
  8.8 0.0 copy-done.2
  8.8 0.5 %shrink.1 = bf16[32,128]{1,0:T(8,128)(2,1)S(1)} custom-call(s32[1]{0:T(128)} %bitcast.1.batch_at, bf16[32,1152]{1,0:T(8,128)(2,1)S(1)} %get-tuple-element.38.refs_0_.tagged.refs_2_, bf16[32,1152]{1,0:T(8,128)(2,1)S(1)} %collective-permute-done.refs_1_.refs_3_, bf16[4,64,1024]{2,1,0:T(8,128)(2,1)S(1)} %bitcast.9, ...), custom_call_target="tpu_custom_call" | custom-call | flops 67108864 | bytes 1179648 | tf_op jit(solution)/shard_map/shrink/pallas_call | solution.py:281
  9.3 2.1 %collective-permute-start.3 = (bf16[32,128]{1,0:T(8,128)(2,1)S(1)}, bf16[32,128]{1,0:T(8,128)(2,1)S(1)}, u32[]{:S(2)}, u32[]{:S(2)}) collective-permute-start(bf16[32,128]{1,0:T(8,128)(2,1)S(1)} %shrink.1), channel_id=1, source_target_pairs={{0,4},{4,0},{8,12},{12,8},{1,5},{5,1},{9,13},{13,9},{2,6},{6,2},{1... | collective-permute-start | bytes 24584 | tf_op jit(solution)/shard_map/ppermute | solution.py:19
  11.4 0.0 copy-start
  11.4 5.8 %copy-done = bf16[1024,8192]{1,0:T(8,128)(2,1)S(1)} copy-done((bf16[1024,8192]{1,0:T(8,128)(2,1)S(1)}, bf16[1024,8192]{1,0:T(8,128)(2,1)}, u32[]{:S(2)}) %copy-start) | copy-done | bytes 16777240
  17.2 0.0 copy-start.1
  17.2 1.5 %base_terms.3 = (bf16[512,128]{1,0:T(8,128)(2,1)S(1)}, bf16[512,128]{1,0:T(8,128)(2,1)S(1)}) custom-call(s32[1]{0:T(128)} %bitcast.tensor_at, bf16[32,1152]{1,0:T(8,128)(2,1)S(1)} %get-tuple-element.38.refs_0_.tagged.refs_2_, bf16[1024,8192]{1,0:T(8,128)(2,1)S(1)} %copy-done), custom_call_target="tpu_custom_call" | custom-call | flops 2684354560 | bytes 8388608 | tf_op jit(solution)/shard_map/base_terms/pallas_call | solution.py:225
  18.7 0.0 collective-permute-done.4
  18.8 0.0 collective-permute-done.3
  18.8 2.7 %collective-permute-start.5 = (bf16[32,128]{1,0:T(8,128)(2,1)S(1)}, bf16[32,128]{1,0:T(8,128)(2,1)S(1)}, u32[]{:S(2)}, u32[]{:S(2)}) collective-permute-start(bf16[32,128]{1,0:T(8,128)(2,1)S(1)} %add_convert_fusion.1.refs_4_), channel_id=1, source_target_pairs={{0,8},{4,12},{8,0},{12,4},{1,9},{5,13},{9,1},{13,5},{2,10},{6,14},... | collective-permute-start | bytes 24584 | tf_op jit(solution)/shard_map/ppermute | solution.py:19
  21.5 0.3 %collective-permute-start.7 = (bf16[512,128]{1,0:T(8,128)(2,1)S(1)}, bf16[512,128]{1,0:T(8,128)(2,1)S(1)}, u32[]{:S(2)}, u32[]{:S(2)}) collective-permute-start(bf16[512,128]{1,0:T(8,128)(2,1)S(1)} %add_convert_fusion), channel_id=1, source_target_pairs={{0,8},{4,12},{8,0},{12,4},{1,9},{5,13},{9,1},{13,5},{2,10},{6,14},... | collective-permute-start | bytes 393224 | tf_op jit(solution)/shard_map/ppermute | solution.py:19
  21.8 0.2 collective-permute-start.8
  22.0 1.6 %collective-permute-done.5.refs_5_ = bf16[32,128]{1,0:T(8,128)(2,1)S(1)} collective-permute-done((bf16[32,128]{1,0:T(8,128)(2,1)S(1)}, bf16[32,128]{1,0:T(8,128)(2,1)S(1)}, u32[]{:S(2)}, u32[]{:S(2)}) %collective-permute-start.5) | collective-permute-done | bytes 8224 | tf_op jit(solution)/shard_map/ppermute | solution.py:19
  23.6 0.0 collective-permute-done.6
  23.6 0.0 copy-done.1
  23.6 0.5 %expand.1 = (bf16[512,128]{1,0:T(8,128)(2,1)S(1)}, bf16[512,128]{1,0:T(8,128)(2,1)S(1)}) custom-call(s32[1]{0:T(128)} %bitcast.1.batch_at, s32[8,128]{1,0:T(8,128)S(1)} %get-tuple-element.26.refs_0_, s32[8,128]{1,0:T(8,128)S(1)} %collective-permute-done.1.refs_1_, bf16[32,1152]{1,0:T(8,128)(2,1)S(1)} %get-tuple-element.38.refs_0_.tagged.refs_2_, ...), custom_call_target="tpu_custom_call" | custom-call | flops 134217728 | bytes 1048576 | tf_op jit(solution)/shard_map/expand/pallas_call | solution.py:341
  24.1 2.7 %collective-permute-start.9 = (bf16[512,128]{1,0:T(8,128)(2,1)S(1)}, bf16[512,128]{1,0:T(8,128)(2,1)S(1)}, u32[]{:S(2)}, u32[]{:S(2)}) collective-permute-start(bf16[512,128]{1,0:T(8,128)(2,1)S(1)} %get-tuple-element.42), channel_id=1, source_target_pairs={{0,2},{1,3},{2,0},{3,1},{4,6},{5,7},{6,4},{7,5},{8,10},{9,11},{10,... | collective-permute-start | bytes 393224 | tf_op jit(solution)/shard_map/ppermute | solution.py:19
  26.9 0.8 %base_terms.5.refs_0_ = f32[512,128]{1,0:T(8,128)S(1)} custom-call(s32[1]{0:T(128)} %bitcast.tensor_at, bf16[32,1152]{1,0:T(8,128)(2,1)S(1)} %get-tuple-element.38.refs_0_.tagged.refs_2_, bf16[1024,8192]{1,0:T(8,128)(2,1)S(1)} %copy-done), custom_call_target="tpu_custom_call" | custom-call | flops 1342177280 | bytes 4194304 | tf_op jit(solution)/shard_map/base_terms/pallas_call | solution.py:225
  27.7 1.2 %collective-permute-done.7.refs_2_ = bf16[512,128]{1,0:T(8,128)(2,1)S(1)} collective-permute-done((bf16[512,128]{1,0:T(8,128)(2,1)S(1)}, bf16[512,128]{1,0:T(8,128)(2,1)S(1)}, u32[]{:S(2)}, u32[]{:S(2)}) %collective-permute-start.7) | collective-permute-done | bytes 131104 | tf_op jit(solution)/shard_map/ppermute | solution.py:19
  29.0 0.0 collective-permute-done.8.refs_1_
  29.0 0.8 %collective-permute-done.9.refs_1_ = bf16[512,128]{1,0:T(8,128)(2,1)S(1)} collective-permute-done((bf16[512,128]{1,0:T(8,128)(2,1)S(1)}, bf16[512,128]{1,0:T(8,128)(2,1)S(1)}, u32[]{:S(2)}, u32[]{:S(2)}) %collective-permute-start.9) | collective-permute-done | bytes 131104 | tf_op jit(solution)/shard_map/ppermute | solution.py:19
  29.8 0.7 %total.1 = bf16[32,2048]{1,0:T(8,128)(2,1)} custom-call(f32[512,128]{1,0:T(8,128)S(1)} %partial_total.3.refs_0_, bf16[512,128]{1,0:T(8,128)(2,1)S(1)} %collective-permute-done.9.refs_1_), custom_call_target="tpu_custom_call" | custom-call | flops 131072 | bytes 393216 | tf_op jit(solution)/shard_map/total/pallas_call | solution.py:374
  (4 shorter events, 0.1 us)
Async XLA Ops:
  0.0 8.8 %collective-permute-start.2 = (bf16[4,64,1024]{2,1,0:T(8,128)(2,1)}, bf16[4,64,1024]{2,1,0:T(8,128)(2,1)S(1)}, u32[]{:S(2)}, u32[]{:S(2)}) collective-permute-start(bf16[4,64,1024]{2,1,0:T(8,128)(2,1)} %bitcast.8), channel_id=1, source_target_pairs={{0,1},{1,0},{2,3},{3,2},{4,5},{5,4},{6,7},{7,6},{8,9},{9,8},{10,11... | collective-permute-start | bytes 1572872 | tf_op jit(solution)/shard_map/ppermute | solution.py:19
  0.5 23.2 %collective-permute-start.6 = (bf16[4,64,2048]{2,1,0:T(8,128)(2,1)}, bf16[4,64,2048]{2,1,0:T(8,128)(2,1)S(1)}, u32[]{:S(2)}, u32[]{:S(2)}) collective-permute-start(bf16[4,64,2048]{2,1,0:T(8,128)(2,1)} %param.20), channel_id=1, source_target_pairs={{0,1},{1,0},{2,3},{3,2},{4,5},{5,4},{6,7},{7,6},{8,9},{9,8},{10,11... | collective-permute-start | bytes 3145736 | tf_op jit(solution)/shard_map/ppermute | solution.py:19
  3.4 5.5 %copy-start.2 = (bf16[4,1024,64]{1,2,0:T(8,128)(2,1)S(1)}, bf16[4,1024,64]{1,2,0:T(8,128)(2,1)}, u32[]{:S(2)}) copy-start(bf16[4,1024,64]{1,2,0:T(8,128)(2,1)} %param.19) | copy-start | bytes 1572868
  3.4 5.4 %collective-permute-start = (bf16[32,1152]{1,0:T(8,128)(2,1)S(1)}, bf16[32,1152]{1,0:T(8,128)(2,1)S(1)}, u32[]{:S(2)}, u32[]{:S(2)}) collective-permute-start(bf16[32,1152]{1,0:T(8,128)(2,1)S(1)} %get-tuple-element.38.refs_0_.tagged.refs_2_), channel_id=1, source_target_pairs={{0,2},{1,3},{2,0},{3,1},{4,6},{5,7},{6,4},{7,5},{8,10},{9,11},{10,... | collective-permute-start | bytes 221192 | tf_op jit(solution)/shard_map/ppermute | solution.py:19
  6.4 2.4 %collective-permute-start.1 = (s32[8,128]{1,0:T(8,128)S(1)}, s32[8,128]{1,0:T(8,128)S(1)}, u32[]{:S(2)}, u32[]{:S(2)}) collective-permute-start(s32[8,128]{1,0:T(8,128)S(1)} %get-tuple-element.26.refs_0_), channel_id=1, source_target_pairs={{0,1},{1,0},{2,3},{3,2},{4,5},{5,4},{6,7},{7,6},{8,9},{9,8},{10,11... | collective-permute-start | bytes 12296 | tf_op jit(solution)/shard_map/ppermute | solution.py:19
  7.2 11.5 %collective-permute-start.4 = (bf16[512,128]{1,0:T(8,128)(2,1)S(1)}, bf16[512,128]{1,0:T(8,128)(2,1)S(1)}, u32[]{:S(2)}, u32[]{:S(2)}) collective-permute-start(bf16[512,128]{1,0:T(8,128)(2,1)S(1)} %base_terms.4), channel_id=1, source_target_pairs={{0,4},{4,0},{8,12},{12,8},{1,5},{5,1},{9,13},{13,9},{2,6},{6,2},{1... | collective-permute-start | bytes 393224 | tf_op jit(solution)/shard_map/ppermute | solution.py:19
  9.3 9.4 %collective-permute-start.3 = (bf16[32,128]{1,0:T(8,128)(2,1)S(1)}, bf16[32,128]{1,0:T(8,128)(2,1)S(1)}, u32[]{:S(2)}, u32[]{:S(2)}) collective-permute-start(bf16[32,128]{1,0:T(8,128)(2,1)S(1)} %shrink.1), channel_id=1, source_target_pairs={{0,4},{4,0},{8,12},{12,8},{1,5},{5,1},{9,13},{13,9},{2,6},{6,2},{1... | collective-permute-start | bytes 24584 | tf_op jit(solution)/shard_map/ppermute | solution.py:19
  11.4 5.8 %copy-start = (bf16[1024,8192]{1,0:T(8,128)(2,1)S(1)}, bf16[1024,8192]{1,0:T(8,128)(2,1)}, u32[]{:S(2)}) copy-start(bf16[1024,8192]{1,0:T(8,128)(2,1)} %weight.3) | copy-start | bytes 50331652
  17.2 6.4 %copy-start.1 = (bf16[4,64,2048]{2,1,0:T(8,128)(2,1)S(1)}, bf16[4,64,2048]{2,1,0:T(8,128)(2,1)}, u32[]{:S(2)}) copy-start(bf16[4,64,2048]{2,1,0:T(8,128)(2,1)} %param.20) | copy-start | bytes 3145732
  18.8 4.8 %collective-permute-start.5 = (bf16[32,128]{1,0:T(8,128)(2,1)S(1)}, bf16[32,128]{1,0:T(8,128)(2,1)S(1)}, u32[]{:S(2)}, u32[]{:S(2)}) collective-permute-start(bf16[32,128]{1,0:T(8,128)(2,1)S(1)} %add_convert_fusion.1.refs_4_), channel_id=1, source_target_pairs={{0,8},{4,12},{8,0},{12,4},{1,9},{5,13},{9,1},{13,5},{2,10},{6,14},... | collective-permute-start | bytes 24584 | tf_op jit(solution)/shard_map/ppermute | solution.py:19
  21.5 7.5 %collective-permute-start.7 = (bf16[512,128]{1,0:T(8,128)(2,1)S(1)}, bf16[512,128]{1,0:T(8,128)(2,1)S(1)}, u32[]{:S(2)}, u32[]{:S(2)}) collective-permute-start(bf16[512,128]{1,0:T(8,128)(2,1)S(1)} %add_convert_fusion), channel_id=1, source_target_pairs={{0,8},{4,12},{8,0},{12,4},{1,9},{5,13},{9,1},{13,5},{2,10},{6,14},... | collective-permute-start | bytes 393224 | tf_op jit(solution)/shard_map/ppermute | solution.py:19
  21.8 7.2 %collective-permute-start.8 = (bf16[512,128]{1,0:T(8,128)(2,1)S(1)}, bf16[512,128]{1,0:T(8,128)(2,1)S(1)}, u32[]{:S(2)}, u32[]{:S(2)}) collective-permute-start(bf16[512,128]{1,0:T(8,128)(2,1)S(1)} %get-tuple-element.41), channel_id=1, source_target_pairs={{0,4},{4,0},{8,12},{12,8},{1,5},{5,1},{9,13},{13,9},{2,6},{6,2},{1... | collective-permute-start | bytes 393224 | tf_op jit(solution)/shard_map/ppermute | solution.py:19
  24.1 5.7 %collective-permute-start.9 = (bf16[512,128]{1,0:T(8,128)(2,1)S(1)}, bf16[512,128]{1,0:T(8,128)(2,1)S(1)}, u32[]{:S(2)}, u32[]{:S(2)}) collective-permute-start(bf16[512,128]{1,0:T(8,128)(2,1)S(1)} %get-tuple-element.42), channel_id=1, source_target_pairs={{0,2},{1,3},{2,0},{3,1},{4,6},{5,7},{6,4},{7,5},{8,10},{9,11},{10,... | collective-permute-start | bytes 393224 | tf_op jit(solution)/shard_map/ppermute | solution.py:19

commit v17 on v8

--- a/solution.py
+++ b/solution.py
@@ -248,7 +248,7 @@
             copy(at + deep).start()
 
 
-def base_block(tensor_at, tagged, out_weight, block, ahead, early=(), arrived=()):
+def base_block(tensor_at, tagged, out_weight, block, ahead, early=(), arrived=(), cost=2):
     rows = tagged.shape[0]
     width = out_weight.shape[0]
     deep, deep_rows = 4, min(width, 256)
@@ -268,7 +268,7 @@
         ],
         compiler_params=pltpu.CompilerParams(vmem_limit_bytes=12 << 20),
         cost_estimate=pl.CostEstimate(
-            flops=2 * rows * width * block * count,
+            flops=cost * rows * width * block * count,
             bytes_accessed=2 * width * block * (2 if arrived else count),
             transcendentals=0,
         ),
@@ -502,17 +502,17 @@
     shrink_factors = [shrink_weight, to_sibling(shrink_weight)]
     expand_factors = [expand_weight, to_sibling(expand_weight)]
     visiting = [to_chip(tagged, shift) for shift in range(1, chips)]
-    third, next_door = base_block(tensor_at, tagged, out_weight, block, 1, [early])
-    visiting, third, next_door, limits = lax.optimization_barrier(
-        (visiting, third, next_door, limits)
-    )
+    third, next_door = base_block(
+        tensor_at, tagged, out_weight, block, 1, [early], (), 30
+    )
+    visiting, next_door, limits = lax.optimization_barrier((visiting, next_door, limits))
     blocks = [tagged] + visiting
     third = across(third, 1)
 
     part = shrink_part(blocks, shrink_factors, batch_at)
     parts = [part, across(part, 1)]
     part, later_tagged = lax.optimization_barrier((part, tagged))
-    (second,) = base_block(tensor_at, later_tagged, out_weight, block, 2)
+    (second,) = base_block(tensor_at, later_tagged, out_weight, block, 2, (), (), 120)
     second = (wide(second) + wide(third)).astype(BF16)
     parts, second = lax.optimization_barrier((parts, second))
     bit = 2
@@ -529,7 +529,7 @@
 
     deltas = expand(blocks, parts, expand_factors, limits, batch_at)
     deltas, late_tagged = lax.optimization_barrier((deltas, tagged))
-    (own,) = base_block(tensor_at, late_tagged, out_weight, block, 0)
+    (own,) = base_block(tensor_at, late_tagged, out_weight, block, 0, (), (), 60)
     so_far = partial_total([own, deltas[0], arrived[0], *arrived[2:]], 0)
     terms = [partial_total([so_far, arrived[1]], 8 << 20)]
     terms += [to_chip(home, -shift) for shift, home in enumerate(deltas[1:], 1)]

time: 27.1 us -> 28.2 us (1.041)
  starting transfers between devices: 11.8 us -> 10.4 us
  waiting for transfers between devices: 2.76 us -> 3.85 us
  other arithmetic: 0.04 us -> 0.95 us
  Pallas kernels: 12.2 us -> 12.7 us
    ppermute x10, starting transfers between devices: 11.8 us -> 10.4 us  [permuted(): return lax.ppermute(array, axis, [(i, partner(i)) for i in range(size)])]
    ppermute x10, waiting for transfers between devices: 2.76 us -> 3.85 us  [permuted(): return lax.ppermute(array, axis, [(i, partner(i)) for i in range(size)])]
    convert_element_type x1, other arithmetic: 0.04 us -> 0.94 us  [local(): second = (wide(second) + wide(third)).astype(BF16)]
    pallas_call x3, Pallas kernels: 7.59 us -> 8.06 us  [base_block(): pl.pallas_call(functools.partial(base_kernel, ahead, deep, len(arrived)),...]
  transfers between devices with their start and end apart: 10 -> 10, of which waited for: 2 -> 3; matrix products, arithmetic and copies ran while one was open for 0% -> 3% of each run, Pallas kernels for 43% -> 43%
where the time goes in v17:
time: 28.2 us; the launch traced here: 28 us
  Pallas kernels  12.7 us (45%)
  starting transfers between devices  10.4 us (37%)
  waiting for transfers between devices  3.85 us (14%)
  other arithmetic  0.95 us (3%)
    ppermute x10, starting transfers between devices, permuted(): return lax.ppermute(array, axis, [(i, partner(i)) for i in range(size)])  10.4 us
    pallas_call x3, Pallas kernels, base_block(): pl.pallas_call(functools.partial(base_kernel, ahead, deep, len(arrived)),...  8.06 us
    ppermute x10, waiting for transfers between devices, permuted(): return lax.ppermute(array, axis, [(i, partner(i)) for i in range(size)])  3.85 us
    pallas_call x1, Pallas kernels, attend(): pl.pallas_call(functools.partial(attend_kernel, parts, rank_width), out_s...  2.85 us
    convert_element_type x1, other arithmetic, local(): second = (wide(second) + wide(third)).astype(BF16)  0.94 us
    pallas_call x1, Pallas kernels, total(): pl.pallas_call(total_kernel, out_shape=jax.ShapeDtypeStruct((rows, block)...  0.69 us
  transfers between devices with their start and end apart: 10, of which 3 were waited for; matrix products, arithmetic and copies ran while one was open for 3% of the time, Pallas kernels for 43%

profile of v17, /device:TPU:0, one launch (start us, length us, event | category | flops | bytes accessed | tf_op | source)
XLA Modules:
  0.0 28.0 jit_solution(17611586114637028549)
XLA Ops:
  0.0 0.5 %collective-permute-start.2 = (bf16[4,64,1024]{2,1,0:T(8,128)(2,1)}, bf16[4,64,1024]{2,1,0:T(8,128)(2,1)S(1)}, u32[]{:S(2)}, u32[]{:S(2)}) collective-permute-start(bf16[4,64,1024]{2,1,0:T(8,128)(2,1)} %bitcast.8), channel_id=1, source_target_pairs={{0,1},{1,0},{2,3},{3,2},{4,5},{5,4},{6,7},{7,6},{8,9},{9,8},{10,11... | collective-permute-start | bytes 1572872 | tf_op jit(solution)/shard_map/ppermute | solution.py:19
  0.5 2.8 %attention.1 = (bf16[32,1152]{1,0:T(8,128)(2,1)S(1)}, bf16[1024,2048]{1,0:T(8,128)(2,1)S(1)}, s32[8,128]{1,0:T(8,128)S(1)}) custom-call(s32[1]{0:T(128)} %bitcast.2.group_at, s32[1]{0:T(128)S(6)} %xor.3.early_at, bf16[32,4,96,128]{3,2,1,0:T(8,128)(2,1)} %refs_0_.1, bf16[32,4,96,128]{3,2,1,0:T(8,128)(2,1)} %refs_1_.1, bf16[32,8,128]{2,1,0:T(8,128)(2,1)} %refs_2_.1, ...), custom_call_target="tpu_custom_call" | custom-call | flops 12582912 | bytes 1572864 | tf_op jit(solution)/shard_map/attention/pallas_call | solution.py:147
  3.3 2.6 %collective-permute-start = (bf16[32,1152]{1,0:T(8,128)(2,1)S(1)}, bf16[32,1152]{1,0:T(8,128)(2,1)S(1)}, u32[]{:S(2)}, u32[]{:S(2)}) collective-permute-start(bf16[32,1152]{1,0:T(8,128)(2,1)S(1)} %get-tuple-element.40.tagged.refs_0_.refs_2_), channel_id=1, source_target_pairs={{0,2},{1,3},{2,0},{3,1},{4,6},{5,7},{6,4},{7,5},{8,10},{9,11},{10,... | collective-permute-start | bytes 221192 | tf_op jit(solution)/shard_map/ppermute | solution.py:19
  5.9 0.2 collective-permute-start.1
  6.1 0.0 copy-start
  6.1 0.0 copy-start.1
  6.1 3.1 %base_terms.3 = (bf16[512,128]{1,0:T(8,128)(2,1)}, bf16[512,128]{1,0:T(8,128)(2,1)S(1)}) custom-call(s32[1]{0:T(128)} %bitcast.tensor_at, bf16[32,1152]{1,0:T(8,128)(2,1)S(1)} %get-tuple-element.40.tagged.refs_0_.refs_2_, bf16[1024,8192]{1,0:T(8,128)(2,1)} %out_weight.5, bf16[1024,2048]{1,0:T(8,128)(2,1)S(1)} %get-tuple-element.26.refs_0_), custom_call_target="tpu_custom_call" | custom-call | flops 4026531840 | bytes 8388608 | tf_op jit(solution)/shard_map/base_terms/pallas_call | solution.py:257
  9.2 1.6 %collective-permute-start.4 = (bf16[512,128]{1,0:T(8,128)(2,1)}, bf16[512,128]{1,0:T(8,128)(2,1)}, u32[]{:S(2)}, u32[]{:S(2)}) collective-permute-start(bf16[512,128]{1,0:T(8,128)(2,1)} %get-tuple-element.33), channel_id=1, source_target_pairs={{0,4},{4,0},{8,12},{12,8},{1,5},{5,1},{9,13},{13,9},{2,6},{6,2},{1... | collective-permute-start | bytes 393224 | tf_op jit(solution)/shard_map/ppermute | solution.py:19
  10.8 0.0 copy-done
  10.8 0.0 collective-permute-start.6
  10.8 0.0 collective-permute-done.1.refs_1_
  10.8 0.0 collective-permute-done.refs_1_.refs_3_
  10.8 0.0 collective-permute-done.2.refs_3_
  10.8 0.0 copy-done.1
  10.8 0.5 %shrink.1 = bf16[32,128]{1,0:T(8,128)(2,1)S(1)} custom-call(s32[1]{0:T(128)} %bitcast.1.batch_at, bf16[32,1152]{1,0:T(8,128)(2,1)S(1)} %get-tuple-element.40.tagged.refs_0_.refs_2_, bf16[32,1152]{1,0:T(8,128)(2,1)S(1)} %collective-permute-done.refs_1_.refs_3_, bf16[4,64,1024]{2,1,0:T(8,128)(2,1)S(1)} %bitcast.9, ...), custom_call_target="tpu_custom_call" | custom-call | flops 67108864 | bytes 1179648 | tf_op jit(solution)/shard_map/shrink/pallas_call | solution.py:317
  11.4 0.5 %collective-permute-start.3 = (bf16[32,128]{1,0:T(8,128)(2,1)S(1)}, bf16[32,128]{1,0:T(8,128)(2,1)S(1)}, u32[]{:S(2)}, u32[]{:S(2)}) collective-permute-start(bf16[32,128]{1,0:T(8,128)(2,1)S(1)} %shrink.1), channel_id=1, source_target_pairs={{0,4},{4,0},{8,12},{12,8},{1,5},{5,1},{9,13},{13,9},{2,6},{6,2},{1... | collective-permute-start | bytes 24584 | tf_op jit(solution)/shard_map/ppermute | solution.py:19
  11.9 2.5 %base_terms.4 = bf16[512,128]{1,0:T(8,128)(2,1)S(1)} custom-call(s32[1]{0:T(128)} %bitcast.tensor_at, bf16[32,1152]{1,0:T(8,128)(2,1)S(1)} %get-tuple-element.40.tagged.refs_0_.refs_2_, bf16[1024,8192]{1,0:T(8,128)(2,1)} %out_weight.5), custom_call_target="tpu_custom_call" | custom-call | flops 8053063680 | bytes 4194304 | tf_op jit(solution)/shard_map/base_terms/pallas_call | solution.py:257
  14.4 0.9 %collective-permute-done.4 = bf16[512,128]{1,0:T(8,128)(2,1)} collective-permute-done((bf16[512,128]{1,0:T(8,128)(2,1)}, bf16[512,128]{1,0:T(8,128)(2,1)}, u32[]{:S(2)}, u32[]{:S(2)}) %collective-permute-start.4) | collective-permute-done | bytes 131104 | tf_op jit(solution)/shard_map/ppermute | solution.py:19
  15.3 0.9 %add_convert_fusion = bf16[512,128]{1,0:T(8,128)(2,1)S(1)} fusion(bf16[512,128]{1,0:T(8,128)(2,1)} %collective-permute-done.4, bf16[512,128]{1,0:T(8,128)(2,1)S(1)} %base_terms.4), kind=kLoop, calls=%fused_computation | loop fusion | flops 262144 | bytes 393216 | tf_op jit(solution)/shard_map/convert_element_type | solution.py:516
  16.3 0.0 collective-permute-done.3
  16.3 2.7 %collective-permute-start.5 = (bf16[32,128]{1,0:T(8,128)(2,1)S(1)}, bf16[32,128]{1,0:T(8,128)(2,1)S(1)}, u32[]{:S(2)}, u32[]{:S(2)}) collective-permute-start(bf16[32,128]{1,0:T(8,128)(2,1)S(1)} %add_convert_fusion.1.refs_4_), channel_id=1, source_target_pairs={{0,8},{4,12},{8,0},{12,4},{1,9},{5,13},{9,1},{13,5},{2,10},{6,14},... | collective-permute-start | bytes 24584 | tf_op jit(solution)/shard_map/ppermute | solution.py:19
  18.9 0.3 %collective-permute-start.7 = (bf16[512,128]{1,0:T(8,128)(2,1)S(1)}, bf16[512,128]{1,0:T(8,128)(2,1)S(1)}, u32[]{:S(2)}, u32[]{:S(2)}) collective-permute-start(bf16[512,128]{1,0:T(8,128)(2,1)S(1)} %add_convert_fusion), channel_id=1, source_target_pairs={{0,8},{4,12},{8,0},{12,4},{1,9},{5,13},{9,1},{13,5},{2,10},{6,14},... | collective-permute-start | bytes 393224 | tf_op jit(solution)/shard_map/ppermute | solution.py:19
  19.3 1.6 %collective-permute-start.8 = (bf16[512,128]{1,0:T(8,128)(2,1)S(1)}, bf16[512,128]{1,0:T(8,128)(2,1)S(1)}, u32[]{:S(2)}, u32[]{:S(2)}) collective-permute-start(bf16[512,128]{1,0:T(8,128)(2,1)S(1)} %get-tuple-element.43), channel_id=1, source_target_pairs={{0,4},{4,0},{8,12},{12,8},{1,5},{5,1},{9,13},{13,9},{2,6},{6,2},{1... | collective-permute-start | bytes 393224 | tf_op jit(solution)/shard_map/ppermute | solution.py:19
  20.9 0.2 collective-permute-done.5.refs_5_
  21.0 0.0 collective-permute-done.6
  21.0 0.5 %expand.1 = (bf16[512,128]{1,0:T(8,128)(2,1)S(1)}, bf16[512,128]{1,0:T(8,128)(2,1)S(1)}) custom-call(s32[1]{0:T(128)} %bitcast.1.batch_at, s32[8,128]{1,0:T(8,128)S(1)} %get-tuple-element.29.refs_0_, s32[8,128]{1,0:T(8,128)S(1)} %collective-permute-done.1.refs_1_, bf16[32,1152]{1,0:T(8,128)(2,1)S(1)} %get-tuple-element.40.tagged.refs_0_.refs_2_, ...), custom_call_target="tpu_custom_call" | custom-call | flops 134217728 | bytes 1048576 | tf_op jit(solution)/shard_map/expand/pallas_call | solution.py:377
  21.6 0.4 %collective-permute-start.9 = (bf16[512,128]{1,0:T(8,128)(2,1)S(1)}, bf16[512,128]{1,0:T(8,128)(2,1)S(1)}, u32[]{:S(2)}, u32[]{:S(2)}) collective-permute-start(bf16[512,128]{1,0:T(8,128)(2,1)S(1)} %get-tuple-element.44), channel_id=1, source_target_pairs={{0,2},{1,3},{2,0},{3,1},{4,6},{5,7},{6,4},{7,5},{8,10},{9,11},{10,... | collective-permute-start | bytes 393224 | tf_op jit(solution)/shard_map/ppermute | solution.py:19
  22.0 2.5 %base_terms.5.refs_0_ = f32[512,128]{1,0:T(8,128)S(1)} custom-call(s32[1]{0:T(128)} %bitcast.tensor_at, bf16[32,1152]{1,0:T(8,128)(2,1)S(1)} %get-tuple-element.40.tagged.refs_0_.refs_2_, bf16[1024,8192]{1,0:T(8,128)(2,1)} %out_weight.5), custom_call_target="tpu_custom_call" | custom-call | flops 4026531840 | bytes 4194304 | tf_op jit(solution)/shard_map/base_terms/pallas_call | solution.py:257
  24.5 2.7 %collective-permute-done.7.refs_2_ = bf16[512,128]{1,0:T(8,128)(2,1)S(1)} collective-permute-done((bf16[512,128]{1,0:T(8,128)(2,1)S(1)}, bf16[512,128]{1,0:T(8,128)(2,1)S(1)}, u32[]{:S(2)}, u32[]{:S(2)}) %collective-permute-start.7) | collective-permute-done | bytes 131104 | tf_op jit(solution)/shard_map/ppermute | solution.py:19
  27.3 0.0 collective-permute-done.8.refs_1_
  27.3 0.0 collective-permute-done.9.refs_1_
  27.4 0.7 %total.1 = bf16[32,2048]{1,0:T(8,128)(2,1)} custom-call(f32[512,128]{1,0:T(8,128)S(1)} %partial_total.3.refs_0_, bf16[512,128]{1,0:T(8,128)(2,1)S(1)} %collective-permute-done.9.refs_1_), custom_call_target="tpu_custom_call" | custom-call | flops 131072 | bytes 393216 | tf_op jit(solution)/shard_map/total/pallas_call | solution.py:410
  (3 shorter events, 0.1 us)
Async XLA Ops:
  0.0 10.8 %collective-permute-start.2 = (bf16[4,64,1024]{2,1,0:T(8,128)(2,1)}, bf16[4,64,1024]{2,1,0:T(8,128)(2,1)S(1)}, u32[]{:S(2)}, u32[]{:S(2)}) collective-permute-start(bf16[4,64,1024]{2,1,0:T(8,128)(2,1)} %bitcast.8), channel_id=1, source_target_pairs={{0,1},{1,0},{2,3},{3,2},{4,5},{5,4},{6,7},{7,6},{8,9},{9,8},{10,11... | collective-permute-start | bytes 1572872 | tf_op jit(solution)/shard_map/ppermute | solution.py:19
  3.3 7.5 %collective-permute-start = (bf16[32,1152]{1,0:T(8,128)(2,1)S(1)}, bf16[32,1152]{1,0:T(8,128)(2,1)S(1)}, u32[]{:S(2)}, u32[]{:S(2)}) collective-permute-start(bf16[32,1152]{1,0:T(8,128)(2,1)S(1)} %get-tuple-element.40.tagged.refs_0_.refs_2_), channel_id=1, source_target_pairs={{0,2},{1,3},{2,0},{3,1},{4,6},{5,7},{6,4},{7,5},{8,10},{9,11},{10,... | collective-permute-start | bytes 221192 | tf_op jit(solution)/shard_map/ppermute | solution.py:19
  5.9 5.0 %collective-permute-start.1 = (s32[8,128]{1,0:T(8,128)S(1)}, s32[8,128]{1,0:T(8,128)S(1)}, u32[]{:S(2)}, u32[]{:S(2)}) collective-permute-start(s32[8,128]{1,0:T(8,128)S(1)} %get-tuple-element.29.refs_0_), channel_id=1, source_target_pairs={{0,1},{1,0},{2,3},{3,2},{4,5},{5,4},{6,7},{7,6},{8,9},{9,8},{10,11... | collective-permute-start | bytes 12296 | tf_op jit(solution)/shard_map/ppermute | solution.py:19
  6.1 4.7 %copy-start = (bf16[4,64,2048]{2,1,0:T(8,128)(2,1)S(1)}, bf16[4,64,2048]{2,1,0:T(8,128)(2,1)}, u32[]{:S(2)}) copy-start(bf16[4,64,2048]{2,1,0:T(8,128)(2,1)} %param.20) | copy-start | bytes 3145732
  6.1 4.7 %copy-start.1 = (bf16[4,1024,64]{1,2,0:T(8,128)(2,1)S(1)}, bf16[4,1024,64]{1,2,0:T(8,128)(2,1)}, u32[]{:S(2)}) copy-start(bf16[4,1024,64]{1,2,0:T(8,128)(2,1)} %param.19) | copy-start | bytes 1572868
  9.2 6.2 %collective-permute-start.4 = (bf16[512,128]{1,0:T(8,128)(2,1)}, bf16[512,128]{1,0:T(8,128)(2,1)}, u32[]{:S(2)}, u32[]{:S(2)}) collective-permute-start(bf16[512,128]{1,0:T(8,128)(2,1)} %get-tuple-element.33), channel_id=1, source_target_pairs={{0,4},{4,0},{8,12},{12,8},{1,5},{5,1},{9,13},{13,9},{2,6},{6,2},{1... | collective-permute-start | bytes 393224 | tf_op jit(solution)/shard_map/ppermute | solution.py:19
  10.8 10.2 %collective-permute-start.6 = (bf16[4,64,2048]{2,1,0:T(8,128)(2,1)S(1)}, bf16[4,64,2048]{2,1,0:T(8,128)(2,1)S(1)}, u32[]{:S(2)}, u32[]{:S(2)}) collective-permute-start(bf16[4,64,2048]{2,1,0:T(8,128)(2,1)S(1)} %copy-done), channel_id=1, source_target_pairs={{0,1},{1,0},{2,3},{3,2},{4,5},{5,4},{6,7},{7,6},{8,9},{9,8},{10,11... | collective-permute-start | bytes 3145736 | tf_op jit(solution)/shard_map/ppermute | solution.py:19
  11.4 4.9 %collective-permute-start.3 = (bf16[32,128]{1,0:T(8,128)(2,1)S(1)}, bf16[32,128]{1,0:T(8,128)(2,1)S(1)}, u32[]{:S(2)}, u32[]{:S(2)}) collective-permute-start(bf16[32,128]{1,0:T(8,128)(2,1)S(1)} %shrink.1), channel_id=1, source_target_pairs={{0,4},{4,0},{8,12},{12,8},{1,5},{5,1},{9,13},{13,9},{2,6},{6,2},{1... | collective-permute-start | bytes 24584 | tf_op jit(solution)/shard_map/ppermute | solution.py:19
  16.3 4.7 %collective-permute-start.5 = (bf16[32,128]{1,0:T(8,128)(2,1)S(1)}, bf16[32,128]{1,0:T(8,128)(2,1)S(1)}, u32[]{:S(2)}, u32[]{:S(2)}) collective-permute-start(bf16[32,128]{1,0:T(8,128)(2,1)S(1)} %add_convert_fusion.1.refs_4_), channel_id=1, source_target_pairs={{0,8},{4,12},{8,0},{12,4},{1,9},{5,13},{9,1},{13,5},{2,10},{6,14},... | collective-permute-start | bytes 24584 | tf_op jit(solution)/shard_map/ppermute | solution.py:19
  18.9 8.3 %collective-permute-start.7 = (bf16[512,128]{1,0:T(8,128)(2,1)S(1)}, bf16[512,128]{1,0:T(8,128)(2,1)S(1)}, u32[]{:S(2)}, u32[]{:S(2)}) collective-permute-start(bf16[512,128]{1,0:T(8,128)(2,1)S(1)} %add_convert_fusion), channel_id=1, source_target_pairs={{0,8},{4,12},{8,0},{12,4},{1,9},{5,13},{9,1},{13,5},{2,10},{6,14},... | collective-permute-start | bytes 393224 | tf_op jit(solution)/shard_map/ppermute | solution.py:19
  19.3 8.0 %collective-permute-start.8 = (bf16[512,128]{1,0:T(8,128)(2,1)S(1)}, bf16[512,128]{1,0:T(8,128)(2,1)S(1)}, u32[]{:S(2)}, u32[]{:S(2)}) collective-permute-start(bf16[512,128]{1,0:T(8,128)(2,1)S(1)} %get-tuple-element.43), channel_id=1, source_target_pairs={{0,4},{4,0},{8,12},{12,8},{1,5},{5,1},{9,13},{13,9},{2,6},{6,2},{1... | collective-permute-start | bytes 393224 | tf_op jit(solution)/shard_map/ppermute | solution.py:19
  21.6 5.8 %collective-permute-start.9 = (bf16[512,128]{1,0:T(8,128)(2,1)S(1)}, bf16[512,128]{1,0:T(8,128)(2,1)S(1)}, u32[]{:S(2)}, u32[]{:S(2)}) collective-permute-start(bf16[512,128]{1,0:T(8,128)(2,1)S(1)} %get-tuple-element.44), channel_id=1, source_target_pairs={{0,2},{1,3},{2,0},{3,1},{4,6},{5,7},{6,4},{7,5},{8,10},{9,11},{10,... | collective-permute-start | bytes 393224 | tf_op jit(solution)/shard_map/ppermute | solution.py:19

commit v18 on v17

--- a/solution.py
+++ b/solution.py
@@ -503,7 +503,7 @@
     expand_factors = [expand_weight, to_sibling(expand_weight)]
     visiting = [to_chip(tagged, shift) for shift in range(1, chips)]
     third, next_door = base_block(
-        tensor_at, tagged, out_weight, block, 1, [early], (), 30
+        tensor_at, tagged, out_weight, block, 1, [early], (), 2
     )
     visiting, next_door, limits = lax.optimization_barrier((visiting, next_door, limits))
     blocks = [tagged] + visiting
@@ -512,7 +512,7 @@
     part = shrink_part(blocks, shrink_factors, batch_at)
     parts = [part, across(part, 1)]
     part, later_tagged = lax.optimization_barrier((part, tagged))
-    (second,) = base_block(tensor_at, later_tagged, out_weight, block, 2, (), (), 120)
+    (second,) = base_block(tensor_at, later_tagged, out_weight, block, 2, (), (), 60)
     second = (wide(second) + wide(third)).astype(BF16)
     parts, second = lax.optimization_barrier((parts, second))
     bit = 2
@@ -529,7 +529,7 @@
 
     deltas = expand(blocks, parts, expand_factors, limits, batch_at)
     deltas, late_tagged = lax.optimization_barrier((deltas, tagged))
-    (own,) = base_block(tensor_at, late_tagged, out_weight, block, 0, (), (), 60)
+    (own,) = base_block(tensor_at, late_tagged, out_weight, block, 0, (), (), 2)
     so_far = partial_total([own, deltas[0], arrived[0], *arrived[2:]], 0)
     terms = [partial_total([so_far, arrived[1]], 8 << 20)]
     terms += [to_chip(home, -shift) for shift, home in enumerate(deltas[1:], 1)]

time: 28.2 us -> 27.3 us (0.968)
  other arithmetic: 0.95 us -> 0.04 us
  Pallas kernels: 12.7 us -> 12.2 us
  starting transfers between devices: 10.4 us -> 10.8 us
    convert_element_type x1, other arithmetic: 0.94 us -> 0.04 us  [local(): second = (wide(second) + wide(third)).astype(BF16)]
    pallas_call x3, Pallas kernels: 8.06 us -> 7.59 us  [base_block(): pl.pallas_call(functools.partial(base_kernel, ahead, deep, len(arrived)),...]
    ppermute x10, starting transfers between devices: 10.4 us -> 10.8 us  [permuted(): return lax.ppermute(array, axis, [(i, partner(i)) for i in range(size)])]
  transfers between devices with their start and end apart: 10 -> 10, of which waited for: 3 -> 2; matrix products, arithmetic and copies ran while one was open for 3% -> 0% of each run, Pallas kernels for 43% -> 43%
where the time goes in v18:
time: 27.3 us; the launch traced here: 27.1 us
  Pallas kernels  12.2 us (45%)
  starting transfers between devices  10.8 us (40%)
  waiting for transfers between devices  3.98 us (15%)
    ppermute x10, starting transfers between devices, permuted(): return lax.ppermute(array, axis, [(i, partner(i)) for i in range(size)])  10.8 us
    pallas_call x3, Pallas kernels, base_block(): pl.pallas_call(functools.partial(base_kernel, ahead, deep, len(arrived)),...  7.59 us
    ppermute x10, waiting for transfers between devices, permuted(): return lax.ppermute(array, axis, [(i, partner(i)) for i in range(size)])  3.98 us
    pallas_call x1, Pallas kernels, attend(): pl.pallas_call(functools.partial(attend_kernel, parts, rank_width), out_s...  2.85 us
    pallas_call x1, Pallas kernels, total(): pl.pallas_call(total_kernel, out_shape=jax.ShapeDtypeStruct((rows, block)...  0.69 us
  transfers between devices with their start and end apart: 10, of which 2 were waited for; matrix products, arithmetic and copies ran while one was open for 0% of the time, Pallas kernels for 43%

profile of v18, /device:TPU:0, one launch (start us, length us, event | category | flops | bytes accessed | tf_op | source)
XLA Modules:
  0.0 27.1 jit_solution(6157917815339227320)
XLA Ops:
  0.0 0.5 %collective-permute-start.2 = (bf16[4,64,1024]{2,1,0:T(8,128)(2,1)}, bf16[4,64,1024]{2,1,0:T(8,128)(2,1)S(1)}, u32[]{:S(2)}, u32[]{:S(2)}) collective-permute-start(bf16[4,64,1024]{2,1,0:T(8,128)(2,1)} %bitcast.8), channel_id=1, source_target_pairs={{0,1},{1,0},{2,3},{3,2},{4,5},{5,4},{6,7},{7,6},{8,9},{9,8},{10,11... | collective-permute-start | bytes 1572872 | tf_op jit(solution)/shard_map/ppermute | solution.py:19
  0.5 0.1 collective-permute-start.6
  0.5 2.8 %attention.1 = (bf16[32,1152]{1,0:T(8,128)(2,1)S(1)}, bf16[1024,2048]{1,0:T(8,128)(2,1)S(1)}, s32[8,128]{1,0:T(8,128)S(1)}) custom-call(s32[1]{0:T(128)} %bitcast.2.group_at, s32[1]{0:T(128)S(6)} %xor.3.early_at, bf16[32,4,96,128]{3,2,1,0:T(8,128)(2,1)} %refs_0_.1, bf16[32,4,96,128]{3,2,1,0:T(8,128)(2,1)} %refs_1_.1, bf16[32,8,128]{2,1,0:T(8,128)(2,1)} %refs_2_.1, ...), custom_call_target="tpu_custom_call" | custom-call | flops 12582912 | bytes 1572864 | tf_op jit(solution)/shard_map/attention/pallas_call | solution.py:147
  3.4 3.0 %collective-permute-start = (bf16[32,1152]{1,0:T(8,128)(2,1)S(1)}, bf16[32,1152]{1,0:T(8,128)(2,1)S(1)}, u32[]{:S(2)}, u32[]{:S(2)}) collective-permute-start(bf16[32,1152]{1,0:T(8,128)(2,1)S(1)} %get-tuple-element.40.tagged.refs_0_.refs_2_), channel_id=1, source_target_pairs={{0,2},{1,3},{2,0},{3,1},{4,6},{5,7},{6,4},{7,5},{8,10},{9,11},{10,... | collective-permute-start | bytes 221192 | tf_op jit(solution)/shard_map/ppermute | solution.py:19
  6.4 0.0 collective-permute-start.1
  6.4 0.0 copy-start.1
  6.4 2.6 %base_terms.3 = (bf16[512,128]{1,0:T(8,128)(2,1)S(1)}, bf16[512,128]{1,0:T(8,128)(2,1)S(1)}) custom-call(s32[1]{0:T(128)} %bitcast.tensor_at, bf16[32,1152]{1,0:T(8,128)(2,1)S(1)} %get-tuple-element.40.tagged.refs_0_.refs_2_, bf16[1024,8192]{1,0:T(8,128)(2,1)} %out_weight.5, bf16[1024,2048]{1,0:T(8,128)(2,1)S(1)} %get-tuple-element.26.refs_0_), custom_call_target="tpu_custom_call" | custom-call | flops 268435456 | bytes 8388608 | tf_op jit(solution)/shard_map/base_terms/pallas_call | solution.py:257
  9.0 1.6 %collective-permute-start.4 = (bf16[512,128]{1,0:T(8,128)(2,1)S(1)}, bf16[512,128]{1,0:T(8,128)(2,1)S(1)}, u32[]{:S(2)}, u32[]{:S(2)}) collective-permute-start(bf16[512,128]{1,0:T(8,128)(2,1)S(1)} %get-tuple-element.33), channel_id=1, source_target_pairs={{0,4},{4,0},{8,12},{12,8},{1,5},{5,1},{9,13},{13,9},{2,6},{6,2},{1... | collective-permute-start | bytes 393224 | tf_op jit(solution)/shard_map/ppermute | solution.py:19
  10.6 0.0 collective-permute-done.1.refs_1_
  10.6 0.0 collective-permute-done.refs_1_.refs_3_
  10.6 0.0 collective-permute-done.2.refs_3_
  10.6 0.0 copy-done.1
  10.6 0.5 %shrink.1 = bf16[32,128]{1,0:T(8,128)(2,1)S(1)} custom-call(s32[1]{0:T(128)} %bitcast.1.batch_at, bf16[32,1152]{1,0:T(8,128)(2,1)S(1)} %get-tuple-element.40.tagged.refs_0_.refs_2_, bf16[32,1152]{1,0:T(8,128)(2,1)S(1)} %collective-permute-done.refs_1_.refs_3_, bf16[4,64,1024]{2,1,0:T(8,128)(2,1)S(1)} %bitcast.9, ...), custom_call_target="tpu_custom_call" | custom-call | flops 67108864 | bytes 1179648 | tf_op jit(solution)/shard_map/shrink/pallas_call | solution.py:317
  11.2 0.0 copy-start
  11.2 0.5 %collective-permute-start.3 = (bf16[32,128]{1,0:T(8,128)(2,1)S(1)}, bf16[32,128]{1,0:T(8,128)(2,1)S(1)}, u32[]{:S(2)}, u32[]{:S(2)}) collective-permute-start(bf16[32,128]{1,0:T(8,128)(2,1)S(1)} %shrink.1), channel_id=1, source_target_pairs={{0,4},{4,0},{8,12},{12,8},{1,5},{5,1},{9,13},{13,9},{2,6},{6,2},{1... | collective-permute-start | bytes 24584 | tf_op jit(solution)/shard_map/ppermute | solution.py:19
  11.7 2.5 %base_terms.4 = bf16[512,128]{1,0:T(8,128)(2,1)S(1)} custom-call(s32[1]{0:T(128)} %bitcast.tensor_at, bf16[32,1152]{1,0:T(8,128)(2,1)S(1)} %get-tuple-element.40.tagged.refs_0_.refs_2_, bf16[1024,8192]{1,0:T(8,128)(2,1)} %out_weight.5), custom_call_target="tpu_custom_call" | custom-call | flops 4026531840 | bytes 4194304 | tf_op jit(solution)/shard_map/base_terms/pallas_call | solution.py:257
  14.2 0.8 %collective-permute-done.4 = bf16[512,128]{1,0:T(8,128)(2,1)S(1)} collective-permute-done((bf16[512,128]{1,0:T(8,128)(2,1)S(1)}, bf16[512,128]{1,0:T(8,128)(2,1)S(1)}, u32[]{:S(2)}, u32[]{:S(2)}) %collective-permute-start.4) | collective-permute-done | bytes 131104 | tf_op jit(solution)/shard_map/ppermute | solution.py:19
  15.1 0.0 collective-permute-done.3
  15.1 2.6 %collective-permute-start.5 = (bf16[32,128]{1,0:T(8,128)(2,1)S(1)}, bf16[32,128]{1,0:T(8,128)(2,1)S(1)}, u32[]{:S(2)}, u32[]{:S(2)}) collective-permute-start(bf16[32,128]{1,0:T(8,128)(2,1)S(1)} %add_convert_fusion.1.refs_4_), channel_id=1, source_target_pairs={{0,8},{4,12},{8,0},{12,4},{1,9},{5,13},{9,1},{13,5},{2,10},{6,14},... | collective-permute-start | bytes 24584 | tf_op jit(solution)/shard_map/ppermute | solution.py:19
  17.8 0.3 %collective-permute-start.7 = (bf16[512,128]{1,0:T(8,128)(2,1)S(1)}, bf16[512,128]{1,0:T(8,128)(2,1)S(1)}, u32[]{:S(2)}, u32[]{:S(2)}) collective-permute-start(bf16[512,128]{1,0:T(8,128)(2,1)S(1)} %add_convert_fusion), channel_id=1, source_target_pairs={{0,8},{4,12},{8,0},{12,4},{1,9},{5,13},{9,1},{13,5},{2,10},{6,14},... | collective-permute-start | bytes 393224 | tf_op jit(solution)/shard_map/ppermute | solution.py:19
  18.1 1.6 %collective-permute-start.8 = (bf16[512,128]{1,0:T(8,128)(2,1)S(1)}, bf16[512,128]{1,0:T(8,128)(2,1)S(1)}, u32[]{:S(2)}, u32[]{:S(2)}) collective-permute-start(bf16[512,128]{1,0:T(8,128)(2,1)S(1)} %get-tuple-element.43), channel_id=1, source_target_pairs={{0,4},{4,0},{8,12},{12,8},{1,5},{5,1},{9,13},{13,9},{2,6},{6,2},{1... | collective-permute-start | bytes 393224 | tf_op jit(solution)/shard_map/ppermute | solution.py:19
  19.7 0.0 collective-permute-done.5.refs_5_
  19.7 0.0 collective-permute-done.6
  19.7 0.0 copy-done
  19.7 0.5 %expand.1 = (bf16[512,128]{1,0:T(8,128)(2,1)S(1)}, bf16[512,128]{1,0:T(8,128)(2,1)S(1)}) custom-call(s32[1]{0:T(128)} %bitcast.1.batch_at, s32[8,128]{1,0:T(8,128)S(1)} %get-tuple-element.29.refs_0_, s32[8,128]{1,0:T(8,128)S(1)} %collective-permute-done.1.refs_1_, bf16[32,1152]{1,0:T(8,128)(2,1)S(1)} %get-tuple-element.40.tagged.refs_0_.refs_2_, ...), custom_call_target="tpu_custom_call" | custom-call | flops 134217728 | bytes 1048576 | tf_op jit(solution)/shard_map/expand/pallas_call | solution.py:377
  20.3 0.6 %collective-permute-start.9 = (bf16[512,128]{1,0:T(8,128)(2,1)S(1)}, bf16[512,128]{1,0:T(8,128)(2,1)S(1)}, u32[]{:S(2)}, u32[]{:S(2)}) collective-permute-start(bf16[512,128]{1,0:T(8,128)(2,1)S(1)} %get-tuple-element.44), channel_id=1, source_target_pairs={{0,2},{1,3},{2,0},{3,1},{4,6},{5,7},{6,4},{7,5},{8,10},{9,11},{10,... | collective-permute-start | bytes 393224 | tf_op jit(solution)/shard_map/ppermute | solution.py:19
  20.8 2.5 %base_terms.5.refs_0_ = f32[512,128]{1,0:T(8,128)S(1)} custom-call(s32[1]{0:T(128)} %bitcast.tensor_at, bf16[32,1152]{1,0:T(8,128)(2,1)S(1)} %get-tuple-element.40.tagged.refs_0_.refs_2_, bf16[1024,8192]{1,0:T(8,128)(2,1)} %out_weight.5), custom_call_target="tpu_custom_call" | custom-call | flops 134217728 | bytes 4194304 | tf_op jit(solution)/shard_map/base_terms/pallas_call | solution.py:257
  23.3 3.0 %collective-permute-done.7.refs_2_ = bf16[512,128]{1,0:T(8,128)(2,1)S(1)} collective-permute-done((bf16[512,128]{1,0:T(8,128)(2,1)S(1)}, bf16[512,128]{1,0:T(8,128)(2,1)S(1)}, u32[]{:S(2)}, u32[]{:S(2)}) %collective-permute-start.7) | collective-permute-done | bytes 131104 | tf_op jit(solution)/shard_map/ppermute | solution.py:19
  26.4 0.0 collective-permute-done.8.refs_1_
  26.4 0.0 collective-permute-done.9.refs_1_
  26.4 0.7 %total.1 = bf16[32,2048]{1,0:T(8,128)(2,1)} custom-call(f32[512,128]{1,0:T(8,128)S(1)} %partial_total.3.refs_0_, bf16[512,128]{1,0:T(8,128)(2,1)S(1)} %collective-permute-done.9.refs_1_), custom_call_target="tpu_custom_call" | custom-call | flops 131072 | bytes 393216 | tf_op jit(solution)/shard_map/total/pallas_call | solution.py:410
  (4 shorter events, 0.1 us)
Async XLA Ops:
  0.0 10.6 %collective-permute-start.2 = (bf16[4,64,1024]{2,1,0:T(8,128)(2,1)}, bf16[4,64,1024]{2,1,0:T(8,128)(2,1)S(1)}, u32[]{:S(2)}, u32[]{:S(2)}) collective-permute-start(bf16[4,64,1024]{2,1,0:T(8,128)(2,1)} %bitcast.8), channel_id=1, source_target_pairs={{0,1},{1,0},{2,3},{3,2},{4,5},{5,4},{6,7},{7,6},{8,9},{9,8},{10,11... | collective-permute-start | bytes 1572872 | tf_op jit(solution)/shard_map/ppermute | solution.py:19
  0.5 19.3 %collective-permute-start.6 = (bf16[4,64,2048]{2,1,0:T(8,128)(2,1)}, bf16[4,64,2048]{2,1,0:T(8,128)(2,1)S(1)}, u32[]{:S(2)}, u32[]{:S(2)}) collective-permute-start(bf16[4,64,2048]{2,1,0:T(8,128)(2,1)} %param.20), channel_id=1, source_target_pairs={{0,1},{1,0},{2,3},{3,2},{4,5},{5,4},{6,7},{7,6},{8,9},{9,8},{10,11... | collective-permute-start | bytes 3145736 | tf_op jit(solution)/shard_map/ppermute | solution.py:19
  3.4 7.3 %collective-permute-start = (bf16[32,1152]{1,0:T(8,128)(2,1)S(1)}, bf16[32,1152]{1,0:T(8,128)(2,1)S(1)}, u32[]{:S(2)}, u32[]{:S(2)}) collective-permute-start(bf16[32,1152]{1,0:T(8,128)(2,1)S(1)} %get-tuple-element.40.tagged.refs_0_.refs_2_), channel_id=1, source_target_pairs={{0,2},{1,3},{2,0},{3,1},{4,6},{5,7},{6,4},{7,5},{8,10},{9,11},{10,... | collective-permute-start | bytes 221192 | tf_op jit(solution)/shard_map/ppermute | solution.py:19
  6.4 4.2 %collective-permute-start.1 = (s32[8,128]{1,0:T(8,128)S(1)}, s32[8,128]{1,0:T(8,128)S(1)}, u32[]{:S(2)}, u32[]{:S(2)}) collective-permute-start(s32[8,128]{1,0:T(8,128)S(1)} %get-tuple-element.29.refs_0_), channel_id=1, source_target_pairs={{0,1},{1,0},{2,3},{3,2},{4,5},{5,4},{6,7},{7,6},{8,9},{9,8},{10,11... | collective-permute-start | bytes 12296 | tf_op jit(solution)/shard_map/ppermute | solution.py:19
  6.4 4.3 %copy-start.1 = (bf16[4,1024,64]{1,2,0:T(8,128)(2,1)S(1)}, bf16[4,1024,64]{1,2,0:T(8,128)(2,1)}, u32[]{:S(2)}) copy-start(bf16[4,1024,64]{1,2,0:T(8,128)(2,1)} %param.19) | copy-start | bytes 1572868
  9.0 6.1 %collective-permute-start.4 = (bf16[512,128]{1,0:T(8,128)(2,1)S(1)}, bf16[512,128]{1,0:T(8,128)(2,1)S(1)}, u32[]{:S(2)}, u32[]{:S(2)}) collective-permute-start(bf16[512,128]{1,0:T(8,128)(2,1)S(1)} %get-tuple-element.33), channel_id=1, source_target_pairs={{0,4},{4,0},{8,12},{12,8},{1,5},{5,1},{9,13},{13,9},{2,6},{6,2},{1... | collective-permute-start | bytes 393224 | tf_op jit(solution)/shard_map/ppermute | solution.py:19
  11.2 8.6 %copy-start = (bf16[4,64,2048]{2,1,0:T(8,128)(2,1)S(1)}, bf16[4,64,2048]{2,1,0:T(8,128)(2,1)}, u32[]{:S(2)}) copy-start(bf16[4,64,2048]{2,1,0:T(8,128)(2,1)} %param.20) | copy-start | bytes 3145732
  11.2 4.0 %collective-permute-start.3 = (bf16[32,128]{1,0:T(8,128)(2,1)S(1)}, bf16[32,128]{1,0:T(8,128)(2,1)S(1)}, u32[]{:S(2)}, u32[]{:S(2)}) collective-permute-start(bf16[32,128]{1,0:T(8,128)(2,1)S(1)} %shrink.1), channel_id=1, source_target_pairs={{0,4},{4,0},{8,12},{12,8},{1,5},{5,1},{9,13},{13,9},{2,6},{6,2},{1... | collective-permute-start | bytes 24584 | tf_op jit(solution)/shard_map/ppermute | solution.py:19
  15.1 4.6 %collective-permute-start.5 = (bf16[32,128]{1,0:T(8,128)(2,1)S(1)}, bf16[32,128]{1,0:T(8,128)(2,1)S(1)}, u32[]{:S(2)}, u32[]{:S(2)}) collective-permute-start(bf16[32,128]{1,0:T(8,128)(2,1)S(1)} %add_convert_fusion.1.refs_4_), channel_id=1, source_target_pairs={{0,8},{4,12},{8,0},{12,4},{1,9},{5,13},{9,1},{13,5},{2,10},{6,14},... | collective-permute-start | bytes 24584 | tf_op jit(solution)/shard_map/ppermute | solution.py:19
  17.8 8.6 %collective-permute-start.7 = (bf16[512,128]{1,0:T(8,128)(2,1)S(1)}, bf16[512,128]{1,0:T(8,128)(2,1)S(1)}, u32[]{:S(2)}, u32[]{:S(2)}) collective-permute-start(bf16[512,128]{1,0:T(8,128)(2,1)S(1)} %add_convert_fusion), channel_id=1, source_target_pairs={{0,8},{4,12},{8,0},{12,4},{1,9},{5,13},{9,1},{13,5},{2,10},{6,14},... | collective-permute-start | bytes 393224 | tf_op jit(solution)/shard_map/ppermute | solution.py:19
  18.1 8.3 %collective-permute-start.8 = (bf16[512,128]{1,0:T(8,128)(2,1)S(1)}, bf16[512,128]{1,0:T(8,128)(2,1)S(1)}, u32[]{:S(2)}, u32[]{:S(2)}) collective-permute-start(bf16[512,128]{1,0:T(8,128)(2,1)S(1)} %get-tuple-element.43), channel_id=1, source_target_pairs={{0,4},{4,0},{8,12},{12,8},{1,5},{5,1},{9,13},{13,9},{2,6},{6,2},{1... | collective-permute-start | bytes 393224 | tf_op jit(solution)/shard_map/ppermute | solution.py:19
  20.3 6.2 %collective-permute-start.9 = (bf16[512,128]{1,0:T(8,128)(2,1)S(1)}, bf16[512,128]{1,0:T(8,128)(2,1)S(1)}, u32[]{:S(2)}, u32[]{:S(2)}) collective-permute-start(bf16[512,128]{1,0:T(8,128)(2,1)S(1)} %get-tuple-element.44), channel_id=1, source_target_pairs={{0,2},{1,3},{2,0},{3,1},{4,6},{5,7},{6,4},{7,5},{8,10},{9,11},{10,... | collective-permute-start | bytes 393224 | tf_op jit(solution)/shard_map/ppermute | solution.py:19

commit v19 on v18

--- a/solution.py
+++ b/solution.py
@@ -511,27 +511,27 @@
 
     part = shrink_part(blocks, shrink_factors, batch_at)
     parts = [part, across(part, 1)]
-    part, later_tagged = lax.optimization_barrier((part, tagged))
-    (second,) = base_block(tensor_at, later_tagged, out_weight, block, 2, (), (), 60)
+    part, later_tagged, next_door = lax.optimization_barrier((part, tagged, next_door))
+    next_door = across(next_door, 1)
+    (second,) = base_block(tensor_at, later_tagged, out_weight, block, 2, (), (), 30)
     second = (wide(second) + wide(third)).astype(BF16)
     parts, second = lax.optimization_barrier((parts, second))
     bit = 2
     while bit < tensor_size:
         part = (wide(parts[0]) + wide(parts[1])).astype(BF16)
-        part, next_door = lax.optimization_barrier((part, next_door))
         parts = [part, across(part, bit)]
         bit *= 2
-    arrived = [across(second, 2), across(next_door, 1)]
+    arrived = [across(second, 2)]
     for ahead in range(4, tensor_size, 2):
         (near,) = base_block(tensor_at, tagged, out_weight, block, ahead)
         (far,) = base_block(tensor_at, tagged, out_weight, block, ahead + 1)
         arrived.append(across((wide(near) + wide(across(far, 1))).astype(BF16), ahead))
 
+    parts, next_door = lax.optimization_barrier((parts, next_door))
     deltas = expand(blocks, parts, expand_factors, limits, batch_at)
     deltas, late_tagged = lax.optimization_barrier((deltas, tagged))
     (own,) = base_block(tensor_at, late_tagged, out_weight, block, 0, (), (), 2)
-    so_far = partial_total([own, deltas[0], arrived[0], *arrived[2:]], 0)
-    terms = [partial_total([so_far, arrived[1]], 8 << 20)]
+    terms = [partial_total([own, deltas[0], next_door, *arrived], 8 << 20)]
     terms += [to_chip(home, -shift) for shift, home in enumerate(deltas[1:], 1)]
     return total(rows, block, terms)
 

time: 27.3 us -> 27.9 us (1.022)
  waiting for transfers between devices: 3.98 us -> 4.52 us
    ppermute x10, waiting for transfers between devices: 3.98 us -> 4.52 us  [permuted(): return lax.ppermute(array, axis, [(i, partner(i)) for i in range(size)])]
  transfers between devices with their start and end apart: 10 -> 10, of which waited for: 2 -> 2; matrix products, arithmetic and copies ran while one was open for 0% -> 0% of each run, Pallas kernels for 43% -> 42%
where the time goes in v19:
time: 27.9 us; the launch traced here: 27.8 us
  Pallas kernels  12.2 us (44%)
  starting transfers between devices  10.8 us (39%)
  waiting for transfers between devices  4.52 us (16%)
    ppermute x10, starting transfers between devices, permuted(): return lax.ppermute(array, axis, [(i, partner(i)) for i in range(size)])  10.8 us
    pallas_call x3, Pallas kernels, base_block(): pl.pallas_call(functools.partial(base_kernel, ahead, deep, len(arrived)),...  7.59 us
    ppermute x10, waiting for transfers between devices, permuted(): return lax.ppermute(array, axis, [(i, partner(i)) for i in range(size)])  4.52 us
    pallas_call x1, Pallas kernels, attend(): pl.pallas_call(functools.partial(attend_kernel, parts, rank_width), out_s...  2.85 us
    pallas_call x1, Pallas kernels, total(): pl.pallas_call(total_kernel, out_shape=jax.ShapeDtypeStruct((rows, block)...  0.69 us
  transfers between devices with their start and end apart: 10, of which 2 were waited for; matrix products, arithmetic and copies ran while one was open for 0% of the time, Pallas kernels for 42%

profile of v19, /device:TPU:0, one launch (start us, length us, event | category | flops | bytes accessed | tf_op | source)
XLA Modules:
  0.0 27.8 jit_solution(16325271757246322628)
XLA Ops:
  0.0 0.5 %collective-permute-start.2 = (bf16[4,64,1024]{2,1,0:T(8,128)(2,1)}, bf16[4,64,1024]{2,1,0:T(8,128)(2,1)S(1)}, u32[]{:S(2)}, u32[]{:S(2)}) collective-permute-start(bf16[4,64,1024]{2,1,0:T(8,128)(2,1)} %bitcast.8), channel_id=1, source_target_pairs={{0,1},{1,0},{2,3},{3,2},{4,5},{5,4},{6,7},{7,6},{8,9},{9,8},{10,11... | collective-permute-start | bytes 1572872 | tf_op jit(solution)/shard_map/ppermute | solution.py:19
  0.5 0.1 collective-permute-start.7
  0.5 2.8 %attention.1 = (bf16[32,1152]{1,0:T(8,128)(2,1)S(1)}, bf16[1024,2048]{1,0:T(8,128)(2,1)S(1)}, s32[8,128]{1,0:T(8,128)S(1)}) custom-call(s32[1]{0:T(128)} %bitcast.2.group_at, s32[1]{0:T(128)S(6)} %xor.3.early_at, bf16[32,4,96,128]{3,2,1,0:T(8,128)(2,1)} %refs_0_.1, bf16[32,4,96,128]{3,2,1,0:T(8,128)(2,1)} %refs_1_.1, bf16[32,8,128]{2,1,0:T(8,128)(2,1)} %refs_2_.1, ...), custom_call_target="tpu_custom_call" | custom-call | flops 12582912 | bytes 1572864 | tf_op jit(solution)/shard_map/attention/pallas_call | solution.py:147
  3.4 3.0 %collective-permute-start = (bf16[32,1152]{1,0:T(8,128)(2,1)S(1)}, bf16[32,1152]{1,0:T(8,128)(2,1)S(1)}, u32[]{:S(2)}, u32[]{:S(2)}) collective-permute-start(bf16[32,1152]{1,0:T(8,128)(2,1)S(1)} %get-tuple-element.44.tagged.refs_0_.refs_2_), channel_id=1, source_target_pairs={{0,2},{1,3},{2,0},{3,1},{4,6},{5,7},{6,4},{7,5},{8,10},{9,11},{10,... | collective-permute-start | bytes 221192 | tf_op jit(solution)/shard_map/ppermute | solution.py:19
  6.4 0.0 collective-permute-start.1
  6.4 0.0 copy-start.1
  6.4 2.6 %base_terms.3 = (bf16[512,128]{1,0:T(8,128)(2,1)S(1)}, bf16[512,128]{1,0:T(8,128)(2,1)S(1)}) custom-call(s32[1]{0:T(128)} %bitcast.tensor_at, bf16[32,1152]{1,0:T(8,128)(2,1)S(1)} %get-tuple-element.44.tagged.refs_0_.refs_2_, bf16[1024,8192]{1,0:T(8,128)(2,1)} %out_weight.5, bf16[1024,2048]{1,0:T(8,128)(2,1)S(1)} %get-tuple-element.28.refs_0_), custom_call_target="tpu_custom_call" | custom-call | flops 268435456 | bytes 8388608 | tf_op jit(solution)/shard_map/base_terms/pallas_call | solution.py:257
  9.0 1.6 %collective-permute-start.4 = (bf16[512,128]{1,0:T(8,128)(2,1)S(1)}, bf16[512,128]{1,0:T(8,128)(2,1)S(1)}, u32[]{:S(2)}, u32[]{:S(2)}) collective-permute-start(bf16[512,128]{1,0:T(8,128)(2,1)S(1)} %get-tuple-element.36), channel_id=1, source_target_pairs={{0,4},{4,0},{8,12},{12,8},{1,5},{5,1},{9,13},{13,9},{2,6},{6,2},{1... | collective-permute-start | bytes 393224 | tf_op jit(solution)/shard_map/ppermute | solution.py:19
  10.6 0.0 collective-permute-done.1.refs_1_
  10.6 0.0 collective-permute-done.refs_1_.refs_3_
  10.6 0.0 collective-permute-done.2.refs_3_
  10.6 0.0 copy-done.1
  10.6 0.5 %shrink.1 = bf16[32,128]{1,0:T(8,128)(2,1)S(1)} custom-call(s32[1]{0:T(128)} %bitcast.1.batch_at, bf16[32,1152]{1,0:T(8,128)(2,1)S(1)} %get-tuple-element.44.tagged.refs_0_.refs_2_, bf16[32,1152]{1,0:T(8,128)(2,1)S(1)} %collective-permute-done.refs_1_.refs_3_, bf16[4,64,1024]{2,1,0:T(8,128)(2,1)S(1)} %bitcast.9, ...), custom_call_target="tpu_custom_call" | custom-call | flops 67108864 | bytes 1179648 | tf_op jit(solution)/shard_map/shrink/pallas_call | solution.py:317
  11.2 0.0 copy-start
  11.2 0.5 %collective-permute-start.3 = (bf16[32,128]{1,0:T(8,128)(2,1)S(1)}, bf16[32,128]{1,0:T(8,128)(2,1)S(1)}, u32[]{:S(2)}, u32[]{:S(2)}) collective-permute-start(bf16[32,128]{1,0:T(8,128)(2,1)S(1)} %shrink.1), channel_id=1, source_target_pairs={{0,4},{4,0},{8,12},{12,8},{1,5},{5,1},{9,13},{13,9},{2,6},{6,2},{1... | collective-permute-start | bytes 24584 | tf_op jit(solution)/shard_map/ppermute | solution.py:19
  11.7 1.6 %collective-permute-start.6 = (bf16[512,128]{1,0:T(8,128)(2,1)S(1)}, bf16[512,128]{1,0:T(8,128)(2,1)S(1)}, u32[]{:S(2)}, u32[]{:S(2)}) collective-permute-start(bf16[512,128]{1,0:T(8,128)(2,1)S(1)} %get-tuple-element.39), channel_id=1, source_target_pairs={{0,4},{4,0},{8,12},{12,8},{1,5},{5,1},{9,13},{13,9},{2,6},{6,2},{1... | collective-permute-start | bytes 393224 | tf_op jit(solution)/shard_map/ppermute | solution.py:19
  13.3 2.5 %base_terms.4 = bf16[512,128]{1,0:T(8,128)(2,1)S(1)} custom-call(s32[1]{0:T(128)} %bitcast.tensor_at, bf16[32,1152]{1,0:T(8,128)(2,1)S(1)} %get-tuple-element.44.tagged.refs_0_.refs_2_, bf16[1024,8192]{1,0:T(8,128)(2,1)} %out_weight.5), custom_call_target="tpu_custom_call" | custom-call | flops 2013265920 | bytes 4194304 | tf_op jit(solution)/shard_map/base_terms/pallas_call | solution.py:257
  15.8 0.0 collective-permute-done.4
  15.8 0.0 collective-permute-done.3
  15.8 2.7 %collective-permute-start.5 = (bf16[32,128]{1,0:T(8,128)(2,1)S(1)}, bf16[32,128]{1,0:T(8,128)(2,1)S(1)}, u32[]{:S(2)}, u32[]{:S(2)}) collective-permute-start(bf16[32,128]{1,0:T(8,128)(2,1)S(1)} %add_convert_fusion.1.refs_4_), channel_id=1, source_target_pairs={{0,8},{4,12},{8,0},{12,4},{1,9},{5,13},{9,1},{13,5},{2,10},{6,14},... | collective-permute-start | bytes 24584 | tf_op jit(solution)/shard_map/ppermute | solution.py:19
  18.5 0.3 %collective-permute-start.8 = (bf16[512,128]{1,0:T(8,128)(2,1)S(1)}, bf16[512,128]{1,0:T(8,128)(2,1)S(1)}, u32[]{:S(2)}, u32[]{:S(2)}) collective-permute-start(bf16[512,128]{1,0:T(8,128)(2,1)S(1)} %add_convert_fusion), channel_id=1, source_target_pairs={{0,8},{4,12},{8,0},{12,4},{1,9},{5,13},{9,1},{13,5},{2,10},{6,14},... | collective-permute-start | bytes 393224 | tf_op jit(solution)/shard_map/ppermute | solution.py:19
  18.8 1.6 %collective-permute-done.5.refs_5_ = bf16[32,128]{1,0:T(8,128)(2,1)S(1)} collective-permute-done((bf16[32,128]{1,0:T(8,128)(2,1)S(1)}, bf16[32,128]{1,0:T(8,128)(2,1)S(1)}, u32[]{:S(2)}, u32[]{:S(2)}) %collective-permute-start.5) | collective-permute-done | bytes 8224 | tf_op jit(solution)/shard_map/ppermute | solution.py:19
  20.5 0.0 collective-permute-done.6.refs_2_
  20.5 0.0 collective-permute-done.7
  20.5 0.0 copy-done
  20.5 0.5 %expand.1 = (bf16[512,128]{1,0:T(8,128)(2,1)S(1)}, bf16[512,128]{1,0:T(8,128)(2,1)S(1)}) custom-call(s32[1]{0:T(128)} %bitcast.1.batch_at, s32[8,128]{1,0:T(8,128)S(1)} %get-tuple-element.31.refs_0_, s32[8,128]{1,0:T(8,128)S(1)} %collective-permute-done.1.refs_1_, bf16[32,1152]{1,0:T(8,128)(2,1)S(1)} %get-tuple-element.44.tagged.refs_0_.refs_2_, ...), custom_call_target="tpu_custom_call" | custom-call | flops 134217728 | bytes 1048576 | tf_op jit(solution)/shard_map/expand/pallas_call | solution.py:377
  21.0 0.6 %collective-permute-start.9 = (bf16[512,128]{1,0:T(8,128)(2,1)S(1)}, bf16[512,128]{1,0:T(8,128)(2,1)S(1)}, u32[]{:S(2)}, u32[]{:S(2)}) collective-permute-start(bf16[512,128]{1,0:T(8,128)(2,1)S(1)} %get-tuple-element.48), channel_id=1, source_target_pairs={{0,2},{1,3},{2,0},{3,1},{4,6},{5,7},{6,4},{7,5},{8,10},{9,11},{10,... | collective-permute-start | bytes 393224 | tf_op jit(solution)/shard_map/ppermute | solution.py:19
  21.6 2.5 %base_terms.5.refs_0_ = f32[512,128]{1,0:T(8,128)S(1)} custom-call(s32[1]{0:T(128)} %bitcast.tensor_at, bf16[32,1152]{1,0:T(8,128)(2,1)S(1)} %get-tuple-element.44.tagged.refs_0_.refs_2_, bf16[1024,8192]{1,0:T(8,128)(2,1)} %out_weight.5), custom_call_target="tpu_custom_call" | custom-call | flops 134217728 | bytes 4194304 | tf_op jit(solution)/shard_map/base_terms/pallas_call | solution.py:257
  24.1 2.9 %collective-permute-done.8.refs_3_ = bf16[512,128]{1,0:T(8,128)(2,1)S(1)} collective-permute-done((bf16[512,128]{1,0:T(8,128)(2,1)S(1)}, bf16[512,128]{1,0:T(8,128)(2,1)S(1)}, u32[]{:S(2)}, u32[]{:S(2)}) %collective-permute-start.8) | collective-permute-done | bytes 131104 | tf_op jit(solution)/shard_map/ppermute | solution.py:19
  27.0 0.1 partial_total.1.refs_0_
  27.1 0.0 collective-permute-done.9.refs_1_
  27.1 0.7 %total.1 = bf16[32,2048]{1,0:T(8,128)(2,1)} custom-call(f32[512,128]{1,0:T(8,128)S(1)} %partial_total.1.refs_0_, bf16[512,128]{1,0:T(8,128)(2,1)S(1)} %collective-permute-done.9.refs_1_), custom_call_target="tpu_custom_call" | custom-call | flops 131072 | bytes 393216 | tf_op jit(solution)/shard_map/total/pallas_call | solution.py:410
  (2 shorter events, 0.0 us)
Async XLA Ops:
  0.0 10.6 %collective-permute-start.2 = (bf16[4,64,1024]{2,1,0:T(8,128)(2,1)}, bf16[4,64,1024]{2,1,0:T(8,128)(2,1)S(1)}, u32[]{:S(2)}, u32[]{:S(2)}) collective-permute-start(bf16[4,64,1024]{2,1,0:T(8,128)(2,1)} %bitcast.8), channel_id=1, source_target_pairs={{0,1},{1,0},{2,3},{3,2},{4,5},{5,4},{6,7},{7,6},{8,9},{9,8},{10,11... | collective-permute-start | bytes 1572872 | tf_op jit(solution)/shard_map/ppermute | solution.py:19
  0.5 20.0 %collective-permute-start.7 = (bf16[4,64,2048]{2,1,0:T(8,128)(2,1)}, bf16[4,64,2048]{2,1,0:T(8,128)(2,1)S(1)}, u32[]{:S(2)}, u32[]{:S(2)}) collective-permute-start(bf16[4,64,2048]{2,1,0:T(8,128)(2,1)} %param.20), channel_id=1, source_target_pairs={{0,1},{1,0},{2,3},{3,2},{4,5},{5,4},{6,7},{7,6},{8,9},{9,8},{10,11... | collective-permute-start | bytes 3145736 | tf_op jit(solution)/shard_map/ppermute | solution.py:19
  3.4 7.3 %collective-permute-start = (bf16[32,1152]{1,0:T(8,128)(2,1)S(1)}, bf16[32,1152]{1,0:T(8,128)(2,1)S(1)}, u32[]{:S(2)}, u32[]{:S(2)}) collective-permute-start(bf16[32,1152]{1,0:T(8,128)(2,1)S(1)} %get-tuple-element.44.tagged.refs_0_.refs_2_), channel_id=1, source_target_pairs={{0,2},{1,3},{2,0},{3,1},{4,6},{5,7},{6,4},{7,5},{8,10},{9,11},{10,... | collective-permute-start | bytes 221192 | tf_op jit(solution)/shard_map/ppermute | solution.py:19
  6.4 4.2 %collective-permute-start.1 = (s32[8,128]{1,0:T(8,128)S(1)}, s32[8,128]{1,0:T(8,128)S(1)}, u32[]{:S(2)}, u32[]{:S(2)}) collective-permute-start(s32[8,128]{1,0:T(8,128)S(1)} %get-tuple-element.31.refs_0_), channel_id=1, source_target_pairs={{0,1},{1,0},{2,3},{3,2},{4,5},{5,4},{6,7},{7,6},{8,9},{9,8},{10,11... | collective-permute-start | bytes 12296 | tf_op jit(solution)/shard_map/ppermute | solution.py:19
  6.4 4.3 %copy-start.1 = (bf16[4,1024,64]{1,2,0:T(8,128)(2,1)S(1)}, bf16[4,1024,64]{1,2,0:T(8,128)(2,1)}, u32[]{:S(2)}) copy-start(bf16[4,1024,64]{1,2,0:T(8,128)(2,1)} %param.19) | copy-start | bytes 1572868
  9.0 6.8 %collective-permute-start.4 = (bf16[512,128]{1,0:T(8,128)(2,1)S(1)}, bf16[512,128]{1,0:T(8,128)(2,1)S(1)}, u32[]{:S(2)}, u32[]{:S(2)}) collective-permute-start(bf16[512,128]{1,0:T(8,128)(2,1)S(1)} %get-tuple-element.36), channel_id=1, source_target_pairs={{0,4},{4,0},{8,12},{12,8},{1,5},{5,1},{9,13},{13,9},{2,6},{6,2},{1... | collective-permute-start | bytes 393224 | tf_op jit(solution)/shard_map/ppermute | solution.py:19
  11.2 9.3 %copy-start = (bf16[4,64,2048]{2,1,0:T(8,128)(2,1)S(1)}, bf16[4,64,2048]{2,1,0:T(8,128)(2,1)}, u32[]{:S(2)}) copy-start(bf16[4,64,2048]{2,1,0:T(8,128)(2,1)} %param.20) | copy-start | bytes 3145732
  11.2 4.7 %collective-permute-start.3 = (bf16[32,128]{1,0:T(8,128)(2,1)S(1)}, bf16[32,128]{1,0:T(8,128)(2,1)S(1)}, u32[]{:S(2)}, u32[]{:S(2)}) collective-permute-start(bf16[32,128]{1,0:T(8,128)(2,1)S(1)} %shrink.1), channel_id=1, source_target_pairs={{0,4},{4,0},{8,12},{12,8},{1,5},{5,1},{9,13},{13,9},{2,6},{6,2},{1... | collective-permute-start | bytes 24584 | tf_op jit(solution)/shard_map/ppermute | solution.py:19
  11.7 8.8 %collective-permute-start.6 = (bf16[512,128]{1,0:T(8,128)(2,1)S(1)}, bf16[512,128]{1,0:T(8,128)(2,1)S(1)}, u32[]{:S(2)}, u32[]{:S(2)}) collective-permute-start(bf16[512,128]{1,0:T(8,128)(2,1)S(1)} %get-tuple-element.39), channel_id=1, source_target_pairs={{0,4},{4,0},{8,12},{12,8},{1,5},{5,1},{9,13},{13,9},{2,6},{6,2},{1... | collective-permute-start | bytes 393224 | tf_op jit(solution)/shard_map/ppermute | solution.py:19
  15.8 4.6 %collective-permute-start.5 = (bf16[32,128]{1,0:T(8,128)(2,1)S(1)}, bf16[32,128]{1,0:T(8,128)(2,1)S(1)}, u32[]{:S(2)}, u32[]{:S(2)}) collective-permute-start(bf16[32,128]{1,0:T(8,128)(2,1)S(1)} %add_convert_fusion.1.refs_4_), channel_id=1, source_target_pairs={{0,8},{4,12},{8,0},{12,4},{1,9},{5,13},{9,1},{13,5},{2,10},{6,14},... | collective-permute-start | bytes 24584 | tf_op jit(solution)/shard_map/ppermute | solution.py:19
  18.5 8.5 %collective-permute-start.8 = (bf16[512,128]{1,0:T(8,128)(2,1)S(1)}, bf16[512,128]{1,0:T(8,128)(2,1)S(1)}, u32[]{:S(2)}, u32[]{:S(2)}) collective-permute-start(bf16[512,128]{1,0:T(8,128)(2,1)S(1)} %add_convert_fusion), channel_id=1, source_target_pairs={{0,8},{4,12},{8,0},{12,4},{1,9},{5,13},{9,1},{13,5},{2,10},{6,14},... | collective-permute-start | bytes 393224 | tf_op jit(solution)/shard_map/ppermute | solution.py:19
  21.0 6.0 %collective-permute-start.9 = (bf16[512,128]{1,0:T(8,128)(2,1)S(1)}, bf16[512,128]{1,0:T(8,128)(2,1)S(1)}, u32[]{:S(2)}, u32[]{:S(2)}) collective-permute-start(bf16[512,128]{1,0:T(8,128)(2,1)S(1)} %get-tuple-element.48), channel_id=1, source_target_pairs={{0,2},{1,3},{2,0},{3,1},{4,6},{5,7},{6,4},{7,5},{8,10},{9,11},{10,... | collective-permute-start | bytes 393224 | tf_op jit(solution)/shard_map/ppermute | solution.py:19

commit v20 on v8

--- a/solution.py
+++ b/solution.py
@@ -55,7 +55,7 @@
     block = early.shape[1]
     start = pl.multiple_of(early_at[0] * block, block)
     early_copy = pltpu.make_async_copy(out_weight.at[:, pl.ds(start, block)], early, early_sem)
-    early_copy.start()
+    early_copy.start(priority=1)
     for copy in small:
         copy.wait()
     at_row = lax.broadcasted_iota(jnp.int32, (rows, LANES), 0)
@@ -222,7 +222,7 @@
         )
 
     for at in range(min(deep, count)):
-        copy(at).start()
+        copy(at).start(priority=at % 2)
     piece = min(block, 512)
     if near:
         early, early_out = near
@@ -245,7 +245,7 @@
             else:
                 put_stacked(out, start, term, 0, arrived)
         if at + deep < count:
-            copy(at + deep).start()
+            copy(at + deep).start(priority=at % 2)
 
 
 def base_block(tensor_at, tagged, out_weight, block, ahead, early=(), arrived=()):

time: 27.1 us -> 27.2 us (level)
  no operation moved by 1% of the time
where the time goes in v20:
time: 27.2 us; the launch traced here: 27 us
  Pallas kernels  12.4 us (46%)
  starting transfers between devices  11.8 us (43%)
  waiting for transfers between devices  2.74 us (10%)
    ppermute x10, starting transfers between devices, permuted(): return lax.ppermute(array, axis, [(i, partner(i)) for i in range(size)])  11.8 us
    pallas_call x3, Pallas kernels, base_block(): pl.pallas_call(functools.partial(base_kernel, ahead, deep, len(arrived)),...  7.76 us
    pallas_call x1, Pallas kernels, attend(): pl.pallas_call(functools.partial(attend_kernel, parts, rank_width), out_s...  2.83 us
    ppermute x10, waiting for transfers between devices, permuted(): return lax.ppermute(array, axis, [(i, partner(i)) for i in range(size)])  2.74 us
    pallas_call x1, Pallas kernels, total(): pl.pallas_call(total_kernel, out_shape=jax.ShapeDtypeStruct((rows, block)...  0.69 us
  transfers between devices with their start and end apart: 10, of which 2 were waited for; matrix products, arithmetic and copies ran while one was open for 0% of the time, Pallas kernels for 43%

profile of v20, /device:TPU:0, one launch (start us, length us, event | category | flops | bytes accessed | tf_op | source)
XLA Modules:
  0.0 27.0 jit_solution(2986965774743611540)
XLA Ops:
  0.0 0.5 %collective-permute-start.6 = (bf16[4,64,2048]{2,1,0:T(8,128)(2,1)}, bf16[4,64,2048]{2,1,0:T(8,128)(2,1)S(1)}, u32[]{:S(2)}, u32[]{:S(2)}) collective-permute-start(bf16[4,64,2048]{2,1,0:T(8,128)(2,1)} %param.20), channel_id=1, source_target_pairs={{0,1},{1,0},{2,3},{3,2},{4,5},{5,4},{6,7},{7,6},{8,9},{9,8},{10,11... | collective-permute-start | bytes 3145736 | tf_op jit(solution)/shard_map/ppermute | solution.py:19
  0.5 0.1 collective-permute-start.2
  0.5 2.8 %attention.1 = (bf16[32,1152]{1,0:T(8,128)(2,1)S(1)}, bf16[1024,2048]{1,0:T(8,128)(2,1)S(1)}, s32[8,128]{1,0:T(8,128)S(1)}) custom-call(s32[1]{0:T(128)} %bitcast.2.group_at, s32[1]{0:T(128)S(6)} %xor.3.early_at, bf16[32,4,96,128]{3,2,1,0:T(8,128)(2,1)} %refs_0_.1, bf16[32,4,96,128]{3,2,1,0:T(8,128)(2,1)} %refs_1_.1, bf16[32,8,128]{2,1,0:T(8,128)(2,1)} %refs_2_.1, ...), custom_call_target="tpu_custom_call" | custom-call | flops 12582912 | bytes 1572864 | tf_op jit(solution)/shard_map/attention/pallas_call | solution.py:147
  3.4 3.0 %collective-permute-start = (bf16[32,1152]{1,0:T(8,128)(2,1)S(1)}, bf16[32,1152]{1,0:T(8,128)(2,1)S(1)}, u32[]{:S(2)}, u32[]{:S(2)}) collective-permute-start(bf16[32,1152]{1,0:T(8,128)(2,1)S(1)} %get-tuple-element.42.tagged.refs_0_.refs_2_), channel_id=1, source_target_pairs={{0,2},{1,3},{2,0},{3,1},{4,6},{5,7},{6,4},{7,5},{8,10},{9,11},{10,... | collective-permute-start | bytes 221192 | tf_op jit(solution)/shard_map/ppermute | solution.py:19
  6.4 0.0 collective-permute-start.1
  6.4 0.0 copy-start.1
  6.4 2.6 %base_terms.3 = (bf16[512,128]{1,0:T(8,128)(2,1)S(1)}, bf16[512,128]{1,0:T(8,128)(2,1)S(1)}) custom-call(s32[1]{0:T(128)} %bitcast.tensor_at, bf16[32,1152]{1,0:T(8,128)(2,1)S(1)} %get-tuple-element.42.tagged.refs_0_.refs_2_, bf16[1024,8192]{1,0:T(8,128)(2,1)} %out_weight.5, bf16[1024,2048]{1,0:T(8,128)(2,1)S(1)} %get-tuple-element.27.refs_0_), custom_call_target="tpu_custom_call" | custom-call | flops 268435456 | bytes 8388608 | tf_op jit(solution)/shard_map/base_terms/pallas_call | solution.py:257
  9.0 0.0 collective-permute-done.1.refs_1_
  9.0 0.0 collective-permute-done.refs_1_.refs_3_
  9.0 1.8 %collective-permute-start.4 = (bf16[512,128]{1,0:T(8,128)(2,1)S(1)}, bf16[512,128]{1,0:T(8,128)(2,1)S(1)}, u32[]{:S(2)}, u32[]{:S(2)}) collective-permute-start(bf16[512,128]{1,0:T(8,128)(2,1)S(1)} %get-tuple-element.35), channel_id=1, source_target_pairs={{0,4},{4,0},{8,12},{12,8},{1,5},{5,1},{9,13},{13,9},{2,6},{6,2},{1... | collective-permute-start | bytes 393224 | tf_op jit(solution)/shard_map/ppermute | solution.py:19
  10.8 0.0 collective-permute-done.2.refs_3_
  10.8 0.0 copy-done.1
  10.8 0.5 %shrink.1 = bf16[32,128]{1,0:T(8,128)(2,1)S(1)} custom-call(s32[1]{0:T(128)} %bitcast.1.batch_at, bf16[32,1152]{1,0:T(8,128)(2,1)S(1)} %get-tuple-element.42.tagged.refs_0_.refs_2_, bf16[32,1152]{1,0:T(8,128)(2,1)S(1)} %collective-permute-done.refs_1_.refs_3_, bf16[4,64,1024]{2,1,0:T(8,128)(2,1)S(1)} %bitcast.9, ...), custom_call_target="tpu_custom_call" | custom-call | flops 67108864 | bytes 1179648 | tf_op jit(solution)/shard_map/shrink/pallas_call | solution.py:317
  11.3 0.0 copy-start
  11.3 0.4 %collective-permute-start.3 = (bf16[32,128]{1,0:T(8,128)(2,1)S(1)}, bf16[32,128]{1,0:T(8,128)(2,1)S(1)}, u32[]{:S(2)}, u32[]{:S(2)}) collective-permute-start(bf16[32,128]{1,0:T(8,128)(2,1)S(1)} %shrink.1), channel_id=1, source_target_pairs={{0,4},{4,0},{8,12},{12,8},{1,5},{5,1},{9,13},{13,9},{2,6},{6,2},{1... | collective-permute-start | bytes 24584 | tf_op jit(solution)/shard_map/ppermute | solution.py:19
  11.7 2.6 %base_terms.4 = bf16[512,128]{1,0:T(8,128)(2,1)S(1)} custom-call(s32[1]{0:T(128)} %bitcast.tensor_at, bf16[32,1152]{1,0:T(8,128)(2,1)S(1)} %get-tuple-element.42.tagged.refs_0_.refs_2_, bf16[1024,8192]{1,0:T(8,128)(2,1)} %out_weight.5), custom_call_target="tpu_custom_call" | custom-call | flops 134217728 | bytes 4194304 | tf_op jit(solution)/shard_map/base_terms/pallas_call | solution.py:257
  14.3 0.8 %collective-permute-done.4 = bf16[512,128]{1,0:T(8,128)(2,1)S(1)} collective-permute-done((bf16[512,128]{1,0:T(8,128)(2,1)S(1)}, bf16[512,128]{1,0:T(8,128)(2,1)S(1)}, u32[]{:S(2)}, u32[]{:S(2)}) %collective-permute-start.4) | collective-permute-done | bytes 131104 | tf_op jit(solution)/shard_map/ppermute | solution.py:19
  15.1 0.0 collective-permute-done.3
  15.2 2.6 %collective-permute-start.5 = (bf16[32,128]{1,0:T(8,128)(2,1)S(1)}, bf16[32,128]{1,0:T(8,128)(2,1)S(1)}, u32[]{:S(2)}, u32[]{:S(2)}) collective-permute-start(bf16[32,128]{1,0:T(8,128)(2,1)S(1)} %add_convert_fusion.1.refs_4_), channel_id=1, source_target_pairs={{0,8},{4,12},{8,0},{12,4},{1,9},{5,13},{9,1},{13,5},{2,10},{6,14},... | collective-permute-start | bytes 24584 | tf_op jit(solution)/shard_map/ppermute | solution.py:19
  17.8 0.3 %collective-permute-start.7 = (bf16[512,128]{1,0:T(8,128)(2,1)S(1)}, bf16[512,128]{1,0:T(8,128)(2,1)S(1)}, u32[]{:S(2)}, u32[]{:S(2)}) collective-permute-start(bf16[512,128]{1,0:T(8,128)(2,1)S(1)} %add_convert_fusion), channel_id=1, source_target_pairs={{0,8},{4,12},{8,0},{12,4},{1,9},{5,13},{9,1},{13,5},{2,10},{6,14},... | collective-permute-start | bytes 393224 | tf_op jit(solution)/shard_map/ppermute | solution.py:19
  18.2 1.6 %collective-permute-start.8 = (bf16[512,128]{1,0:T(8,128)(2,1)S(1)}, bf16[512,128]{1,0:T(8,128)(2,1)S(1)}, u32[]{:S(2)}, u32[]{:S(2)}) collective-permute-start(bf16[512,128]{1,0:T(8,128)(2,1)S(1)} %get-tuple-element.45), channel_id=1, source_target_pairs={{0,4},{4,0},{8,12},{12,8},{1,5},{5,1},{9,13},{13,9},{2,6},{6,2},{1... | collective-permute-start | bytes 393224 | tf_op jit(solution)/shard_map/ppermute | solution.py:19
  19.7 0.0 collective-permute-done.5.refs_5_
  19.8 0.0 collective-permute-done.6
  19.8 0.0 copy-done
  19.8 0.5 %expand.1 = (bf16[512,128]{1,0:T(8,128)(2,1)S(1)}, bf16[512,128]{1,0:T(8,128)(2,1)S(1)}) custom-call(s32[1]{0:T(128)} %bitcast.1.batch_at, s32[8,128]{1,0:T(8,128)S(1)} %get-tuple-element.31.refs_0_, s32[8,128]{1,0:T(8,128)S(1)} %collective-permute-done.1.refs_1_, bf16[32,1152]{1,0:T(8,128)(2,1)S(1)} %get-tuple-element.42.tagged.refs_0_.refs_2_, ...), custom_call_target="tpu_custom_call" | custom-call | flops 134217728 | bytes 1048576 | tf_op jit(solution)/shard_map/expand/pallas_call | solution.py:377
  20.3 1.6 %collective-permute-start.9 = (bf16[512,128]{1,0:T(8,128)(2,1)S(1)}, bf16[512,128]{1,0:T(8,128)(2,1)S(1)}, u32[]{:S(2)}, u32[]{:S(2)}) collective-permute-start(bf16[512,128]{1,0:T(8,128)(2,1)S(1)} %get-tuple-element.46), channel_id=1, source_target_pairs={{0,2},{1,3},{2,0},{3,1},{4,6},{5,7},{6,4},{7,5},{8,10},{9,11},{10,... | collective-permute-start | bytes 393224 | tf_op jit(solution)/shard_map/ppermute | solution.py:19
  21.9 2.6 %base_terms.5.refs_0_ = f32[512,128]{1,0:T(8,128)S(1)} custom-call(s32[1]{0:T(128)} %bitcast.tensor_at, bf16[32,1152]{1,0:T(8,128)(2,1)S(1)} %get-tuple-element.42.tagged.refs_0_.refs_2_, bf16[1024,8192]{1,0:T(8,128)(2,1)} %out_weight.5), custom_call_target="tpu_custom_call" | custom-call | flops 134217728 | bytes 4194304 | tf_op jit(solution)/shard_map/base_terms/pallas_call | solution.py:257
  24.4 1.8 %collective-permute-done.7.refs_2_ = bf16[512,128]{1,0:T(8,128)(2,1)S(1)} collective-permute-done((bf16[512,128]{1,0:T(8,128)(2,1)S(1)}, bf16[512,128]{1,0:T(8,128)(2,1)S(1)}, u32[]{:S(2)}, u32[]{:S(2)}) %collective-permute-start.7) | collective-permute-done | bytes 131104 | tf_op jit(solution)/shard_map/ppermute | solution.py:19
  26.3 0.0 collective-permute-done.8.refs_1_
  26.3 0.0 collective-permute-done.9.refs_1_
  26.4 0.7 %total.1 = bf16[32,2048]{1,0:T(8,128)(2,1)} custom-call(f32[512,128]{1,0:T(8,128)S(1)} %partial_total.3.refs_0_, bf16[512,128]{1,0:T(8,128)(2,1)S(1)} %collective-permute-done.9.refs_1_), custom_call_target="tpu_custom_call" | custom-call | flops 131072 | bytes 393216 | tf_op jit(solution)/shard_map/total/pallas_call | solution.py:410
  (4 shorter events, 0.1 us)
Async XLA Ops:
  0.0 19.8 %collective-permute-start.6 = (bf16[4,64,2048]{2,1,0:T(8,128)(2,1)}, bf16[4,64,2048]{2,1,0:T(8,128)(2,1)S(1)}, u32[]{:S(2)}, u32[]{:S(2)}) collective-permute-start(bf16[4,64,2048]{2,1,0:T(8,128)(2,1)} %param.20), channel_id=1, source_target_pairs={{0,1},{1,0},{2,3},{3,2},{4,5},{5,4},{6,7},{7,6},{8,9},{9,8},{10,11... | collective-permute-start | bytes 3145736 | tf_op jit(solution)/shard_map/ppermute | solution.py:19
  0.5 10.4 %collective-permute-start.2 = (bf16[4,64,1024]{2,1,0:T(8,128)(2,1)}, bf16[4,64,1024]{2,1,0:T(8,128)(2,1)S(1)}, u32[]{:S(2)}, u32[]{:S(2)}) collective-permute-start(bf16[4,64,1024]{2,1,0:T(8,128)(2,1)} %bitcast.8), channel_id=1, source_target_pairs={{0,1},{1,0},{2,3},{3,2},{4,5},{5,4},{6,7},{7,6},{8,9},{9,8},{10,11... | collective-permute-start | bytes 1572872 | tf_op jit(solution)/shard_map/ppermute | solution.py:19
  3.4 5.7 %collective-permute-start = (bf16[32,1152]{1,0:T(8,128)(2,1)S(1)}, bf16[32,1152]{1,0:T(8,128)(2,1)S(1)}, u32[]{:S(2)}, u32[]{:S(2)}) collective-permute-start(bf16[32,1152]{1,0:T(8,128)(2,1)S(1)} %get-tuple-element.42.tagged.refs_0_.refs_2_), channel_id=1, source_target_pairs={{0,2},{1,3},{2,0},{3,1},{4,6},{5,7},{6,4},{7,5},{8,10},{9,11},{10,... | collective-permute-start | bytes 221192 | tf_op jit(solution)/shard_map/ppermute | solution.py:19
  6.4 2.7 %collective-permute-start.1 = (s32[8,128]{1,0:T(8,128)S(1)}, s32[8,128]{1,0:T(8,128)S(1)}, u32[]{:S(2)}, u32[]{:S(2)}) collective-permute-start(s32[8,128]{1,0:T(8,128)S(1)} %get-tuple-element.31.refs_0_), channel_id=1, source_target_pairs={{0,1},{1,0},{2,3},{3,2},{4,5},{5,4},{6,7},{7,6},{8,9},{9,8},{10,11... | collective-permute-start | bytes 12296 | tf_op jit(solution)/shard_map/ppermute | solution.py:19
  6.4 4.5 %copy-start.1 = (bf16[4,1024,64]{1,2,0:T(8,128)(2,1)S(1)}, bf16[4,1024,64]{1,2,0:T(8,128)(2,1)}, u32[]{:S(2)}) copy-start(bf16[4,1024,64]{1,2,0:T(8,128)(2,1)} %param.19) | copy-start | bytes 1572868
  9.0 6.1 %collective-permute-start.4 = (bf16[512,128]{1,0:T(8,128)(2,1)S(1)}, bf16[512,128]{1,0:T(8,128)(2,1)S(1)}, u32[]{:S(2)}, u32[]{:S(2)}) collective-permute-start(bf16[512,128]{1,0:T(8,128)(2,1)S(1)} %get-tuple-element.35), channel_id=1, source_target_pairs={{0,4},{4,0},{8,12},{12,8},{1,5},{5,1},{9,13},{13,9},{2,6},{6,2},{1... | collective-permute-start | bytes 393224 | tf_op jit(solution)/shard_map/ppermute | solution.py:19
  11.3 8.4 %copy-start = (bf16[4,64,2048]{2,1,0:T(8,128)(2,1)S(1)}, bf16[4,64,2048]{2,1,0:T(8,128)(2,1)}, u32[]{:S(2)}) copy-start(bf16[4,64,2048]{2,1,0:T(8,128)(2,1)} %param.20) | copy-start | bytes 3145732
  11.3 3.8 %collective-permute-start.3 = (bf16[32,128]{1,0:T(8,128)(2,1)S(1)}, bf16[32,128]{1,0:T(8,128)(2,1)S(1)}, u32[]{:S(2)}, u32[]{:S(2)}) collective-permute-start(bf16[32,128]{1,0:T(8,128)(2,1)S(1)} %shrink.1), channel_id=1, source_target_pairs={{0,4},{4,0},{8,12},{12,8},{1,5},{5,1},{9,13},{13,9},{2,6},{6,2},{1... | collective-permute-start | bytes 24584 | tf_op jit(solution)/shard_map/ppermute | solution.py:19
  15.2 4.6 %collective-permute-start.5 = (bf16[32,128]{1,0:T(8,128)(2,1)S(1)}, bf16[32,128]{1,0:T(8,128)(2,1)S(1)}, u32[]{:S(2)}, u32[]{:S(2)}) collective-permute-start(bf16[32,128]{1,0:T(8,128)(2,1)S(1)} %add_convert_fusion.1.refs_4_), channel_id=1, source_target_pairs={{0,8},{4,12},{8,0},{12,4},{1,9},{5,13},{9,1},{13,5},{2,10},{6,14},... | collective-permute-start | bytes 24584 | tf_op jit(solution)/shard_map/ppermute | solution.py:19
  17.8 8.4 %collective-permute-start.7 = (bf16[512,128]{1,0:T(8,128)(2,1)S(1)}, bf16[512,128]{1,0:T(8,128)(2,1)S(1)}, u32[]{:S(2)}, u32[]{:S(2)}) collective-permute-start(bf16[512,128]{1,0:T(8,128)(2,1)S(1)} %add_convert_fusion), channel_id=1, source_target_pairs={{0,8},{4,12},{8,0},{12,4},{1,9},{5,13},{9,1},{13,5},{2,10},{6,14},... | collective-permute-start | bytes 393224 | tf_op jit(solution)/shard_map/ppermute | solution.py:19
  18.2 8.1 %collective-permute-start.8 = (bf16[512,128]{1,0:T(8,128)(2,1)S(1)}, bf16[512,128]{1,0:T(8,128)(2,1)S(1)}, u32[]{:S(2)}, u32[]{:S(2)}) collective-permute-start(bf16[512,128]{1,0:T(8,128)(2,1)S(1)} %get-tuple-element.45), channel_id=1, source_target_pairs={{0,4},{4,0},{8,12},{12,8},{1,5},{5,1},{9,13},{13,9},{2,6},{6,2},{1... | collective-permute-start | bytes 393224 | tf_op jit(solution)/shard_map/ppermute | solution.py:19
  20.3 6.0 %collective-permute-start.9 = (bf16[512,128]{1,0:T(8,128)(2,1)S(1)}, bf16[512,128]{1,0:T(8,128)(2,1)S(1)}, u32[]{:S(2)}, u32[]{:S(2)}) collective-permute-start(bf16[512,128]{1,0:T(8,128)(2,1)S(1)} %get-tuple-element.46), channel_id=1, source_target_pairs={{0,2},{1,3},{2,0},{3,1},{4,6},{5,7},{6,4},{7,5},{8,10},{9,11},{10,... | collective-permute-start | bytes 393224 | tf_op jit(solution)/shard_map/ppermute | solution.py:19

commit v21 on v8

--- a/solution.py
+++ b/solution.py
@@ -510,17 +510,17 @@
     third = across(third, 1)
 
     part = shrink_part(blocks, shrink_factors, batch_at)
-    parts = [part, across(part, 1)]
+    bit = tensor_size // 2
+    parts = [part, across(part, bit)]
     part, later_tagged = lax.optimization_barrier((part, tagged))
     (second,) = base_block(tensor_at, later_tagged, out_weight, block, 2)
     second = (wide(second) + wide(third)).astype(BF16)
     parts, second = lax.optimization_barrier((parts, second))
-    bit = 2
-    while bit < tensor_size:
+    while bit > 1:
+        bit //= 2
         part = (wide(parts[0]) + wide(parts[1])).astype(BF16)
         part, next_door = lax.optimization_barrier((part, next_door))
         parts = [part, across(part, bit)]
-        bit *= 2
     arrived = [across(second, 2), across(next_door, 1)]
     for ahead in range(4, tensor_size, 2):
         (near,) = base_block(tensor_at, tagged, out_weight, block, ahead)

time: 27.1 us -> 27.7 us (1.022)
  starting transfers between devices: 11.8 us -> 12.8 us
  waiting for transfers between devices: 2.76 us -> 2.35 us
    ppermute x10, starting transfers between devices: 11.8 us -> 12.8 us  [permuted(): return lax.ppermute(array, axis, [(i, partner(i)) for i in range(size)])]
    ppermute x10, waiting for transfers between devices: 2.76 us -> 2.35 us  [permuted(): return lax.ppermute(array, axis, [(i, partner(i)) for i in range(size)])]
  transfers between devices with their start and end apart: 10 -> 10, of which waited for: 2 -> 4; matrix products, arithmetic and copies ran while one was open for 0% -> 0% of each run, Pallas kernels for 43% -> 42%
where the time goes in v21:
time: 27.7 us; the launch traced here: 27.6 us
  starting transfers between devices  12.8 us (46%)
  Pallas kernels  12.2 us (44%)
  waiting for transfers between devices  2.35 us (8%)
    ppermute x10, starting transfers between devices, permuted(): return lax.ppermute(array, axis, [(i, partner(i)) for i in range(size)])  12.8 us
    pallas_call x3, Pallas kernels, base_block(): pl.pallas_call(functools.partial(base_kernel, ahead, deep, len(arrived)),...  7.59 us
    pallas_call x1, Pallas kernels, attend(): pl.pallas_call(functools.partial(attend_kernel, parts, rank_width), out_s...  2.85 us
    ppermute x10, waiting for transfers between devices, permuted(): return lax.ppermute(array, axis, [(i, partner(i)) for i in range(size)])  2.35 us
    pallas_call x1, Pallas kernels, total(): pl.pallas_call(total_kernel, out_shape=jax.ShapeDtypeStruct((rows, block)...  0.69 us
  transfers between devices with their start and end apart: 10, of which 4 were waited for; matrix products, arithmetic and copies ran while one was open for 0% of the time, Pallas kernels for 42%

profile of v21, /device:TPU:0, one launch (start us, length us, event | category | flops | bytes accessed | tf_op | source)
XLA Modules:
  0.0 27.6 jit_solution(13936407575088535118)
XLA Ops:
  0.0 0.5 %collective-permute-start.6 = (bf16[4,64,2048]{2,1,0:T(8,128)(2,1)}, bf16[4,64,2048]{2,1,0:T(8,128)(2,1)S(1)}, u32[]{:S(2)}, u32[]{:S(2)}) collective-permute-start(bf16[4,64,2048]{2,1,0:T(8,128)(2,1)} %param.20), channel_id=1, source_target_pairs={{0,1},{1,0},{2,3},{3,2},{4,5},{5,4},{6,7},{7,6},{8,9},{9,8},{10,11... | collective-permute-start | bytes 3145736 | tf_op jit(solution)/shard_map/ppermute | solution.py:19
  0.5 0.1 collective-permute-start.2
  0.5 2.8 %attention.1 = (bf16[32,1152]{1,0:T(8,128)(2,1)S(1)}, bf16[1024,2048]{1,0:T(8,128)(2,1)S(1)}, s32[8,128]{1,0:T(8,128)S(1)}) custom-call(s32[1]{0:T(128)} %bitcast.2.group_at, s32[1]{0:T(128)S(6)} %xor.3.early_at, bf16[32,4,96,128]{3,2,1,0:T(8,128)(2,1)} %refs_0_.1, bf16[32,4,96,128]{3,2,1,0:T(8,128)(2,1)} %refs_1_.1, bf16[32,8,128]{2,1,0:T(8,128)(2,1)} %refs_2_.1, ...), custom_call_target="tpu_custom_call" | custom-call | flops 12582912 | bytes 1572864 | tf_op jit(solution)/shard_map/attention/pallas_call | solution.py:147
  3.4 3.0 %collective-permute-start = (bf16[32,1152]{1,0:T(8,128)(2,1)S(1)}, bf16[32,1152]{1,0:T(8,128)(2,1)S(1)}, u32[]{:S(2)}, u32[]{:S(2)}) collective-permute-start(bf16[32,1152]{1,0:T(8,128)(2,1)S(1)} %get-tuple-element.42.tagged.refs_0_.refs_2_), channel_id=1, source_target_pairs={{0,2},{1,3},{2,0},{3,1},{4,6},{5,7},{6,4},{7,5},{8,10},{9,11},{10,... | collective-permute-start | bytes 221192 | tf_op jit(solution)/shard_map/ppermute | solution.py:19
  6.4 0.0 collective-permute-start.1
  6.4 0.0 copy-start.1
  6.4 2.6 %base_terms.3 = (bf16[512,128]{1,0:T(8,128)(2,1)S(1)}, bf16[512,128]{1,0:T(8,128)(2,1)S(1)}) custom-call(s32[1]{0:T(128)} %bitcast.tensor_at, bf16[32,1152]{1,0:T(8,128)(2,1)S(1)} %get-tuple-element.42.tagged.refs_0_.refs_2_, bf16[1024,8192]{1,0:T(8,128)(2,1)} %out_weight.5, bf16[1024,2048]{1,0:T(8,128)(2,1)S(1)} %get-tuple-element.27.refs_0_), custom_call_target="tpu_custom_call" | custom-call | flops 268435456 | bytes 8388608 | tf_op jit(solution)/shard_map/base_terms/pallas_call | solution.py:257
  9.0 0.0 collective-permute-done.1.refs_1_
  9.0 0.0 collective-permute-done.refs_1_.refs_3_
  9.0 1.8 %collective-permute-start.4 = (bf16[512,128]{1,0:T(8,128)(2,1)S(1)}, bf16[512,128]{1,0:T(8,128)(2,1)S(1)}, u32[]{:S(2)}, u32[]{:S(2)}) collective-permute-start(bf16[512,128]{1,0:T(8,128)(2,1)S(1)} %get-tuple-element.35), channel_id=1, source_target_pairs={{0,4},{4,0},{8,12},{12,8},{1,5},{5,1},{9,13},{13,9},{2,6},{6,2},{1... | collective-permute-start | bytes 393224 | tf_op jit(solution)/shard_map/ppermute | solution.py:19
  10.8 0.0 collective-permute-done.2.refs_3_
  10.8 0.0 copy-done.1
  10.8 0.5 %shrink.1 = bf16[32,128]{1,0:T(8,128)(2,1)S(1)} custom-call(s32[1]{0:T(128)} %bitcast.1.batch_at, bf16[32,1152]{1,0:T(8,128)(2,1)S(1)} %get-tuple-element.42.tagged.refs_0_.refs_2_, bf16[32,1152]{1,0:T(8,128)(2,1)S(1)} %collective-permute-done.refs_1_.refs_3_, bf16[4,64,1024]{2,1,0:T(8,128)(2,1)S(1)} %bitcast.9, ...), custom_call_target="tpu_custom_call" | custom-call | flops 67108864 | bytes 1179648 | tf_op jit(solution)/shard_map/shrink/pallas_call | solution.py:317
  11.3 0.0 copy-start
  11.3 2.7 %collective-permute-start.3 = (bf16[32,128]{1,0:T(8,128)(2,1)S(1)}, bf16[32,128]{1,0:T(8,128)(2,1)S(1)}, u32[]{:S(2)}, u32[]{:S(2)}) collective-permute-start(bf16[32,128]{1,0:T(8,128)(2,1)S(1)} %shrink.1), channel_id=1, source_target_pairs={{0,8},{4,12},{8,0},{12,4},{1,9},{5,13},{9,1},{13,5},{2,10},{6,14},... | collective-permute-start | bytes 24584 | tf_op jit(solution)/shard_map/ppermute | solution.py:19
  14.0 2.5 %base_terms.4 = bf16[512,128]{1,0:T(8,128)(2,1)S(1)} custom-call(s32[1]{0:T(128)} %bitcast.tensor_at, bf16[32,1152]{1,0:T(8,128)(2,1)S(1)} %get-tuple-element.42.tagged.refs_0_.refs_2_, bf16[1024,8192]{1,0:T(8,128)(2,1)} %out_weight.5), custom_call_target="tpu_custom_call" | custom-call | flops 134217728 | bytes 4194304 | tf_op jit(solution)/shard_map/base_terms/pallas_call | solution.py:257
  16.5 0.0 collective-permute-done.4
  16.6 0.0 collective-permute-done.3
  16.6 1.2 %collective-permute-start.5 = (bf16[32,128]{1,0:T(8,128)(2,1)S(1)}, bf16[32,128]{1,0:T(8,128)(2,1)S(1)}, u32[]{:S(2)}, u32[]{:S(2)}) collective-permute-start(bf16[32,128]{1,0:T(8,128)(2,1)S(1)} %add_convert_fusion.1.refs_4_), channel_id=1, source_target_pairs={{0,4},{4,0},{8,12},{12,8},{1,5},{5,1},{9,13},{13,9},{2,6},{6,2},{1... | collective-permute-start | bytes 24584 | tf_op jit(solution)/shard_map/ppermute | solution.py:19
  17.7 1.7 %collective-permute-start.7 = (bf16[512,128]{1,0:T(8,128)(2,1)S(1)}, bf16[512,128]{1,0:T(8,128)(2,1)S(1)}, u32[]{:S(2)}, u32[]{:S(2)}) collective-permute-start(bf16[512,128]{1,0:T(8,128)(2,1)S(1)} %add_convert_fusion), channel_id=1, source_target_pairs={{0,8},{4,12},{8,0},{12,4},{1,9},{5,13},{9,1},{13,5},{2,10},{6,14},... | collective-permute-start | bytes 393224 | tf_op jit(solution)/shard_map/ppermute | solution.py:19
  19.4 1.1 %collective-permute-start.8 = (bf16[512,128]{1,0:T(8,128)(2,1)S(1)}, bf16[512,128]{1,0:T(8,128)(2,1)S(1)}, u32[]{:S(2)}, u32[]{:S(2)}) collective-permute-start(bf16[512,128]{1,0:T(8,128)(2,1)S(1)} %get-tuple-element.45), channel_id=1, source_target_pairs={{0,4},{4,0},{8,12},{12,8},{1,5},{5,1},{9,13},{13,9},{2,6},{6,2},{1... | collective-permute-start | bytes 393224 | tf_op jit(solution)/shard_map/ppermute | solution.py:19
  20.6 0.7 %collective-permute-done.5.refs_5_ = bf16[32,128]{1,0:T(8,128)(2,1)S(1)} collective-permute-done((bf16[32,128]{1,0:T(8,128)(2,1)S(1)}, bf16[32,128]{1,0:T(8,128)(2,1)S(1)}, u32[]{:S(2)}, u32[]{:S(2)}) %collective-permute-start.5) | collective-permute-done | bytes 8224 | tf_op jit(solution)/shard_map/ppermute | solution.py:19
  21.3 0.0 collective-permute-done.6
  21.3 0.0 copy-done
  21.3 0.5 %expand.1 = (bf16[512,128]{1,0:T(8,128)(2,1)S(1)}, bf16[512,128]{1,0:T(8,128)(2,1)S(1)}) custom-call(s32[1]{0:T(128)} %bitcast.1.batch_at, s32[8,128]{1,0:T(8,128)S(1)} %get-tuple-element.31.refs_0_, s32[8,128]{1,0:T(8,128)S(1)} %collective-permute-done.1.refs_1_, bf16[32,1152]{1,0:T(8,128)(2,1)S(1)} %get-tuple-element.42.tagged.refs_0_.refs_2_, ...), custom_call_target="tpu_custom_call" | custom-call | flops 134217728 | bytes 1048576 | tf_op jit(solution)/shard_map/expand/pallas_call | solution.py:377
  21.8 0.8 %collective-permute-start.9 = (bf16[512,128]{1,0:T(8,128)(2,1)S(1)}, bf16[512,128]{1,0:T(8,128)(2,1)S(1)}, u32[]{:S(2)}, u32[]{:S(2)}) collective-permute-start(bf16[512,128]{1,0:T(8,128)(2,1)S(1)} %get-tuple-element.46), channel_id=1, source_target_pairs={{0,2},{1,3},{2,0},{3,1},{4,6},{5,7},{6,4},{7,5},{8,10},{9,11},{10,... | collective-permute-start | bytes 393224 | tf_op jit(solution)/shard_map/ppermute | solution.py:19
  22.7 2.5 %base_terms.5.refs_0_ = f32[512,128]{1,0:T(8,128)S(1)} custom-call(s32[1]{0:T(128)} %bitcast.tensor_at, bf16[32,1152]{1,0:T(8,128)(2,1)S(1)} %get-tuple-element.42.tagged.refs_0_.refs_2_, bf16[1024,8192]{1,0:T(8,128)(2,1)} %out_weight.5), custom_call_target="tpu_custom_call" | custom-call | flops 134217728 | bytes 4194304 | tf_op jit(solution)/shard_map/base_terms/pallas_call | solution.py:257
  25.2 0.7 %collective-permute-done.7.refs_2_ = bf16[512,128]{1,0:T(8,128)(2,1)S(1)} collective-permute-done((bf16[512,128]{1,0:T(8,128)(2,1)S(1)}, bf16[512,128]{1,0:T(8,128)(2,1)S(1)}, u32[]{:S(2)}, u32[]{:S(2)}) %collective-permute-start.7) | collective-permute-done | bytes 131104 | tf_op jit(solution)/shard_map/ppermute | solution.py:19
  25.9 0.1 collective-permute-done.8.refs_1_
  26.0 0.9 %collective-permute-done.9.refs_1_ = bf16[512,128]{1,0:T(8,128)(2,1)S(1)} collective-permute-done((bf16[512,128]{1,0:T(8,128)(2,1)S(1)}, bf16[512,128]{1,0:T(8,128)(2,1)S(1)}, u32[]{:S(2)}, u32[]{:S(2)}) %collective-permute-start.9) | collective-permute-done | bytes 131104 | tf_op jit(solution)/shard_map/ppermute | solution.py:19
  26.9 0.7 %total.1 = bf16[32,2048]{1,0:T(8,128)(2,1)} custom-call(f32[512,128]{1,0:T(8,128)S(1)} %partial_total.3.refs_0_, bf16[512,128]{1,0:T(8,128)(2,1)S(1)} %collective-permute-done.9.refs_1_), custom_call_target="tpu_custom_call" | custom-call | flops 131072 | bytes 393216 | tf_op jit(solution)/shard_map/total/pallas_call | solution.py:410
  (4 shorter events, 0.1 us)
Async XLA Ops:
  0.0 21.3 %collective-permute-start.6 = (bf16[4,64,2048]{2,1,0:T(8,128)(2,1)}, bf16[4,64,2048]{2,1,0:T(8,128)(2,1)S(1)}, u32[]{:S(2)}, u32[]{:S(2)}) collective-permute-start(bf16[4,64,2048]{2,1,0:T(8,128)(2,1)} %param.20), channel_id=1, source_target_pairs={{0,1},{1,0},{2,3},{3,2},{4,5},{5,4},{6,7},{7,6},{8,9},{9,8},{10,11... | collective-permute-start | bytes 3145736 | tf_op jit(solution)/shard_map/ppermute | solution.py:19
  0.5 10.4 %collective-permute-start.2 = (bf16[4,64,1024]{2,1,0:T(8,128)(2,1)}, bf16[4,64,1024]{2,1,0:T(8,128)(2,1)S(1)}, u32[]{:S(2)}, u32[]{:S(2)}) collective-permute-start(bf16[4,64,1024]{2,1,0:T(8,128)(2,1)} %bitcast.8), channel_id=1, source_target_pairs={{0,1},{1,0},{2,3},{3,2},{4,5},{5,4},{6,7},{7,6},{8,9},{9,8},{10,11... | collective-permute-start | bytes 1572872 | tf_op jit(solution)/shard_map/ppermute | solution.py:19
  3.4 5.6 %collective-permute-start = (bf16[32,1152]{1,0:T(8,128)(2,1)S(1)}, bf16[32,1152]{1,0:T(8,128)(2,1)S(1)}, u32[]{:S(2)}, u32[]{:S(2)}) collective-permute-start(bf16[32,1152]{1,0:T(8,128)(2,1)S(1)} %get-tuple-element.42.tagged.refs_0_.refs_2_), channel_id=1, source_target_pairs={{0,2},{1,3},{2,0},{3,1},{4,6},{5,7},{6,4},{7,5},{8,10},{9,11},{10,... | collective-permute-start | bytes 221192 | tf_op jit(solution)/shard_map/ppermute | solution.py:19
  6.4 2.6 %collective-permute-start.1 = (s32[8,128]{1,0:T(8,128)S(1)}, s32[8,128]{1,0:T(8,128)S(1)}, u32[]{:S(2)}, u32[]{:S(2)}) collective-permute-start(s32[8,128]{1,0:T(8,128)S(1)} %get-tuple-element.31.refs_0_), channel_id=1, source_target_pairs={{0,1},{1,0},{2,3},{3,2},{4,5},{5,4},{6,7},{7,6},{8,9},{9,8},{10,11... | collective-permute-start | bytes 12296 | tf_op jit(solution)/shard_map/ppermute | solution.py:19
  6.4 4.4 %copy-start.1 = (bf16[4,1024,64]{1,2,0:T(8,128)(2,1)S(1)}, bf16[4,1024,64]{1,2,0:T(8,128)(2,1)}, u32[]{:S(2)}) copy-start(bf16[4,1024,64]{1,2,0:T(8,128)(2,1)} %param.19) | copy-start | bytes 1572868
  9.0 7.5 %collective-permute-start.4 = (bf16[512,128]{1,0:T(8,128)(2,1)S(1)}, bf16[512,128]{1,0:T(8,128)(2,1)S(1)}, u32[]{:S(2)}, u32[]{:S(2)}) collective-permute-start(bf16[512,128]{1,0:T(8,128)(2,1)S(1)} %get-tuple-element.35), channel_id=1, source_target_pairs={{0,4},{4,0},{8,12},{12,8},{1,5},{5,1},{9,13},{13,9},{2,6},{6,2},{1... | collective-permute-start | bytes 393224 | tf_op jit(solution)/shard_map/ppermute | solution.py:19
  11.3 10.0 %copy-start = (bf16[4,64,2048]{2,1,0:T(8,128)(2,1)S(1)}, bf16[4,64,2048]{2,1,0:T(8,128)(2,1)}, u32[]{:S(2)}) copy-start(bf16[4,64,2048]{2,1,0:T(8,128)(2,1)} %param.20) | copy-start | bytes 3145732
  11.3 5.2 %collective-permute-start.3 = (bf16[32,128]{1,0:T(8,128)(2,1)S(1)}, bf16[32,128]{1,0:T(8,128)(2,1)S(1)}, u32[]{:S(2)}, u32[]{:S(2)}) collective-permute-start(bf16[32,128]{1,0:T(8,128)(2,1)S(1)} %shrink.1), channel_id=1, source_target_pairs={{0,8},{4,12},{8,0},{12,4},{1,9},{5,13},{9,1},{13,5},{2,10},{6,14},... | collective-permute-start | bytes 24584 | tf_op jit(solution)/shard_map/ppermute | solution.py:19
  16.6 4.7 %collective-permute-start.5 = (bf16[32,128]{1,0:T(8,128)(2,1)S(1)}, bf16[32,128]{1,0:T(8,128)(2,1)S(1)}, u32[]{:S(2)}, u32[]{:S(2)}) collective-permute-start(bf16[32,128]{1,0:T(8,128)(2,1)S(1)} %add_convert_fusion.1.refs_4_), channel_id=1, source_target_pairs={{0,4},{4,0},{8,12},{12,8},{1,5},{5,1},{9,13},{13,9},{2,6},{6,2},{1... | collective-permute-start | bytes 24584 | tf_op jit(solution)/shard_map/ppermute | solution.py:19
  17.7 8.1 %collective-permute-start.7 = (bf16[512,128]{1,0:T(8,128)(2,1)S(1)}, bf16[512,128]{1,0:T(8,128)(2,1)S(1)}, u32[]{:S(2)}, u32[]{:S(2)}) collective-permute-start(bf16[512,128]{1,0:T(8,128)(2,1)S(1)} %add_convert_fusion), channel_id=1, source_target_pairs={{0,8},{4,12},{8,0},{12,4},{1,9},{5,13},{9,1},{13,5},{2,10},{6,14},... | collective-permute-start | bytes 393224 | tf_op jit(solution)/shard_map/ppermute | solution.py:19
  19.4 6.5 %collective-permute-start.8 = (bf16[512,128]{1,0:T(8,128)(2,1)S(1)}, bf16[512,128]{1,0:T(8,128)(2,1)S(1)}, u32[]{:S(2)}, u32[]{:S(2)}) collective-permute-start(bf16[512,128]{1,0:T(8,128)(2,1)S(1)} %get-tuple-element.45), channel_id=1, source_target_pairs={{0,4},{4,0},{8,12},{12,8},{1,5},{5,1},{9,13},{13,9},{2,6},{6,2},{1... | collective-permute-start | bytes 393224 | tf_op jit(solution)/shard_map/ppermute | solution.py:19
  21.8 5.0 %collective-permute-start.9 = (bf16[512,128]{1,0:T(8,128)(2,1)S(1)}, bf16[512,128]{1,0:T(8,128)(2,1)S(1)}, u32[]{:S(2)}, u32[]{:S(2)}) collective-permute-start(bf16[512,128]{1,0:T(8,128)(2,1)S(1)} %get-tuple-element.46), channel_id=1, source_target_pairs={{0,2},{1,3},{2,0},{3,1},{4,6},{5,7},{6,4},{7,5},{8,10},{9,11},{10,... | collective-permute-start | bytes 393224 | tf_op jit(solution)/shard_map/ppermute | solution.py:19

commit v22 on v8

--- a/solution.py
+++ b/solution.py
@@ -47,11 +47,11 @@
     small = [
         pltpu.make_async_copy(given[i], held[i], small_sems.at[i - 2]) for i in range(2, 9)
     ]
-    for copy in small:
-        copy.start()
     for part in range(parts):
         for copy in cache_copies(part):
             copy.start()
+    for copy in small:
+        copy.start()
     block = early.shape[1]
     start = pl.multiple_of(early_at[0] * block, block)
     early_copy = pltpu.make_async_copy(out_weight.at[:, pl.ds(start, block)], early, early_sem)
@@ -141,7 +141,7 @@
     full = -(-heads // 8) * 8
     if full != heads:
         queries = jnp.pad(queries, ((0, 0), (0, full - heads), (0, 0)))
-    parts = 2
+    parts = 1
     smem = pl.BlockSpec(memory_space=pltpu.SMEM)
     away = pl.BlockSpec(memory_space=pl.ANY)
     tagged, early, limits = pl.pallas_call(

time: 27.1 us -> 27.1 us (level)
  no operation moved by 1% of the time
where the time goes in v22:
time: 27.1 us; the launch traced here: 27 us
  Pallas kernels  12.2 us (45%)
  starting transfers between devices  11.8 us (44%)
  waiting for transfers between devices  2.76 us (10%)
    ppermute x10, starting transfers between devices, permuted(): return lax.ppermute(array, axis, [(i, partner(i)) for i in range(size)])  11.8 us
    pallas_call x3, Pallas kernels, base_block(): pl.pallas_call(functools.partial(base_kernel, ahead, deep, len(arrived)),...  7.59 us
    pallas_call x1, Pallas kernels, attend(): pl.pallas_call(functools.partial(attend_kernel, parts, rank_width), out_s...  2.83 us
    ppermute x10, waiting for transfers between devices, permuted(): return lax.ppermute(array, axis, [(i, partner(i)) for i in range(size)])  2.76 us
    pallas_call x1, Pallas kernels, total(): pl.pallas_call(total_kernel, out_shape=jax.ShapeDtypeStruct((rows, block)...  0.69 us
  transfers between devices with their start and end apart: 10, of which 2 were waited for; matrix products, arithmetic and copies ran while one was open for 0% of the time, Pallas kernels for 43%

profile of v22, /device:TPU:0, one launch (start us, length us, event | category | flops | bytes accessed | tf_op | source)
XLA Modules:
  0.0 27.0 jit_solution(14065872439322206804)
XLA Ops:
  0.0 0.5 %collective-permute-start.6 = (bf16[4,64,2048]{2,1,0:T(8,128)(2,1)}, bf16[4,64,2048]{2,1,0:T(8,128)(2,1)S(1)}, u32[]{:S(2)}, u32[]{:S(2)}) collective-permute-start(bf16[4,64,2048]{2,1,0:T(8,128)(2,1)} %param.20), channel_id=1, source_target_pairs={{0,1},{1,0},{2,3},{3,2},{4,5},{5,4},{6,7},{7,6},{8,9},{9,8},{10,11... | collective-permute-start | bytes 3145736 | tf_op jit(solution)/shard_map/ppermute | solution.py:19
  0.5 0.1 collective-permute-start.2
  0.5 2.8 %attention.1 = (bf16[32,1152]{1,0:T(8,128)(2,1)S(1)}, bf16[1024,2048]{1,0:T(8,128)(2,1)S(1)}, s32[8,128]{1,0:T(8,128)S(1)}) custom-call(s32[1]{0:T(128)} %bitcast.2.group_at, s32[1]{0:T(128)S(6)} %xor.3.early_at, bf16[32,4,96,128]{3,2,1,0:T(8,128)(2,1)} %refs_0_.1, bf16[32,4,96,128]{3,2,1,0:T(8,128)(2,1)} %refs_1_.1, bf16[32,8,128]{2,1,0:T(8,128)(2,1)} %refs_2_.1, ...), custom_call_target="tpu_custom_call" | custom-call | flops 12582912 | bytes 1572864 | tf_op jit(solution)/shard_map/attention/pallas_call | solution.py:147
  3.4 3.0 %collective-permute-start = (bf16[32,1152]{1,0:T(8,128)(2,1)S(1)}, bf16[32,1152]{1,0:T(8,128)(2,1)S(1)}, u32[]{:S(2)}, u32[]{:S(2)}) collective-permute-start(bf16[32,1152]{1,0:T(8,128)(2,1)S(1)} %get-tuple-element.42.tagged.refs_0_.refs_2_), channel_id=1, source_target_pairs={{0,2},{1,3},{2,0},{3,1},{4,6},{5,7},{6,4},{7,5},{8,10},{9,11},{10,... | collective-permute-start | bytes 221192 | tf_op jit(solution)/shard_map/ppermute | solution.py:19
  6.4 0.0 collective-permute-start.1
  6.4 0.0 copy-start.1
  6.4 2.6 %base_terms.3 = (bf16[512,128]{1,0:T(8,128)(2,1)S(1)}, bf16[512,128]{1,0:T(8,128)(2,1)S(1)}) custom-call(s32[1]{0:T(128)} %bitcast.tensor_at, bf16[32,1152]{1,0:T(8,128)(2,1)S(1)} %get-tuple-element.42.tagged.refs_0_.refs_2_, bf16[1024,8192]{1,0:T(8,128)(2,1)} %out_weight.5, bf16[1024,2048]{1,0:T(8,128)(2,1)S(1)} %get-tuple-element.27.refs_0_), custom_call_target="tpu_custom_call" | custom-call | flops 268435456 | bytes 8388608 | tf_op jit(solution)/shard_map/base_terms/pallas_call | solution.py:257
  9.0 0.0 collective-permute-done.1.refs_1_
  9.0 0.0 collective-permute-done.refs_1_.refs_3_
  9.0 1.8 %collective-permute-start.4 = (bf16[512,128]{1,0:T(8,128)(2,1)S(1)}, bf16[512,128]{1,0:T(8,128)(2,1)S(1)}, u32[]{:S(2)}, u32[]{:S(2)}) collective-permute-start(bf16[512,128]{1,0:T(8,128)(2,1)S(1)} %get-tuple-element.35), channel_id=1, source_target_pairs={{0,4},{4,0},{8,12},{12,8},{1,5},{5,1},{9,13},{13,9},{2,6},{6,2},{1... | collective-permute-start | bytes 393224 | tf_op jit(solution)/shard_map/ppermute | solution.py:19
  10.8 0.0 collective-permute-done.2.refs_3_
  10.8 0.0 copy-done.1
  10.8 0.5 %shrink.1 = bf16[32,128]{1,0:T(8,128)(2,1)S(1)} custom-call(s32[1]{0:T(128)} %bitcast.1.batch_at, bf16[32,1152]{1,0:T(8,128)(2,1)S(1)} %get-tuple-element.42.tagged.refs_0_.refs_2_, bf16[32,1152]{1,0:T(8,128)(2,1)S(1)} %collective-permute-done.refs_1_.refs_3_, bf16[4,64,1024]{2,1,0:T(8,128)(2,1)S(1)} %bitcast.9, ...), custom_call_target="tpu_custom_call" | custom-call | flops 67108864 | bytes 1179648 | tf_op jit(solution)/shard_map/shrink/pallas_call | solution.py:317
  11.3 0.0 copy-start
  11.3 0.3 %collective-permute-start.3 = (bf16[32,128]{1,0:T(8,128)(2,1)S(1)}, bf16[32,128]{1,0:T(8,128)(2,1)S(1)}, u32[]{:S(2)}, u32[]{:S(2)}) collective-permute-start(bf16[32,128]{1,0:T(8,128)(2,1)S(1)} %shrink.1), channel_id=1, source_target_pairs={{0,4},{4,0},{8,12},{12,8},{1,5},{5,1},{9,13},{13,9},{2,6},{6,2},{1... | collective-permute-start | bytes 24584 | tf_op jit(solution)/shard_map/ppermute | solution.py:19
  11.7 2.5 %base_terms.4 = bf16[512,128]{1,0:T(8,128)(2,1)S(1)} custom-call(s32[1]{0:T(128)} %bitcast.tensor_at, bf16[32,1152]{1,0:T(8,128)(2,1)S(1)} %get-tuple-element.42.tagged.refs_0_.refs_2_, bf16[1024,8192]{1,0:T(8,128)(2,1)} %out_weight.5), custom_call_target="tpu_custom_call" | custom-call | flops 134217728 | bytes 4194304 | tf_op jit(solution)/shard_map/base_terms/pallas_call | solution.py:257
  14.2 0.9 %collective-permute-done.4 = bf16[512,128]{1,0:T(8,128)(2,1)S(1)} collective-permute-done((bf16[512,128]{1,0:T(8,128)(2,1)S(1)}, bf16[512,128]{1,0:T(8,128)(2,1)S(1)}, u32[]{:S(2)}, u32[]{:S(2)}) %collective-permute-start.4) | collective-permute-done | bytes 131104 | tf_op jit(solution)/shard_map/ppermute | solution.py:19
  15.1 0.0 collective-permute-done.3
  15.1 2.6 %collective-permute-start.5 = (bf16[32,128]{1,0:T(8,128)(2,1)S(1)}, bf16[32,128]{1,0:T(8,128)(2,1)S(1)}, u32[]{:S(2)}, u32[]{:S(2)}) collective-permute-start(bf16[32,128]{1,0:T(8,128)(2,1)S(1)} %add_convert_fusion.1.refs_4_), channel_id=1, source_target_pairs={{0,8},{4,12},{8,0},{12,4},{1,9},{5,13},{9,1},{13,5},{2,10},{6,14},... | collective-permute-start | bytes 24584 | tf_op jit(solution)/shard_map/ppermute | solution.py:19
  17.8 0.3 %collective-permute-start.7 = (bf16[512,128]{1,0:T(8,128)(2,1)S(1)}, bf16[512,128]{1,0:T(8,128)(2,1)S(1)}, u32[]{:S(2)}, u32[]{:S(2)}) collective-permute-start(bf16[512,128]{1,0:T(8,128)(2,1)S(1)} %add_convert_fusion), channel_id=1, source_target_pairs={{0,8},{4,12},{8,0},{12,4},{1,9},{5,13},{9,1},{13,5},{2,10},{6,14},... | collective-permute-start | bytes 393224 | tf_op jit(solution)/shard_map/ppermute | solution.py:19
  18.1 1.6 %collective-permute-start.8 = (bf16[512,128]{1,0:T(8,128)(2,1)S(1)}, bf16[512,128]{1,0:T(8,128)(2,1)S(1)}, u32[]{:S(2)}, u32[]{:S(2)}) collective-permute-start(bf16[512,128]{1,0:T(8,128)(2,1)S(1)} %get-tuple-element.45), channel_id=1, source_target_pairs={{0,4},{4,0},{8,12},{12,8},{1,5},{5,1},{9,13},{13,9},{2,6},{6,2},{1... | collective-permute-start | bytes 393224 | tf_op jit(solution)/shard_map/ppermute | solution.py:19
  19.7 0.0 collective-permute-done.5.refs_5_
  19.7 0.0 collective-permute-done.6
  19.7 0.0 copy-done
  19.7 0.5 %expand.1 = (bf16[512,128]{1,0:T(8,128)(2,1)S(1)}, bf16[512,128]{1,0:T(8,128)(2,1)S(1)}) custom-call(s32[1]{0:T(128)} %bitcast.1.batch_at, s32[8,128]{1,0:T(8,128)S(1)} %get-tuple-element.31.refs_0_, s32[8,128]{1,0:T(8,128)S(1)} %collective-permute-done.1.refs_1_, bf16[32,1152]{1,0:T(8,128)(2,1)S(1)} %get-tuple-element.42.tagged.refs_0_.refs_2_, ...), custom_call_target="tpu_custom_call" | custom-call | flops 134217728 | bytes 1048576 | tf_op jit(solution)/shard_map/expand/pallas_call | solution.py:377
  20.3 1.6 %collective-permute-start.9 = (bf16[512,128]{1,0:T(8,128)(2,1)S(1)}, bf16[512,128]{1,0:T(8,128)(2,1)S(1)}, u32[]{:S(2)}, u32[]{:S(2)}) collective-permute-start(bf16[512,128]{1,0:T(8,128)(2,1)S(1)} %get-tuple-element.46), channel_id=1, source_target_pairs={{0,2},{1,3},{2,0},{3,1},{4,6},{5,7},{6,4},{7,5},{8,10},{9,11},{10,... | collective-permute-start | bytes 393224 | tf_op jit(solution)/shard_map/ppermute | solution.py:19
  21.9 2.5 %base_terms.5.refs_0_ = f32[512,128]{1,0:T(8,128)S(1)} custom-call(s32[1]{0:T(128)} %bitcast.tensor_at, bf16[32,1152]{1,0:T(8,128)(2,1)S(1)} %get-tuple-element.42.tagged.refs_0_.refs_2_, bf16[1024,8192]{1,0:T(8,128)(2,1)} %out_weight.5), custom_call_target="tpu_custom_call" | custom-call | flops 134217728 | bytes 4194304 | tf_op jit(solution)/shard_map/base_terms/pallas_call | solution.py:257
  24.4 1.8 %collective-permute-done.7.refs_2_ = bf16[512,128]{1,0:T(8,128)(2,1)S(1)} collective-permute-done((bf16[512,128]{1,0:T(8,128)(2,1)S(1)}, bf16[512,128]{1,0:T(8,128)(2,1)S(1)}, u32[]{:S(2)}, u32[]{:S(2)}) %collective-permute-start.7) | collective-permute-done | bytes 131104 | tf_op jit(solution)/shard_map/ppermute | solution.py:19
  26.2 0.0 collective-permute-done.8.refs_1_
  26.3 0.0 collective-permute-done.9.refs_1_
  26.3 0.7 %total.1 = bf16[32,2048]{1,0:T(8,128)(2,1)} custom-call(f32[512,128]{1,0:T(8,128)S(1)} %partial_total.3.refs_0_, bf16[512,128]{1,0:T(8,128)(2,1)S(1)} %collective-permute-done.9.refs_1_), custom_call_target="tpu_custom_call" | custom-call | flops 131072 | bytes 393216 | tf_op jit(solution)/shard_map/total/pallas_call | solution.py:410
  (4 shorter events, 0.1 us)
Async XLA Ops:
  0.0 19.7 %collective-permute-start.6 = (bf16[4,64,2048]{2,1,0:T(8,128)(2,1)}, bf16[4,64,2048]{2,1,0:T(8,128)(2,1)S(1)}, u32[]{:S(2)}, u32[]{:S(2)}) collective-permute-start(bf16[4,64,2048]{2,1,0:T(8,128)(2,1)} %param.20), channel_id=1, source_target_pairs={{0,1},{1,0},{2,3},{3,2},{4,5},{5,4},{6,7},{7,6},{8,9},{9,8},{10,11... | collective-permute-start | bytes 3145736 | tf_op jit(solution)/shard_map/ppermute | solution.py:19
  0.5 10.3 %collective-permute-start.2 = (bf16[4,64,1024]{2,1,0:T(8,128)(2,1)}, bf16[4,64,1024]{2,1,0:T(8,128)(2,1)S(1)}, u32[]{:S(2)}, u32[]{:S(2)}) collective-permute-start(bf16[4,64,1024]{2,1,0:T(8,128)(2,1)} %bitcast.8), channel_id=1, source_target_pairs={{0,1},{1,0},{2,3},{3,2},{4,5},{5,4},{6,7},{7,6},{8,9},{9,8},{10,11... | collective-permute-start | bytes 1572872 | tf_op jit(solution)/shard_map/ppermute | solution.py:19
  3.4 5.6 %collective-permute-start = (bf16[32,1152]{1,0:T(8,128)(2,1)S(1)}, bf16[32,1152]{1,0:T(8,128)(2,1)S(1)}, u32[]{:S(2)}, u32[]{:S(2)}) collective-permute-start(bf16[32,1152]{1,0:T(8,128)(2,1)S(1)} %get-tuple-element.42.tagged.refs_0_.refs_2_), channel_id=1, source_target_pairs={{0,2},{1,3},{2,0},{3,1},{4,6},{5,7},{6,4},{7,5},{8,10},{9,11},{10,... | collective-permute-start | bytes 221192 | tf_op jit(solution)/shard_map/ppermute | solution.py:19
  6.4 2.6 %collective-permute-start.1 = (s32[8,128]{1,0:T(8,128)S(1)}, s32[8,128]{1,0:T(8,128)S(1)}, u32[]{:S(2)}, u32[]{:S(2)}) collective-permute-start(s32[8,128]{1,0:T(8,128)S(1)} %get-tuple-element.31.refs_0_), channel_id=1, source_target_pairs={{0,1},{1,0},{2,3},{3,2},{4,5},{5,4},{6,7},{7,6},{8,9},{9,8},{10,11... | collective-permute-start | bytes 12296 | tf_op jit(solution)/shard_map/ppermute | solution.py:19
  6.4 4.4 %copy-start.1 = (bf16[4,1024,64]{1,2,0:T(8,128)(2,1)S(1)}, bf16[4,1024,64]{1,2,0:T(8,128)(2,1)}, u32[]{:S(2)}) copy-start(bf16[4,1024,64]{1,2,0:T(8,128)(2,1)} %param.19) | copy-start | bytes 1572868
  9.0 6.1 %collective-permute-start.4 = (bf16[512,128]{1,0:T(8,128)(2,1)S(1)}, bf16[512,128]{1,0:T(8,128)(2,1)S(1)}, u32[]{:S(2)}, u32[]{:S(2)}) collective-permute-start(bf16[512,128]{1,0:T(8,128)(2,1)S(1)} %get-tuple-element.35), channel_id=1, source_target_pairs={{0,4},{4,0},{8,12},{12,8},{1,5},{5,1},{9,13},{13,9},{2,6},{6,2},{1... | collective-permute-start | bytes 393224 | tf_op jit(solution)/shard_map/ppermute | solution.py:19
  11.3 8.4 %copy-start = (bf16[4,64,2048]{2,1,0:T(8,128)(2,1)S(1)}, bf16[4,64,2048]{2,1,0:T(8,128)(2,1)}, u32[]{:S(2)}) copy-start(bf16[4,64,2048]{2,1,0:T(8,128)(2,1)} %param.20) | copy-start | bytes 3145732
  11.3 3.8 %collective-permute-start.3 = (bf16[32,128]{1,0:T(8,128)(2,1)S(1)}, bf16[32,128]{1,0:T(8,128)(2,1)S(1)}, u32[]{:S(2)}, u32[]{:S(2)}) collective-permute-start(bf16[32,128]{1,0:T(8,128)(2,1)S(1)} %shrink.1), channel_id=1, source_target_pairs={{0,4},{4,0},{8,12},{12,8},{1,5},{5,1},{9,13},{13,9},{2,6},{6,2},{1... | collective-permute-start | bytes 24584 | tf_op jit(solution)/shard_map/ppermute | solution.py:19
  15.1 4.6 %collective-permute-start.5 = (bf16[32,128]{1,0:T(8,128)(2,1)S(1)}, bf16[32,128]{1,0:T(8,128)(2,1)S(1)}, u32[]{:S(2)}, u32[]{:S(2)}) collective-permute-start(bf16[32,128]{1,0:T(8,128)(2,1)S(1)} %add_convert_fusion.1.refs_4_), channel_id=1, source_target_pairs={{0,8},{4,12},{8,0},{12,4},{1,9},{5,13},{9,1},{13,5},{2,10},{6,14},... | collective-permute-start | bytes 24584 | tf_op jit(solution)/shard_map/ppermute | solution.py:19
  17.8 8.4 %collective-permute-start.7 = (bf16[512,128]{1,0:T(8,128)(2,1)S(1)}, bf16[512,128]{1,0:T(8,128)(2,1)S(1)}, u32[]{:S(2)}, u32[]{:S(2)}) collective-permute-start(bf16[512,128]{1,0:T(8,128)(2,1)S(1)} %add_convert_fusion), channel_id=1, source_target_pairs={{0,8},{4,12},{8,0},{12,4},{1,9},{5,13},{9,1},{13,5},{2,10},{6,14},... | collective-permute-start | bytes 393224 | tf_op jit(solution)/shard_map/ppermute | solution.py:19
  18.1 8.1 %collective-permute-start.8 = (bf16[512,128]{1,0:T(8,128)(2,1)S(1)}, bf16[512,128]{1,0:T(8,128)(2,1)S(1)}, u32[]{:S(2)}, u32[]{:S(2)}) collective-permute-start(bf16[512,128]{1,0:T(8,128)(2,1)S(1)} %get-tuple-element.45), channel_id=1, source_target_pairs={{0,4},{4,0},{8,12},{12,8},{1,5},{5,1},{9,13},{13,9},{2,6},{6,2},{1... | collective-permute-start | bytes 393224 | tf_op jit(solution)/shard_map/ppermute | solution.py:19
  20.3 6.0 %collective-permute-start.9 = (bf16[512,128]{1,0:T(8,128)(2,1)S(1)}, bf16[512,128]{1,0:T(8,128)(2,1)S(1)}, u32[]{:S(2)}, u32[]{:S(2)}) collective-permute-start(bf16[512,128]{1,0:T(8,128)(2,1)S(1)} %get-tuple-element.46), channel_id=1, source_target_pairs={{0,2},{1,3},{2,0},{3,1},{4,6},{5,7},{6,4},{7,5},{8,10},{9,11},{10,... | collective-permute-start | bytes 393224 | tf_op jit(solution)/shard_map/ppermute | solution.py:19

commit v23 on v22

--- a/solution.py
+++ b/solution.py
@@ -510,17 +510,11 @@
     third = across(third, 1)
 
     part = shrink_part(blocks, shrink_factors, batch_at)
-    parts = [part, across(part, 1)]
+    parts = [part] + [across(part, ahead) for ahead in range(1, tensor_size)]
     part, later_tagged = lax.optimization_barrier((part, tagged))
     (second,) = base_block(tensor_at, later_tagged, out_weight, block, 2)
     second = (wide(second) + wide(third)).astype(BF16)
-    parts, second = lax.optimization_barrier((parts, second))
-    bit = 2
-    while bit < tensor_size:
-        part = (wide(parts[0]) + wide(parts[1])).astype(BF16)
-        part, next_door = lax.optimization_barrier((part, next_door))
-        parts = [part, across(part, bit)]
-        bit *= 2
+    parts[1], second, next_door = lax.optimization_barrier((parts[1], second, next_door))
     arrived = [across(second, 2), across(next_door, 1)]
     for ahead in range(4, tensor_size, 2):
         (near,) = base_block(tensor_at, tagged, out_weight, block, ahead)

time: 27.1 us -> 28.1 us (1.037)
  starting transfers between devices: 11.8 us -> 14.4 us
  waiting for transfers between devices: 2.76 us -> 1.11 us
    ppermute x10 -> x11, starting transfers between devices: 11.8 us -> 14.4 us  [permuted(): return lax.ppermute(array, axis, [(i, partner(i)) for i in range(size)])]
    ppermute x10 -> x11, waiting for transfers between devices: 2.76 us -> 1.11 us  [permuted(): return lax.ppermute(array, axis, [(i, partner(i)) for i in range(size)])]
  transfers between devices with their start and end apart: 10 -> 11, of which waited for: 2 -> 2; matrix products, arithmetic and copies ran while one was open for 0% -> 0% of each run, Pallas kernels for 43% -> 41%
where the time goes in v23:
time: 28.1 us; the launch traced here: 27.9 us
  starting transfers between devices  14.4 us (51%)
  Pallas kernels  12.2 us (43%)
  waiting for transfers between devices  1.11 us (4%)
    ppermute x11, starting transfers between devices, permuted(): return lax.ppermute(array, axis, [(i, partner(i)) for i in range(size)])  14.4 us
    pallas_call x3, Pallas kernels, base_block(): pl.pallas_call(functools.partial(base_kernel, ahead, deep, len(arrived)),...  7.59 us
    pallas_call x1, Pallas kernels, attend(): pl.pallas_call(functools.partial(attend_kernel, parts, rank_width), out_s...  2.83 us
    ppermute x11, waiting for transfers between devices, permuted(): return lax.ppermute(array, axis, [(i, partner(i)) for i in range(size)])  1.11 us
    pallas_call x1, Pallas kernels, total(): pl.pallas_call(total_kernel, out_shape=jax.ShapeDtypeStruct((rows, block)...  0.69 us
  transfers between devices with their start and end apart: 11, of which 2 were waited for; matrix products, arithmetic and copies ran while one was open for 0% of the time, Pallas kernels for 41%

profile of v23, /device:TPU:0, one launch (start us, length us, event | category | flops | bytes accessed | tf_op | source)
XLA Modules:
  0.0 27.9 jit_solution(13882791604435778864)
XLA Ops:
  0.0 0.5 %collective-permute-start.7 = (bf16[4,64,2048]{2,1,0:T(8,128)(2,1)}, bf16[4,64,2048]{2,1,0:T(8,128)(2,1)S(1)}, u32[]{:S(2)}, u32[]{:S(2)}) collective-permute-start(bf16[4,64,2048]{2,1,0:T(8,128)(2,1)} %param.20), channel_id=1, source_target_pairs={{0,1},{1,0},{2,3},{3,2},{4,5},{5,4},{6,7},{7,6},{8,9},{9,8},{10,11... | collective-permute-start | bytes 3145736 | tf_op jit(solution)/shard_map/ppermute | solution.py:19
  0.5 0.1 collective-permute-start.2
  0.5 2.8 %attention.1 = (bf16[32,1152]{1,0:T(8,128)(2,1)S(1)}, bf16[1024,2048]{1,0:T(8,128)(2,1)S(1)}, s32[8,128]{1,0:T(8,128)S(1)}) custom-call(s32[1]{0:T(128)} %bitcast.2.group_at, s32[1]{0:T(128)S(6)} %xor.3.early_at, bf16[32,4,96,128]{3,2,1,0:T(8,128)(2,1)} %refs_0_.1, bf16[32,4,96,128]{3,2,1,0:T(8,128)(2,1)} %refs_1_.1, bf16[32,8,128]{2,1,0:T(8,128)(2,1)} %refs_2_.1, ...), custom_call_target="tpu_custom_call" | custom-call | flops 12582912 | bytes 1572864 | tf_op jit(solution)/shard_map/attention/pallas_call | solution.py:147
  3.4 3.0 %collective-permute-start = (bf16[32,1152]{1,0:T(8,128)(2,1)S(1)}, bf16[32,1152]{1,0:T(8,128)(2,1)S(1)}, u32[]{:S(2)}, u32[]{:S(2)}) collective-permute-start(bf16[32,1152]{1,0:T(8,128)(2,1)S(1)} %get-tuple-element.38.tagged.refs_0_.refs_2_), channel_id=1, source_target_pairs={{0,2},{1,3},{2,0},{3,1},{4,6},{5,7},{6,4},{7,5},{8,10},{9,11},{10,... | collective-permute-start | bytes 221192 | tf_op jit(solution)/shard_map/ppermute | solution.py:19
  6.4 0.0 collective-permute-start.1
  6.4 0.0 copy-start.1
  6.4 2.6 %base_terms.3 = (bf16[512,128]{1,0:T(8,128)(2,1)S(1)}, bf16[512,128]{1,0:T(8,128)(2,1)S(1)}) custom-call(s32[1]{0:T(128)} %bitcast.tensor_at, bf16[32,1152]{1,0:T(8,128)(2,1)S(1)} %get-tuple-element.38.tagged.refs_0_.refs_2_, bf16[1024,8192]{1,0:T(8,128)(2,1)} %out_weight.5, bf16[1024,2048]{1,0:T(8,128)(2,1)S(1)} %get-tuple-element.25.refs_0_), custom_call_target="tpu_custom_call" | custom-call | flops 268435456 | bytes 8388608 | tf_op jit(solution)/shard_map/base_terms/pallas_call | solution.py:257
  9.0 0.0 collective-permute-done.1.refs_1_
  9.0 0.0 collective-permute-done.refs_1_.refs_3_
  9.0 1.8 %collective-permute-start.4 = (bf16[512,128]{1,0:T(8,128)(2,1)S(1)}, bf16[512,128]{1,0:T(8,128)(2,1)S(1)}, u32[]{:S(2)}, u32[]{:S(2)}) collective-permute-start(bf16[512,128]{1,0:T(8,128)(2,1)S(1)} %get-tuple-element.33), channel_id=1, source_target_pairs={{0,4},{4,0},{8,12},{12,8},{1,5},{5,1},{9,13},{13,9},{2,6},{6,2},{1... | collective-permute-start | bytes 393224 | tf_op jit(solution)/shard_map/ppermute | solution.py:19
  10.8 0.0 collective-permute-done.2.refs_3_
  10.8 0.0 copy-done.1
  10.8 0.5 %shrink.1.refs_4_ = bf16[32,128]{1,0:T(8,128)(2,1)S(1)} custom-call(s32[1]{0:T(128)} %bitcast.1.batch_at, bf16[32,1152]{1,0:T(8,128)(2,1)S(1)} %get-tuple-element.38.tagged.refs_0_.refs_2_, bf16[32,1152]{1,0:T(8,128)(2,1)S(1)} %collective-permute-done.refs_1_.refs_3_, bf16[4,64,1024]{2,1,0:T(8,128)(2,1)S(1)} %bitcast.9, ...), custom_call_target="tpu_custom_call" | custom-call | flops 67108864 | bytes 1179648 | tf_op jit(solution)/shard_map/shrink/pallas_call | solution.py:317
  11.3 0.0 copy-start
  11.3 0.3 %collective-permute-start.3 = (bf16[32,128]{1,0:T(8,128)(2,1)S(1)}, bf16[32,128]{1,0:T(8,128)(2,1)S(1)}, u32[]{:S(2)}, u32[]{:S(2)}) collective-permute-start(bf16[32,128]{1,0:T(8,128)(2,1)S(1)} %shrink.1.refs_4_), channel_id=1, source_target_pairs={{0,4},{4,0},{8,12},{12,8},{1,5},{5,1},{9,13},{13,9},{2,6},{6,2},{1... | collective-permute-start | bytes 24584 | tf_op jit(solution)/shard_map/ppermute | solution.py:19
  11.7 2.8 %collective-permute-start.5 = (bf16[32,128]{1,0:T(8,128)(2,1)S(1)}, bf16[32,128]{1,0:T(8,128)(2,1)S(1)}, u32[]{:S(2)}, u32[]{:S(2)}) collective-permute-start(bf16[32,128]{1,0:T(8,128)(2,1)S(1)} %shrink.1.refs_4_), channel_id=1, source_target_pairs={{0,8},{4,12},{8,0},{12,4},{1,9},{5,13},{9,1},{13,5},{2,10},{6,14},... | collective-permute-start | bytes 24584 | tf_op jit(solution)/shard_map/ppermute | solution.py:19
  14.4 1.3 %collective-permute-start.6 = (bf16[32,128]{1,0:T(8,128)(2,1)S(1)}, bf16[32,128]{1,0:T(8,128)(2,1)S(1)}, u32[]{:S(2)}, u32[]{:S(2)}) collective-permute-start(bf16[32,128]{1,0:T(8,128)(2,1)S(1)} %shrink.1.refs_4_), channel_id=1, source_target_pairs={{0,12},{4,8},{8,4},{12,0},{1,13},{5,9},{9,5},{13,1},{2,14},{6,10},... | collective-permute-start | bytes 24584 | tf_op jit(solution)/shard_map/ppermute | solution.py:19
  15.8 2.5 %base_terms.4 = bf16[512,128]{1,0:T(8,128)(2,1)S(1)} custom-call(s32[1]{0:T(128)} %bitcast.tensor_at, bf16[32,1152]{1,0:T(8,128)(2,1)S(1)} %get-tuple-element.38.tagged.refs_0_.refs_2_, bf16[1024,8192]{1,0:T(8,128)(2,1)} %out_weight.5), custom_call_target="tpu_custom_call" | custom-call | flops 134217728 | bytes 4194304 | tf_op jit(solution)/shard_map/base_terms/pallas_call | solution.py:257
  18.3 0.0 collective-permute-done.4
  18.3 0.0 collective-permute-done.3.refs_5_
  18.4 1.8 %collective-permute-start.8 = (bf16[512,128]{1,0:T(8,128)(2,1)S(1)}, bf16[512,128]{1,0:T(8,128)(2,1)S(1)}, u32[]{:S(2)}, u32[]{:S(2)}) collective-permute-start(bf16[512,128]{1,0:T(8,128)(2,1)S(1)} %add_convert_fusion), channel_id=1, source_target_pairs={{0,8},{4,12},{8,0},{12,4},{1,9},{5,13},{9,1},{13,5},{2,10},{6,14},... | collective-permute-start | bytes 393224 | tf_op jit(solution)/shard_map/ppermute | solution.py:19
  20.1 1.3 %collective-permute-start.9 = (bf16[512,128]{1,0:T(8,128)(2,1)S(1)}, bf16[512,128]{1,0:T(8,128)(2,1)S(1)}, u32[]{:S(2)}, u32[]{:S(2)}) collective-permute-start(bf16[512,128]{1,0:T(8,128)(2,1)S(1)} %get-tuple-element.41), channel_id=1, source_target_pairs={{0,4},{4,0},{8,12},{12,8},{1,5},{5,1},{9,13},{13,9},{2,6},{6,2},{1... | collective-permute-start | bytes 393224 | tf_op jit(solution)/shard_map/ppermute | solution.py:19
  21.5 0.0 collective-permute-done.5.refs_6_
  21.5 0.0 collective-permute-done.6.refs_7_
  21.5 0.0 collective-permute-done.7
  21.5 0.0 copy-done
  21.5 0.5 %expand.1 = (bf16[512,128]{1,0:T(8,128)(2,1)S(1)}, bf16[512,128]{1,0:T(8,128)(2,1)S(1)}) custom-call(s32[1]{0:T(128)} %bitcast.1.batch_at, s32[8,128]{1,0:T(8,128)S(1)} %get-tuple-element.29.refs_0_, s32[8,128]{1,0:T(8,128)S(1)} %collective-permute-done.1.refs_1_, bf16[32,1152]{1,0:T(8,128)(2,1)S(1)} %get-tuple-element.38.tagged.refs_0_.refs_2_, ...), custom_call_target="tpu_custom_call" | custom-call | flops 134217728 | bytes 1048576 | tf_op jit(solution)/shard_map/expand/pallas_call | solution.py:377
  22.0 1.6 %collective-permute-start.10 = (bf16[512,128]{1,0:T(8,128)(2,1)S(1)}, bf16[512,128]{1,0:T(8,128)(2,1)S(1)}, u32[]{:S(2)}, u32[]{:S(2)}) collective-permute-start(bf16[512,128]{1,0:T(8,128)(2,1)S(1)} %get-tuple-element.42), channel_id=1, source_target_pairs={{0,2},{1,3},{2,0},{3,1},{4,6},{5,7},{6,4},{7,5},{8,10},{9,11},{10,... | collective-permute-start | bytes 393224 | tf_op jit(solution)/shard_map/ppermute | solution.py:19
  23.6 2.5 %base_terms.5.refs_0_ = f32[512,128]{1,0:T(8,128)S(1)} custom-call(s32[1]{0:T(128)} %bitcast.tensor_at, bf16[32,1152]{1,0:T(8,128)(2,1)S(1)} %get-tuple-element.38.tagged.refs_0_.refs_2_, bf16[1024,8192]{1,0:T(8,128)(2,1)} %out_weight.5), custom_call_target="tpu_custom_call" | custom-call | flops 134217728 | bytes 4194304 | tf_op jit(solution)/shard_map/base_terms/pallas_call | solution.py:257
  26.1 0.7 %collective-permute-done.8.refs_2_ = bf16[512,128]{1,0:T(8,128)(2,1)S(1)} collective-permute-done((bf16[512,128]{1,0:T(8,128)(2,1)S(1)}, bf16[512,128]{1,0:T(8,128)(2,1)S(1)}, u32[]{:S(2)}, u32[]{:S(2)}) %collective-permute-start.8) | collective-permute-done | bytes 131104 | tf_op jit(solution)/shard_map/ppermute | solution.py:19
  26.8 0.4 %collective-permute-done.9.refs_1_ = bf16[512,128]{1,0:T(8,128)(2,1)S(1)} collective-permute-done((bf16[512,128]{1,0:T(8,128)(2,1)S(1)}, bf16[512,128]{1,0:T(8,128)(2,1)S(1)}, u32[]{:S(2)}, u32[]{:S(2)}) %collective-permute-start.9) | collective-permute-done | bytes 131104 | tf_op jit(solution)/shard_map/ppermute | solution.py:19
  27.2 0.0 collective-permute-done.10.refs_1_
  27.3 0.7 %total.1 = bf16[32,2048]{1,0:T(8,128)(2,1)} custom-call(f32[512,128]{1,0:T(8,128)S(1)} %partial_total.3.refs_0_, bf16[512,128]{1,0:T(8,128)(2,1)S(1)} %collective-permute-done.10.refs_1_), custom_call_target="tpu_custom_call" | custom-call | flops 131072 | bytes 393216 | tf_op jit(solution)/shard_map/total/pallas_call | solution.py:410
  (3 shorter events, 0.1 us)
Async XLA Ops:
  0.0 21.5 %collective-permute-start.7 = (bf16[4,64,2048]{2,1,0:T(8,128)(2,1)}, bf16[4,64,2048]{2,1,0:T(8,128)(2,1)S(1)}, u32[]{:S(2)}, u32[]{:S(2)}) collective-permute-start(bf16[4,64,2048]{2,1,0:T(8,128)(2,1)} %param.20), channel_id=1, source_target_pairs={{0,1},{1,0},{2,3},{3,2},{4,5},{5,4},{6,7},{7,6},{8,9},{9,8},{10,11... | collective-permute-start | bytes 3145736 | tf_op jit(solution)/shard_map/ppermute | solution.py:19
  0.5 10.3 %collective-permute-start.2 = (bf16[4,64,1024]{2,1,0:T(8,128)(2,1)}, bf16[4,64,1024]{2,1,0:T(8,128)(2,1)S(1)}, u32[]{:S(2)}, u32[]{:S(2)}) collective-permute-start(bf16[4,64,1024]{2,1,0:T(8,128)(2,1)} %bitcast.8), channel_id=1, source_target_pairs={{0,1},{1,0},{2,3},{3,2},{4,5},{5,4},{6,7},{7,6},{8,9},{9,8},{10,11... | collective-permute-start | bytes 1572872 | tf_op jit(solution)/shard_map/ppermute | solution.py:19
  3.4 5.6 %collective-permute-start = (bf16[32,1152]{1,0:T(8,128)(2,1)S(1)}, bf16[32,1152]{1,0:T(8,128)(2,1)S(1)}, u32[]{:S(2)}, u32[]{:S(2)}) collective-permute-start(bf16[32,1152]{1,0:T(8,128)(2,1)S(1)} %get-tuple-element.38.tagged.refs_0_.refs_2_), channel_id=1, source_target_pairs={{0,2},{1,3},{2,0},{3,1},{4,6},{5,7},{6,4},{7,5},{8,10},{9,11},{10,... | collective-permute-start | bytes 221192 | tf_op jit(solution)/shard_map/ppermute | solution.py:19
  6.4 2.6 %collective-permute-start.1 = (s32[8,128]{1,0:T(8,128)S(1)}, s32[8,128]{1,0:T(8,128)S(1)}, u32[]{:S(2)}, u32[]{:S(2)}) collective-permute-start(s32[8,128]{1,0:T(8,128)S(1)} %get-tuple-element.29.refs_0_), channel_id=1, source_target_pairs={{0,1},{1,0},{2,3},{3,2},{4,5},{5,4},{6,7},{7,6},{8,9},{9,8},{10,11... | collective-permute-start | bytes 12296 | tf_op jit(solution)/shard_map/ppermute | solution.py:19
  6.4 4.4 %copy-start.1 = (bf16[4,1024,64]{1,2,0:T(8,128)(2,1)S(1)}, bf16[4,1024,64]{1,2,0:T(8,128)(2,1)}, u32[]{:S(2)}) copy-start(bf16[4,1024,64]{1,2,0:T(8,128)(2,1)} %param.19) | copy-start | bytes 1572868
  9.0 9.3 %collective-permute-start.4 = (bf16[512,128]{1,0:T(8,128)(2,1)S(1)}, bf16[512,128]{1,0:T(8,128)(2,1)S(1)}, u32[]{:S(2)}, u32[]{:S(2)}) collective-permute-start(bf16[512,128]{1,0:T(8,128)(2,1)S(1)} %get-tuple-element.33), channel_id=1, source_target_pairs={{0,4},{4,0},{8,12},{12,8},{1,5},{5,1},{9,13},{13,9},{2,6},{6,2},{1... | collective-permute-start | bytes 393224 | tf_op jit(solution)/shard_map/ppermute | solution.py:19
  11.3 10.2 %copy-start = (bf16[4,64,2048]{2,1,0:T(8,128)(2,1)S(1)}, bf16[4,64,2048]{2,1,0:T(8,128)(2,1)}, u32[]{:S(2)}) copy-start(bf16[4,64,2048]{2,1,0:T(8,128)(2,1)} %param.20) | copy-start | bytes 3145732
  11.3 7.0 %collective-permute-start.3 = (bf16[32,128]{1,0:T(8,128)(2,1)S(1)}, bf16[32,128]{1,0:T(8,128)(2,1)S(1)}, u32[]{:S(2)}, u32[]{:S(2)}) collective-permute-start(bf16[32,128]{1,0:T(8,128)(2,1)S(1)} %shrink.1.refs_4_), channel_id=1, source_target_pairs={{0,4},{4,0},{8,12},{12,8},{1,5},{5,1},{9,13},{13,9},{2,6},{6,2},{1... | collective-permute-start | bytes 24584 | tf_op jit(solution)/shard_map/ppermute | solution.py:19
  11.7 9.8 %collective-permute-start.5 = (bf16[32,128]{1,0:T(8,128)(2,1)S(1)}, bf16[32,128]{1,0:T(8,128)(2,1)S(1)}, u32[]{:S(2)}, u32[]{:S(2)}) collective-permute-start(bf16[32,128]{1,0:T(8,128)(2,1)S(1)} %shrink.1.refs_4_), channel_id=1, source_target_pairs={{0,8},{4,12},{8,0},{12,4},{1,9},{5,13},{9,1},{13,5},{2,10},{6,14},... | collective-permute-start | bytes 24584 | tf_op jit(solution)/shard_map/ppermute | solution.py:19
  14.4 7.0 %collective-permute-start.6 = (bf16[32,128]{1,0:T(8,128)(2,1)S(1)}, bf16[32,128]{1,0:T(8,128)(2,1)S(1)}, u32[]{:S(2)}, u32[]{:S(2)}) collective-permute-start(bf16[32,128]{1,0:T(8,128)(2,1)S(1)} %shrink.1.refs_4_), channel_id=1, source_target_pairs={{0,12},{4,8},{8,4},{12,0},{1,13},{5,9},{9,5},{13,1},{2,14},{6,10},... | collective-permute-start | bytes 24584 | tf_op jit(solution)/shard_map/ppermute | solution.py:19
  18.4 8.4 %collective-permute-start.8 = (bf16[512,128]{1,0:T(8,128)(2,1)S(1)}, bf16[512,128]{1,0:T(8,128)(2,1)S(1)}, u32[]{:S(2)}, u32[]{:S(2)}) collective-permute-start(bf16[512,128]{1,0:T(8,128)(2,1)S(1)} %add_convert_fusion), channel_id=1, source_target_pairs={{0,8},{4,12},{8,0},{12,4},{1,9},{5,13},{9,1},{13,5},{2,10},{6,14},... | collective-permute-start | bytes 393224 | tf_op jit(solution)/shard_map/ppermute | solution.py:19
  20.1 7.1 %collective-permute-start.9 = (bf16[512,128]{1,0:T(8,128)(2,1)S(1)}, bf16[512,128]{1,0:T(8,128)(2,1)S(1)}, u32[]{:S(2)}, u32[]{:S(2)}) collective-permute-start(bf16[512,128]{1,0:T(8,128)(2,1)S(1)} %get-tuple-element.41), channel_id=1, source_target_pairs={{0,4},{4,0},{8,12},{12,8},{1,5},{5,1},{9,13},{13,9},{2,6},{6,2},{1... | collective-permute-start | bytes 393224 | tf_op jit(solution)/shard_map/ppermute | solution.py:19
  22.0 5.2 %collective-permute-start.10 = (bf16[512,128]{1,0:T(8,128)(2,1)S(1)}, bf16[512,128]{1,0:T(8,128)(2,1)S(1)}, u32[]{:S(2)}, u32[]{:S(2)}) collective-permute-start(bf16[512,128]{1,0:T(8,128)(2,1)S(1)} %get-tuple-element.42), channel_id=1, source_target_pairs={{0,2},{1,3},{2,0},{3,1},{4,6},{5,7},{6,4},{7,5},{8,10},{9,11},{10,... | collective-permute-start | bytes 393224 | tf_op jit(solution)/shard_map/ppermute | solution.py:19

commit v24 on v22

--- a/solution.py
+++ b/solution.py
@@ -251,7 +251,7 @@
 def base_block(tensor_at, tagged, out_weight, block, ahead, early=(), arrived=()):
     rows = tagged.shape[0]
     width = out_weight.shape[0]
-    deep, deep_rows = 4, min(width, 256)
+    deep, deep_rows = 8, min(width, 128)
     whole = pl.BlockSpec(memory_space=VMEM)
     count = 1 + len(early)
     return pl.pallas_call(

time: 27.1 us -> 27.3 us (level)
  waiting for transfers between devices: 2.76 us -> 3.09 us
    ppermute x10, waiting for transfers between devices: 2.76 us -> 3.09 us  [permuted(): return lax.ppermute(array, axis, [(i, partner(i)) for i in range(size)])]
  transfers between devices with their start and end apart: 10 -> 10, of which waited for: 2 -> 2; matrix products, arithmetic and copies ran while one was open for 0% -> 0% of each run, Pallas kernels for 43% -> 42%
where the time goes in v24:
time: 27.3 us; the launch traced here: 27.2 us
  Pallas kernels  12.2 us (45%)
  starting transfers between devices  11.8 us (43%)
  waiting for transfers between devices  3.09 us (11%)
    ppermute x10, starting transfers between devices, permuted(): return lax.ppermute(array, axis, [(i, partner(i)) for i in range(size)])  11.8 us
    pallas_call x3, Pallas kernels, base_block(): pl.pallas_call(functools.partial(base_kernel, ahead, deep, len(arrived)),...  7.52 us
    ppermute x10, waiting for transfers between devices, permuted(): return lax.ppermute(array, axis, [(i, partner(i)) for i in range(size)])  3.09 us
    pallas_call x1, Pallas kernels, attend(): pl.pallas_call(functools.partial(attend_kernel, parts, rank_width), out_s...  2.83 us
    pallas_call x1, Pallas kernels, total(): pl.pallas_call(total_kernel, out_shape=jax.ShapeDtypeStruct((rows, block)...  0.69 us
  transfers between devices with their start and end apart: 10, of which 2 were waited for; matrix products, arithmetic and copies ran while one was open for 0% of the time, Pallas kernels for 42%

profile of v24, /device:TPU:0, one launch (start us, length us, event | category | flops | bytes accessed | tf_op | source)
XLA Modules:
  0.0 27.2 jit_solution(7959662044229020049)
XLA Ops:
  0.0 0.5 %collective-permute-start.6 = (bf16[4,64,2048]{2,1,0:T(8,128)(2,1)}, bf16[4,64,2048]{2,1,0:T(8,128)(2,1)S(1)}, u32[]{:S(2)}, u32[]{:S(2)}) collective-permute-start(bf16[4,64,2048]{2,1,0:T(8,128)(2,1)} %param.20), channel_id=1, source_target_pairs={{0,1},{1,0},{2,3},{3,2},{4,5},{5,4},{6,7},{7,6},{8,9},{9,8},{10,11... | collective-permute-start | bytes 3145736 | tf_op jit(solution)/shard_map/ppermute | solution.py:19
  0.5 0.1 collective-permute-start.2
  0.5 2.8 %attention.1 = (bf16[32,1152]{1,0:T(8,128)(2,1)S(1)}, bf16[1024,2048]{1,0:T(8,128)(2,1)S(1)}, s32[8,128]{1,0:T(8,128)S(1)}) custom-call(s32[1]{0:T(128)} %bitcast.2.group_at, s32[1]{0:T(128)S(6)} %xor.3.early_at, bf16[32,4,96,128]{3,2,1,0:T(8,128)(2,1)} %refs_0_.1, bf16[32,4,96,128]{3,2,1,0:T(8,128)(2,1)} %refs_1_.1, bf16[32,8,128]{2,1,0:T(8,128)(2,1)} %refs_2_.1, ...), custom_call_target="tpu_custom_call" | custom-call | flops 12582912 | bytes 1572864 | tf_op jit(solution)/shard_map/attention/pallas_call | solution.py:147
  3.4 3.0 %collective-permute-start = (bf16[32,1152]{1,0:T(8,128)(2,1)S(1)}, bf16[32,1152]{1,0:T(8,128)(2,1)S(1)}, u32[]{:S(2)}, u32[]{:S(2)}) collective-permute-start(bf16[32,1152]{1,0:T(8,128)(2,1)S(1)} %get-tuple-element.42.tagged.refs_0_.refs_2_), channel_id=1, source_target_pairs={{0,2},{1,3},{2,0},{3,1},{4,6},{5,7},{6,4},{7,5},{8,10},{9,11},{10,... | collective-permute-start | bytes 221192 | tf_op jit(solution)/shard_map/ppermute | solution.py:19
  6.4 0.0 collective-permute-start.1
  6.4 0.0 copy-start.1
  6.4 2.7 %base_terms.3 = (bf16[512,128]{1,0:T(8,128)(2,1)S(1)}, bf16[512,128]{1,0:T(8,128)(2,1)S(1)}) custom-call(s32[1]{0:T(128)} %bitcast.tensor_at, bf16[32,1152]{1,0:T(8,128)(2,1)S(1)} %get-tuple-element.42.tagged.refs_0_.refs_2_, bf16[1024,8192]{1,0:T(8,128)(2,1)} %out_weight.5, bf16[1024,2048]{1,0:T(8,128)(2,1)S(1)} %get-tuple-element.27.refs_0_), custom_call_target="tpu_custom_call" | custom-call | flops 268435456 | bytes 8388608 | tf_op jit(solution)/shard_map/base_terms/pallas_call | solution.py:257
  9.0 0.0 collective-permute-done.1.refs_1_
  9.0 0.0 collective-permute-done.refs_1_.refs_3_
  9.1 1.7 %collective-permute-start.4 = (bf16[512,128]{1,0:T(8,128)(2,1)S(1)}, bf16[512,128]{1,0:T(8,128)(2,1)S(1)}, u32[]{:S(2)}, u32[]{:S(2)}) collective-permute-start(bf16[512,128]{1,0:T(8,128)(2,1)S(1)} %get-tuple-element.35), channel_id=1, source_target_pairs={{0,4},{4,0},{8,12},{12,8},{1,5},{5,1},{9,13},{13,9},{2,6},{6,2},{1... | collective-permute-start | bytes 393224 | tf_op jit(solution)/shard_map/ppermute | solution.py:19
  10.8 0.0 collective-permute-done.2.refs_3_
  10.8 0.0 copy-done.1
  10.8 0.5 %shrink.1 = bf16[32,128]{1,0:T(8,128)(2,1)S(1)} custom-call(s32[1]{0:T(128)} %bitcast.1.batch_at, bf16[32,1152]{1,0:T(8,128)(2,1)S(1)} %get-tuple-element.42.tagged.refs_0_.refs_2_, bf16[32,1152]{1,0:T(8,128)(2,1)S(1)} %collective-permute-done.refs_1_.refs_3_, bf16[4,64,1024]{2,1,0:T(8,128)(2,1)S(1)} %bitcast.9, ...), custom_call_target="tpu_custom_call" | custom-call | flops 67108864 | bytes 1179648 | tf_op jit(solution)/shard_map/shrink/pallas_call | solution.py:317
  11.3 0.0 copy-start
  11.3 0.4 %collective-permute-start.3 = (bf16[32,128]{1,0:T(8,128)(2,1)S(1)}, bf16[32,128]{1,0:T(8,128)(2,1)S(1)}, u32[]{:S(2)}, u32[]{:S(2)}) collective-permute-start(bf16[32,128]{1,0:T(8,128)(2,1)S(1)} %shrink.1), channel_id=1, source_target_pairs={{0,4},{4,0},{8,12},{12,8},{1,5},{5,1},{9,13},{13,9},{2,6},{6,2},{1... | collective-permute-start | bytes 24584 | tf_op jit(solution)/shard_map/ppermute | solution.py:19
  11.7 2.4 %base_terms.4 = bf16[512,128]{1,0:T(8,128)(2,1)S(1)} custom-call(s32[1]{0:T(128)} %bitcast.tensor_at, bf16[32,1152]{1,0:T(8,128)(2,1)S(1)} %get-tuple-element.42.tagged.refs_0_.refs_2_, bf16[1024,8192]{1,0:T(8,128)(2,1)} %out_weight.5), custom_call_target="tpu_custom_call" | custom-call | flops 134217728 | bytes 4194304 | tf_op jit(solution)/shard_map/base_terms/pallas_call | solution.py:257
  14.2 0.9 %collective-permute-done.4 = bf16[512,128]{1,0:T(8,128)(2,1)S(1)} collective-permute-done((bf16[512,128]{1,0:T(8,128)(2,1)S(1)}, bf16[512,128]{1,0:T(8,128)(2,1)S(1)}, u32[]{:S(2)}, u32[]{:S(2)}) %collective-permute-start.4) | collective-permute-done | bytes 131104 | tf_op jit(solution)/shard_map/ppermute | solution.py:19
  15.2 0.0 collective-permute-done.3
  15.2 2.6 %collective-permute-start.5 = (bf16[32,128]{1,0:T(8,128)(2,1)S(1)}, bf16[32,128]{1,0:T(8,128)(2,1)S(1)}, u32[]{:S(2)}, u32[]{:S(2)}) collective-permute-start(bf16[32,128]{1,0:T(8,128)(2,1)S(1)} %add_convert_fusion.1.refs_4_), channel_id=1, source_target_pairs={{0,8},{4,12},{8,0},{12,4},{1,9},{5,13},{9,1},{13,5},{2,10},{6,14},... | collective-permute-start | bytes 24584 | tf_op jit(solution)/shard_map/ppermute | solution.py:19
  17.9 0.3 %collective-permute-start.7 = (bf16[512,128]{1,0:T(8,128)(2,1)S(1)}, bf16[512,128]{1,0:T(8,128)(2,1)S(1)}, u32[]{:S(2)}, u32[]{:S(2)}) collective-permute-start(bf16[512,128]{1,0:T(8,128)(2,1)S(1)} %add_convert_fusion), channel_id=1, source_target_pairs={{0,8},{4,12},{8,0},{12,4},{1,9},{5,13},{9,1},{13,5},{2,10},{6,14},... | collective-permute-start | bytes 393224 | tf_op jit(solution)/shard_map/ppermute | solution.py:19
  18.2 1.6 %collective-permute-start.8 = (bf16[512,128]{1,0:T(8,128)(2,1)S(1)}, bf16[512,128]{1,0:T(8,128)(2,1)S(1)}, u32[]{:S(2)}, u32[]{:S(2)}) collective-permute-start(bf16[512,128]{1,0:T(8,128)(2,1)S(1)} %get-tuple-element.45), channel_id=1, source_target_pairs={{0,4},{4,0},{8,12},{12,8},{1,5},{5,1},{9,13},{13,9},{2,6},{6,2},{1... | collective-permute-start | bytes 393224 | tf_op jit(solution)/shard_map/ppermute | solution.py:19
  19.8 0.0 collective-permute-done.5.refs_5_
  19.8 0.0 collective-permute-done.6
  19.8 0.0 copy-done
  19.8 0.5 %expand.1 = (bf16[512,128]{1,0:T(8,128)(2,1)S(1)}, bf16[512,128]{1,0:T(8,128)(2,1)S(1)}) custom-call(s32[1]{0:T(128)} %bitcast.1.batch_at, s32[8,128]{1,0:T(8,128)S(1)} %get-tuple-element.31.refs_0_, s32[8,128]{1,0:T(8,128)S(1)} %collective-permute-done.1.refs_1_, bf16[32,1152]{1,0:T(8,128)(2,1)S(1)} %get-tuple-element.42.tagged.refs_0_.refs_2_, ...), custom_call_target="tpu_custom_call" | custom-call | flops 134217728 | bytes 1048576 | tf_op jit(solution)/shard_map/expand/pallas_call | solution.py:377
  20.3 1.5 %collective-permute-start.9 = (bf16[512,128]{1,0:T(8,128)(2,1)S(1)}, bf16[512,128]{1,0:T(8,128)(2,1)S(1)}, u32[]{:S(2)}, u32[]{:S(2)}) collective-permute-start(bf16[512,128]{1,0:T(8,128)(2,1)S(1)} %get-tuple-element.46), channel_id=1, source_target_pairs={{0,2},{1,3},{2,0},{3,1},{4,6},{5,7},{6,4},{7,5},{8,10},{9,11},{10,... | collective-permute-start | bytes 393224 | tf_op jit(solution)/shard_map/ppermute | solution.py:19
  21.9 2.4 %base_terms.5.refs_0_ = f32[512,128]{1,0:T(8,128)S(1)} custom-call(s32[1]{0:T(128)} %bitcast.tensor_at, bf16[32,1152]{1,0:T(8,128)(2,1)S(1)} %get-tuple-element.42.tagged.refs_0_.refs_2_, bf16[1024,8192]{1,0:T(8,128)(2,1)} %out_weight.5), custom_call_target="tpu_custom_call" | custom-call | flops 134217728 | bytes 4194304 | tf_op jit(solution)/shard_map/base_terms/pallas_call | solution.py:257
  24.3 2.1 %collective-permute-done.7.refs_2_ = bf16[512,128]{1,0:T(8,128)(2,1)S(1)} collective-permute-done((bf16[512,128]{1,0:T(8,128)(2,1)S(1)}, bf16[512,128]{1,0:T(8,128)(2,1)S(1)}, u32[]{:S(2)}, u32[]{:S(2)}) %collective-permute-start.7) | collective-permute-done | bytes 131104 | tf_op jit(solution)/shard_map/ppermute | solution.py:19
  26.4 0.0 collective-permute-done.8.refs_1_
  26.5 0.0 collective-permute-done.9.refs_1_
  26.5 0.7 %total.1 = bf16[32,2048]{1,0:T(8,128)(2,1)} custom-call(f32[512,128]{1,0:T(8,128)S(1)} %partial_total.3.refs_0_, bf16[512,128]{1,0:T(8,128)(2,1)S(1)} %collective-permute-done.9.refs_1_), custom_call_target="tpu_custom_call" | custom-call | flops 131072 | bytes 393216 | tf_op jit(solution)/shard_map/total/pallas_call | solution.py:410
  (4 shorter events, 0.1 us)
Async XLA Ops:
  0.0 19.8 %collective-permute-start.6 = (bf16[4,64,2048]{2,1,0:T(8,128)(2,1)}, bf16[4,64,2048]{2,1,0:T(8,128)(2,1)S(1)}, u32[]{:S(2)}, u32[]{:S(2)}) collective-permute-start(bf16[4,64,2048]{2,1,0:T(8,128)(2,1)} %param.20), channel_id=1, source_target_pairs={{0,1},{1,0},{2,3},{3,2},{4,5},{5,4},{6,7},{7,6},{8,9},{9,8},{10,11... | collective-permute-start | bytes 3145736 | tf_op jit(solution)/shard_map/ppermute | solution.py:19
  0.5 10.3 %collective-permute-start.2 = (bf16[4,64,1024]{2,1,0:T(8,128)(2,1)}, bf16[4,64,1024]{2,1,0:T(8,128)(2,1)S(1)}, u32[]{:S(2)}, u32[]{:S(2)}) collective-permute-start(bf16[4,64,1024]{2,1,0:T(8,128)(2,1)} %bitcast.8), channel_id=1, source_target_pairs={{0,1},{1,0},{2,3},{3,2},{4,5},{5,4},{6,7},{7,6},{8,9},{9,8},{10,11... | collective-permute-start | bytes 1572872 | tf_op jit(solution)/shard_map/ppermute | solution.py:19
  3.4 5.7 %collective-permute-start = (bf16[32,1152]{1,0:T(8,128)(2,1)S(1)}, bf16[32,1152]{1,0:T(8,128)(2,1)S(1)}, u32[]{:S(2)}, u32[]{:S(2)}) collective-permute-start(bf16[32,1152]{1,0:T(8,128)(2,1)S(1)} %get-tuple-element.42.tagged.refs_0_.refs_2_), channel_id=1, source_target_pairs={{0,2},{1,3},{2,0},{3,1},{4,6},{5,7},{6,4},{7,5},{8,10},{9,11},{10,... | collective-permute-start | bytes 221192 | tf_op jit(solution)/shard_map/ppermute | solution.py:19
  6.4 2.7 %collective-permute-start.1 = (s32[8,128]{1,0:T(8,128)S(1)}, s32[8,128]{1,0:T(8,128)S(1)}, u32[]{:S(2)}, u32[]{:S(2)}) collective-permute-start(s32[8,128]{1,0:T(8,128)S(1)} %get-tuple-element.31.refs_0_), channel_id=1, source_target_pairs={{0,1},{1,0},{2,3},{3,2},{4,5},{5,4},{6,7},{7,6},{8,9},{9,8},{10,11... | collective-permute-start | bytes 12296 | tf_op jit(solution)/shard_map/ppermute | solution.py:19
  6.4 4.4 %copy-start.1 = (bf16[4,1024,64]{1,2,0:T(8,128)(2,1)S(1)}, bf16[4,1024,64]{1,2,0:T(8,128)(2,1)}, u32[]{:S(2)}) copy-start(bf16[4,1024,64]{1,2,0:T(8,128)(2,1)} %param.19) | copy-start | bytes 1572868
  9.1 6.1 %collective-permute-start.4 = (bf16[512,128]{1,0:T(8,128)(2,1)S(1)}, bf16[512,128]{1,0:T(8,128)(2,1)S(1)}, u32[]{:S(2)}, u32[]{:S(2)}) collective-permute-start(bf16[512,128]{1,0:T(8,128)(2,1)S(1)} %get-tuple-element.35), channel_id=1, source_target_pairs={{0,4},{4,0},{8,12},{12,8},{1,5},{5,1},{9,13},{13,9},{2,6},{6,2},{1... | collective-permute-start | bytes 393224 | tf_op jit(solution)/shard_map/ppermute | solution.py:19
  11.3 8.5 %copy-start = (bf16[4,64,2048]{2,1,0:T(8,128)(2,1)S(1)}, bf16[4,64,2048]{2,1,0:T(8,128)(2,1)}, u32[]{:S(2)}) copy-start(bf16[4,64,2048]{2,1,0:T(8,128)(2,1)} %param.20) | copy-start | bytes 3145732
  11.3 3.9 %collective-permute-start.3 = (bf16[32,128]{1,0:T(8,128)(2,1)S(1)}, bf16[32,128]{1,0:T(8,128)(2,1)S(1)}, u32[]{:S(2)}, u32[]{:S(2)}) collective-permute-start(bf16[32,128]{1,0:T(8,128)(2,1)S(1)} %shrink.1), channel_id=1, source_target_pairs={{0,4},{4,0},{8,12},{12,8},{1,5},{5,1},{9,13},{13,9},{2,6},{6,2},{1... | collective-permute-start | bytes 24584 | tf_op jit(solution)/shard_map/ppermute | solution.py:19
  15.2 4.6 %collective-permute-start.5 = (bf16[32,128]{1,0:T(8,128)(2,1)S(1)}, bf16[32,128]{1,0:T(8,128)(2,1)S(1)}, u32[]{:S(2)}, u32[]{:S(2)}) collective-permute-start(bf16[32,128]{1,0:T(8,128)(2,1)S(1)} %add_convert_fusion.1.refs_4_), channel_id=1, source_target_pairs={{0,8},{4,12},{8,0},{12,4},{1,9},{5,13},{9,1},{13,5},{2,10},{6,14},... | collective-permute-start | bytes 24584 | tf_op jit(solution)/shard_map/ppermute | solution.py:19
  17.9 8.5 %collective-permute-start.7 = (bf16[512,128]{1,0:T(8,128)(2,1)S(1)}, bf16[512,128]{1,0:T(8,128)(2,1)S(1)}, u32[]{:S(2)}, u32[]{:S(2)}) collective-permute-start(bf16[512,128]{1,0:T(8,128)(2,1)S(1)} %add_convert_fusion), channel_id=1, source_target_pairs={{0,8},{4,12},{8,0},{12,4},{1,9},{5,13},{9,1},{13,5},{2,10},{6,14},... | collective-permute-start | bytes 393224 | tf_op jit(solution)/shard_map/ppermute | solution.py:19
  18.2 8.2 %collective-permute-start.8 = (bf16[512,128]{1,0:T(8,128)(2,1)S(1)}, bf16[512,128]{1,0:T(8,128)(2,1)S(1)}, u32[]{:S(2)}, u32[]{:S(2)}) collective-permute-start(bf16[512,128]{1,0:T(8,128)(2,1)S(1)} %get-tuple-element.45), channel_id=1, source_target_pairs={{0,4},{4,0},{8,12},{12,8},{1,5},{5,1},{9,13},{13,9},{2,6},{6,2},{1... | collective-permute-start | bytes 393224 | tf_op jit(solution)/shard_map/ppermute | solution.py:19
  20.3 6.1 %collective-permute-start.9 = (bf16[512,128]{1,0:T(8,128)(2,1)S(1)}, bf16[512,128]{1,0:T(8,128)(2,1)S(1)}, u32[]{:S(2)}, u32[]{:S(2)}) collective-permute-start(bf16[512,128]{1,0:T(8,128)(2,1)S(1)} %get-tuple-element.46), channel_id=1, source_target_pairs={{0,2},{1,3},{2,0},{3,1},{4,6},{5,7},{6,4},{7,5},{8,10},{9,11},{10,... | collective-permute-start | bytes 393224 | tf_op jit(solution)/shard_map/ppermute | solution.py:19
